TPU v7x, 32 devices: a whole 2x2x4 slice. The times are simulated.
32 devices in a mesh: dp: 2 (over y), ha: 4 (over x, core), wa: 4 (over z).
Axes of the slice: x: 2, y: 2, z: 4, core: 2. Of those that a mesh axis runs over, the one named last changes fastest.
Arguments:
- latents: bfloat16 [2, 64, 32, 1280], P('dp', 'ha', 'wa'), may hold values from -40 to 40
- norm_gain: float32 [1280], replicated, may hold values from 0.5 to 1.5
- norm_shift: float32 [1280], replicated, may hold values from -3 to 3
- conv_weight: bfloat16 [3, 3, 1280, 640], P(None, None, 'dp'), may hold values from -0.0546875 to 0.0546875
- conv_bias: float32 [640], replicated, may hold values from -3 to 3
- cotangent: bfloat16 [2, 64, 32, 640], P('dp', 'ha', 'wa'), may hold values from -12 to 12
Outputs:
- conv_out: bfloat16 [2, 64, 32, 640], P('dp', 'ha', 'wa')
- grad_latents: bfloat16 [2, 64, 32, 1280], P('dp', 'ha', 'wa')
All inputs are finite; a program needn't handle non-finite values.
Results may differ from a plain program's by a relative error of at most 0.0044.
Values may be sent and summed in bfloat16 or wider, within the bound.
No kernel may reach another device: no remote copies, remote signals or barrier semaphores. Data moves between devices by JAX's collectives and lax.ppermute only.
A program may use at most 64 MiB of HBM per device.

v0:
```python
import jax
import jax.numpy as jnp
from jax import lax
from jax.sharding import PartitionSpec as P

GROUPS = 32


def padded_2(cells, sides, width):
    for axis, dim in sides:
        count = lax.axis_size(axis)
        ends = count - 1
        head = lax.slice_in_dim(cells, 0, width, axis=dim)
        tail = lax.slice_in_dim(cells, cells.shape[dim] - width, cells.shape[dim], axis=dim)
        cells = jnp.concatenate(
            [
                lax.ppermute(tail, axis, [(i, (i + 1) % count) for i in range(ends)]),
                cells,
                lax.ppermute(head, axis, [((i + 1) % count, i) for i in range(ends)]),
            ],
            axis=dim,
        )
    return cells


def forward_taps(padded, kernel, rows, cols):
    total = None
    for ky in range(3):
        for kx in range(3):
            window = padded[:, ky : ky + rows, kx : kx + cols, :].reshape(-1, padded.shape[3])
            term = jnp.dot(window, kernel[ky, kx], preferred_element_type=jnp.float32)
            total = term if total is None else total + term
    return total


def backward_taps(padded, kernel, rows, cols):
    total = None
    for ky in range(3):
        for kx in range(3):
            window = padded[:, ky : ky + rows, kx : kx + cols, :].reshape(-1, padded.shape[3])
            term = lax.dot_general(
                window,
                kernel[2 - ky, 2 - kx],
                (((1,), (1,)), ((), ())),
                preferred_element_type=jnp.float32,
            )
            total = term if total is None else total + term
    return total


def body(latents, norm_gain, norm_shift, conv_weight, conv_bias, cotangent):
    images, rows, cols, chans = latents.shape
    per_group = chans // GROUPS
    count = rows * cols * per_group * lax.axis_size("ha") * lax.axis_size("wa")
    xg = latents.astype(jnp.float32).reshape(images, rows, cols, GROUPS, per_group)
    total = lax.psum(jnp.sum(xg, axis=(1, 2, 4)), ("ha", "wa"))
    group_mean = (total / count)[:, None, None, :, None]
    centered_input = xg - group_mean
    spread = lax.psum(jnp.sum(centered_input * centered_input, axis=(1, 2, 4)), ("ha", "wa"))
    var = (spread / count)[:, None, None, :, None]
    inverse_deviation = lax.rsqrt(var + 1e-05)
    normalized_input = centered_input * inverse_deviation
    group_gains = norm_gain.reshape(GROUPS, per_group)
    group_shifts = norm_shift.reshape(GROUPS, per_group)
    preactivation_value = normalized_input * group_gains + group_shifts
    sig = jax.nn.sigmoid(preactivation_value)
    act = (preactivation_value * sig).astype(jnp.bfloat16).reshape(images, rows, cols, chans)
    padded = padded_2(act, (("ha", 1), ("wa", 2)), 1)
    cot_padded = padded_2(cotangent, (("ha", 1), ("wa", 2)), 1)
    outs = conv_weight.shape[3]
    full_kernel = lax.all_gather(conv_weight, "dp", axis=2, tiled=True)
    summed = forward_taps(padded, full_kernel, rows, cols)
    grad_act = backward_taps(cot_padded, full_kernel, rows, cols)
    conv_out = (summed + conv_bias).astype(jnp.bfloat16).reshape(images, rows, cols, outs)
    grad_act = grad_act.reshape(images, rows, cols, GROUPS, per_group)
    normalized_gradient = grad_act * sig * (1.0 + preactivation_value * (1.0 - sig)) * group_gains
    first_moment, second_moment = lax.psum(
        (
            jnp.sum(normalized_gradient, axis=(1, 2, 4)),
            jnp.sum(normalized_gradient * normalized_input, axis=(1, 2, 4)),
        ),
        ("ha", "wa"),
    )
    first_moment = (first_moment / count)[:, None, None, :, None]
    second_moment = (second_moment / count)[:, None, None, :, None]
    input_gradient = inverse_deviation * (
        normalized_gradient - first_moment - normalized_input * second_moment
    )
    return (conv_out, input_gradient.reshape(images, rows, cols, chans).astype(jnp.bfloat16))


def solution(mesh):
    return jax.shard_map(
        body,
        mesh=mesh,
        in_specs=(
            P("dp", "ha", "wa", None),
            P(),
            P(),
            P(None, None, "dp", None),
            P(),
            P("dp", "ha", "wa", None),
        ),
        out_specs=(P("dp", "ha", "wa", None), P("dp", "ha", "wa", None)),
        check_vma=False,
    )
```

profile of v0, /device:TPU:0, one launch (start us, length us, event | category | flops | bytes accessed | tf_op | source)
XLA Modules:
  0.0 278.3 jit_solution(8089752161083231889)
XLA Ops:
  8.1 1.3 collective-permute-start.5
  9.4 3.0 %collective-permute-start.4 = (bf16[1,1,8,640]{3,2,1,0:T(8,128)(2,1)S(1)}, bf16[1,1,8,640]{3,2,1,0:T(8,128)(2,1)S(1)}, u32[]{:S(2)}, u32[]{:S(2)}) collective-permute-start(bf16[1,1,8,640]{3,2,1,0:T(8,128)(2,1)S(1)} %get-tuple-element.17), channel_id=1, source_target_pairs={{0,4},{4,8},{8,12},{1,5},{5,9},{9,13},{2,6},{6,10},{10,14},{3,7},{... | collective-permute-start | bytes 30728 | tf_op jit(solution)/shard_map/ppermute | solution.py:17
  12.7 34.7 %psum.28 = f32[1,32]{1,0:T(1,128)S(1)} all-reduce(f32[1,32]{1,0:T(1,128)S(1)} %bitcast.172), channel_id=1, replica_groups=mesh['dp'=2,'ha'=4,'wa'=4] {'ha','wa'}, use_global_device_ids=true, to_apply=%region_2.0 | all-reduce | flops 32 | bytes 256 | tf_op jit(solution)/shard_map/psum | solution.py:56
  47.9 29.7 %psum.29 = f32[1,32]{1,0:T(1,128)S(1)} all-reduce(f32[1,32]{1,0:T(1,128)S(1)} %bitcast.173), channel_id=1, replica_groups=mesh['dp'=2,'ha'=4,'wa'=4] {'ha','wa'}, use_global_device_ids=true, to_apply=%region_5.0 | all-reduce | flops 32 | bytes 256 | tf_op jit(solution)/shard_map/psum | solution.py:59
  77.8 4.2 %collective-permute-start.6 = (bf16[1,18,1,640]{3,2,1,0:T(2,128)(2,1)S(1)}, bf16[1,18,1,640]{3,2,1,0:T(2,128)(2,1)S(1)}, u32[]{:S(2)}, u32[]{:S(2)}) collective-permute-start(bf16[1,18,1,640]{3,2,1,0:T(2,128)(2,1)S(1)} %get-tuple-element.14), channel_id=1, source_target_pairs={{0,1},{1,2},{2,3},{4,5},{5,6},{6,7},{8,9},{9,10},{10,11},{12,13},{... | collective-permute-start | bytes 69128 | tf_op jit(solution)/shard_map/ppermute | solution.py:17
  82.0 1.3 collective-permute-start.7
  83.3 105.1 %all-gather.2.cloned.1.call-done = bf16[3,3,1280,640]{3,2,1,0:T(8,128)(2,1)} async-done(((bf16[3,3,640,640]{3,2,1,0:T(8,128)(2,1)}), bf16[3,3,1280,640]{3,2,1,0:T(8,128)(2,1)}) %all-gather.2.cloned.1.call-update) | async-done | bytes 14745616 | tf_op jit(solution)/shard_map/all_gather | solution.py:71
  188.4 2.0 fusion.4
  190.5 2.0 fusion.11
  192.5 2.0 fusion.2
  194.6 2.0 convolution_add_fusion.5
  196.6 2.0 convolution_add_fusion.4
  198.6 2.0 convolution_add_fusion.3
  200.7 2.0 convolution_add_fusion.2
  202.7 2.0 convolution_add_fusion.1
  204.8 2.2 fusion.101
  207.4 33.4 %all-reduce = (f32[1,32]{1,0:T(1,128)S(1)}, f32[1,32]{1,0:T(1,128)S(1)}) all-reduce(f32[1,32]{1,0:T(1,128)S(1)} %bitcast.171, f32[1,32]{1,0:T(1,128)S(1)} %bitcast.170), channel_id=1, replica_groups=mesh['dp'=2,'ha'=4,'wa'=4] {'ha','wa'}, use_global_device_ids=true, to_apply=%region_11.12 | all-reduce | flops 64 | bytes 512 | tf_op jit(solution)/shard_map/psum | solution.py:77
  242.3 1.3 collective-permute-start
  243.6 1.3 collective-permute-start.1
  244.9 2.6 collective-permute-done.1
  247.6 1.3 collective-permute-start.2
  249.0 1.3 collective-permute-start.3
  250.3 1.9 fusion.5
  252.2 3.3 %collective-permute-done.3 = bf16[1,18,1,1280]{3,2,1,0:T(2,128)(2,1)S(1)} collective-permute-done((bf16[1,18,1,1280]{3,2,1,0:T(2,128)(2,1)S(1)}, bf16[1,18,1,1280]{3,2,1,0:T(2,128)(2,1)S(1)}, u32[]{:S(2)}, u32[]{:S(2)}) %collective-permute-start.3) | collective-permute-done | bytes 46112 | tf_op jit(solution)/shard_map/ppermute | solution.py:19
  255.8 1.9 fusion.13
  257.7 1.9 fusion.22
  259.5 1.9 fusion.21
  261.4 1.9 fusion.20
  263.3 1.9 fusion.19
  265.1 1.9 fusion.18
  267.0 1.9 fusion.17
  268.9 2.5 fusion.24
  (48 shorter events, 4.3 us)
Async XLA Ops:
  7.2 0.9 copy-start.1
  7.2 5.2 %copy-start = (bf16[1,16,8,1280]{3,2,1,0:T(8,128)(2,1)S(1)}, bf16[1,16,8,1280]{3,2,1,0:T(8,128)(2,1)}, u32[]{:S(2)}) copy-start(bf16[1,16,8,1280]{3,2,1,0:T(8,128)(2,1)} %param.6) | copy-start | bytes 983044
  7.2 181.3 %all-gather.2.cloned.1.call-start = ((), (), s32[]{:S(2)}) async-start(), calls=%async_computation | async-start | bytes 22118400 | tf_op jit(solution)/shard_map/all_gather | solution.py:71
  8.1 69.7 %collective-permute-start.5 = (bf16[1,1,8,640]{3,2,1,0:T(8,128)(2,1)S(1)}, bf16[1,1,8,640]{3,2,1,0:T(8,128)(2,1)S(1)}, u32[]{:S(2)}, u32[]{:S(2)}) collective-permute-start(bf16[1,1,8,640]{3,2,1,0:T(8,128)(2,1)S(1)} %get-tuple-element.16), channel_id=1, source_target_pairs={{4,0},{8,4},{12,8},{5,1},{9,5},{13,9},{6,2},{10,6},{14,10},{7,3},{... | collective-permute-start | bytes 30728 | tf_op jit(solution)/shard_map/ppermute | solution.py:19
  9.4 68.3 %collective-permute-start.4 = (bf16[1,1,8,640]{3,2,1,0:T(8,128)(2,1)S(1)}, bf16[1,1,8,640]{3,2,1,0:T(8,128)(2,1)S(1)}, u32[]{:S(2)}, u32[]{:S(2)}) collective-permute-start(bf16[1,1,8,640]{3,2,1,0:T(8,128)(2,1)S(1)} %get-tuple-element.17), channel_id=1, source_target_pairs={{0,4},{4,8},{8,12},{1,5},{5,9},{9,13},{2,6},{6,10},{10,14},{3,7},{... | collective-permute-start | bytes 30728 | tf_op jit(solution)/shard_map/ppermute | solution.py:17
  77.8 116.7 %collective-permute-start.6 = (bf16[1,18,1,640]{3,2,1,0:T(2,128)(2,1)S(1)}, bf16[1,18,1,640]{3,2,1,0:T(2,128)(2,1)S(1)}, u32[]{:S(2)}, u32[]{:S(2)}) collective-permute-start(bf16[1,18,1,640]{3,2,1,0:T(2,128)(2,1)S(1)} %get-tuple-element.14), channel_id=1, source_target_pairs={{0,1},{1,2},{2,3},{4,5},{5,6},{6,7},{8,9},{9,10},{10,11},{12,13},{... | collective-permute-start | bytes 69128 | tf_op jit(solution)/shard_map/ppermute | solution.py:17
  82.0 110.5 %collective-permute-start.7 = (bf16[1,18,1,640]{3,2,1,0:T(2,128)(2,1)S(1)}, bf16[1,18,1,640]{3,2,1,0:T(2,128)(2,1)S(1)}, u32[]{:S(2)}, u32[]{:S(2)}) collective-permute-start(bf16[1,18,1,640]{3,2,1,0:T(2,128)(2,1)S(1)} %get-tuple-element.15), channel_id=1, source_target_pairs={{1,0},{2,1},{3,2},{5,4},{6,5},{7,6},{9,8},{10,9},{11,10},{13,12},{... | collective-permute-start | bytes 69128 | tf_op jit(solution)/shard_map/ppermute | solution.py:19
  202.7 2.1 copy-start.2
  202.7 2.1 copy-start.3
  242.3 2.6 collective-permute-start
  243.6 3.9 %collective-permute-start.1 = (bf16[1,1,8,1280]{3,2,1,0:T(8,128)(2,1)S(1)}, bf16[1,1,8,1280]{3,2,1,0:T(8,128)(2,1)S(1)}, u32[]{:S(2)}, u32[]{:S(2)}) collective-permute-start(bf16[1,1,8,1280]{3,2,1,0:T(8,128)(2,1)S(1)} %get-tuple-element.13), channel_id=1, source_target_pairs={{4,0},{8,4},{12,8},{5,1},{9,5},{13,9},{6,2},{10,6},{14,10},{7,3},{... | collective-permute-start | bytes 61448 | tf_op jit(solution)/shard_map/ppermute | solution.py:19
  247.6 4.5 %collective-permute-start.2 = (bf16[1,18,1,1280]{3,2,1,0:T(2,128)(2,1)S(1)}, bf16[1,18,1,1280]{3,2,1,0:T(2,128)(2,1)S(1)}, u32[]{:S(2)}, u32[]{:S(2)}) collective-permute-start(bf16[1,18,1,1280]{3,2,1,0:T(2,128)(2,1)S(1)} %get-tuple-element.8), channel_id=1, source_target_pairs={{0,1},{1,2},{2,3},{4,5},{5,6},{6,7},{8,9},{9,10},{10,11},{12,13},{... | collective-permute-start | bytes 138248 | tf_op jit(solution)/shard_map/ppermute | solution.py:17
  249.0 6.4 %collective-permute-start.3 = (bf16[1,18,1,1280]{3,2,1,0:T(2,128)(2,1)S(1)}, bf16[1,18,1,1280]{3,2,1,0:T(2,128)(2,1)S(1)}, u32[]{:S(2)}, u32[]{:S(2)}) collective-permute-start(bf16[1,18,1,1280]{3,2,1,0:T(2,128)(2,1)S(1)} %get-tuple-element.9), channel_id=1, source_target_pairs={{1,0},{2,1},{3,2},{5,4},{6,5},{7,6},{9,8},{10,9},{11,10},{13,12},{... | collective-permute-start | bytes 138248 | tf_op jit(solution)/shard_map/ppermute | solution.py:19
  267.0 1.9 copy-start.4
Sparse Core Ops, SparseCore 0:
  9.6 178.8 all-gather.1
where the time goes:
time: 280 us; the launch traced here: 278 us
  waiting for transfers between devices  112 us (40%)
  blocking collectives  97.7 us (35%)
  matrix products  35.9 us (13%)
  starting transfers between devices  15 us (5%)
  between operations  14.4 us (5%)
    all_gather x1, waiting for transfers between devices, body(): full_kernel = lax.all_gather(conv_weight, 'dp', axis=2, tiled=True)  105 us
    psum x1, blocking collectives, body(): total = lax.psum(jnp.sum(xg, axis=(1, 2, 4)), ('ha', 'wa'))  34.7 us
    psum x1, blocking collectives, body(): lax.psum((jnp.sum(normalized_gradient, axis=(1, 2, 4)), jnp.sum(normalize...  33.4 us
    psum x1, blocking collectives, body(): lax.psum(jnp.sum(centered_input * centered_input, axis=(1, 2, 4)), ('ha',...  29.7 us
    dot_general x9, matrix products, backward_taps(): lax.dot_general(window, kernel[2 - ky, 2 - kx], (((1,), (1,)), ((), ())),...  18.5 us
    dot_general x9, matrix products, forward_taps(): term = jnp.dot(window, kernel[ky, kx], preferred_element_type=jnp.float32)  17.5 us
    ppermute x4, starting transfers between devices, padded_2(): lax.ppermute(tail, axis, [(i, (i + 1) % count) for i in range(ends)])  9.83 us
    ppermute x4, waiting for transfers between devices, padded_2(): lax.ppermute(head, axis, [((i + 1) % count, i) for i in range(ends)])  5.85 us
  transfers between devices with their start and end apart: 9, of which 3 were waited for; matrix products, arithmetic and copies ran while one was open for 3% of the time, Pallas kernels for 0%

commit v1 on v0

v1 whole, which is shorter than its diff:
```python
import functools

import jax
import jax.numpy as jnp
from jax import lax
from jax.experimental import pallas as pl
from jax.experimental.pallas import tpu as pltpu
from jax.sharding import PartitionSpec as P

GROUPS = 32
EPS = 1e-05
F32 = jnp.float32
BF16 = jnp.bfloat16


def swap(values, axis, partner):
    count = lax.axis_size(axis)
    pairs = [(i, partner(i) % count) for i in range(count)]
    return [lax.ppermute(v, axis, pairs) for v in values]


def near(i):
    return i ^ 1


def across(i):
    return i - 1 if i % 2 == 0 else i + 1


def merged(stats, other, n):
    delta = other[0] - stats[0]
    return jnp.stack([stats[0] + 0.5 * delta, stats[1] + other[1] + (0.5 * n) * delta * delta])


def conv_windows(padded_ref, windows_ref, images, rows, cols):
    chans = windows_ref.shape[3]
    for kx in range(3):
        windows_ref[kx] = padded_ref[:, kx : kx + cols, :].reshape(rows + 2, images * cols, chans).astype(BF16)


def expanded(values, chans):
    groups = values.shape[-1]
    per_group = chans // groups
    chan = lax.broadcasted_iota(jnp.int32, (groups, chans), 1)
    group = lax.broadcasted_iota(jnp.int32, (groups, chans), 0)
    member = ((chan >= group * per_group) & (chan < (group + 1) * per_group)).astype(F32)
    return jnp.dot(values, member, precision=lax.Precision.HIGHEST, preferred_element_type=F32)


def gathered(values, groups):
    chans = values.shape[-1]
    per_group = chans // groups
    chan = lax.broadcasted_iota(jnp.int32, (chans, groups), 0)
    group = lax.broadcasted_iota(jnp.int32, (chans, groups), 1)
    member = ((chan >= group * per_group) & (chan < (group + 1) * per_group)).astype(F32)
    return jnp.dot(values, member, precision=lax.Precision.HIGHEST, preferred_element_type=F32)


def backward_kernel(
    images, rows, cols, count,
    inside_ref, stats_ref, gain_ref, shift_ref, x_ref, cot_ref, w_ref,
    gx_own_ref, gx_other_ref, moments_ref, act_ref,
    padded_ref, pad_cot_ref, windows_ref,
):
    chans = x_ref.shape[2]
    outs = cot_ref.shape[2]
    groups = stats_ref.shape[2]
    pix = rows * images * cols
    pad_cot_ref[:, : cols + 2, :] = cot_ref[...].astype(F32)
    conv_windows(pad_cot_ref, windows_ref, images, rows, cols)
    total = None
    for ky in range(3):
        for kx in range(3):
            window = windows_ref[kx, ky : ky + rows].reshape(pix, outs)
            term = lax.dot_general(
                w_ref[2 - ky, 2 - kx], window, (((1,), (1,)), ((), ())), preferred_element_type=F32
            )
            total = term if total is None else total + term
    grad_act = total.T.reshape(rows, images, cols, chans)
    mean = expanded(stats_ref[0], chans)
    inv = expanded(lax.rsqrt(stats_ref[1] / count + EPS), chans)
    gain = gain_ref[...]
    shift = shift_ref[...]
    xhat = (x_ref[...].astype(F32).reshape(rows + 2, images, cols + 2, chans) - mean[None, :, None, :]) * inv[None, :, None, :]
    z = xhat * gain.reshape(1, 1, 1, chans) + shift.reshape(1, 1, 1, chans)
    sig = jax.nn.sigmoid(z)
    row = lax.broadcasted_iota(jnp.int32, z.shape, 0)
    col = lax.broadcasted_iota(jnp.int32, z.shape, 2)
    keep = (
        ((row > 0) | (inside_ref[0] > 0))
        & ((row < rows + 1) | (inside_ref[1] > 0))
        & ((col > 0) | (inside_ref[2] > 0))
        & ((col < cols + 1) | (inside_ref[3] > 0))
    )
    act = jnp.where(keep, z * sig, 0.0)
    padded_ref[:, : cols + 2, :] = act.reshape((rows + 2) * images, cols + 2, chans)
    conv_windows(padded_ref, act_ref, images, rows, cols)
    slope = sig * (1.0 + z * (1.0 - sig)) * gain.reshape(1, 1, 1, chans)
    padded_ref[:, : cols + 2, :] = slope.reshape((rows + 2) * images, cols + 2, chans)
    slope = padded_ref[images : (rows + 1) * images, 1 : cols + 1, :].reshape(rows, images, cols, chans)
    padded_ref[:, : cols + 2, :] = xhat.reshape((rows + 2) * images, cols + 2, chans)
    xhat = padded_ref[images : (rows + 1) * images, 1 : cols + 1, :].reshape(rows, images, cols, chans)
    gx = grad_act * slope
    gx_own_ref[...] = gx[:, 0]
    for k in range(1, images):
        gx_other_ref[k - 1] = gx[:, k].astype(BF16)
    first = jnp.sum(gx, axis=(0, 2))
    second = jnp.sum(gx * xhat, axis=(0, 2))
    moments_ref[0] = gathered(first, groups)
    moments_ref[1] = gathered(second, groups)


def forward_kernel(images, rows, cols, act_ref, w_ref, own_ref, other_ref):
    chans = act_ref.shape[3]
    outs = w_ref.shape[3]
    pix = rows * images * cols
    total = None
    for ky in range(3):
        for kx in range(3):
            window = act_ref[kx, ky : ky + rows].reshape(pix, chans)
            term = jnp.dot(window, w_ref[ky, kx], preferred_element_type=F32)
            total = term if total is None else total + term
    total = total.reshape(rows, images, cols, outs)
    own_ref[...] = total[:, 0]
    for k in range(1, images):
        other_ref[k - 1] = total[:, k].astype(BF16)


def call(kernel, outs, scratch, name, *operands, smem=0):
    vmem = pl.BlockSpec(memory_space=pltpu.VMEM)
    return pl.pallas_call(
        kernel,
        out_shape=outs,
        in_specs=[pl.BlockSpec(memory_space=pltpu.SMEM)] * smem + [vmem] * (len(operands) - smem),
        out_specs=[vmem] * len(outs),
        scratch_shapes=scratch,
        compiler_params=pltpu.CompilerParams(vmem_limit_bytes=40 * 2**20),
        name=name,
    )(*operands)


def edges_exchanged(axis, first, last, stats, n):
    count = lax.axis_size(axis)
    index = lax.axis_index(axis)
    even = index % 2 == 0
    pick = lambda a, b: [jnp.where(even, x, y) for x, y in zip(a, b)]
    got_near = swap(pick(last, first) + [stats], axis, near)
    stats, n = merged(stats, got_near[-1], n), 2 * n
    got_across = swap(pick(first, last) + ([stats] if count == 4 else []), axis, across)
    if count == 4:
        stats, n = merged(stats, got_across.pop(), n), 2 * n
    else:
        step = 2
        while step < count:
            (other,) = swap([stats], axis, lambda i: i ^ step)
            stats, n = merged(stats, other, n), 2 * n
            step *= 2
    lower = [jnp.where(index > 0, v, jnp.zeros_like(v)) for v in pick(got_across, got_near)]
    upper = [jnp.where(index < count - 1, v, jnp.zeros_like(v)) for v in pick(got_near[:-1], got_across)]
    return lower, upper, stats, n


def summed(value, axis):
    count = lax.axis_size(axis)
    step = 1
    while step < count:
        (other,) = swap([value], axis, lambda i: i ^ step)
        value = value + other
        step *= 2
    return value


def body(latents, norm_gain, norm_shift, conv_weight, conv_bias, cotangent):
    _, rows, cols, cin = latents.shape
    outs = cotangent.shape[3]
    chans = conv_weight.shape[2]
    parts = lax.axis_size("dp")
    me = lax.axis_index("dp")
    groups = GROUPS * chans // cin
    per_group = cin // GROUPS
    tiles = lax.axis_size("ha") * lax.axis_size("wa")
    n_local = rows * cols * per_group
    count = n_local * tiles
    x, cot = latents[0], cotangent[0]

    def to_peer(k):
        return lambda i: i + k

    def shard_of(a, axis, k, size):
        return lax.dynamic_slice_in_dim(a, (me + k) % parts * size, size, axis)

    xg = x.astype(F32).reshape(rows, cols, GROUPS, per_group)
    local_mean = jnp.mean(xg, axis=(0, 1, 3))
    centered = xg - local_mean[None, None, :, None]
    local = jnp.stack([local_mean, jnp.sum(centered * centered, axis=(0, 1, 3))])

    stats = [shard_of(local, 1, 0, groups)]
    x_all, cot_all = [shard_of(x, 2, 0, chans)], [cot]
    x_edges, cot_edges = [], []
    def edges(t):
        return jnp.concatenate([t[:1], t[-1:]], 0), jnp.concatenate([t[:, :1], t[:, -1:]], 1)
    x_edges.append(edges(x_all[0]))
    cot_edges.append(edges(cot))
    for k in range(1, parts):
        mine = shard_of(x, 2, k, chans)
        xr, xc = edges(mine)
        cr, cc = cot_edges[0]
        got = swap([shard_of(local, 1, k, groups), xr, cr, xc, cc, cot, mine], "dp", to_peer(k))
        stats.append(got[0])
        x_edges.append((got[1], got[3]))
        cot_edges.append((got[2], got[4]))
        cot_all.append(got[5])
        x_all.append(got[6])
    stats = jnp.stack(stats, 1)
    stack = lambda e, j, i, axis: jnp.stack([lax.index_in_dim(v[j], i, axis, keepdims=False) for v in e], axis)

    top = [stack(e, 0, 0, 0) for e in (x_edges, cot_edges)]
    bottom = [stack(e, 0, 1, 0) for e in (x_edges, cot_edges)]
    above, below, stats, n = edges_exchanged("ha", top, bottom, stats, n_local)
    cols_of = lambda e, i: jnp.stack([lax.index_in_dim(v[1], i, 1, keepdims=False) for v in e], 1)
    left = [jnp.concatenate([a[None, :, 0], cols_of(e, 0), b[None, :, 0]], 0) for a, b, e in zip(above, below, (x_edges, cot_edges))]
    right = [jnp.concatenate([a[None, :, -1], cols_of(e, 1), b[None, :, -1]], 0) for a, b, e in zip(above, below, (x_edges, cot_edges))]
    before, after, stats, n = edges_exchanged("wa", left, right, stats, n)

    def padded(tiles_, a, b, l, r):
        t = jnp.stack(tiles_, 1)
        t = jnp.concatenate([a[None], t, b[None]], 0)
        t = jnp.concatenate([l[:, :, None], t, r[:, :, None]], 2)
        return t.reshape((rows + 2) * parts, cols + 2, t.shape[3])

    x_pad = padded(x_all, above[0], below[0], before[0], after[0])
    cot_pad = padded(cot_all, above[1], below[1], before[1], after[1])
    at = lambda axis: (lax.axis_index(axis) > 0, lax.axis_index(axis) < lax.axis_size(axis) - 1)
    inside = jnp.stack(at("ha") + at("wa")).astype(jnp.int32)
    gain = shard_of(norm_gain, 0, 0, chans)[None]
    shift = shard_of(norm_shift, 0, 0, chans)[None]
    sds = jax.ShapeDtypeStruct
    gx_own, gx_other, moments, act = call(
        functools.partial(backward_kernel, parts, rows, cols, float(count)),
        [
            sds((rows, cols, chans), F32),
            sds((parts - 1, rows, cols, chans), BF16),
            sds((2, parts, groups), F32),
            sds((3, rows + 2, parts * cols, chans), BF16),
        ],
        [
            pltpu.VMEM(((rows + 2) * parts, cols + 8, chans), F32),
            pltpu.VMEM(((rows + 2) * parts, cols + 8, outs), F32),
            pltpu.VMEM((3, rows + 2, parts * cols, outs), BF16),
        ],
        "conv_backward",
        inside, stats, gain, shift, x_pad, cot_pad, conv_weight,
        smem=1,
    )
    conv_own, conv_other = call(
        functools.partial(forward_kernel, parts, rows, cols),
        [sds((rows, cols, outs), F32), sds((parts - 1, rows, cols, outs), BF16)],
        [],
        "conv_forward",
        act, conv_weight,
    )

    small = jnp.concatenate([moments, stats], 0)
    whole = jnp.zeros((4, GROUPS), F32)
    place = lambda a, v, k, axis, size: lax.dynamic_update_slice_in_dim(a, v, (me + k) % parts * size, axis)
    whole = place(whole, small[:, 0], 0, 1, groups)
    gx = place(jnp.zeros((rows, cols, cin), F32), gx_own, 0, 2, chans)
    conv = conv_own
    for k in range(1, parts):
        got = swap([small[:, k], gx_other[k - 1], conv_other[k - 1]], "dp", to_peer(-k))
        whole = place(whole, got[0], k, 1, groups)
        gx = place(gx, got[1].astype(F32), k, 2, chans)
        conv = conv + got[2].astype(F32)
    conv_out = (conv + conv_bias).astype(BF16)
    sums = summed(summed(whole[:2], "ha"), "wa") / count
    wide = lambda v: jnp.broadcast_to(v[:, None], (GROUPS, per_group)).reshape(cin)
    inv = lax.rsqrt(whole[3] / count + EPS)
    xhat = (x.astype(F32) - wide(whole[2])) * wide(inv)
    grad = wide(inv) * (gx - wide(sums[0]) - xhat * wide(sums[1]))
    return conv_out[None], grad.astype(BF16)[None]


def solution(mesh):
    tile = P("dp", "ha", "wa", None)
    return jax.shard_map(
        body,
        mesh=mesh,
        in_specs=(tile, P(), P(), P(None, None, "dp", None), P(), tile),
        out_specs=(tile, tile),
        check_vma=False,
    )
```

time: 280 us -> 82.8 us (0.30)
  blocking collectives: 97.7 us -> 0 us
  waiting for transfers between devices: 112 us -> 27.3 us
  matrix products: 35.9 us -> 0 us
  starting transfers between devices: 15 us -> 30.2 us
  between operations: 14.4 us -> 1.2 us
  local copies, waits for them, and re-layouts: 1.25 us -> 11.4 us
  Pallas kernels: 0 us -> 8.2 us
    all_gather x1 -> x0, waiting for transfers between devices: 105 us -> none  [body(): full_kernel = lax.all_gather(conv_weight, 'dp', axis=2, tiled=True)]
    psum x3 -> x0, blocking collectives: 97.7 us -> none  [the longest x1 34.7 us: body(): total = lax.psum(jnp.sum(xg, axis=(1, 2, 4)), ('ha', 'wa'))]
    dot_general x18 -> x0, matrix products: 35.9 us -> none  [the longest x9 18.5 us: backward_taps(): lax.dot_general(window, kernel[2 - ky, 2 - kx], (((1,), (1,)), ((), ())),...]
    ppermute x8 -> x26, waiting for transfers between devices: 5.87 us -> 27.3 us  [swap(): return [lax.ppermute(v, axis, pairs) for v in values]]
    ppermute x8 -> x26, starting transfers between devices: 15 us -> 30.2 us  [swap(): return [lax.ppermute(v, axis, pairs) for v in values]]
    pallas_call x0 -> x2, Pallas kernels: none -> 8.2 us  [call(): pl.pallas_call(kernel, out_shape=outs, in_specs=[pl.BlockSpec(memory_spac...]
    unnamed x12 -> x22, local copies, waits for them, and re-layouts: 0.21 us -> 6.24 us
  transfers between devices with their start and end apart: 9 -> 26, of which waited for: 3 -> 14; matrix products, arithmetic and copies ran while one was open for 3% -> 8% of each run, Pallas kernels for 0% -> 3%
where the time goes in v1:
time: 82.8 us; the launch traced here: 82.5 us
  starting transfers between devices  30.2 us (36%)
  waiting for transfers between devices  27.3 us (33%)
  local copies, waits for them, and re-layouts  11.4 us (14%)
  Pallas kernels  8.2 us (10%)
  other arithmetic  4.23 us (5%)
  between operations  1.2 us (1%)
    ppermute x26, starting transfers between devices, swap(): return [lax.ppermute(v, axis, pairs) for v in values]  30.2 us
    ppermute x26, waiting for transfers between devices, swap(): return [lax.ppermute(v, axis, pairs) for v in values]  27.3 us
    pallas_call x2, Pallas kernels, call(): pl.pallas_call(kernel, out_shape=outs, in_specs=[pl.BlockSpec(memory_spac...  8.2 us
    unnamed x22, local copies, waits for them, and re-layouts  6.24 us
  transfers between devices with their start and end apart: 26, of which 14 were waited for; matrix products, arithmetic and copies ran while one was open for 8% of the time, Pallas kernels for 3%

profile of v1, /device:TPU:0, one launch (start us, length us, event | category | flops | bytes accessed | tf_op | source)
XLA Modules:
  0.0 82.5 jit_solution(9126083203032962183)
XLA Ops:
  1.4 3.0 %collective-permute-start.12 = (bf16[2,8,640]{2,1,0:T(8,128)(2,1)S(1)}, bf16[2,8,640]{2,1,0:T(8,128)(2,1)S(1)}, u32[]{:S(2)}, u32[]{:S(2)}) collective-permute-start(bf16[2,8,640]{2,1,0:T(8,128)(2,1)S(1)} %pad_maximum_fusion.10), channel_id=1, source_target_pairs={{0,16},{16,0},{1,17},{17,1},{2,18},{18,2},{3,19},{19,3},{4,20},{20... | collective-permute-start | bytes 61448 | tf_op jit(solution)/shard_map/ppermute | solution.py:19
  4.5 1.1 %fusion.18 = (bf16[16,1,640]{2,1,0:T(2,128)(2,1)S(1)}, bf16[16,1,640]{2,1,0:T(2,128)(2,1)S(1)}) fusion(bf16[16,8,640]{2,1,0:T(8,128)(2,1)} %bitcast.110), kind=kLoop, calls=%fused_computation.113 | loop fusion | bytes 81920 | tf_op jit(solution)/shard_map/slice | solution.py:201
  5.8 2.0 %collective-permute-start.15 = (bf16[16,2,640]{2,1,0:T(2,128)(2,1)S(1)}, bf16[16,2,640]{2,1,0:T(2,128)(2,1)S(1)}, u32[]{:S(2)}, u32[]{:S(2)}) collective-permute-start(bf16[16,2,640]{2,1,0:T(2,128)(2,1)S(1)} %pad_maximum_fusion.9), channel_id=1, source_target_pairs={{0,16},{16,0},{1,17},{17,1},{2,18},{18,2},{3,19},{19,3},{4,20},{20... | collective-permute-start | bytes 122888 | tf_op jit(solution)/shard_map/ppermute | solution.py:19
  7.8 1.0 %dynamic-slice_bitcast_fusion.2 = (bf16[16,1,8,640]{3,2,0,1:T(8,128)(2,1)S(1)}, bf16[16,8,640]{2,1,0:T(8,128)(2,1)S(1)}, bf16[16,8,640]{2,1,0:T(8,128)(2,1)S(1)}) fusion(bf16[1,16,8,1280]{3,2,1,0:T(8,128)(2,1)} %param.6, s32[]{:T(128)S(6)} %select_n.169, s32[]{:T(128)S(6)} %select_n.176), kind=kLoop, calls=%fused_computation.21 | loop fusion | bytes 819208 | tf_op jit(solution)/shard_map/stack | solution.py:226
  9.8 2.0 %collective-permute-start = (f32[2,16]{1,0:T(2,128)S(1)}, f32[2,16]{1,0:T(2,128)S(1)}, u32[]{:S(2)}, u32[]{:S(2)}) collective-permute-start(f32[2,16]{1,0:T(2,128)S(1)} %get-tuple-element.77), channel_id=1, source_target_pairs={{0,16},{16,0},{1,17},{17,1},{2,18},{18,2},{3,19},{19,3},{4,20},{20... | collective-permute-start | bytes 392 | tf_op jit(solution)/shard_map/ppermute | solution.py:19
  12.1 2.7 %collective-permute-done = f32[2,16]{1,0:T(2,128)S(1)} collective-permute-done((f32[2,16]{1,0:T(2,128)S(1)}, f32[2,16]{1,0:T(2,128)S(1)}, u32[]{:S(2)}, u32[]{:S(2)}) %collective-permute-start) | collective-permute-done | bytes 160 | tf_op jit(solution)/shard_map/ppermute | solution.py:19
  14.9 1.1 %collective-permute-done.1 = f32[2,2,16]{2,1,0:T(2,128)S(1)} collective-permute-done((f32[2,2,16]{2,1,0:T(2,128)S(1)}, f32[2,2,16]{2,1,0:T(2,128)S(1)}, u32[]{:S(2)}, u32[]{:S(2)}) %collective-permute-start.1) | collective-permute-done | bytes 288 | tf_op jit(solution)/shard_map/ppermute | solution.py:19
  16.0 1.3 %collective-permute-start.2 = (f32[2,2,16]{2,1,0:T(2,128)S(1)}, f32[2,2,16]{2,1,0:T(2,128)S(1)}, u32[]{:S(2)}, u32[]{:S(2)}) collective-permute-start(f32[2,2,16]{2,1,0:T(2,128)S(1)} %pad_maximum_fusion.18), channel_id=1, source_target_pairs={{0,12},{4,8},{8,4},{12,0},{1,13},{5,9},{9,5},{13,1},{2,14},{6,10},... | collective-permute-start | bytes 776 | tf_op jit(solution)/shard_map/ppermute | solution.py:19
  17.4 1.7 %collective-permute-done.2 = f32[2,2,16]{2,1,0:T(2,128)S(1)} collective-permute-done((f32[2,2,16]{2,1,0:T(2,128)S(1)}, f32[2,2,16]{2,1,0:T(2,128)S(1)}, u32[]{:S(2)}, u32[]{:S(2)}) %collective-permute-start.2) | collective-permute-done | bytes 288 | tf_op jit(solution)/shard_map/ppermute | solution.py:19
  19.1 1.6 %collective-permute-start.3 = (f32[2,2,16]{2,1,0:T(2,128)S(1)}, f32[2,2,16]{2,1,0:T(2,128)S(1)}, u32[]{:S(2)}, u32[]{:S(2)}) collective-permute-start(f32[2,2,16]{2,1,0:T(2,128)S(1)} %pad_maximum_fusion.19), channel_id=1, source_target_pairs={{0,1},{1,0},{2,3},{3,2},{4,5},{5,4},{6,7},{7,6},{8,9},{9,8},{10,11... | collective-permute-start | bytes 776 | tf_op jit(solution)/shard_map/ppermute | solution.py:19
  20.8 2.0 %collective-permute-done.3 = f32[2,2,16]{2,1,0:T(2,128)S(1)} collective-permute-done((f32[2,2,16]{2,1,0:T(2,128)S(1)}, f32[2,2,16]{2,1,0:T(2,128)S(1)}, u32[]{:S(2)}, u32[]{:S(2)}) %collective-permute-start.3) | collective-permute-done | bytes 288 | tf_op jit(solution)/shard_map/ppermute | solution.py:19
  22.8 3.7 %collective-permute-start.4 = (f32[2,2,16]{2,1,0:T(2,128)S(1)}, f32[2,2,16]{2,1,0:T(2,128)S(1)}, u32[]{:S(2)}, u32[]{:S(2)}) collective-permute-start(f32[2,2,16]{2,1,0:T(2,128)S(1)} %pad_maximum_fusion.20), channel_id=1, source_target_pairs={{0,3},{1,2},{2,1},{3,0},{4,7},{5,6},{6,5},{7,4},{8,11},{9,10},{10,... | collective-permute-start | bytes 776 | tf_op jit(solution)/shard_map/ppermute | solution.py:19
  26.6 1.6 %collective-permute-done.4 = f32[2,2,16]{2,1,0:T(2,128)S(1)} collective-permute-done((f32[2,2,16]{2,1,0:T(2,128)S(1)}, f32[2,2,16]{2,1,0:T(2,128)S(1)}, u32[]{:S(2)}, u32[]{:S(2)}) %collective-permute-start.4) | collective-permute-done | bytes 288 | tf_op jit(solution)/shard_map/ppermute | solution.py:19
  29.0 3.1 %collective-permute-done.5 = bf16[2,8,640]{2,1,0:T(8,128)(2,1)S(1)} collective-permute-done((bf16[2,8,640]{2,1,0:T(8,128)(2,1)S(1)}, bf16[2,8,640]{2,1,0:T(8,128)(2,1)S(1)}, u32[]{:S(2)}, u32[]{:S(2)}) %collective-permute-start.5) | collective-permute-done | bytes 20512 | tf_op jit(solution)/shard_map/ppermute | solution.py:19
  32.2 1.6 %collective-permute-start.8 = (bf16[16,2,640]{2,1,0:T(2,128)(2,1)S(1)}, bf16[16,2,640]{2,1,0:T(2,128)(2,1)S(1)}, u32[]{:S(2)}, u32[]{:S(2)}) collective-permute-start(bf16[16,2,640]{2,1,0:T(2,128)(2,1)S(1)} %pad_maximum_fusion.8), channel_id=1, source_target_pairs={{0,16},{16,0},{1,17},{17,1},{2,18},{18,2},{3,19},{19,3},{4,20},{20... | collective-permute-start | bytes 122888 | tf_op jit(solution)/shard_map/ppermute | solution.py:19
  35.7 1.5 %collective-permute-done.6 = bf16[2,8,640]{2,1,0:T(8,128)(2,1)S(1)} collective-permute-done((bf16[2,8,640]{2,1,0:T(8,128)(2,1)S(1)}, bf16[2,8,640]{2,1,0:T(8,128)(2,1)S(1)}, u32[]{:S(2)}, u32[]{:S(2)}) %collective-permute-start.6) | collective-permute-done | bytes 20512 | tf_op jit(solution)/shard_map/ppermute | solution.py:19
  37.2 3.6 %collective-permute-start.16 = (bf16[18,2,640]{2,1,0:T(2,128)(2,1)S(1)}, bf16[18,2,640]{2,1,0:T(2,128)(2,1)S(1)}, u32[]{:S(2)}, u32[]{:S(2)}) collective-permute-start(bf16[18,2,640]{2,1,0:T(2,128)(2,1)S(1)} %get-tuple-element.14), channel_id=1, source_target_pairs={{0,3},{1,2},{2,1},{3,0},{4,7},{5,6},{6,5},{7,4},{8,11},{9,10},{10,... | collective-permute-start | bytes 138248 | tf_op jit(solution)/shard_map/ppermute | solution.py:19
  41.3 1.2 %collective-permute-start.10 = (bf16[18,2,640]{2,1,0:T(2,128)(2,1)S(1)}, bf16[18,2,640]{2,1,0:T(2,128)(2,1)S(1)}, u32[]{:S(2)}, u32[]{:S(2)}) collective-permute-start(bf16[18,2,640]{2,1,0:T(2,128)(2,1)S(1)} %broadcast_select_fusion.8), channel_id=1, source_target_pairs={{0,1},{1,0},{2,3},{3,2},{4,5},{5,4},{6,7},{7,6},{8,9},{9,8},{10,11... | collective-permute-start | bytes 138248 | tf_op jit(solution)/shard_map/ppermute | solution.py:19
  42.4 2.6 %collective-permute-start.9 = (bf16[18,2,640]{2,1,0:T(2,128)(2,1)S(1)}, bf16[18,2,640]{2,1,0:T(2,128)(2,1)S(1)}, u32[]{:S(2)}, u32[]{:S(2)}) collective-permute-start(bf16[18,2,640]{2,1,0:T(2,128)(2,1)S(1)} %get-tuple-element.17), channel_id=1, source_target_pairs={{0,3},{1,2},{2,1},{3,0},{4,7},{5,6},{6,5},{7,4},{8,11},{9,10},{10,... | collective-permute-start | bytes 138248 | tf_op jit(solution)/shard_map/ppermute | solution.py:19
  45.4 2.9 %collective-permute-done.9 = bf16[18,2,640]{2,1,0:T(2,128)(2,1)S(1)} collective-permute-done((bf16[18,2,640]{2,1,0:T(2,128)(2,1)S(1)}, bf16[18,2,640]{2,1,0:T(2,128)(2,1)S(1)}, u32[]{:S(2)}, u32[]{:S(2)}) %collective-permute-start.9) | collective-permute-done | bytes 46112 | tf_op jit(solution)/shard_map/ppermute | solution.py:19
  49.9 3.1 %copy-done = bf16[3,3,640,640]{3,2,1,0:T(8,128)(2,1)S(1)} copy-done((bf16[3,3,640,640]{3,2,1,0:T(8,128)(2,1)S(1)}, bf16[3,3,640,640]{3,2,1,0:T(8,128)(2,1)}, u32[]{:S(2)}) %copy-start) | copy-done | bytes 7372824
  53.0 5.4 %conv_backward.1 = (f32[16,8,640]{2,1,0:T(8,128)S(1)}, bf16[1,16,8,640]{3,2,1,0:T(8,128)(2,1)S(1)}, f32[2,2,16]{2,1,0:T(2,128)S(1)}, bf16[3,18,16,640]{3,2,1,0:T(8,128)(2,1)S(1)}) custom-call(s32[4]{0:T(128)S(1)} %add_convert_fusion.1.inside_ref, f32[2,2,16]{2,1,0:T(2,128)S(1)} %pad_maximum_fusion.21.stats_ref, f32[1,640]{1,0:T(1,128)S(1)} %broadcast_in_dim.67.gain_ref, ...), custom_call_target="tpu_custom_call" | custom-call | tf_op jit(solution)/shard_map/conv_backward/pallas_call | solution.py:131
  59.2 1.3 %collective-permute-start.21 = (bf16[16,8,640]{2,1,0:T(8,128)(2,1)S(1)}, bf16[16,8,640]{2,1,0:T(8,128)(2,1)S(1)}, u32[]{:S(2)}, u32[]{:S(2)}) collective-permute-start(bf16[16,8,640]{2,1,0:T(8,128)(2,1)S(1)} %bitcast.105), channel_id=1, source_target_pairs={{0,16},{16,0},{1,17},{17,1},{2,18},{18,2},{3,19},{19,3},{4,20},{20... | collective-permute-start | bytes 491528 | tf_op jit(solution)/shard_map/ppermute | solution.py:19
  60.6 1.5 %collective-permute-done.20 = f32[4,16]{1,0:T(4,128)S(1)} collective-permute-done((f32[4,16]{1,0:T(4,128)S(1)}, f32[4,16]{1,0:T(4,128)S(1)}, u32[]{:S(2)}, u32[]{:S(2)}) %collective-permute-start.20) | collective-permute-done | bytes 288 | tf_op jit(solution)/shard_map/ppermute | solution.py:19
  62.4 3.1 %copy-done.1 = bf16[3,3,640,640]{3,2,1,0:T(8,128)(2,1)S(1)} copy-done((bf16[3,3,640,640]{3,2,1,0:T(8,128)(2,1)S(1)}, bf16[3,3,640,640]{3,2,1,0:T(8,128)(2,1)}, u32[]{:S(2)}) %copy-start.1) | copy-done | bytes 7372824
  65.5 2.8 %conv_forward.1 = (f32[16,8,640]{2,1,0:T(8,128)S(1)}, bf16[1,16,8,640]{3,2,1,0:T(8,128)(2,1)S(1)}) custom-call(bf16[3,18,16,640]{3,2,1,0:T(8,128)(2,1)S(1)} %get-tuple-element.8.act_ref, bf16[3,3,640,640]{3,2,1,0:T(8,128)(2,1)S(1)} %copy-done.1), custom_call_target="tpu_custom_call" | custom-call | tf_op jit(solution)/shard_map/conv_forward/pallas_call | solution.py:131
  68.9 1.2 %collective-permute-start.23 = (f32[2,32]{1,0:T(2,128)S(1)}, f32[2,32]{1,0:T(2,128)S(1)}, u32[]{:S(2)}, u32[]{:S(2)}) collective-permute-start(f32[2,32]{1,0:T(2,128)S(1)} %slice_add_fusion.3), channel_id=1, source_target_pairs={{0,8},{4,12},{8,0},{12,4},{1,9},{5,13},{9,1},{13,5},{2,10},{6,14},... | collective-permute-start | bytes 776 | tf_op jit(solution)/shard_map/ppermute | solution.py:19
  70.2 2.2 %collective-permute-done.23 = f32[2,32]{1,0:T(2,128)S(1)} collective-permute-done((f32[2,32]{1,0:T(2,128)S(1)}, f32[2,32]{1,0:T(2,128)S(1)}, u32[]{:S(2)}, u32[]{:S(2)}) %collective-permute-start.23) | collective-permute-done | bytes 288 | tf_op jit(solution)/shard_map/ppermute | solution.py:19
  72.5 3.6 %collective-permute-done.24 = f32[2,32]{1,0:T(2,128)S(1)} collective-permute-done((f32[2,32]{1,0:T(2,128)S(1)}, f32[2,32]{1,0:T(2,128)S(1)}, u32[]{:S(2)}, u32[]{:S(2)}) %collective-permute-start.24) | collective-permute-done | bytes 288 | tf_op jit(solution)/shard_map/ppermute | solution.py:19
  76.1 1.1 %collective-permute-start.25 = (f32[2,32]{1,0:T(2,128)S(1)}, f32[2,32]{1,0:T(2,128)S(1)}, u32[]{:S(2)}, u32[]{:S(2)}) collective-permute-start(f32[2,32]{1,0:T(2,128)S(1)} %add.179), channel_id=1, source_target_pairs={{0,2},{1,3},{2,0},{3,1},{4,6},{5,7},{6,4},{7,5},{8,10},{9,11},{10,... | collective-permute-start | bytes 776 | tf_op jit(solution)/shard_map/ppermute | solution.py:19
  77.5 3.0 %collective-permute-done.25 = f32[2,32]{1,0:T(2,128)S(1)} collective-permute-done((f32[2,32]{1,0:T(2,128)S(1)}, f32[2,32]{1,0:T(2,128)S(1)}, u32[]{:S(2)}, u32[]{:S(2)}) %collective-permute-start.25) | collective-permute-done | bytes 288 | tf_op jit(solution)/shard_map/ppermute | solution.py:19
  80.9 0.9 %fusion.8 = bf16[1,16,8,1280]{3,2,1,0:T(8,128)(2,1)} fusion(bf16[1,16,8,1280]{3,2,1,0:T(8,128)(2,1)S(1)} %copy-done.2, f32[16,8,1280]{2,1,0:T(8,128)S(1)} %convert_dynamic-update-slice_fusion, f32[1280]{0:T(1024)S(1)} %mul.156, f32[1280]{0:T(1024)S(1)} %sub.79, f32[1280]{0:T(1024)S(1)} %sub.76, f32[1280]{0:T(1024)S(1)} %mul.153), kind=kLoop, calls=%fused_computation.15 | loop fusion | flops 1310720 | bytes 1331200 | tf_op jit(solution)/shard_map/broadcast_in_dim | solution.py:280
  (130 shorter events, 10.7 us)
Async XLA Ops:
  0.6 8.3 %copy-start.2 = (bf16[1,16,8,1280]{3,2,1,0:T(8,128)(2,1)S(1)}, bf16[1,16,8,1280]{3,2,1,0:T(8,128)(2,1)}, u32[]{:S(2)}) copy-start(bf16[1,16,8,1280]{3,2,1,0:T(8,128)(2,1)} %param.6) | copy-start | bytes 983044
  0.6 25.8 %copy-start.5 = (f32[1280]{0:T(1024)S(1)}, f32[1280]{0:T(1024)}, u32[]{:S(2)}) copy-start(f32[1280]{0:T(1024)} %param.7) | copy-start | bytes 15364
  0.7 25.9 %copy-start.6 = (f32[1280]{0:T(1024)S(1)}, f32[1280]{0:T(1024)}, u32[]{:S(2)}) copy-start(f32[1280]{0:T(1024)} %param.8) | copy-start | bytes 15364
  1.4 27.4 %collective-permute-start.12 = (bf16[2,8,640]{2,1,0:T(8,128)(2,1)S(1)}, bf16[2,8,640]{2,1,0:T(8,128)(2,1)S(1)}, u32[]{:S(2)}, u32[]{:S(2)}) collective-permute-start(bf16[2,8,640]{2,1,0:T(8,128)(2,1)S(1)} %pad_maximum_fusion.10), channel_id=1, source_target_pairs={{0,16},{16,0},{1,17},{17,1},{2,18},{18,2},{3,19},{19,3},{4,20},{20... | collective-permute-start | bytes 61448 | tf_op jit(solution)/shard_map/ppermute | solution.py:19
  4.5 44.3 %collective-permute-start.18 = (bf16[16,8,640]{2,1,0:T(8,128)(2,1)}, bf16[16,8,640]{2,1,0:T(8,128)(2,1)S(1)}, u32[]{:S(2)}, u32[]{:S(2)}) collective-permute-start(bf16[16,8,640]{2,1,0:T(8,128)(2,1)} %bitcast.109), channel_id=1, source_target_pairs={{0,16},{16,0},{1,17},{17,1},{2,18},{18,2},{3,19},{19,3},{4,20},{20... | collective-permute-start | bytes 491528 | tf_op jit(solution)/shard_map/ppermute | solution.py:19
  5.8 28.8 %collective-permute-start.15 = (bf16[16,2,640]{2,1,0:T(2,128)(2,1)S(1)}, bf16[16,2,640]{2,1,0:T(2,128)(2,1)S(1)}, u32[]{:S(2)}, u32[]{:S(2)}) collective-permute-start(bf16[16,2,640]{2,1,0:T(2,128)(2,1)S(1)} %pad_maximum_fusion.9), channel_id=1, source_target_pairs={{0,16},{16,0},{1,17},{17,1},{2,18},{18,2},{3,19},{19,3},{4,20},{20... | collective-permute-start | bytes 122888 | tf_op jit(solution)/shard_map/ppermute | solution.py:19
  8.8 40.1 %collective-permute-start.11 = (bf16[16,8,640]{2,1,0:T(8,128)(2,1)S(1)}, bf16[16,8,640]{2,1,0:T(8,128)(2,1)S(1)}, u32[]{:S(2)}, u32[]{:S(2)}) collective-permute-start(bf16[16,8,640]{2,1,0:T(8,128)(2,1)S(1)} %get-tuple-element.22), channel_id=1, source_target_pairs={{0,16},{16,0},{1,17},{17,1},{2,18},{18,2},{3,19},{19,3},{4,20},{20... | collective-permute-start | bytes 491528 | tf_op jit(solution)/shard_map/ppermute | solution.py:19
  9.8 5.0 %collective-permute-start = (f32[2,16]{1,0:T(2,128)S(1)}, f32[2,16]{1,0:T(2,128)S(1)}, u32[]{:S(2)}, u32[]{:S(2)}) collective-permute-start(f32[2,16]{1,0:T(2,128)S(1)} %get-tuple-element.77), channel_id=1, source_target_pairs={{0,16},{16,0},{1,17},{17,1},{2,18},{18,2},{3,19},{19,3},{4,20},{20... | collective-permute-start | bytes 392 | tf_op jit(solution)/shard_map/ppermute | solution.py:19
  12.0 36.7 %copy-start.3 = (bf16[1,16,8,640]{3,2,1,0:T(8,128)(2,1)S(1)}, bf16[1,16,8,640]{3,2,1,0:T(8,128)(2,1)}, u32[]{:S(2)}) copy-start(bf16[1,16,8,640]{3,2,1,0:T(8,128)(2,1)} %param.11) | copy-start | bytes 491524
  14.8 1.2 %collective-permute-start.1 = (f32[2,2,16]{2,1,0:T(2,128)S(1)}, f32[2,2,16]{2,1,0:T(2,128)S(1)}, u32[]{:S(2)}, u32[]{:S(2)}) collective-permute-start(f32[2,2,16]{2,1,0:T(2,128)S(1)} %pad_maximum_fusion.17), channel_id=1, source_target_pairs={{0,4},{4,0},{8,12},{12,8},{1,5},{5,1},{9,13},{13,9},{2,6},{6,2},{1... | collective-permute-start | bytes 776 | tf_op jit(solution)/shard_map/ppermute | solution.py:19
  16.0 3.1 %collective-permute-start.2 = (f32[2,2,16]{2,1,0:T(2,128)S(1)}, f32[2,2,16]{2,1,0:T(2,128)S(1)}, u32[]{:S(2)}, u32[]{:S(2)}) collective-permute-start(f32[2,2,16]{2,1,0:T(2,128)S(1)} %pad_maximum_fusion.18), channel_id=1, source_target_pairs={{0,12},{4,8},{8,4},{12,0},{1,13},{5,9},{9,5},{13,1},{2,14},{6,10},... | collective-permute-start | bytes 776 | tf_op jit(solution)/shard_map/ppermute | solution.py:19
  19.1 3.6 %collective-permute-start.3 = (f32[2,2,16]{2,1,0:T(2,128)S(1)}, f32[2,2,16]{2,1,0:T(2,128)S(1)}, u32[]{:S(2)}, u32[]{:S(2)}) collective-permute-start(f32[2,2,16]{2,1,0:T(2,128)S(1)} %pad_maximum_fusion.19), channel_id=1, source_target_pairs={{0,1},{1,0},{2,3},{3,2},{4,5},{5,4},{6,7},{7,6},{8,9},{9,8},{10,11... | collective-permute-start | bytes 776 | tf_op jit(solution)/shard_map/ppermute | solution.py:19
  22.8 5.4 %collective-permute-start.4 = (f32[2,2,16]{2,1,0:T(2,128)S(1)}, f32[2,2,16]{2,1,0:T(2,128)S(1)}, u32[]{:S(2)}, u32[]{:S(2)}) collective-permute-start(f32[2,2,16]{2,1,0:T(2,128)S(1)} %pad_maximum_fusion.20), channel_id=1, source_target_pairs={{0,3},{1,2},{2,1},{3,0},{4,7},{5,6},{6,5},{7,4},{8,11},{9,10},{10,... | collective-permute-start | bytes 776 | tf_op jit(solution)/shard_map/ppermute | solution.py:19
  28.2 3.8 %collective-permute-start.5 = (bf16[2,8,640]{2,1,0:T(8,128)(2,1)S(1)}, bf16[2,8,640]{2,1,0:T(8,128)(2,1)S(1)}, u32[]{:S(2)}, u32[]{:S(2)}) collective-permute-start(bf16[2,8,640]{2,1,0:T(8,128)(2,1)S(1)} %pad_maximum_fusion.12), channel_id=1, source_target_pairs={{0,16},{16,0},{1,17},{17,1},{2,18},{18,2},{3,19},{19,3},{4,20},{20... | collective-permute-start | bytes 61448 | tf_op jit(solution)/shard_map/ppermute | solution.py:19
  28.9 3.3 %collective-permute-start.13 = (bf16[2,8,640]{2,1,0:T(8,128)(2,1)S(1)}, bf16[2,8,640]{2,1,0:T(8,128)(2,1)S(1)}, u32[]{:S(2)}, u32[]{:S(2)}) collective-permute-start(bf16[2,8,640]{2,1,0:T(8,128)(2,1)S(1)} %get-tuple-element.43), channel_id=1, source_target_pairs={{0,12},{4,8},{8,4},{12,0},{1,13},{5,9},{9,5},{13,1},{2,14},{6,10},... | collective-permute-start | bytes 61448 | tf_op jit(solution)/shard_map/ppermute | solution.py:19
  32.0 1.7 %collective-permute-start.14 = (bf16[2,8,640]{2,1,0:T(8,128)(2,1)S(1)}, bf16[2,8,640]{2,1,0:T(8,128)(2,1)S(1)}, u32[]{:S(2)}, u32[]{:S(2)}) collective-permute-start(bf16[2,8,640]{2,1,0:T(8,128)(2,1)S(1)} %get-tuple-element.44), channel_id=1, source_target_pairs={{0,4},{4,0},{8,12},{12,8},{1,5},{5,1},{9,13},{13,9},{2,6},{6,2},{1... | collective-permute-start | bytes 61448 | tf_op jit(solution)/shard_map/ppermute | solution.py:19
  32.2 8.7 %collective-permute-start.8 = (bf16[16,2,640]{2,1,0:T(2,128)(2,1)S(1)}, bf16[16,2,640]{2,1,0:T(2,128)(2,1)S(1)}, u32[]{:S(2)}, u32[]{:S(2)}) collective-permute-start(bf16[16,2,640]{2,1,0:T(2,128)(2,1)S(1)} %pad_maximum_fusion.8), channel_id=1, source_target_pairs={{0,16},{16,0},{1,17},{17,1},{2,18},{18,2},{3,19},{19,3},{4,20},{20... | collective-permute-start | bytes 122888 | tf_op jit(solution)/shard_map/ppermute | solution.py:19
  33.8 3.4 %collective-permute-start.6 = (bf16[2,8,640]{2,1,0:T(8,128)(2,1)S(1)}, bf16[2,8,640]{2,1,0:T(8,128)(2,1)S(1)}, u32[]{:S(2)}, u32[]{:S(2)}) collective-permute-start(bf16[2,8,640]{2,1,0:T(8,128)(2,1)S(1)} %get-tuple-element.49), channel_id=1, source_target_pairs={{0,12},{4,8},{8,4},{12,0},{1,13},{5,9},{9,5},{13,1},{2,14},{6,10},... | collective-permute-start | bytes 61448 | tf_op jit(solution)/shard_map/ppermute | solution.py:19
  34.6 2.6 %collective-permute-start.7 = (bf16[2,8,640]{2,1,0:T(8,128)(2,1)S(1)}, bf16[2,8,640]{2,1,0:T(8,128)(2,1)S(1)}, u32[]{:S(2)}, u32[]{:S(2)}) collective-permute-start(bf16[2,8,640]{2,1,0:T(8,128)(2,1)S(1)} %get-tuple-element.50), channel_id=1, source_target_pairs={{0,4},{4,0},{8,12},{12,8},{1,5},{5,1},{9,13},{13,9},{2,6},{6,2},{1... | collective-permute-start | bytes 61448 | tf_op jit(solution)/shard_map/ppermute | solution.py:19
  37.2 5.3 %collective-permute-start.17 = (bf16[18,2,640]{2,1,0:T(2,128)(2,1)S(1)}, bf16[18,2,640]{2,1,0:T(2,128)(2,1)S(1)}, u32[]{:S(2)}, u32[]{:S(2)}) collective-permute-start(bf16[18,2,640]{2,1,0:T(2,128)(2,1)S(1)} %broadcast_select_fusion.4), channel_id=1, source_target_pairs={{0,1},{1,0},{2,3},{3,2},{4,5},{5,4},{6,7},{7,6},{8,9},{9,8},{10,11... | collective-permute-start | bytes 138248 | tf_op jit(solution)/shard_map/ppermute | solution.py:19
  37.2 7.8 %collective-permute-start.16 = (bf16[18,2,640]{2,1,0:T(2,128)(2,1)S(1)}, bf16[18,2,640]{2,1,0:T(2,128)(2,1)S(1)}, u32[]{:S(2)}, u32[]{:S(2)}) collective-permute-start(bf16[18,2,640]{2,1,0:T(2,128)(2,1)S(1)} %get-tuple-element.14), channel_id=1, source_target_pairs={{0,3},{1,2},{2,1},{3,0},{4,7},{5,6},{6,5},{7,4},{8,11},{9,10},{10,... | collective-permute-start | bytes 138248 | tf_op jit(solution)/shard_map/ppermute | solution.py:19
  41.3 4.1 %collective-permute-start.10 = (bf16[18,2,640]{2,1,0:T(2,128)(2,1)S(1)}, bf16[18,2,640]{2,1,0:T(2,128)(2,1)S(1)}, u32[]{:S(2)}, u32[]{:S(2)}) collective-permute-start(bf16[18,2,640]{2,1,0:T(2,128)(2,1)S(1)} %broadcast_select_fusion.8), channel_id=1, source_target_pairs={{0,1},{1,0},{2,3},{3,2},{4,5},{5,4},{6,7},{7,6},{8,9},{9,8},{10,11... | collective-permute-start | bytes 138248 | tf_op jit(solution)/shard_map/ppermute | solution.py:19
  42.4 5.9 %collective-permute-start.9 = (bf16[18,2,640]{2,1,0:T(2,128)(2,1)S(1)}, bf16[18,2,640]{2,1,0:T(2,128)(2,1)S(1)}, u32[]{:S(2)}, u32[]{:S(2)}) collective-permute-start(bf16[18,2,640]{2,1,0:T(2,128)(2,1)S(1)} %get-tuple-element.17), channel_id=1, source_target_pairs={{0,3},{1,2},{2,1},{3,0},{4,7},{5,6},{6,5},{7,4},{8,11},{9,10},{10,... | collective-permute-start | bytes 138248 | tf_op jit(solution)/shard_map/ppermute | solution.py:19
  49.9 3.1 %copy-start = (bf16[3,3,640,640]{3,2,1,0:T(8,128)(2,1)S(1)}, bf16[3,3,640,640]{3,2,1,0:T(8,128)(2,1)}, u32[]{:S(2)}) copy-start(bf16[3,3,640,640]{3,2,1,0:T(8,128)(2,1)} %w_ref.3) | copy-start | bytes 22118404
  58.5 3.7 %collective-permute-start.20 = (f32[4,16]{1,0:T(4,128)S(1)}, f32[4,16]{1,0:T(4,128)S(1)}, u32[]{:S(2)}, u32[]{:S(2)}) collective-permute-start(f32[4,16]{1,0:T(4,128)S(1)} %bitcast.132), channel_id=1, source_target_pairs={{0,16},{16,0},{1,17},{17,1},{2,18},{18,2},{3,19},{19,3},{4,20},{20... | collective-permute-start | bytes 776 | tf_op jit(solution)/shard_map/ppermute | solution.py:19
  59.2 21.7 %collective-permute-start.21 = (bf16[16,8,640]{2,1,0:T(8,128)(2,1)S(1)}, bf16[16,8,640]{2,1,0:T(8,128)(2,1)S(1)}, u32[]{:S(2)}, u32[]{:S(2)}) collective-permute-start(bf16[16,8,640]{2,1,0:T(8,128)(2,1)S(1)} %bitcast.105), channel_id=1, source_target_pairs={{0,16},{16,0},{1,17},{17,1},{2,18},{18,2},{3,19},{19,3},{4,20},{20... | collective-permute-start | bytes 491528 | tf_op jit(solution)/shard_map/ppermute | solution.py:19
  62.3 6.6 %collective-permute-start.22 = (f32[2,32]{1,0:T(2,128)S(1)}, f32[2,32]{1,0:T(2,128)S(1)}, u32[]{:S(2)}, u32[]{:S(2)}) collective-permute-start(f32[2,32]{1,0:T(2,128)S(1)} %slice.201), channel_id=1, source_target_pairs={{0,4},{4,0},{8,12},{12,8},{1,5},{5,1},{9,13},{13,9},{2,6},{6,2},{1... | collective-permute-start | bytes 776 | tf_op jit(solution)/shard_map/ppermute | solution.py:19
  68.3 13.6 %collective-permute-start.19 = (bf16[16,8,640]{2,1,0:T(8,128)(2,1)S(1)}, bf16[16,8,640]{2,1,0:T(8,128)(2,1)S(1)}, u32[]{:S(2)}, u32[]{:S(2)}) collective-permute-start(bf16[16,8,640]{2,1,0:T(8,128)(2,1)S(1)} %bitcast.106), channel_id=1, source_target_pairs={{0,16},{16,0},{1,17},{17,1},{2,18},{18,2},{3,19},{19,3},{4,20},{20... | collective-permute-start | bytes 491528 | tf_op jit(solution)/shard_map/ppermute | solution.py:19
  68.9 3.6 %collective-permute-start.23 = (f32[2,32]{1,0:T(2,128)S(1)}, f32[2,32]{1,0:T(2,128)S(1)}, u32[]{:S(2)}, u32[]{:S(2)}) collective-permute-start(f32[2,32]{1,0:T(2,128)S(1)} %slice_add_fusion.3), channel_id=1, source_target_pairs={{0,8},{4,12},{8,0},{12,4},{1,9},{5,13},{9,1},{13,5},{2,10},{6,14},... | collective-permute-start | bytes 776 | tf_op jit(solution)/shard_map/ppermute | solution.py:19
  70.2 11.6 %copy-start.4 = (f32[640]{0:T(1024)S(1)}, f32[640]{0:T(1024)}, u32[]{:S(2)}) copy-start(f32[640]{0:T(1024)} %param.10) | copy-start | bytes 7684
  72.5 3.6 %collective-permute-start.24 = (f32[2,32]{1,0:T(2,128)S(1)}, f32[2,32]{1,0:T(2,128)S(1)}, u32[]{:S(2)}, u32[]{:S(2)}) collective-permute-start(f32[2,32]{1,0:T(2,128)S(1)} %add.178), channel_id=1, source_target_pairs={{0,1},{1,0},{2,3},{3,2},{4,5},{5,4},{6,7},{7,6},{8,9},{9,8},{10,11... | collective-permute-start | bytes 776 | tf_op jit(solution)/shard_map/ppermute | solution.py:19
  76.1 4.5 %collective-permute-start.25 = (f32[2,32]{1,0:T(2,128)S(1)}, f32[2,32]{1,0:T(2,128)S(1)}, u32[]{:S(2)}, u32[]{:S(2)}) collective-permute-start(f32[2,32]{1,0:T(2,128)S(1)} %add.179), channel_id=1, source_target_pairs={{0,2},{1,3},{2,0},{3,1},{4,6},{5,7},{6,4},{7,5},{8,10},{9,11},{10,... | collective-permute-start | bytes 776 | tf_op jit(solution)/shard_map/ppermute | solution.py:19
  (1 other events, 3.1 us)

commit v2 on v0

v2 whole, which is shorter than its diff:
```python
import functools

import jax
import jax.numpy as jnp
from jax import lax
from jax.experimental import pallas as pl
from jax.experimental.pallas import tpu as pltpu
from jax.sharding import PartitionSpec as P

GROUPS = 32
EPS = 1e-05
F32 = jnp.float32
BF16 = jnp.bfloat16

ME, EVEN_H, EVEN_W, UP, DOWN, LEFT, RIGHT = range(7)


def exchange(value, axis, partner, ends=True):
    count = lax.axis_size(axis)
    pairs = [(i, partner(i) % count) for i in range(count)]
    if not ends:
        pairs = [(i, j) for i, j in pairs if abs(i - j) == 1]
    return lax.ppermute(value, axis, pairs)


def near(i):
    return i ^ 1


def across(i):
    return i - 1 if i % 2 == 0 else i + 1


def merged(stats, other, n):
    delta = other[:, :1] - stats[:, :1]
    return jnp.concatenate([stats[:, :1] + 0.5 * delta, stats[:, 1:] + other[:, 1:] + (0.5 * n) * delta * delta], 1)


def packed(strips, stats):
    high = lax.reduce_precision(stats, 8, 7)
    middle = lax.reduce_precision(stats - high, 8, 7)
    low = lax.reduce_precision(stats - high - middle, 8, 7)
    rows = jnp.concatenate([high, middle, low], 1).astype(BF16)
    rows = jnp.pad(rows, ((0, 0), (0, 0), (0, strips.shape[2] - rows.shape[2])))
    return jnp.concatenate([strips, rows], 1)


def unpacked(pack, r, groups):
    rows = pack[:, r : r + 6, :groups].astype(F32)
    return pack[:, :r], rows[:, :2] + rows[:, 2:4] + rows[:, 4:]


def members(groups, chans, dim):
    per_group = chans // groups
    shape = (groups, chans) if dim else (chans, groups)
    chan = lax.broadcasted_iota(jnp.int32, shape, dim)
    group = lax.broadcasted_iota(jnp.int32, shape, 1 - dim)
    return ((chan >= group * per_group) & (chan < (group + 1) * per_group)).astype(F32)


def three_parts(a):
    high = a.astype(BF16)
    rest = a - high.astype(F32)
    middle = rest.astype(BF16)
    return high, middle, (rest - middle.astype(F32)).astype(BF16)


def exact_dot(a, b):
    rows = a.shape[0]
    parts = jnp.concatenate([p.astype(F32) for p in three_parts(a)], 0).astype(BF16)
    sums = jnp.dot(parts, b.astype(BF16), preferred_element_type=F32)
    return sums[:rows] + sums[rows : 2 * rows] + sums[2 * rows :]


def expanded(values, chans):
    return exact_dot(values, members(values.shape[-1], chans, 1))


def gathered(values, groups):
    return exact_dot(values, members(groups, values.shape[-1], 0))


def shard_of(pieces, shard):
    value = pieces[0]
    for i in range(1, len(pieces)):
        value = jnp.where(shard == i, pieces[i], value)
    return value


def first_kernel(parts, groups, info_ref, x_hbm, cot_hbm, *refs):
    out_refs, (x_ref, cot_ref, sems) = refs[:parts], refs[parts:]
    rows, cols, cin = x_ref.shape
    chans = cin // parts
    n = rows * cols * (chans // groups)
    x_copy = pltpu.make_async_copy(x_hbm, x_ref, sems.at[0])
    cot_copy = pltpu.make_async_copy(cot_hbm, cot_ref, sems.at[1])
    x_copy.start()
    cot_copy.start()
    me = info_ref[ME]
    even_h = info_ref[EVEN_H] > 0
    x_copy.wait()
    shards = [x_ref[:, :, s * chans : (s + 1) * chans].astype(F32) for s in range(parts)]
    stats = []
    for x in shards:
        flat = x.reshape(rows * cols, chans)
        mean = gathered(jnp.sum(flat, axis=0, keepdims=True), groups) / n
        centered = flat - expanded(mean, chans)
        squares = gathered(jnp.sum(centered * centered, axis=0, keepdims=True), groups)
        stats.append(jnp.concatenate([p.astype(F32) for p in three_parts(jnp.concatenate([mean, squares], 0))], 0))
    cot_copy.wait()
    ends = lambda t: (jnp.where(even_h, t[rows - 1], t[0]), jnp.where(even_h, t[0], t[rows - 1]))
    cot_ends = ends(cot_ref[...].astype(F32))
    x_ends = [ends(x) for x in shards]
    for k in range(parts):
        shard = lax.rem(me + k, parts)
        out_refs[k][: 2 * cols, :chans] = jnp.concatenate([shard_of([e[i] for e in x_ends], shard) for i in range(2)], 0).astype(BF16)
        out_refs[k][: 2 * cols, chans:] = jnp.concatenate(cot_ends, 0).astype(BF16)
        out_refs[k][2 * cols :, :] = jnp.zeros((8, out_refs[k].shape[1]), BF16)
        out_refs[k][2 * cols : 2 * cols + 6, :groups] = shard_of(stats, shard).astype(BF16)


def second_kernel(parts, info_ref, x_ref, cot_ref, *refs):
    out_refs = refs[parts - 1 :]
    rows, cols, cin = x_ref.shape
    chans = cin // parts
    me = info_ref[ME]
    even_w = info_ref[EVEN_W] > 0

    def ends(t):
        first, last = t[:, 0, :], t[:, cols - 1, :]
        return jnp.concatenate([jnp.where(even_w, last, first), jnp.where(even_w, first, last)], 0).astype(BF16)

    cot_ends = ends(cot_ref[...].astype(F32))
    shards = [x_ref[:, :, s * chans : (s + 1) * chans].astype(F32) for s in range(parts)]
    for k in range(parts):
        tile_ref, ends_ref = out_refs[2 * k : 2 * k + 2]
        x = shard_of(shards, lax.rem(me + k, parts))
        tile_ref[...] = x.astype(BF16)
        ends_ref[:, :chans] = ends(x)
        ends_ref[:, chans:] = cot_ends


def load_kernel(w_hbm, after_ref, w_ref, sem):
    copy = pltpu.make_async_copy(w_hbm, w_ref, sem)
    copy.start()
    copy.wait()


def halos(info_ref, near_h, across_h, near_w, across_w, lanes):
    even_h = info_ref[EVEN_H] > 0
    even_w = info_ref[EVEN_W] > 0
    rows = near_w.shape[1] - 2

    def strips(k):
        a, b = near_h[k, :, lanes].astype(F32), across_h[k, :, lanes].astype(F32)
        above, below = jnp.where(even_h, b, a), jnp.where(even_h, a, b)
        c, d = near_w[k, :, lanes].astype(F32), across_w[k, :, lanes].astype(F32)
        before, after = jnp.where(even_w, d, c), jnp.where(even_w, c, d)

        def ordered(t):
            head, tail = t[0:1], t[rows + 1 : rows + 2]
            return jnp.where(even_h, tail, head), t[1 : rows + 1], jnp.where(even_h, head, tail)

        return above, below, ordered(before), ordered(after)

    return strips


def windows(padded_ref, windows_ref, k_all, cols):
    for kx in range(3):
        view = padded_ref[:, :, kx : kx + cols, :]
        windows_ref[kx] = view.reshape(view.shape[0], k_all * cols, view.shape[3]).astype(BF16)


def backward_kernel(parts, info_ref, *refs):
    tiles, (near_h, across_h, near_w, across_w, w_ref, grad_ref, padded_ref, windows_ref) = refs[:parts], refs[parts:]
    rows, cols, outs = tiles[0].shape
    chans = w_ref.shape[2]
    strips = halos(info_ref, near_h, across_h, near_w, across_w, slice(chans, chans + outs))
    for k in range(parts):
        above, below, before, after = strips(k)
        padded_ref[1 : rows + 1, k, 1 : cols + 1, :] = tiles[k][...].astype(F32)
        padded_ref[0, k, 1 : cols + 1, :] = above
        padded_ref[rows + 1, k, 1 : cols + 1, :] = below
        for at, (top, mid, bottom) in ((0, before), (cols + 1, after)):
            padded_ref[0, k, at : at + 1, :] = top
            padded_ref[1 : rows + 1, k, at, :] = mid
            padded_ref[rows + 1, k, at : at + 1, :] = bottom
    windows(padded_ref, windows_ref, parts, cols)
    total = None
    for ky in range(3):
        for kx in range(3):
            window = windows_ref[kx, ky : ky + rows].reshape(rows * parts * cols, outs)
            term = lax.dot_general(w_ref[2 - ky, 2 - kx], window, (((1,), (1,)), ((), ())), preferred_element_type=F32)
            total = term if total is None else total + term
    grad_ref[...] = total.T.reshape(rows, parts, cols, chans)


def terms_kernel(parts, count, info_ref, *refs):
    tiles = refs[:parts]
    near_h, across_h, near_w, across_w, stats_ref, gain_ref, shift_ref, grad_ref = refs[parts : parts + 8]
    moments_ref, gx_own_ref, gx_other_ref, windows_ref, padded_ref = refs[parts + 8 :]
    rows, cols, _ = tiles[0].shape
    chans = grad_ref.shape[3]
    groups = stats_ref.shape[2]
    lanes = slice(0, chans)
    stats = jnp.concatenate([stats_ref[:, 0], stats_ref[:, 1]], 0)
    strips = halos(info_ref, near_h, across_h, near_w, across_w, lanes)
    wide = expanded(jnp.concatenate([stats[:parts], lax.rsqrt(stats[parts:] / count + EPS)], 0), chans)
    means, invs = wide[:parts], wide[parts:]
    gain, shift = gain_ref[...], shift_ref[...]
    up, down, left, right = (info_ref[i] > 0 for i in (UP, DOWN, LEFT, RIGHT))
    firsts, seconds = [], []
    for k in range(parts):
        mean, inv = means[k : k + 1], invs[k : k + 1]

        def act_of(t, inside):
            z = (t - mean) * inv * gain + shift
            return jnp.where(inside, z * jax.nn.sigmoid(z), 0.0)

        above, below, before, after = strips(k)
        xhat = (tiles[k][...].astype(F32) - mean[None]) * inv[None]
        z = xhat * gain[None] + shift[None]
        sig = jax.nn.sigmoid(z)
        padded_ref[1 : rows + 1, k, 1 : cols + 1, :] = z * sig
        padded_ref[0, k, 1 : cols + 1, :] = act_of(above, up)
        padded_ref[rows + 1, k, 1 : cols + 1, :] = act_of(below, down)
        for at, (top, mid, bottom), side in ((0, before, left), (cols + 1, after, right)):
            padded_ref[0, k, at : at + 1, :] = act_of(top, side & up)
            padded_ref[1 : rows + 1, k, at, :] = act_of(mid, side)
            padded_ref[rows + 1, k, at : at + 1, :] = act_of(bottom, side & down)
        gx = grad_ref[:, k] * sig * (1.0 + z * (1.0 - sig)) * gain[None]
        if k == 0:
            gx_own_ref[...] = gx
        else:
            gx_other_ref[k - 1] = gx.astype(BF16)
        firsts.append(jnp.sum(gx.reshape(rows * cols, chans), axis=0, keepdims=True))
        seconds.append(jnp.sum((gx * xhat).reshape(rows * cols, chans), axis=0, keepdims=True))
    sums = gathered(jnp.concatenate(firsts + seconds, 0), groups)
    moments_ref[0] = sums[:parts]
    moments_ref[1] = sums[parts:]
    moments_ref[2] = stats[:parts]
    moments_ref[3] = stats[parts:]
    windows(padded_ref, windows_ref, parts, cols)


def forward_kernel(parts, info_ref, windows_ref, w_ref, conv_own_ref, conv_other_ref):
    rows, cols, _ = conv_own_ref.shape
    chans, outs = w_ref.shape[2:]
    total = None
    for ky in range(3):
        for kx in range(3):
            window = windows_ref[kx, ky : ky + rows].reshape(rows * parts * cols, chans)
            term = jnp.dot(window, w_ref[ky, kx], preferred_element_type=F32)
            total = term if total is None else total + term
    total = total.reshape(rows, parts, cols, outs)
    conv_own_ref[...] = total[:, 0]
    for k in range(1, parts):
        conv_other_ref[k - 1] = total[:, k].astype(BF16)


def finish_kernel(parts, count, info_ref, x_ref, stats_ref, sums_ref, bias_ref, gx_own_ref, conv_own_ref, *refs):
    gx_refs, conv_refs = refs[: parts - 1], refs[parts - 1 : 2 * parts - 2]
    conv_ref, grad_ref = refs[2 * parts - 2 :]
    cin = x_ref.shape[2]
    chans = cin // parts
    conv = conv_own_ref[...] + bias_ref[...][None]
    for r in conv_refs:
        conv = conv + r[...].astype(F32)
    conv_ref[...] = conv.astype(BF16)
    wide = jnp.concatenate([stats_ref[0:1], lax.rsqrt(stats_ref[1:2] / count + EPS), sums_ref[...] / count], 0)
    wide = expanded(wide, cin)
    mean, inv, first, second = (wide[i : i + 1] for i in range(4))
    me = info_ref[ME]
    for s in range(parts):
        at = slice(s * chans, (s + 1) * chans)
        gx = gx_own_ref[...]
        for k in range(1, parts):
            gx = jnp.where(lax.rem(me + k, parts) == s, gx_refs[k - 1][...].astype(F32), gx)
        xhat = (x_ref[:, :, at].astype(F32) - mean[None, :, at]) * inv[None, :, at]
        grad = inv[None, :, at] * (gx - first[None, :, at] - xhat * second[None, :, at])
        grad_ref[:, :, at] = grad.astype(BF16)


def call(kernel, name, outs, operands, scratch=(), in_hbm=(), limit=28):
    spec = lambda i: pl.BlockSpec(memory_space=pltpu.HBM if i in in_hbm else pltpu.SMEM if i == 0 else pltpu.VMEM)
    return pl.pallas_call(
        kernel,
        out_shape=outs,
        in_specs=[spec(i) for i in range(len(operands))],
        out_specs=[pl.BlockSpec(memory_space=pltpu.VMEM)] * len(outs),
        scratch_shapes=scratch,
        compiler_params=pltpu.CompilerParams(vmem_limit_bytes=limit * 2**20),
        name=name,
    )(*operands)


def tied(value, *others):
    for other in others:
        value = value + 0.0 * other[0, :1, : value.shape[-1]].astype(F32)
    return value


def stats_rounds(axis):
    count = lax.axis_size(axis)
    if count == 4:
        return [near, lambda i: i ^ 2]
    return [functools.partial(lambda step, i: i ^ step, 2**j) for j in range(count.bit_length() - 1)]


def body(latents, norm_gain, norm_shift, conv_weight, conv_bias, cotangent):
    _, rows, cols, cin = latents.shape
    outs = cotangent.shape[3]
    chans = conv_weight.shape[2]
    parts = lax.axis_size("dp")
    me = lax.axis_index("dp")
    groups = GROUPS * chans // cin
    both = chans + outs
    n = rows * cols * (cin // GROUPS)
    count = float(n * lax.axis_size("ha") * lax.axis_size("wa"))
    x, cot = latents[0], cotangent[0]
    sds = jax.ShapeDtypeStruct
    where = [lax.axis_index(a) for a in ("ha", "wa")]
    last = [lax.axis_size(a) - 1 for a in ("ha", "wa")]
    info = jnp.stack(
        [me, where[0] % 2 == 0, where[1] % 2 == 0, where[0] > 0, where[0] < last[0], where[1] > 0, where[1] < last[1]]
    ).astype(jnp.int32)
    gain = lax.dynamic_slice_in_dim(norm_gain, me * chans, chans, 0)[None]
    shift = lax.dynamic_slice_in_dim(norm_shift, me * chans, chans, 0)[None]

    *first, x, cot = call(
        functools.partial(first_kernel, parts, groups),
        "first",
        [sds((2 * cols + 8, both), BF16)] * parts + [sds(x.shape, BF16), sds(cot.shape, BF16)],
        [info, x, cot],
        [pltpu.SemaphoreType.DMA((2,))],
        in_hbm=(1, 2),
        limit=40,
    )
    peers = [[(i, (i + k) % parts) for i in range(parts)] for k in range(1, parts)]
    from_peers = lambda values: [lax.ppermute(v, "dp", pairs) for v, pairs in zip(values, peers)]
    got = from_peers(first[1:])
    ends_h, stats = unpacked(jnp.stack([first[0], *got], 0), 2 * cols, groups)
    second = call(
        functools.partial(second_kernel, parts),
        "second",
        [sds((rows, cols, chans), BF16), sds((2 * rows, both), BF16)] * parts,
        [info, x, cot, *got],
    )
    ends_w = jnp.stack([second[1], *from_peers(second[3::2])], 0)
    cot_tiles = [cot, *from_peers([cot] * (parts - 1))]
    x_tiles = [second[0], *from_peers(second[2::2])]

    def reduced(stats, n, axis, pairings):
        for partner in pairings:
            stats, n = merged(stats, exchange(stats, axis, partner), n), 2 * n
        return stats, n

    rounds_h, rounds_w = stats_rounds("ha"), stats_rounds("wa")
    near_h, other = unpacked(exchange(packed(ends_h[:, :cols], stats), "ha", near), cols, groups)
    stats, n = merged(stats, other, n), 2 * n
    if lax.axis_size("ha") == 4:
        across_h, other = unpacked(exchange(packed(ends_h[:, cols:], tied(stats, near_h)), "ha", across), cols, groups)
        stats, n = merged(stats, other, n), 2 * n
    else:
        across_h = exchange(ends_h[:, cols:], "ha", across)
        stats, n = reduced(stats, n, "ha", rounds_h[1:])
    across_h = jnp.where((where[0] > 0) & (where[0] < last[0]), across_h, jnp.zeros_like(across_h))

    def column(part, end):
        corner = lambda t: jnp.where(end, t[:, cols - 1 :], t[:, :1])
        return jnp.concatenate([corner(near_h), part, corner(across_h)], 1)

    even_w = where[1] % 2 == 0
    pack = packed(column(ends_w[:, :rows], even_w), stats)
    (weight,) = call(
        load_kernel,
        "load",
        [sds(conv_weight.shape, BF16)],
        [conv_weight, stats],
        [pltpu.SemaphoreType.DMA],
        in_hbm=(0,),
        limit=40,
    )
    near_w, other = unpacked(exchange(pack, "wa", near), rows + 2, groups)
    across_w = exchange(column(ends_w[:, rows:], ~even_w), "wa", across, ends=False)
    stats, n = merged(stats, other, n), 2 * n
    stats, n = reduced(tied(stats, weight[0], *cot_tiles[1:]), n, "wa", rounds_w[1:])

    strips = [near_h, across_h, near_w, across_w]
    padded = lambda depth: pltpu.VMEM((rows + 2, parts, cols + 8, depth), F32)
    shifted = (3, rows + 2, parts * cols)
    (grad_act,) = call(
        functools.partial(backward_kernel, parts),
        "conv_backward",
        [sds((rows, parts, cols, chans), F32)],
        [info, *cot_tiles, *strips, weight],
        [padded(outs), pltpu.VMEM((*shifted, outs), BF16)],
    )
    small, gx_own, gx_other, act = call(
        functools.partial(terms_kernel, parts, count),
        "terms",
        [
            sds((4, parts, groups), F32),
            sds((rows, cols, chans), F32),
            sds((parts - 1, rows, cols, chans), BF16),
            sds((*shifted, chans), BF16),
        ],
        [info, *x_tiles, *strips, stats, gain, shift, grad_act],
        [padded(chans)],
    )
    conv_own, conv_other = call(
        functools.partial(forward_kernel, parts),
        "conv_forward",
        [sds((rows, cols, outs), F32), sds((parts - 1, rows, cols, outs), BF16)],
        [info, act, weight],
    )

    place = lambda a, v, k: lax.dynamic_update_slice_in_dim(a, v, (me + k) % parts * groups, 1)
    whole = place(jnp.zeros((4, GROUPS), F32), small[:, 0], 0)
    gx, conv = [], []
    for k in range(1, parts):
        pairs = [(i, (i - k) % parts) for i in range(parts)]
        whole = place(whole, lax.ppermute(small[:, k], "dp", pairs), k)
        gx.append(lax.ppermute(gx_other[k - 1], "dp", pairs))
        conv.append(lax.ppermute(conv_other[k - 1], "dp", pairs))
    sums = whole[:2]
    for axis, pairings in (("ha", rounds_h), ("wa", rounds_w)):
        for partner in pairings:
            sums = sums + exchange(sums, axis, partner)
    conv_out, grad = call(
        functools.partial(finish_kernel, parts, count),
        "finish",
        [sds((rows, cols, outs), BF16), sds((rows, cols, cin), BF16)],
        [info, x, whole[2:], sums, conv_bias[None], gx_own, conv_own, *gx, *conv],
    )
    return conv_out[None], grad[None]


def solution(mesh):
    tile = P("dp", "ha", "wa", None)
    return jax.shard_map(
        body,
        mesh=mesh,
        in_specs=(tile, P(), P(), P(None, None, "dp", None), P(), tile),
        out_specs=(tile, tile),
        check_vma=False,
    )
```

time: 280 us -> 58.5 us (0.21)
  waiting for transfers between devices: 112 us -> 14.2 us
  blocking collectives: 97.7 us -> 0 us
  matrix products: 35.9 us -> 0 us
  Pallas kernels: 0 us -> 16.1 us
  between operations: 14.4 us -> 0.97 us
  starting transfers between devices: 15 us -> 22.4 us
  local copies, waits for them, and re-layouts: 1.25 us -> 4.16 us
    all_gather x1 -> x0, waiting for transfers between devices: 105 us -> none  [body(): full_kernel = lax.all_gather(conv_weight, 'dp', axis=2, tiled=True)]
    psum x3 -> x0, blocking collectives: 97.7 us -> none  [the longest x1 34.7 us: body(): total = lax.psum(jnp.sum(xg, axis=(1, 2, 4)), ('ha', 'wa'))]
    dot_general x18 -> x0, matrix products: 35.9 us -> none  [the longest x9 18.5 us: backward_taps(): lax.dot_general(window, kernel[2 - ky, 2 - kx], (((1,), (1,)), ((), ())),...]
    pallas_call x0 -> x7, Pallas kernels: none -> 16.1 us  [call(): pl.pallas_call(kernel, out_shape=outs, in_specs=[spec(i) for i in range(l...]
    ppermute x8 -> x16, waiting for transfers between devices: 5.87 us -> 14.2 us  [the longest x9 8.34 us: exchange(): return lax.ppermute(value, axis, pairs)]
    ppermute x8 -> x16, starting transfers between devices: 15 us -> 22.4 us  [the longest x9 11.9 us: exchange(): return lax.ppermute(value, axis, pairs)]
  transfers between devices with their start and end apart: 9 -> 16, of which waited for: 3 -> 6; matrix products, arithmetic and copies ran while one was open for 3% -> 4% of each run, Pallas kernels for 0% -> 18%
where the time goes in v2:
time: 58.5 us; the launch traced here: 58.2 us
  starting transfers between devices  22.4 us (38%)
  Pallas kernels  16.1 us (28%)
  waiting for transfers between devices  14.2 us (24%)
  local copies, waits for them, and re-layouts  4.16 us (7%)
  between operations  0.97 us (2%)
    pallas_call x7, Pallas kernels, call(): pl.pallas_call(kernel, out_shape=outs, in_specs=[spec(i) for i in range(l...  16.1 us
    ppermute x9, starting transfers between devices, exchange(): return lax.ppermute(value, axis, pairs)  11.9 us
    ppermute x9, waiting for transfers between devices, exchange(): return lax.ppermute(value, axis, pairs)  8.34 us
    ppermute x4, starting transfers between devices, body(): lax.ppermute(v, 'dp', pairs)  6.78 us
    ppermute x4, waiting for transfers between devices, body(): lax.ppermute(v, 'dp', pairs)  5.81 us
    unnamed x6, local copies, waits for them, and re-layouts  1.89 us
    ppermute x1, starting transfers between devices, body(): whole = place(whole, lax.ppermute(small[:, k], 'dp', pairs), k)  1.58 us
    ppermute x1, starting transfers between devices, body(): conv.append(lax.ppermute(conv_other[k - 1], 'dp', pairs))  1.52 us
  transfers between devices with their start and end apart: 16, of which 6 were waited for; matrix products, arithmetic and copies ran while one was open for 4% of the time, Pallas kernels for 18%

profile of v2, /device:TPU:0, one launch (start us, length us, event | category | flops | bytes accessed | tf_op | source)
XLA Modules:
  0.0 58.2 jit_solution(4523826227945025238)
XLA Ops:
  0.8 1.0 %copy-done = bf16[1,16,8,1280]{3,2,1,0:T(8,128)(2,1)S(1)} copy-done((bf16[1,16,8,1280]{3,2,1,0:T(8,128)(2,1)S(1)}, bf16[1,16,8,1280]{3,2,1,0:T(8,128)(2,1)}, u32[]{:S(2)}) %copy-start) | copy-done | bytes 327704
  1.7 0.9 %copy-done.1 = bf16[1,16,8,640]{3,2,1,0:T(8,128)(2,1)S(1)} copy-done((bf16[1,16,8,640]{3,2,1,0:T(8,128)(2,1)S(1)}, bf16[1,16,8,640]{3,2,1,0:T(8,128)(2,1)}, u32[]{:S(2)}) %copy-start.1) | copy-done | bytes 163864
  2.6 1.8 %first.1 = (bf16[24,1280]{1,0:T(8,128)(2,1)S(1)}, bf16[24,1280]{1,0:T(8,128)(2,1)S(1)}, bf16[16,8,1280]{2,1,0:T(8,128)(2,1)S(1)}, bf16[16,8,640]{2,1,0:T(8,128)(2,1)S(1)}) custom-call(s32[7]{0:T(128)S(1)} %stack.73.info_ref, bf16[16,8,1280]{2,1,0:T(8,128)(2,1)S(1)} %bitcast.36, bf16[16,8,640]{2,1,0:T(8,128)(2,1)S(1)} %bitcast.39), custom_call_target="tpu_custom_call" | custom-call | tf_op jit(solution)/shard_map/first/pallas_call | solution.py:287
  4.4 3.0 %collective-permute-start = (bf16[24,1280]{1,0:T(8,128)(2,1)S(1)}, bf16[24,1280]{1,0:T(8,128)(2,1)S(1)}, u32[]{:S(2)}, u32[]{:S(2)}) collective-permute-start(bf16[24,1280]{1,0:T(8,128)(2,1)S(1)} %get-tuple-element.20), channel_id=1, source_target_pairs={{0,16},{16,0},{1,17},{17,1},{2,18},{18,2},{3,19},{19,3},{4,20},{20... | collective-permute-start | bytes 184328 | tf_op jit(solution)/shard_map/ppermute | solution.py:341
  7.5 2.2 %collective-permute-done.refs_0_ = bf16[24,1280]{1,0:T(8,128)(2,1)S(1)} collective-permute-done((bf16[24,1280]{1,0:T(8,128)(2,1)S(1)}, bf16[24,1280]{1,0:T(8,128)(2,1)S(1)}, u32[]{:S(2)}, u32[]{:S(2)}) %collective-permute-start) | collective-permute-done | bytes 61472 | tf_op jit(solution)/shard_map/ppermute | solution.py:341
  9.8 2.1 %collective-permute-start.7 = (bf16[16,8,640]{2,1,0:T(8,128)(2,1)S(1)}, bf16[16,8,640]{2,1,0:T(8,128)(2,1)S(1)}, u32[]{:S(2)}, u32[]{:S(2)}) collective-permute-start(bf16[16,8,640]{2,1,0:T(8,128)(2,1)S(1)} %get-tuple-element.19.cot_ref.refs_0_), channel_id=1, source_target_pairs={{0,16},{16,0},{1,17},{17,1},{2,18},{18,2},{3,19},{19,3},{4,20},{20... | collective-permute-start | bytes 491528 | tf_op jit(solution)/shard_map/ppermute | solution.py:341
  11.9 0.8 %dynamic_slice.6 = f32[640]{0:T(1024)S(1)} dynamic-slice(f32[1280]{0:T(1024)} %param.7, s32[]{:T(128)S(6)} %select_n.71), dynamic_slice_sizes={640} | dynamic-slice | bytes 5124 | tf_op jit(solution)/shard_map/dynamic_slice | solution.py:328
  12.7 0.8 %dynamic_slice.7 = f32[640]{0:T(1024)S(1)} dynamic-slice(f32[1280]{0:T(1024)} %param.8, s32[]{:T(128)S(6)} %select_n.71), dynamic_slice_sizes={640} | dynamic-slice | bytes 5124 | tf_op jit(solution)/shard_map/dynamic_slice | solution.py:329
  13.5 0.9 %second.1 = (bf16[16,8,640]{2,1,0:T(8,128)(2,1)S(1)}, bf16[32,1280]{1,0:T(8,128)(2,1)S(1)}, bf16[16,8,640]{2,1,0:T(8,128)(2,1)S(1)}, bf16[32,1280]{1,0:T(8,128)(2,1)S(1)}) custom-call(s32[7]{0:T(128)S(1)} %stack.73.info_ref, bf16[16,8,1280]{2,1,0:T(8,128)(2,1)S(1)} %get-tuple-element.18.x_ref, bf16[16,8,640]{2,1,0:T(8,128)(2,1)S(1)} %get-tuple-element.19.cot_ref.refs_0_, ...), custom_call_target="tpu_custom_call" | custom-call | tf_op jit(solution)/shard_map/second/pallas_call | solution.py:287
  14.6 1.5 %collective-permute-start.3 = (bf16[2,14,1280]{2,1,0:T(8,128)(2,1)S(1)}, bf16[2,14,1280]{2,1,0:T(8,128)(2,1)S(1)}, u32[]{:S(2)}, u32[]{:S(2)}) collective-permute-start(bf16[2,14,1280]{2,1,0:T(8,128)(2,1)S(1)} %fusion.10), channel_id=1, source_target_pairs={{0,12},{4,8},{8,4},{12,0},{1,13},{5,9},{9,5},{13,1},{2,14},{6,10},... | collective-permute-start | bytes 215048 | tf_op jit(solution)/shard_map/ppermute | solution.py:23
  16.1 2.8 %collective-permute-done.4 = bf16[32,1280]{1,0:T(8,128)(2,1)S(1)} collective-permute-done((bf16[32,1280]{1,0:T(8,128)(2,1)S(1)}, bf16[32,1280]{1,0:T(8,128)(2,1)S(1)}, u32[]{:S(2)}, u32[]{:S(2)}) %collective-permute-start.4) | collective-permute-done | bytes 81952 | tf_op jit(solution)/shard_map/ppermute | solution.py:341
  19.2 2.4 %collective-permute-start.5 = (bf16[2,24,1280]{2,1,0:T(8,128)(2,1)S(1)}, bf16[2,24,1280]{2,1,0:T(8,128)(2,1)S(1)}, u32[]{:S(2)}, u32[]{:S(2)}) collective-permute-start(bf16[2,24,1280]{2,1,0:T(8,128)(2,1)S(1)} %pad_maximum_fusion), channel_id=1, source_target_pairs={{0,1},{1,0},{2,3},{3,2},{4,5},{5,4},{6,7},{7,6},{8,9},{9,8},{10,11... | collective-permute-start | bytes 368648 | tf_op jit(solution)/shard_map/ppermute | solution.py:23
  21.7 0.7 %collective-permute-start.6 = (bf16[2,18,1280]{2,1,0:T(8,128)(2,1)S(1)}, bf16[2,18,1280]{2,1,0:T(8,128)(2,1)S(1)}, u32[]{:S(2)}, u32[]{:S(2)}) collective-permute-start(bf16[2,18,1280]{2,1,0:T(8,128)(2,1)S(1)} %fusion.7), channel_id=1, source_target_pairs={{1,2},{2,1},{5,6},{6,5},{9,10},{10,9},{13,14},{14,13},{17,18},{18,... | collective-permute-start | bytes 276488 | tf_op jit(solution)/shard_map/ppermute | solution.py:23
  22.4 3.1 %load.1.refs_6_.w_ref = bf16[3,3,640,640]{3,2,1,0:T(8,128)(2,1)S(1)} custom-call(bf16[3,3,640,640]{3,2,1,0:T(8,128)(2,1)} %w_hbm.1, f32[2,2,16]{2,1,0:T(2,128)S(1)} %get-tuple-element.55.after_ref), custom_call_target="tpu_custom_call" | custom-call | tf_op jit(solution)/shard_map/load/pallas_call | solution.py:287
  25.5 0.2 slice_bitcast_fusion
  25.8 3.9 %collective-permute-start.8 = (f32[2,2,16]{2,1,0:T(2,128)S(1)}, f32[2,2,16]{2,1,0:T(2,128)S(1)}, u32[]{:S(2)}, u32[]{:S(2)}) collective-permute-start(f32[2,2,16]{2,1,0:T(2,128)S(1)} %fusion.35), channel_id=1, source_target_pairs={{0,2},{1,3},{2,0},{3,1},{4,6},{5,7},{6,4},{7,5},{8,10},{9,11},{10,... | collective-permute-start | bytes 776 | tf_op jit(solution)/shard_map/ppermute | solution.py:23
  29.7 1.5 %collective-permute-start.1 = (bf16[16,8,640]{2,1,0:T(8,128)(2,1)S(1)}, bf16[16,8,640]{2,1,0:T(8,128)(2,1)S(1)}, u32[]{:S(2)}, u32[]{:S(2)}) collective-permute-start(bf16[16,8,640]{2,1,0:T(8,128)(2,1)S(1)} %get-tuple-element.22), channel_id=1, source_target_pairs={{0,16},{16,0},{1,17},{17,1},{2,18},{18,2},{3,19},{19,3},{4,20},{20... | collective-permute-start | bytes 491528 | tf_op jit(solution)/shard_map/ppermute | solution.py:341
  31.2 3.3 %conv_backward.1.refs_9_ = f32[16,2,8,640]{3,2,1,0:T(8,128)S(1)} custom-call(s32[7]{0:T(128)S(1)} %stack.73.info_ref, bf16[16,8,640]{2,1,0:T(8,128)(2,1)S(1)} %get-tuple-element.19.cot_ref.refs_0_, bf16[16,8,640]{2,1,0:T(8,128)(2,1)S(1)} %collective-permute-done.7.refs_1_, bf16[2,8,1280]{2,1,0:T(8,128)(2,1)S(1)} %slice.207.refs_2_, ...), custom_call_target="tpu_custom_call" | custom-call | tf_op jit(solution)/shard_map/conv_backward/pallas_call | solution.py:287
  34.6 0.8 %collective-permute-done.1.refs_1_ = bf16[16,8,640]{2,1,0:T(8,128)(2,1)S(1)} collective-permute-done((bf16[16,8,640]{2,1,0:T(8,128)(2,1)S(1)}, bf16[16,8,640]{2,1,0:T(8,128)(2,1)S(1)}, u32[]{:S(2)}, u32[]{:S(2)}) %collective-permute-start.1) | collective-permute-done | bytes 163872 | tf_op jit(solution)/shard_map/ppermute | solution.py:341
  35.3 2.0 %terms.1 = (f32[4,2,16]{2,1,0:T(2,128)S(1)}, f32[16,8,640]{2,1,0:T(8,128)S(1)}, bf16[1,16,8,640]{3,2,1,0:T(8,128)(2,1)S(1)}, bf16[3,18,16,640]{3,2,1,0:T(8,128)(2,1)S(1)}) custom-call(s32[7]{0:T(128)S(1)} %stack.73.info_ref, bf16[16,8,640]{2,1,0:T(8,128)(2,1)S(1)} %get-tuple-element.21.refs_0_, bf16[16,8,640]{2,1,0:T(8,128)(2,1)S(1)} %collective-permute-done.1.refs_1_, ...), custom_call_target="tpu_custom_call" | custom-call | tf_op jit(solution)/shard_map/terms/pallas_call | solution.py:287
  37.4 1.6 %collective-permute-start.9 = (f32[4,16]{1,0:T(4,128)S(1)}, f32[4,16]{1,0:T(4,128)S(1)}, u32[]{:S(2)}, u32[]{:S(2)}) collective-permute-start(f32[4,16]{1,0:T(4,128)S(1)} %bitcast.45), channel_id=1, source_target_pairs={{0,16},{16,0},{1,17},{17,1},{2,18},{18,2},{3,19},{19,3},{4,20},{20... | collective-permute-start | bytes 776 | tf_op jit(solution)/shard_map/ppermute | solution.py:424
  39.0 3.4 %conv_forward.1 = (f32[16,8,640]{2,1,0:T(8,128)S(1)}, bf16[1,16,8,640]{3,2,1,0:T(8,128)(2,1)S(1)}) custom-call(s32[7]{0:T(128)S(1)} %stack.73.info_ref, bf16[3,18,16,640]{3,2,1,0:T(8,128)(2,1)S(1)} %get-tuple-element.28.windows_ref, bf16[3,3,640,640]{3,2,1,0:T(8,128)(2,1)S(1)} %load.1.refs_6_.w_ref), custom_call_target="tpu_custom_call" | custom-call | tf_op jit(solution)/shard_map/conv_forward/pallas_call | solution.py:287
  42.5 0.3 dynamic_update_slice.7
  42.8 0.6 collective-permute-start.14
  43.4 1.5 %collective-permute-start.15 = (bf16[16,8,640]{2,1,0:T(8,128)(2,1)S(1)}, bf16[16,8,640]{2,1,0:T(8,128)(2,1)S(1)}, u32[]{:S(2)}, u32[]{:S(2)}) collective-permute-start(bf16[16,8,640]{2,1,0:T(8,128)(2,1)S(1)} %bitcast.41), channel_id=1, source_target_pairs={{0,16},{16,0},{1,17},{17,1},{2,18},{18,2},{3,19},{19,3},{4,20},{20... | collective-permute-start | bytes 491528 | tf_op jit(solution)/shard_map/ppermute | solution.py:426
  44.9 1.5 %collective-permute-start.11 = (f32[2,32]{1,0:T(2,128)S(1)}, f32[2,32]{1,0:T(2,128)S(1)}, u32[]{:S(2)}, u32[]{:S(2)}) collective-permute-start(f32[2,32]{1,0:T(2,128)S(1)} %get-tuple-element.53), channel_id=1, source_target_pairs={{0,8},{4,12},{8,0},{12,4},{1,9},{5,13},{9,1},{13,5},{2,10},{6,14},... | collective-permute-start | bytes 776 | tf_op jit(solution)/shard_map/ppermute | solution.py:23
  46.4 2.1 %collective-permute-done.11 = f32[2,32]{1,0:T(2,128)S(1)} collective-permute-done((f32[2,32]{1,0:T(2,128)S(1)}, f32[2,32]{1,0:T(2,128)S(1)}, u32[]{:S(2)}, u32[]{:S(2)}) %collective-permute-start.11) | collective-permute-done | bytes 288 | tf_op jit(solution)/shard_map/ppermute | solution.py:23
  48.5 0.6 %collective-permute-start.12 = (f32[2,32]{1,0:T(2,128)S(1)}, f32[2,32]{1,0:T(2,128)S(1)}, u32[]{:S(2)}, u32[]{:S(2)}) collective-permute-start(f32[2,32]{1,0:T(2,128)S(1)} %add.173), channel_id=1, source_target_pairs={{0,1},{1,0},{2,3},{3,2},{4,5},{5,4},{6,7},{7,6},{8,9},{9,8},{10,11... | collective-permute-start | bytes 776 | tf_op jit(solution)/shard_map/ppermute | solution.py:23
  49.2 2.9 %collective-permute-done.12 = f32[2,32]{1,0:T(2,128)S(1)} collective-permute-done((f32[2,32]{1,0:T(2,128)S(1)}, f32[2,32]{1,0:T(2,128)S(1)}, u32[]{:S(2)}, u32[]{:S(2)}) %collective-permute-start.12) | collective-permute-done | bytes 288 | tf_op jit(solution)/shard_map/ppermute | solution.py:23
  52.1 1.2 %collective-permute-start.13 = (f32[2,32]{1,0:T(2,128)S(1)}, f32[2,32]{1,0:T(2,128)S(1)}, u32[]{:S(2)}, u32[]{:S(2)}) collective-permute-start(f32[2,32]{1,0:T(2,128)S(1)} %add.174), channel_id=1, source_target_pairs={{0,2},{1,3},{2,0},{3,1},{4,6},{5,7},{6,4},{7,5},{8,10},{9,11},{10,... | collective-permute-start | bytes 776 | tf_op jit(solution)/shard_map/ppermute | solution.py:23
  53.3 3.3 %collective-permute-done.13 = f32[2,32]{1,0:T(2,128)S(1)} collective-permute-done((f32[2,32]{1,0:T(2,128)S(1)}, f32[2,32]{1,0:T(2,128)S(1)}, u32[]{:S(2)}, u32[]{:S(2)}) %collective-permute-start.13) | collective-permute-done | bytes 288 | tf_op jit(solution)/shard_map/ppermute | solution.py:23
  56.6 1.7 %finish.1 = (bf16[16,8,640]{2,1,0:T(8,128)(2,1)}, bf16[16,8,1280]{2,1,0:T(8,128)(2,1)}) custom-call(s32[7]{0:T(128)S(1)} %stack.73.info_ref, bf16[16,8,1280]{2,1,0:T(8,128)(2,1)S(1)} %get-tuple-element.18.x_ref, f32[2,32]{1,0:T(2,128)S(1)} %get-tuple-element.54.stats_ref, f32[2,32]{1,0:T(2,128)S(1)} %add.175.sums_ref, ...), custom_call_target="tpu_custom_call" | custom-call | tf_op jit(solution)/shard_map/finish/pallas_call | solution.py:287
  (62 shorter events, 1.1 us)
Async XLA Ops:
  0.8 1.0 %copy-start = (bf16[1,16,8,1280]{3,2,1,0:T(8,128)(2,1)S(1)}, bf16[1,16,8,1280]{3,2,1,0:T(8,128)(2,1)}, u32[]{:S(2)}) copy-start(bf16[1,16,8,1280]{3,2,1,0:T(8,128)(2,1)} %param.6) | copy-start | bytes 983044
  1.7 0.9 %copy-start.1 = (bf16[1,16,8,640]{3,2,1,0:T(8,128)(2,1)S(1)}, bf16[1,16,8,640]{3,2,1,0:T(8,128)(2,1)}, u32[]{:S(2)}) copy-start(bf16[1,16,8,640]{3,2,1,0:T(8,128)(2,1)} %param.11) | copy-start | bytes 491524
  4.4 5.2 %collective-permute-start = (bf16[24,1280]{1,0:T(8,128)(2,1)S(1)}, bf16[24,1280]{1,0:T(8,128)(2,1)S(1)}, u32[]{:S(2)}, u32[]{:S(2)}) collective-permute-start(bf16[24,1280]{1,0:T(8,128)(2,1)S(1)} %get-tuple-element.20), channel_id=1, source_target_pairs={{0,16},{16,0},{1,17},{17,1},{2,18},{18,2},{3,19},{19,3},{4,20},{20... | collective-permute-start | bytes 184328 | tf_op jit(solution)/shard_map/ppermute | solution.py:341
  9.7 4.8 %collective-permute-start.2 = (bf16[2,14,1280]{2,1,0:T(8,128)(2,1)S(1)}, bf16[2,14,1280]{2,1,0:T(8,128)(2,1)S(1)}, u32[]{:S(2)}, u32[]{:S(2)}) collective-permute-start(bf16[2,14,1280]{2,1,0:T(8,128)(2,1)S(1)} %pad_maximum_fusion.1), channel_id=1, source_target_pairs={{0,4},{4,0},{8,12},{12,8},{1,5},{5,1},{9,13},{13,9},{2,6},{6,2},{1... | collective-permute-start | bytes 215048 | tf_op jit(solution)/shard_map/ppermute | solution.py:23
  9.8 9.1 %collective-permute-start.7 = (bf16[16,8,640]{2,1,0:T(8,128)(2,1)S(1)}, bf16[16,8,640]{2,1,0:T(8,128)(2,1)S(1)}, u32[]{:S(2)}, u32[]{:S(2)}) collective-permute-start(bf16[16,8,640]{2,1,0:T(8,128)(2,1)S(1)} %get-tuple-element.19.cot_ref.refs_0_), channel_id=1, source_target_pairs={{0,16},{16,0},{1,17},{17,1},{2,18},{18,2},{3,19},{19,3},{4,20},{20... | collective-permute-start | bytes 491528 | tf_op jit(solution)/shard_map/ppermute | solution.py:341
  14.4 4.6 %collective-permute-start.4 = (bf16[32,1280]{1,0:T(8,128)(2,1)S(1)}, bf16[32,1280]{1,0:T(8,128)(2,1)S(1)}, u32[]{:S(2)}, u32[]{:S(2)}) collective-permute-start(bf16[32,1280]{1,0:T(8,128)(2,1)S(1)} %get-tuple-element.25), channel_id=1, source_target_pairs={{0,16},{16,0},{1,17},{17,1},{2,18},{18,2},{3,19},{19,3},{4,20},{20... | collective-permute-start | bytes 245768 | tf_op jit(solution)/shard_map/ppermute | solution.py:341
  14.6 4.4 %collective-permute-start.3 = (bf16[2,14,1280]{2,1,0:T(8,128)(2,1)S(1)}, bf16[2,14,1280]{2,1,0:T(8,128)(2,1)S(1)}, u32[]{:S(2)}, u32[]{:S(2)}) collective-permute-start(bf16[2,14,1280]{2,1,0:T(8,128)(2,1)S(1)} %fusion.10), channel_id=1, source_target_pairs={{0,12},{4,8},{8,4},{12,0},{1,13},{5,9},{9,5},{13,1},{2,14},{6,10},... | collective-permute-start | bytes 215048 | tf_op jit(solution)/shard_map/ppermute | solution.py:23
  19.2 6.5 %collective-permute-start.5 = (bf16[2,24,1280]{2,1,0:T(8,128)(2,1)S(1)}, bf16[2,24,1280]{2,1,0:T(8,128)(2,1)S(1)}, u32[]{:S(2)}, u32[]{:S(2)}) collective-permute-start(bf16[2,24,1280]{2,1,0:T(8,128)(2,1)S(1)} %pad_maximum_fusion), channel_id=1, source_target_pairs={{0,1},{1,0},{2,3},{3,2},{4,5},{5,4},{6,7},{7,6},{8,9},{9,8},{10,11... | collective-permute-start | bytes 368648 | tf_op jit(solution)/shard_map/ppermute | solution.py:23
  21.7 9.5 %collective-permute-start.6 = (bf16[2,18,1280]{2,1,0:T(8,128)(2,1)S(1)}, bf16[2,18,1280]{2,1,0:T(8,128)(2,1)S(1)}, u32[]{:S(2)}, u32[]{:S(2)}) collective-permute-start(bf16[2,18,1280]{2,1,0:T(8,128)(2,1)S(1)} %fusion.7), channel_id=1, source_target_pairs={{1,2},{2,1},{5,6},{6,5},{9,10},{10,9},{13,14},{14,13},{17,18},{18,... | collective-permute-start | bytes 276488 | tf_op jit(solution)/shard_map/ppermute | solution.py:23
  25.8 8.7 %collective-permute-start.8 = (f32[2,2,16]{2,1,0:T(2,128)S(1)}, f32[2,2,16]{2,1,0:T(2,128)S(1)}, u32[]{:S(2)}, u32[]{:S(2)}) collective-permute-start(f32[2,2,16]{2,1,0:T(2,128)S(1)} %fusion.35), channel_id=1, source_target_pairs={{0,2},{1,3},{2,0},{3,1},{4,6},{5,7},{6,4},{7,5},{8,10},{9,11},{10,... | collective-permute-start | bytes 776 | tf_op jit(solution)/shard_map/ppermute | solution.py:23
  29.7 5.7 %collective-permute-start.1 = (bf16[16,8,640]{2,1,0:T(8,128)(2,1)S(1)}, bf16[16,8,640]{2,1,0:T(8,128)(2,1)S(1)}, u32[]{:S(2)}, u32[]{:S(2)}) collective-permute-start(bf16[16,8,640]{2,1,0:T(8,128)(2,1)S(1)} %get-tuple-element.22), channel_id=1, source_target_pairs={{0,16},{16,0},{1,17},{17,1},{2,18},{18,2},{3,19},{19,3},{4,20},{20... | collective-permute-start | bytes 491528 | tf_op jit(solution)/shard_map/ppermute | solution.py:341
  37.4 5.1 %collective-permute-start.9 = (f32[4,16]{1,0:T(4,128)S(1)}, f32[4,16]{1,0:T(4,128)S(1)}, u32[]{:S(2)}, u32[]{:S(2)}) collective-permute-start(f32[4,16]{1,0:T(4,128)S(1)} %bitcast.45), channel_id=1, source_target_pairs={{0,16},{16,0},{1,17},{17,1},{2,18},{18,2},{3,19},{19,3},{4,20},{20... | collective-permute-start | bytes 776 | tf_op jit(solution)/shard_map/ppermute | solution.py:424
  39.0 14.3 %copy-start.2 = (f32[640]{0:T(1024)S(1)}, f32[640]{0:T(1024)}, u32[]{:S(2)}) copy-start(f32[640]{0:T(1024)} %param.10) | copy-start | bytes 7684
  42.8 2.2 %collective-permute-start.10 = (f32[2,32]{1,0:T(2,128)S(1)}, f32[2,32]{1,0:T(2,128)S(1)}, u32[]{:S(2)}, u32[]{:S(2)}) collective-permute-start(f32[2,32]{1,0:T(2,128)S(1)} %slice.199), channel_id=1, source_target_pairs={{0,4},{4,0},{8,12},{12,8},{1,5},{5,1},{9,13},{13,9},{2,6},{6,2},{1... | collective-permute-start | bytes 776 | tf_op jit(solution)/shard_map/ppermute | solution.py:23
  42.8 13.7 %collective-permute-start.14 = (bf16[16,8,640]{2,1,0:T(8,128)(2,1)S(1)}, bf16[16,8,640]{2,1,0:T(8,128)(2,1)S(1)}, u32[]{:S(2)}, u32[]{:S(2)}) collective-permute-start(bf16[16,8,640]{2,1,0:T(8,128)(2,1)S(1)} %bitcast.40), channel_id=1, source_target_pairs={{0,16},{16,0},{1,17},{17,1},{2,18},{18,2},{3,19},{19,3},{4,20},{20... | collective-permute-start | bytes 491528 | tf_op jit(solution)/shard_map/ppermute | solution.py:425
  43.4 13.1 %collective-permute-start.15 = (bf16[16,8,640]{2,1,0:T(8,128)(2,1)S(1)}, bf16[16,8,640]{2,1,0:T(8,128)(2,1)S(1)}, u32[]{:S(2)}, u32[]{:S(2)}) collective-permute-start(bf16[16,8,640]{2,1,0:T(8,128)(2,1)S(1)} %bitcast.41), channel_id=1, source_target_pairs={{0,16},{16,0},{1,17},{17,1},{2,18},{18,2},{3,19},{19,3},{4,20},{20... | collective-permute-start | bytes 491528 | tf_op jit(solution)/shard_map/ppermute | solution.py:426
  44.9 3.6 %collective-permute-start.11 = (f32[2,32]{1,0:T(2,128)S(1)}, f32[2,32]{1,0:T(2,128)S(1)}, u32[]{:S(2)}, u32[]{:S(2)}) collective-permute-start(f32[2,32]{1,0:T(2,128)S(1)} %get-tuple-element.53), channel_id=1, source_target_pairs={{0,8},{4,12},{8,0},{12,4},{1,9},{5,13},{9,1},{13,5},{2,10},{6,14},... | collective-permute-start | bytes 776 | tf_op jit(solution)/shard_map/ppermute | solution.py:23
  48.5 3.6 %collective-permute-start.12 = (f32[2,32]{1,0:T(2,128)S(1)}, f32[2,32]{1,0:T(2,128)S(1)}, u32[]{:S(2)}, u32[]{:S(2)}) collective-permute-start(f32[2,32]{1,0:T(2,128)S(1)} %add.173), channel_id=1, source_target_pairs={{0,1},{1,0},{2,3},{3,2},{4,5},{5,4},{6,7},{7,6},{8,9},{9,8},{10,11... | collective-permute-start | bytes 776 | tf_op jit(solution)/shard_map/ppermute | solution.py:23
  52.1 4.5 %collective-permute-start.13 = (f32[2,32]{1,0:T(2,128)S(1)}, f32[2,32]{1,0:T(2,128)S(1)}, u32[]{:S(2)}, u32[]{:S(2)}) collective-permute-start(f32[2,32]{1,0:T(2,128)S(1)} %add.174), channel_id=1, source_target_pairs={{0,2},{1,3},{2,0},{3,1},{4,6},{5,7},{6,4},{7,5},{8,10},{9,11},{10,... | collective-permute-start | bytes 776 | tf_op jit(solution)/shard_map/ppermute | solution.py:23

commit v3 on v2

v3 whole, which is shorter than its diff:
```python
import functools

import jax
import jax.numpy as jnp
from jax import lax
from jax.experimental import pallas as pl
from jax.experimental.pallas import tpu as pltpu
from jax.sharding import PartitionSpec as P

GROUPS = 32
EPS = 1e-05
F32 = jnp.float32
BF16 = jnp.bfloat16

ME, EVEN_H, EVEN_W, UP, DOWN, LEFT, RIGHT = range(7)


def exchange(value, axis, partner, ends=True):
    count = lax.axis_size(axis)
    pairs = [(i, partner(i) % count) for i in range(count)]
    if not ends:
        pairs = [(i, j) for i, j in pairs if abs(i - j) == 1]
    return lax.ppermute(value, axis, pairs)


def near(i):
    return i ^ 1


def across(i):
    return i - 1 if i % 2 == 0 else i + 1


def merged(stats, other, n):
    half = stats.shape[1] // 2
    delta = other[:, :half] - stats[:, :half]
    return jnp.concatenate([stats[:, :half] + 0.5 * delta, stats[:, half:] + other[:, half:] + (0.5 * n) * delta * delta], 1)


def packed(strips, stats):
    high = lax.reduce_precision(stats, 8, 7)
    middle = lax.reduce_precision(stats - high, 8, 7)
    low = lax.reduce_precision(stats - high - middle, 8, 7)
    rows = jnp.concatenate([high, middle, low], 0).astype(BF16)
    rows = jnp.pad(rows, ((0, 0), (0, strips[0].shape[1] - rows.shape[1])))
    return jnp.concatenate([*strips, rows], 0)


def unpacked(pack, r, size):
    rows = pack[r : r + 3, :size].astype(F32)
    return rows[:1] + rows[1:2] + rows[2:]


def members(groups, chans, dim):
    per_group = chans // groups
    shape = (groups, chans) if dim else (chans, groups)
    chan = lax.broadcasted_iota(jnp.int32, shape, dim)
    group = lax.broadcasted_iota(jnp.int32, shape, 1 - dim)
    return ((chan >= group * per_group) & (chan < (group + 1) * per_group)).astype(F32)


def three_parts(a):
    high = a.astype(BF16)
    rest = a - high.astype(F32)
    middle = rest.astype(BF16)
    return high, middle, (rest - middle.astype(F32)).astype(BF16)


def exact_dot(a, b):
    rows = a.shape[0]
    parts = jnp.concatenate([p.astype(F32) for p in three_parts(a)], 0).astype(BF16)
    sums = jnp.dot(parts, b.astype(BF16), preferred_element_type=F32)
    return sums[:rows] + sums[rows : 2 * rows] + sums[2 * rows :]


def expanded(values, chans):
    return exact_dot(values, members(values.shape[-1], chans, 1))


def gathered(values, groups):
    return exact_dot(values, members(groups, values.shape[-1], 0))


def shard_of(pieces, shard):
    value = pieces[0]
    for i in range(1, len(pieces)):
        value = jnp.where(shard == i, pieces[i], value)
    return value


def first_kernel(parts, groups, info_ref, x_hbm, cot_hbm, *refs):
    out_refs, (x_ref, cot_ref, sems) = refs[:parts], refs[parts:]
    rows, cols, cin = x_ref.shape
    chans = cin // parts
    n = rows * cols * (chans // groups)
    x_copy = pltpu.make_async_copy(x_hbm, x_ref, sems.at[0])
    cot_copy = pltpu.make_async_copy(cot_hbm, cot_ref, sems.at[1])
    x_copy.start()
    cot_copy.start()
    me = info_ref[ME]
    even_h = info_ref[EVEN_H] > 0
    x_copy.wait()
    shards = [x_ref[:, :, s * chans : (s + 1) * chans].astype(F32) for s in range(parts)]
    stats = []
    for x in shards:
        flat = x.reshape(rows * cols, chans)
        mean = gathered(jnp.sum(flat, axis=0, keepdims=True), groups) / n
        centered = flat - expanded(mean, chans)
        squares = gathered(jnp.sum(centered * centered, axis=0, keepdims=True), groups)
        stats.append(jnp.concatenate([p.astype(F32) for p in three_parts(jnp.concatenate([mean, squares], 1))], 0))
    cot_copy.wait()
    ends = lambda t: (jnp.where(even_h, t[rows - 1], t[0]), jnp.where(even_h, t[0], t[rows - 1]))
    cot_ends = ends(cot_ref[...].astype(F32))
    x_ends = [ends(x) for x in shards]
    for k in range(parts):
        shard = lax.rem(me + k, parts)
        out_refs[k][: 2 * cols, :chans] = jnp.concatenate([shard_of([e[i] for e in x_ends], shard) for i in range(2)], 0).astype(BF16)
        out_refs[k][: 2 * cols, chans:] = jnp.concatenate(cot_ends, 0).astype(BF16)
        out_refs[k][2 * cols :, :] = jnp.zeros((8, out_refs[k].shape[1]), BF16)
        out_refs[k][2 * cols : 2 * cols + 3, : 2 * groups] = shard_of(stats, shard).astype(BF16)


def columns_kernel(parts, info_ref, x_ref, cot_ref, w_ref, *out_refs):
    rows, cols, cin = x_ref.shape
    chans = cin // parts
    me = info_ref[ME]
    even_w = info_ref[EVEN_W] > 0

    def ends(t):
        first, last = t[:, 0, :], t[:, cols - 1, :]
        return jnp.concatenate([jnp.where(even_w, last, first), jnp.where(even_w, first, last)], 0).astype(BF16)

    cot_ends = ends(cot_ref[...].astype(F32))
    x_ends = ends(x_ref[...].astype(F32)).astype(F32)
    x_ends = [x_ends[:, s * chans : (s + 1) * chans] for s in range(parts)]
    for k in range(parts):
        out_refs[k][:, :chans] = shard_of(x_ends, lax.rem(me + k, parts)).astype(BF16)
        out_refs[k][:, chans:] = cot_ends


def tiles_kernel(parts, info_ref, x_ref, after_ref, *out_refs):
    chans = x_ref.shape[2] // parts
    me = info_ref[ME]
    shards = [x_ref[:, :, s * chans : (s + 1) * chans].astype(F32) for s in range(parts)]
    for k in range(parts):
        out_refs[k][...] = shard_of(shards, lax.rem(me + k, parts)).astype(BF16)


def pack_kernel(parts, rows, cols, info_ref, near_h, across_h, stats_ref, *refs):
    ends, (near_ref, across_ref) = refs[:parts], refs[parts:]
    even_w = info_ref[EVEN_W] > 0
    both = near_ref.shape[1]
    near_rows = near_h[...].astype(F32)
    across_rows = jnp.where((info_ref[UP] > 0) & (info_ref[DOWN] > 0), across_h[...].astype(F32), 0.0)
    columns = [ref[...].astype(F32) for ref in ends]
    stats = jnp.concatenate([p.astype(F32) for p in three_parts(stats_ref[...])], 0)
    stats = jnp.concatenate([stats, jnp.zeros((3, both - stats.shape[1]), F32)], 1)
    for half, ref, pick_last in ((0, near_ref, even_w), (1, across_ref, jnp.logical_not(even_w))):
        corners = []
        for t in (near_rows, across_rows):
            for k in range(parts):
                first, last = t[k * cols : k * cols + 1], t[(k + 1) * cols - 1 : (k + 1) * cols]
                corners.append(jnp.where(pick_last, last, first))
        pieces = [v[half * rows : (half + 1) * rows] for v in columns] + corners + ([stats] if half == 0 else [])
        used = parts * (rows + 2) + (3 if half == 0 else 0)
        if ref.shape[0] > used:
            pieces.append(jnp.zeros((ref.shape[0] - used, both), F32))
        ref[...] = jnp.concatenate(pieces, 0).astype(BF16)


def halos(parts, rows, cols, info_ref, near_h, across_h, near_w, across_w, lanes):
    even_h = info_ref[EVEN_H] > 0
    even_w = info_ref[EVEN_W] > 0
    part = lambda ref, r: ref[:, lanes].astype(F32)[:r]
    a, b = (part(ref, parts * cols) for ref in (near_h, across_h))
    b = jnp.where((info_ref[UP] > 0) & (info_ref[DOWN] > 0), b, 0.0)
    above_all, below_all = jnp.where(even_h, b, a), jnp.where(even_h, a, b)
    c, d = (part(ref, parts * (rows + 2)) for ref in (near_w, across_w))
    before_all, after_all = jnp.where(even_w, d, c), jnp.where(even_w, c, d)

    def strips(k):
        def ordered(t):
            head, tail = t[parts * rows + k :][:1], t[parts * (rows + 1) + k :][:1]
            return jnp.where(even_h, tail, head), t[k * rows : (k + 1) * rows], jnp.where(even_h, head, tail)

        at = slice(k * cols, (k + 1) * cols)
        return above_all[at], below_all[at], ordered(before_all), ordered(after_all)

    return strips


def windows(padded_ref, windows_ref, k_all, cols):
    for kx in range(3):
        view = padded_ref[:, :, kx : kx + cols, :]
        windows_ref[kx] = view.reshape(view.shape[0], k_all * cols, view.shape[3]).astype(BF16)


def backward_kernel(parts, info_ref, *refs):
    tiles, (near_h, across_h, near_w, across_w, w_ref, grad_ref, padded_ref, windows_ref) = refs[:parts], refs[parts:]
    rows, cols, outs = tiles[0].shape
    chans = w_ref.shape[2]
    strips = halos(parts, rows, cols, info_ref, near_h, across_h, near_w, across_w, slice(chans, chans + outs))
    for k in range(parts):
        above, below, before, after = strips(k)
        padded_ref[1 : rows + 1, k, 1 : cols + 1, :] = tiles[k][...].astype(F32)
        padded_ref[0, k, 1 : cols + 1, :] = above
        padded_ref[rows + 1, k, 1 : cols + 1, :] = below
        for at, (top, mid, bottom) in ((0, before), (cols + 1, after)):
            padded_ref[0, k, at : at + 1, :] = top
            padded_ref[1 : rows + 1, k, at, :] = mid
            padded_ref[rows + 1, k, at : at + 1, :] = bottom
    windows(padded_ref, windows_ref, parts, cols)
    total = None
    for ky in range(3):
        for kx in range(3):
            window = windows_ref[kx, ky : ky + rows].reshape(rows * parts * cols, outs)
            term = lax.dot_general(w_ref[2 - ky, 2 - kx], window, (((1,), (1,)), ((), ())), preferred_element_type=F32)
            total = term if total is None else total + term
    grad_ref[...] = total.T.reshape(rows, parts, cols, chans)


def terms_kernel(parts, count, info_ref, *refs):
    tiles = refs[:parts]
    near_h, across_h, near_w, across_w, stats_ref, gain_ref, shift_ref, grad_ref = refs[parts : parts + 8]
    moments_refs, (gx_own_ref, gx_other_ref, padded_ref) = refs[parts + 8 : -3], refs[-3:]
    rows, cols, _ = tiles[0].shape
    chans = grad_ref.shape[3]
    groups = stats_ref.shape[1] // (2 * parts)
    stats = jnp.concatenate([stats_ref[:, i * groups : (i + 1) * groups] for i in range(2 * parts)], 0)
    strips = halos(parts, rows, cols, info_ref, near_h, across_h, near_w, across_w, slice(0, chans))
    wide = expanded(jnp.concatenate([stats[:parts], lax.rsqrt(stats[parts:] / count + EPS)], 0), chans)
    means, invs = wide[:parts], wide[parts:]
    mine = lambda ref: shard_of([ref[s * chans : (s + 1) * chans].reshape(1, chans) for s in range(parts)], info_ref[ME])
    gain, shift = mine(gain_ref), mine(shift_ref)
    up, down, left, right = (info_ref[i] > 0 for i in (UP, DOWN, LEFT, RIGHT))
    firsts, seconds = [], []
    for k in range(parts):
        mean, inv = means[k : k + 1], invs[k : k + 1]

        def act_of(t, inside):
            z = (t - mean) * inv * gain + shift
            return jnp.where(inside, z * jax.nn.sigmoid(z), 0.0)

        above, below, before, after = strips(k)
        xhat = (tiles[k][...].astype(F32) - mean[None]) * inv[None]
        z = xhat * gain[None] + shift[None]
        sig = jax.nn.sigmoid(z)
        padded_ref[1 : rows + 1, k, 1 : cols + 1, :] = z * sig
        padded_ref[0, k, 1 : cols + 1, :] = act_of(above, up)
        padded_ref[rows + 1, k, 1 : cols + 1, :] = act_of(below, down)
        for at, (top, mid, bottom), side in ((0, before, left), (cols + 1, after, right)):
            padded_ref[0, k, at : at + 1, :] = act_of(top, side & up)
            padded_ref[1 : rows + 1, k, at, :] = act_of(mid, side)
            padded_ref[rows + 1, k, at : at + 1, :] = act_of(bottom, side & down)
        gx = grad_ref[:, k] * sig * (1.0 + z * (1.0 - sig)) * gain[None]
        if k == 0:
            gx_own_ref[...] = gx
        else:
            gx_other_ref[k - 1] = gx.astype(BF16)
        firsts.append(jnp.sum(gx.reshape(rows * cols, chans), axis=0, keepdims=True))
        seconds.append(jnp.sum((gx * xhat).reshape(rows * cols, chans), axis=0, keepdims=True))
    sums = gathered(jnp.concatenate(firsts + seconds, 0), groups)
    for k, ref in enumerate(moments_refs):
        ref[...] = jnp.concatenate([v[k : k + 1] for v in (sums[:parts], sums[parts:], stats[:parts], stats[parts:])], 0)


def forward_kernel(parts, padded_ref, w_ref, conv_own_ref, conv_other_ref, windows_ref):
    rows, cols, outs = conv_own_ref.shape
    chans = windows_ref.shape[3]
    windows(padded_ref, windows_ref, parts, cols)
    total = None
    for ky in range(3):
        for kx in range(3):
            window = windows_ref[kx, ky : ky + rows].reshape(rows * parts * cols, chans)
            term = jnp.dot(window, w_ref[ky, kx], preferred_element_type=F32)
            total = term if total is None else total + term
    total = total.reshape(rows, parts, cols, outs)
    conv_own_ref[...] = total[:, 0]
    for k in range(1, parts):
        conv_other_ref[k - 1] = total[:, k].astype(BF16)


def finish_kernel(parts, count, info_ref, x_ref, small_ref, sums_ref, bias_ref, gx_own_ref, conv_own_ref, *refs):
    gx_refs, conv_refs = refs[: parts - 1], refs[parts - 1 : 2 * parts - 2]
    conv_ref, grad_ref = refs[2 * parts - 2 :]
    cin = x_ref.shape[2]
    chans = cin // parts
    conv = conv_own_ref[...] + bias_ref[...].reshape(1, 1, -1)
    for r in conv_refs:
        conv = conv + r[...].astype(F32)
    conv_ref[...] = conv.astype(BF16)
    wide = []
    for k in range(parts):
        stats = small_ref[k]
        wide.append(jnp.concatenate([stats[2:3], lax.rsqrt(stats[3:4] / count + EPS), sums_ref[k] / count], 0))
    wide = expanded(jnp.concatenate(wide, 0), chans)
    gx_all = [gx_own_ref[...]] + [r[...].astype(F32) for r in gx_refs]
    for s in range(parts):
        at = slice(s * chans, (s + 1) * chans)
        k = lax.rem(s - info_ref[ME] + parts, parts)
        mean, inv, first, second = (shard_of([wide[4 * j + i : 4 * j + i + 1] for j in range(parts)], k)[None] for i in range(4))
        xhat = (x_ref[:, :, at].astype(F32) - mean) * inv
        grad_ref[:, :, at] = (inv * (shard_of(gx_all, k) - first - xhat * second)).astype(BF16)


def call(kernel, name, outs, operands, scratch=(), in_hbm=(), limit=28, scalars=True, cost=None):
    spec = lambda i: pl.BlockSpec(memory_space=pltpu.HBM if i in in_hbm else pltpu.SMEM if scalars and i == 0 else pltpu.VMEM)
    return pl.pallas_call(
        kernel,
        out_shape=outs,
        in_specs=[spec(i) for i in range(len(operands))],
        out_specs=[pl.BlockSpec(memory_space=pltpu.VMEM)] * len(outs),
        scratch_shapes=scratch,
        compiler_params=pltpu.CompilerParams(vmem_limit_bytes=limit * 2**20),
        cost_estimate=cost,
        name=name,
    )(*operands)


def tied(value, *others):
    for other in others:
        value = value + 0.0 * other[0, :1, : value.shape[-1]].astype(F32)
    return value


def stats_rounds(axis):
    count = lax.axis_size(axis)
    if count == 4:
        return [near, lambda i: i ^ 2]
    return [functools.partial(lambda step, i: i ^ step, 2**j) for j in range(count.bit_length() - 1)]


def body(latents, norm_gain, norm_shift, conv_weight, conv_bias, cotangent):
    _, rows, cols, cin = latents.shape
    outs = cotangent.shape[3]
    chans = conv_weight.shape[2]
    parts = lax.axis_size("dp")
    me = lax.axis_index("dp")
    groups = GROUPS * chans // cin
    both = chans + outs
    n = rows * cols * (cin // GROUPS)
    count = float(n * lax.axis_size("ha") * lax.axis_size("wa"))
    x, cot = latents[0], cotangent[0]
    sds = jax.ShapeDtypeStruct
    where = [lax.axis_index(a) for a in ("ha", "wa")]
    last = [lax.axis_size(a) - 1 for a in ("ha", "wa")]
    info = jnp.stack(
        [me, where[0] % 2 == 0, where[1] % 2 == 0, where[0] > 0, where[0] < last[0], where[1] > 0, where[1] < last[1]]
    ).astype(jnp.int32)

    *first, x, cot = call(
        functools.partial(first_kernel, parts, groups),
        "first",
        [sds((2 * cols + 8, both), BF16)] * parts + [sds(x.shape, BF16), sds(cot.shape, BF16)],
        [info, x, cot],
        [pltpu.SemaphoreType.DMA((2,))],
        in_hbm=(1, 2),
        limit=40,
        cost=pl.CostEstimate(flops=10**10, bytes_accessed=1, transcendentals=0),
    )
    peers = [[(i, (i + k) % parts) for i in range(parts)] for k in range(1, parts)]
    from_peers = lambda values: [lax.ppermute(v, "dp", pairs) for v, pairs in zip(values, peers)]
    got = from_peers(first[1:])
    ends_h = [first[0], *got]
    local = [unpacked(v, 2 * cols, 2 * groups) for v in ends_h]
    stats = jnp.concatenate([v[:, :groups] for v in local] + [v[:, groups:] for v in local], 1)
    size = stats.shape[1]
    ends_w = call(
        functools.partial(columns_kernel, parts),
        "columns",
        [sds((2 * rows, both), BF16)] * parts,
        [info, x, cot, conv_weight],
    )
    ends_w = [ends_w[0], *from_peers([v + (0.0 * got[0][:1]).astype(BF16) for v in ends_w[1:]])]

    def reduced(stats, n, axis, pairings):
        for partner in pairings:
            stats, n = merged(stats, exchange(stats, axis, partner), n), 2 * n
        return stats, n

    rounds_h, rounds_w = stats_rounds("ha"), stats_rounds("wa")
    near_h = exchange(packed([v[:cols] for v in ends_h], stats), "ha", near)
    stats, n = merged(stats, unpacked(near_h, parts * cols, size), n), 2 * n
    x_tiles = call(
        functools.partial(tiles_kernel, parts),
        "tiles",
        [sds((rows, cols, chans), BF16)] * parts,
        [info, x, near_h],
    )
    cot_tiles = [cot, *from_peers([cotangent[0]] * (parts - 1))]
    x_tiles = [x_tiles[0], *from_peers(x_tiles[1:])]

    strips = [v[cols : 2 * cols] for v in ends_h]
    if lax.axis_size("ha") == 4:
        across_h = exchange(packed(strips, stats), "ha", across)
        stats, n = merged(stats, unpacked(across_h, parts * cols, size), n), 2 * n
    else:
        across_h = exchange(jnp.concatenate(strips, 0), "ha", across)
        stats, n = reduced(stats, n, "ha", rounds_h[1:])
    used = parts * (rows + 2)
    near_w, across_w = call(
        functools.partial(pack_kernel, parts, rows, cols),
        "pack",
        [sds((-(-(used + 3) // 8) * 8, both), BF16), sds((used, both), BF16)],
        [info, near_h, across_h, stats, *ends_w],
    )
    near_w = exchange(near_w, "wa", near)
    across_w = exchange(across_w, "wa", across, ends=False)
    stats, n = merged(stats, unpacked(near_w, used, size), n), 2 * n
    stats, n = reduced(stats, n, "wa", rounds_w[1:])

    strips = [near_h, across_h, near_w, across_w]
    padded = lambda depth: pltpu.VMEM((rows + 2, parts, cols + 8, depth), F32)
    shifted = (3, rows + 2, parts * cols)
    (grad_act,) = call(
        functools.partial(backward_kernel, parts),
        "conv_backward",
        [sds((rows, parts, cols, chans), F32)],
        [info, *cot_tiles, *strips, conv_weight],
        [padded(outs), pltpu.VMEM((*shifted, outs), BF16)],
    )
    *small, gx_own, gx_other, act = call(
        functools.partial(terms_kernel, parts, count),
        "terms",
        [
            *[sds((4, groups), F32)] * parts,
            sds((rows, cols, chans), F32),
            sds((parts - 1, rows, cols, chans), BF16),
            sds((rows + 2, parts, cols + 8, chans), F32),
        ],
        [info, *x_tiles, *strips, stats, norm_gain, norm_shift, grad_act],
    )

    to_owners = lambda values: [lax.ppermute(v, "dp", [(j, i) for i, j in pairs]) for v, pairs in zip(values, peers)]
    small = jnp.stack([small[0], *to_owners(small[1:])], 0)
    gx = to_owners([gx_other[k] for k in range(parts - 1)])
    conv_own, conv_other = call(
        functools.partial(forward_kernel, parts),
        "conv_forward",
        [sds((rows, cols, outs), F32), sds((parts - 1, rows, cols, outs), BF16)],
        [act, conv_weight],
        [pltpu.VMEM((*shifted, chans), BF16)],
        scalars=False,
    )
    conv = to_owners([conv_other[k] for k in range(parts - 1)])
    sums = tied(small[:, :2], conv_own)
    for axis, pairings in (("ha", rounds_h), ("wa", rounds_w)):
        for partner in pairings:
            sums = sums + exchange(sums, axis, partner)
    conv_out, grad = call(
        functools.partial(finish_kernel, parts, count),
        "finish",
        [sds((rows, cols, outs), BF16), sds((rows, cols, cin), BF16)],
        [info, x, small, sums, conv_bias, gx_own, conv_own, *gx, *conv],
    )
    return conv_out[None], grad[None]


def solution(mesh):
    tile = P("dp", "ha", "wa", None)
    return jax.shard_map(
        body,
        mesh=mesh,
        in_specs=(tile, P(), P(), P(None, None, "dp", None), P(), tile),
        out_specs=(tile, tile),
        check_vma=False,
    )
```

time: 58.5 us -> 52.6 us (0.90)
  Pallas kernels: 16.1 us -> 13.4 us
  local copies, waits for them, and re-layouts: 4.16 us -> 2.09 us
  starting transfers between devices: 22.4 us -> 21.5 us
  waiting for transfers between devices: 14.2 us -> 13.6 us
    pallas_call x7 -> x8, Pallas kernels: 16.1 us -> 13.4 us  [call(): pl.pallas_call(kernel, out_shape=outs, in_specs=[spec(i) for i in range(l...]
    dynamic_slice x2 -> x0, local copies, waits for them, and re-layouts: 1.54 us -> none  [the longest x1 0.77 us: body(): gain = lax.dynamic_slice_in_dim(norm_gain, me * chans, chans, 0)[None]]
    ppermute x3, starting transfers between devices: 3.68 us -> 2.54 us  [body(): lax.ppermute(v, 'dp', [(j, i) for i, j in pairs])]
    ppermute x4, waiting for transfers between devices: 5.81 us -> 5.19 us  [body(): lax.ppermute(v, 'dp', pairs)]
    unnamed x6 -> x14, local copies, waits for them, and re-layouts: 1.89 us -> 1.92 us
  transfers between devices with their start and end apart: 16 -> 16, of which waited for: 6 -> 11; matrix products, arithmetic and copies ran while one was open for 4% -> 1% of each run, Pallas kernels for 18% -> 15%
where the time goes in v3:
time: 52.6 us; the launch traced here: 52.4 us
  starting transfers between devices  21.5 us (41%)
  waiting for transfers between devices  13.6 us (26%)
  Pallas kernels  13.4 us (25%)
  local copies, waits for them, and re-layouts  2.09 us (4%)
  other arithmetic  0.89 us (2%)
  between operations  0.85 us (2%)
    pallas_call x8, Pallas kernels, call(): pl.pallas_call(kernel, out_shape=outs, in_specs=[spec(i) for i in range(l...  13.4 us
    ppermute x9, starting transfers between devices, exchange(): return lax.ppermute(value, axis, pairs)  12.4 us
    ppermute x9, waiting for transfers between devices, exchange(): return lax.ppermute(value, axis, pairs)  8.17 us
    ppermute x4, starting transfers between devices, body(): lax.ppermute(v, 'dp', pairs)  6.64 us
    ppermute x4, waiting for transfers between devices, body(): lax.ppermute(v, 'dp', pairs)  5.19 us
    ppermute x3, starting transfers between devices, body(): lax.ppermute(v, 'dp', [(j, i) for i, j in pairs])  2.54 us
    unnamed x14, local copies, waits for them, and re-layouts  1.92 us
  transfers between devices with their start and end apart: 16, of which 11 were waited for; matrix products, arithmetic and copies ran while one was open for 1% of the time, Pallas kernels for 15%

profile of v3, /device:TPU:0, one launch (start us, length us, event | category | flops | bytes accessed | tf_op | source)
XLA Modules:
  0.0 52.4 jit_solution(9527087865370085461)
XLA Ops:
  0.7 1.0 %copy-done.4 = bf16[1,16,8,1280]{3,2,1,0:T(8,128)(2,1)S(1)} copy-done((bf16[1,16,8,1280]{3,2,1,0:T(8,128)(2,1)S(1)}, bf16[1,16,8,1280]{3,2,1,0:T(8,128)(2,1)}, u32[]{:S(2)}) %copy-start.4) | copy-done | bytes 327704
  1.7 0.9 %copy-done.5 = bf16[1,16,8,640]{3,2,1,0:T(8,128)(2,1)S(1)} copy-done((bf16[1,16,8,640]{3,2,1,0:T(8,128)(2,1)S(1)}, bf16[1,16,8,640]{3,2,1,0:T(8,128)(2,1)}, u32[]{:S(2)}) %copy-start.5) | copy-done | bytes 163864
  2.6 1.9 %first.1 = (bf16[24,1280]{1,0:T(8,128)(2,1)S(1)}, bf16[24,1280]{1,0:T(8,128)(2,1)S(1)}, bf16[16,8,1280]{2,1,0:T(8,128)(2,1)S(1)}, bf16[16,8,640]{2,1,0:T(8,128)(2,1)S(1)}) custom-call(s32[7]{0:T(128)S(1)} %stack.64.info_ref, bf16[16,8,1280]{2,1,0:T(8,128)(2,1)S(1)} %bitcast.21, bf16[16,8,640]{2,1,0:T(8,128)(2,1)S(1)} %bitcast.22), custom_call_target="tpu_custom_call" | custom-call | flops 10000000000 | bytes 1 | tf_op jit(solution)/shard_map/first/pallas_call | solution.py:308
  4.5 3.0 %collective-permute-start = (bf16[24,1280]{1,0:T(8,128)(2,1)S(1)}, bf16[24,1280]{1,0:T(8,128)(2,1)S(1)}, u32[]{:S(2)}, u32[]{:S(2)}) collective-permute-start(bf16[24,1280]{1,0:T(8,128)(2,1)S(1)} %get-tuple-element.23), channel_id=1, source_target_pairs={{0,16},{16,0},{1,17},{17,1},{2,18},{18,2},{3,19},{19,3},{4,20},{20... | collective-permute-start | bytes 184328 | tf_op jit(solution)/shard_map/ppermute | solution.py:362
  7.6 0.8 %columns.1 = (bf16[32,1280]{1,0:T(8,128)(2,1)S(1)}, bf16[32,1280]{1,0:T(8,128)(2,1)S(1)}) custom-call(s32[7]{0:T(128)S(1)} %stack.64.info_ref, bf16[16,8,1280]{2,1,0:T(8,128)(2,1)S(1)} %get-tuple-element.21.x_ref, bf16[16,8,640]{2,1,0:T(8,128)(2,1)S(1)} %get-tuple-element.26.cot_ref.refs_0_, bf16[3,3,640,640]{3,2,1,0:T(8,128)(2,1)S(1)} %copy-done), custom_call_target="tpu_custom_call" | custom-call | tf_op jit(solution)/shard_map/columns/pallas_call | solution.py:308
  8.4 1.3 %collective-permute-done = bf16[24,1280]{1,0:T(8,128)(2,1)S(1)} collective-permute-done((bf16[24,1280]{1,0:T(8,128)(2,1)S(1)}, bf16[24,1280]{1,0:T(8,128)(2,1)S(1)}, u32[]{:S(2)}, u32[]{:S(2)}) %collective-permute-start) | collective-permute-done | bytes 61472 | tf_op jit(solution)/shard_map/ppermute | solution.py:362
  10.1 1.2 %collective-permute-done.1.after_ref.near_h.refs_2_ = bf16[19,1280]{1,0:T(8,128)(2,1)S(1)} collective-permute-done((bf16[19,1280]{1,0:T(8,128)(2,1)S(1)}, bf16[19,1280]{1,0:T(8,128)(2,1)S(1)}, u32[]{:S(2)}, u32[]{:S(2)}) %collective-permute-start.1) | collective-permute-done | bytes 48672 | tf_op jit(solution)/shard_map/ppermute | solution.py:23
  11.5 1.8 %collective-permute-start.3 = (bf16[19,1280]{1,0:T(8,128)(2,1)S(1)}, bf16[19,1280]{1,0:T(8,128)(2,1)S(1)}, u32[]{:S(2)}, u32[]{:S(2)}) collective-permute-start(bf16[19,1280]{1,0:T(8,128)(2,1)S(1)} %pad_maximum_fusion.1), channel_id=1, source_target_pairs={{0,12},{4,8},{8,4},{12,0},{1,13},{5,9},{9,5},{13,1},{2,14},{6,10},... | collective-permute-start | bytes 145928 | tf_op jit(solution)/shard_map/ppermute | solution.py:23
  13.3 1.6 %collective-permute-start.4 = (bf16[32,1280]{1,0:T(8,128)(2,1)S(1)}, bf16[32,1280]{1,0:T(8,128)(2,1)S(1)}, u32[]{:S(2)}, u32[]{:S(2)}) collective-permute-start(bf16[32,1280]{1,0:T(8,128)(2,1)S(1)} %broadcast_add_fusion), channel_id=1, source_target_pairs={{0,16},{16,0},{1,17},{17,1},{2,18},{18,2},{3,19},{19,3},{4,20},{20... | collective-permute-start | bytes 245768 | tf_op jit(solution)/shard_map/ppermute | solution.py:362
  15.6 2.5 %collective-permute-done.4.refs_1_ = bf16[32,1280]{1,0:T(8,128)(2,1)S(1)} collective-permute-done((bf16[32,1280]{1,0:T(8,128)(2,1)S(1)}, bf16[32,1280]{1,0:T(8,128)(2,1)S(1)}, u32[]{:S(2)}, u32[]{:S(2)}) %collective-permute-start.4) | collective-permute-done | bytes 81952 | tf_op jit(solution)/shard_map/ppermute | solution.py:362
  18.1 0.6 %pack.1 = (bf16[40,1280]{1,0:T(8,128)(2,1)S(1)}, bf16[36,1280]{1,0:T(8,128)(2,1)S(1)}) custom-call(s32[7]{0:T(128)S(1)} %stack.64.info_ref, bf16[19,1280]{1,0:T(8,128)(2,1)S(1)} %collective-permute-done.1.after_ref.near_h.refs_2_, bf16[19,1280]{1,0:T(8,128)(2,1)S(1)} %collective-permute-done.3.across_h.refs_3_, f32[1,64]{1,0:T(1,128)S(1)} %pad_maximum_fusion.6.stats_ref, ...), custom_call_target="tpu_custom_call" | custom-call | tf_op jit(solution)/shard_map/pack/pallas_call | solution.py:308
  18.7 1.6 %collective-permute-start.5 = (bf16[40,1280]{1,0:T(8,128)(2,1)S(1)}, bf16[40,1280]{1,0:T(8,128)(2,1)S(1)}, u32[]{:S(2)}, u32[]{:S(2)}) collective-permute-start(bf16[40,1280]{1,0:T(8,128)(2,1)S(1)} %get-tuple-element.29), channel_id=1, source_target_pairs={{0,1},{1,0},{2,3},{3,2},{4,5},{5,4},{6,7},{7,6},{8,9},{9,8},{10,11... | collective-permute-start | bytes 307208 | tf_op jit(solution)/shard_map/ppermute | solution.py:23
  20.3 1.5 %collective-permute-start.8 = (bf16[16,8,640]{2,1,0:T(8,128)(2,1)S(1)}, bf16[16,8,640]{2,1,0:T(8,128)(2,1)S(1)}, u32[]{:S(2)}, u32[]{:S(2)}) collective-permute-start(bf16[16,8,640]{2,1,0:T(8,128)(2,1)S(1)} %bitcast.23), channel_id=1, source_target_pairs={{0,16},{16,0},{1,17},{17,1},{2,18},{18,2},{3,19},{19,3},{4,20},{20... | collective-permute-start | bytes 491528 | tf_op jit(solution)/shard_map/ppermute | solution.py:362
  21.9 0.6 %tiles.1 = (bf16[16,8,640]{2,1,0:T(8,128)(2,1)S(1)}, bf16[16,8,640]{2,1,0:T(8,128)(2,1)S(1)}) custom-call(s32[7]{0:T(128)S(1)} %stack.64.info_ref, bf16[16,8,1280]{2,1,0:T(8,128)(2,1)S(1)} %get-tuple-element.21.x_ref, bf16[19,1280]{1,0:T(8,128)(2,1)S(1)} %collective-permute-done.1.after_ref.near_h.refs_2_), custom_call_target="tpu_custom_call" | custom-call | tf_op jit(solution)/shard_map/tiles/pallas_call | solution.py:308
  22.5 0.7 %collective-permute-start.6 = (bf16[36,1280]{1,0:T(8,128)(2,1)S(1)}, bf16[36,1280]{1,0:T(8,128)(2,1)S(1)}, u32[]{:S(2)}, u32[]{:S(2)}) collective-permute-start(bf16[36,1280]{1,0:T(8,128)(2,1)S(1)} %get-tuple-element.30), channel_id=1, source_target_pairs={{1,2},{2,1},{5,6},{6,5},{9,10},{10,9},{13,14},{14,13},{17,18},{18,... | collective-permute-start | bytes 276488 | tf_op jit(solution)/shard_map/ppermute | solution.py:23
  23.6 3.6 %collective-permute-start.7 = (f32[1,64]{1,0:T(1,128)S(1)}, f32[1,64]{1,0:T(1,128)S(1)}, u32[]{:S(2)}, u32[]{:S(2)}) collective-permute-start(f32[1,64]{1,0:T(1,128)S(1)} %pad_maximum_fusion.7), channel_id=1, source_target_pairs={{0,2},{1,3},{2,0},{3,1},{4,6},{5,7},{6,4},{7,5},{8,10},{9,11},{10,... | collective-permute-start | bytes 776 | tf_op jit(solution)/shard_map/ppermute | solution.py:23
  27.2 0.5 collective-permute-start.2
  27.7 3.3 %conv_backward.1.refs_9_ = f32[16,2,8,640]{3,2,1,0:T(8,128)S(1)} custom-call(s32[7]{0:T(128)S(1)} %stack.64.info_ref, bf16[16,8,640]{2,1,0:T(8,128)(2,1)S(1)} %get-tuple-element.26.cot_ref.refs_0_, bf16[16,8,640]{2,1,0:T(8,128)(2,1)S(1)} %collective-permute-done.8.refs_1_, bf16[19,1280]{1,0:T(8,128)(2,1)S(1)} %collective-permute-done.1.after_ref.near_h.refs_2_, ...), custom_call_target="tpu_custom_call" | custom-call | tf_op jit(solution)/shard_map/conv_backward/pallas_call | solution.py:308
  31.2 1.4 %collective-permute-done.2.refs_1_ = bf16[16,8,640]{2,1,0:T(8,128)(2,1)S(1)} collective-permute-done((bf16[16,8,640]{2,1,0:T(8,128)(2,1)S(1)}, bf16[16,8,640]{2,1,0:T(8,128)(2,1)S(1)}, u32[]{:S(2)}, u32[]{:S(2)}) %collective-permute-start.2) | collective-permute-done | bytes 163872 | tf_op jit(solution)/shard_map/ppermute | solution.py:362
  32.5 1.6 %terms.1 = (f32[4,16]{1,0:T(4,128)S(1)}, f32[4,16]{1,0:T(4,128)S(1)}, f32[16,8,640]{2,1,0:T(8,128)S(1)}, bf16[1,16,8,640]{3,2,1,0:T(8,128)(2,1)S(1)}, f32[18,2,16,640]{3,2,1,0:T(8,128)S(1)}) custom-call(s32[7]{0:T(128)S(1)} %stack.64.info_ref, bf16[16,8,640]{2,1,0:T(8,128)(2,1)S(1)} %get-tuple-element.24.refs_0_, ...), custom_call_target="tpu_custom_call" | custom-call | tf_op jit(solution)/shard_map/terms/pallas_call | solution.py:308
  34.2 0.5 collective-permute-start.9
  34.7 2.9 %conv_forward.1 = (f32[16,8,640]{2,1,0:T(8,128)S(1)}, bf16[1,16,8,640]{3,2,1,0:T(8,128)(2,1)S(1)}) custom-call(f32[18,2,16,640]{3,2,1,0:T(8,128)S(1)} %get-tuple-element.33.padded_ref, bf16[3,3,640,640]{3,2,1,0:T(8,128)(2,1)S(1)} %copy-done), custom_call_target="tpu_custom_call" | custom-call | tf_op jit(solution)/shard_map/conv_forward/pallas_call | solution.py:308
  37.8 1.1 %collective-permute-done.10 = f32[2,2,16]{2,1,0:T(2,128)S(1)} collective-permute-done((f32[2,2,16]{2,1,0:T(2,128)S(1)}, f32[2,2,16]{2,1,0:T(2,128)S(1)}, u32[]{:S(2)}, u32[]{:S(2)}) %collective-permute-start.10) | collective-permute-done | bytes 288 | tf_op jit(solution)/shard_map/ppermute | solution.py:23
  38.9 0.5 %collective-permute-start.11 = (f32[2,2,16]{2,1,0:T(2,128)S(1)}, f32[2,2,16]{2,1,0:T(2,128)S(1)}, u32[]{:S(2)}, u32[]{:S(2)}) collective-permute-start(f32[2,2,16]{2,1,0:T(2,128)S(1)} %fusion.25), channel_id=1, source_target_pairs={{0,8},{4,12},{8,0},{12,4},{1,9},{5,13},{9,1},{13,5},{2,10},{6,14},... | collective-permute-start | bytes 776 | tf_op jit(solution)/shard_map/ppermute | solution.py:23
  39.5 1.4 %collective-permute-start.14 = (bf16[16,8,640]{2,1,0:T(8,128)(2,1)S(1)}, bf16[16,8,640]{2,1,0:T(8,128)(2,1)S(1)}, u32[]{:S(2)}, u32[]{:S(2)}) collective-permute-start(bf16[16,8,640]{2,1,0:T(8,128)(2,1)S(1)} %bitcast.24), channel_id=1, source_target_pairs={{16,0},{0,16},{17,1},{1,17},{18,2},{2,18},{19,3},{3,19},{20,4},{4,... | collective-permute-start | bytes 491528 | tf_op jit(solution)/shard_map/ppermute | solution.py:434
  40.9 0.6 %collective-permute-start.15 = (bf16[16,8,640]{2,1,0:T(8,128)(2,1)S(1)}, bf16[16,8,640]{2,1,0:T(8,128)(2,1)S(1)}, u32[]{:S(2)}, u32[]{:S(2)}) collective-permute-start(bf16[16,8,640]{2,1,0:T(8,128)(2,1)S(1)} %bitcast.25), channel_id=1, source_target_pairs={{16,0},{0,16},{17,1},{1,17},{18,2},{2,18},{19,3},{3,19},{20,4},{4,... | collective-permute-start | bytes 491528 | tf_op jit(solution)/shard_map/ppermute | solution.py:434
  41.5 1.0 %collective-permute-done.11 = f32[2,2,16]{2,1,0:T(2,128)S(1)} collective-permute-done((f32[2,2,16]{2,1,0:T(2,128)S(1)}, f32[2,2,16]{2,1,0:T(2,128)S(1)}, u32[]{:S(2)}, u32[]{:S(2)}) %collective-permute-start.11) | collective-permute-done | bytes 288 | tf_op jit(solution)/shard_map/ppermute | solution.py:23
  42.5 1.4 %collective-permute-start.12 = (f32[2,2,16]{2,1,0:T(2,128)S(1)}, f32[2,2,16]{2,1,0:T(2,128)S(1)}, u32[]{:S(2)}, u32[]{:S(2)}) collective-permute-start(f32[2,2,16]{2,1,0:T(2,128)S(1)} %fusion.26), channel_id=1, source_target_pairs={{0,1},{1,0},{2,3},{3,2},{4,5},{5,4},{6,7},{7,6},{8,9},{9,8},{10,11... | collective-permute-start | bytes 776 | tf_op jit(solution)/shard_map/ppermute | solution.py:23
  44.0 2.1 %collective-permute-done.12 = f32[2,2,16]{2,1,0:T(2,128)S(1)} collective-permute-done((f32[2,2,16]{2,1,0:T(2,128)S(1)}, f32[2,2,16]{2,1,0:T(2,128)S(1)}, u32[]{:S(2)}, u32[]{:S(2)}) %collective-permute-start.12) | collective-permute-done | bytes 288 | tf_op jit(solution)/shard_map/ppermute | solution.py:23
  46.1 2.6 %collective-permute-start.13 = (f32[2,2,16]{2,1,0:T(2,128)S(1)}, f32[2,2,16]{2,1,0:T(2,128)S(1)}, u32[]{:S(2)}, u32[]{:S(2)}) collective-permute-start(f32[2,2,16]{2,1,0:T(2,128)S(1)} %add.141), channel_id=1, source_target_pairs={{0,2},{1,3},{2,0},{3,1},{4,6},{5,7},{6,4},{7,5},{8,10},{9,11},{10,... | collective-permute-start | bytes 776 | tf_op jit(solution)/shard_map/ppermute | solution.py:23
  48.7 1.9 %collective-permute-done.13 = f32[2,2,16]{2,1,0:T(2,128)S(1)} collective-permute-done((f32[2,2,16]{2,1,0:T(2,128)S(1)}, f32[2,2,16]{2,1,0:T(2,128)S(1)}, u32[]{:S(2)}, u32[]{:S(2)}) %collective-permute-start.13) | collective-permute-done | bytes 288 | tf_op jit(solution)/shard_map/ppermute | solution.py:23
  50.6 1.8 %finish.1 = (bf16[16,8,640]{2,1,0:T(8,128)(2,1)}, bf16[16,8,1280]{2,1,0:T(8,128)(2,1)}) custom-call(s32[7]{0:T(128)S(1)} %stack.64.info_ref, bf16[16,8,1280]{2,1,0:T(8,128)(2,1)S(1)} %get-tuple-element.21.x_ref, f32[2,4,16]{2,1,0:T(4,128)S(1)} %pad_maximum_fusion.2.small_ref, f32[2,2,16]{2,1,0:T(2,128)S(1)} %add.142.sums_ref, f32[640]{0:T(1024)S(1)} %copy-done.3, ...), custom_call_target="tpu_custom_call" | custom-call | tf_op jit(solution)/shard_map/finish/pallas_call | solution.py:308
  (60 shorter events, 2.1 us)
Async XLA Ops:
  0.7 1.0 %copy-start.4 = (bf16[1,16,8,1280]{3,2,1,0:T(8,128)(2,1)S(1)}, bf16[1,16,8,1280]{3,2,1,0:T(8,128)(2,1)}, u32[]{:S(2)}) copy-start(bf16[1,16,8,1280]{3,2,1,0:T(8,128)(2,1)} %param.6) | copy-start | bytes 983044
  1.7 0.9 %copy-start.5 = (bf16[1,16,8,640]{3,2,1,0:T(8,128)(2,1)S(1)}, bf16[1,16,8,640]{3,2,1,0:T(8,128)(2,1)}, u32[]{:S(2)}) copy-start(bf16[1,16,8,640]{3,2,1,0:T(8,128)(2,1)} %param.11) | copy-start | bytes 491524
  2.6 4.9 %copy-start = (bf16[3,3,640,640]{3,2,1,0:T(8,128)(2,1)S(1)}, bf16[3,3,640,640]{3,2,1,0:T(8,128)(2,1)}, u32[]{:S(2)}) copy-start(bf16[3,3,640,640]{3,2,1,0:T(8,128)(2,1)} %w_ref.3) | copy-start | bytes 22118404
  4.5 15.8 %copy-start.6 = (bf16[1,16,8,640]{3,2,1,0:T(8,128)(2,1)S(1)}, bf16[1,16,8,640]{3,2,1,0:T(8,128)(2,1)}, u32[]{:S(2)}) copy-start(bf16[1,16,8,640]{3,2,1,0:T(8,128)(2,1)} %param.11) | copy-start | bytes 491524
  4.5 5.2 %collective-permute-start = (bf16[24,1280]{1,0:T(8,128)(2,1)S(1)}, bf16[24,1280]{1,0:T(8,128)(2,1)S(1)}, u32[]{:S(2)}, u32[]{:S(2)}) collective-permute-start(bf16[24,1280]{1,0:T(8,128)(2,1)S(1)} %get-tuple-element.23), channel_id=1, source_target_pairs={{0,16},{16,0},{1,17},{17,1},{2,18},{18,2},{3,19},{19,3},{4,20},{20... | collective-permute-start | bytes 184328 | tf_op jit(solution)/shard_map/ppermute | solution.py:362
  7.6 25.0 %copy-start.1 = (f32[1280]{0:T(1024)S(1)}, f32[1280]{0:T(1024)}, u32[]{:S(2)}) copy-start(f32[1280]{0:T(1024)} %refs_7_.1) | copy-start | bytes 15364
  7.6 25.0 %copy-start.2 = (f32[1280]{0:T(1024)S(1)}, f32[1280]{0:T(1024)}, u32[]{:S(2)}) copy-start(f32[1280]{0:T(1024)} %refs_8_.1) | copy-start | bytes 15364
  10.0 1.3 %collective-permute-start.1 = (bf16[19,1280]{1,0:T(8,128)(2,1)S(1)}, bf16[19,1280]{1,0:T(8,128)(2,1)S(1)}, u32[]{:S(2)}, u32[]{:S(2)}) collective-permute-start(bf16[19,1280]{1,0:T(8,128)(2,1)S(1)} %pad_maximum_fusion), channel_id=1, source_target_pairs={{0,4},{4,0},{8,12},{12,8},{1,5},{5,1},{9,13},{13,9},{2,6},{6,2},{1... | collective-permute-start | bytes 145928 | tf_op jit(solution)/shard_map/ppermute | solution.py:23
  11.5 3.9 %collective-permute-start.3 = (bf16[19,1280]{1,0:T(8,128)(2,1)S(1)}, bf16[19,1280]{1,0:T(8,128)(2,1)S(1)}, u32[]{:S(2)}, u32[]{:S(2)}) collective-permute-start(bf16[19,1280]{1,0:T(8,128)(2,1)S(1)} %pad_maximum_fusion.1), channel_id=1, source_target_pairs={{0,12},{4,8},{8,4},{12,0},{1,13},{5,9},{9,5},{13,1},{2,14},{6,10},... | collective-permute-start | bytes 145928 | tf_op jit(solution)/shard_map/ppermute | solution.py:23
  13.3 4.8 %collective-permute-start.4 = (bf16[32,1280]{1,0:T(8,128)(2,1)S(1)}, bf16[32,1280]{1,0:T(8,128)(2,1)S(1)}, u32[]{:S(2)}, u32[]{:S(2)}) collective-permute-start(bf16[32,1280]{1,0:T(8,128)(2,1)S(1)} %broadcast_add_fusion), channel_id=1, source_target_pairs={{0,16},{16,0},{1,17},{17,1},{2,18},{18,2},{3,19},{19,3},{4,20},{20... | collective-permute-start | bytes 245768 | tf_op jit(solution)/shard_map/ppermute | solution.py:362
  18.7 4.7 %collective-permute-start.5 = (bf16[40,1280]{1,0:T(8,128)(2,1)S(1)}, bf16[40,1280]{1,0:T(8,128)(2,1)S(1)}, u32[]{:S(2)}, u32[]{:S(2)}) collective-permute-start(bf16[40,1280]{1,0:T(8,128)(2,1)S(1)} %get-tuple-element.29), channel_id=1, source_target_pairs={{0,1},{1,0},{2,3},{3,2},{4,5},{5,4},{6,7},{7,6},{8,9},{9,8},{10,11... | collective-permute-start | bytes 307208 | tf_op jit(solution)/shard_map/ppermute | solution.py:23
  20.3 7.4 %collective-permute-start.8 = (bf16[16,8,640]{2,1,0:T(8,128)(2,1)S(1)}, bf16[16,8,640]{2,1,0:T(8,128)(2,1)S(1)}, u32[]{:S(2)}, u32[]{:S(2)}) collective-permute-start(bf16[16,8,640]{2,1,0:T(8,128)(2,1)S(1)} %bitcast.23), channel_id=1, source_target_pairs={{0,16},{16,0},{1,17},{17,1},{2,18},{18,2},{3,19},{19,3},{4,20},{20... | collective-permute-start | bytes 491528 | tf_op jit(solution)/shard_map/ppermute | solution.py:362
  22.5 5.2 %collective-permute-start.6 = (bf16[36,1280]{1,0:T(8,128)(2,1)S(1)}, bf16[36,1280]{1,0:T(8,128)(2,1)S(1)}, u32[]{:S(2)}, u32[]{:S(2)}) collective-permute-start(bf16[36,1280]{1,0:T(8,128)(2,1)S(1)} %get-tuple-element.30), channel_id=1, source_target_pairs={{1,2},{2,1},{5,6},{6,5},{9,10},{10,9},{13,14},{14,13},{17,18},{18,... | collective-permute-start | bytes 276488 | tf_op jit(solution)/shard_map/ppermute | solution.py:23
  23.6 7.4 %collective-permute-start.7 = (f32[1,64]{1,0:T(1,128)S(1)}, f32[1,64]{1,0:T(1,128)S(1)}, u32[]{:S(2)}, u32[]{:S(2)}) collective-permute-start(f32[1,64]{1,0:T(1,128)S(1)} %pad_maximum_fusion.7), channel_id=1, source_target_pairs={{0,2},{1,3},{2,0},{3,1},{4,6},{5,7},{6,4},{7,5},{8,10},{9,11},{10,... | collective-permute-start | bytes 776 | tf_op jit(solution)/shard_map/ppermute | solution.py:23
  27.2 23.4 %copy-start.3 = (f32[640]{0:T(1024)S(1)}, f32[640]{0:T(1024)}, u32[]{:S(2)}) copy-start(f32[640]{0:T(1024)} %bias_ref.1) | copy-start | bytes 7684
  27.2 5.3 %collective-permute-start.2 = (bf16[16,8,640]{2,1,0:T(8,128)(2,1)S(1)}, bf16[16,8,640]{2,1,0:T(8,128)(2,1)S(1)}, u32[]{:S(2)}, u32[]{:S(2)}) collective-permute-start(bf16[16,8,640]{2,1,0:T(8,128)(2,1)S(1)} %get-tuple-element.25), channel_id=1, source_target_pairs={{0,16},{16,0},{1,17},{17,1},{2,18},{18,2},{3,19},{19,3},{4,20},{20... | collective-permute-start | bytes 491528 | tf_op jit(solution)/shard_map/ppermute | solution.py:362
  34.2 3.6 %collective-permute-start.9 = (f32[4,16]{1,0:T(4,128)S(1)}, f32[4,16]{1,0:T(4,128)S(1)}, u32[]{:S(2)}, u32[]{:S(2)}) collective-permute-start(f32[4,16]{1,0:T(4,128)S(1)} %get-tuple-element.32), channel_id=1, source_target_pairs={{16,0},{0,16},{17,1},{1,17},{18,2},{2,18},{19,3},{3,19},{20,4},{4,... | collective-permute-start | bytes 776 | tf_op jit(solution)/shard_map/ppermute | solution.py:434
  37.8 1.2 %collective-permute-start.10 = (f32[2,2,16]{2,1,0:T(2,128)S(1)}, f32[2,2,16]{2,1,0:T(2,128)S(1)}, u32[]{:S(2)}, u32[]{:S(2)}) collective-permute-start(f32[2,2,16]{2,1,0:T(2,128)S(1)} %fusion.12), channel_id=1, source_target_pairs={{0,4},{4,0},{8,12},{12,8},{1,5},{5,1},{9,13},{13,9},{2,6},{6,2},{1... | collective-permute-start | bytes 776 | tf_op jit(solution)/shard_map/ppermute | solution.py:23
  38.9 3.6 %collective-permute-start.11 = (f32[2,2,16]{2,1,0:T(2,128)S(1)}, f32[2,2,16]{2,1,0:T(2,128)S(1)}, u32[]{:S(2)}, u32[]{:S(2)}) collective-permute-start(f32[2,2,16]{2,1,0:T(2,128)S(1)} %fusion.25), channel_id=1, source_target_pairs={{0,8},{4,12},{8,0},{12,4},{1,9},{5,13},{9,1},{13,5},{2,10},{6,14},... | collective-permute-start | bytes 776 | tf_op jit(solution)/shard_map/ppermute | solution.py:23
  39.5 11.1 %collective-permute-start.14 = (bf16[16,8,640]{2,1,0:T(8,128)(2,1)S(1)}, bf16[16,8,640]{2,1,0:T(8,128)(2,1)S(1)}, u32[]{:S(2)}, u32[]{:S(2)}) collective-permute-start(bf16[16,8,640]{2,1,0:T(8,128)(2,1)S(1)} %bitcast.24), channel_id=1, source_target_pairs={{16,0},{0,16},{17,1},{1,17},{18,2},{2,18},{19,3},{3,19},{20,4},{4,... | collective-permute-start | bytes 491528 | tf_op jit(solution)/shard_map/ppermute | solution.py:434
  40.9 9.7 %collective-permute-start.15 = (bf16[16,8,640]{2,1,0:T(8,128)(2,1)S(1)}, bf16[16,8,640]{2,1,0:T(8,128)(2,1)S(1)}, u32[]{:S(2)}, u32[]{:S(2)}) collective-permute-start(bf16[16,8,640]{2,1,0:T(8,128)(2,1)S(1)} %bitcast.25), channel_id=1, source_target_pairs={{16,0},{0,16},{17,1},{1,17},{18,2},{2,18},{19,3},{3,19},{20,4},{4,... | collective-permute-start | bytes 491528 | tf_op jit(solution)/shard_map/ppermute | solution.py:434
  42.5 3.6 %collective-permute-start.12 = (f32[2,2,16]{2,1,0:T(2,128)S(1)}, f32[2,2,16]{2,1,0:T(2,128)S(1)}, u32[]{:S(2)}, u32[]{:S(2)}) collective-permute-start(f32[2,2,16]{2,1,0:T(2,128)S(1)} %fusion.26), channel_id=1, source_target_pairs={{0,1},{1,0},{2,3},{3,2},{4,5},{5,4},{6,7},{7,6},{8,9},{9,8},{10,11... | collective-permute-start | bytes 776 | tf_op jit(solution)/shard_map/ppermute | solution.py:23
  46.1 4.5 %collective-permute-start.13 = (f32[2,2,16]{2,1,0:T(2,128)S(1)}, f32[2,2,16]{2,1,0:T(2,128)S(1)}, u32[]{:S(2)}, u32[]{:S(2)}) collective-permute-start(f32[2,2,16]{2,1,0:T(2,128)S(1)} %add.141), channel_id=1, source_target_pairs={{0,2},{1,3},{2,0},{3,1},{4,6},{5,7},{6,4},{7,5},{8,10},{9,11},{10,... | collective-permute-start | bytes 776 | tf_op jit(solution)/shard_map/ppermute | solution.py:23

commit v4 on v3

--- a/solution.py
+++ b/solution.py
@@ -88,18 +88,12 @@
     return value
 
 
-def first_kernel(parts, groups, info_ref, x_hbm, cot_hbm, *refs):
-    out_refs, (x_ref, cot_ref, sems) = refs[:parts], refs[parts:]
+def first_kernel(parts, groups, info_ref, x_ref, *out_refs):
     rows, cols, cin = x_ref.shape
     chans = cin // parts
     n = rows * cols * (chans // groups)
-    x_copy = pltpu.make_async_copy(x_hbm, x_ref, sems.at[0])
-    cot_copy = pltpu.make_async_copy(cot_hbm, cot_ref, sems.at[1])
-    x_copy.start()
-    cot_copy.start()
     me = info_ref[ME]
     even_h = info_ref[EVEN_H] > 0
-    x_copy.wait()
     shards = [x_ref[:, :, s * chans : (s + 1) * chans].astype(F32) for s in range(parts)]
     stats = []
     for x in shards:
@@ -108,51 +102,63 @@
         centered = flat - expanded(mean, chans)
         squares = gathered(jnp.sum(centered * centered, axis=0, keepdims=True), groups)
         stats.append(jnp.concatenate([p.astype(F32) for p in three_parts(jnp.concatenate([mean, squares], 1))], 0))
-    cot_copy.wait()
-    ends = lambda t: (jnp.where(even_h, t[rows - 1], t[0]), jnp.where(even_h, t[0], t[rows - 1]))
-    cot_ends = ends(cot_ref[...].astype(F32))
-    x_ends = [ends(x) for x in shards]
+    ends = [jnp.concatenate(row_ends(x, even_h), 0) for x in shards]
+    for k, ref in enumerate(out_refs):
+        shard = lax.rem(me + k, parts)
+        ref[: 2 * cols, :] = shard_of(ends, shard).astype(BF16)
+        ref[2 * cols :, :] = jnp.zeros((8, chans), BF16)
+        ref[2 * cols : 2 * cols + 3, : 2 * groups] = shard_of(stats, shard).astype(BF16)
+
+
+def row_ends(t, even_h):
+    first, last = t[0], t[t.shape[0] - 1]
+    return jnp.where(even_h, last, first), jnp.where(even_h, first, last)
+
+
+def column_ends(t, even_w):
+    first, last = t[:, 0, :], t[:, t.shape[1] - 1, :]
+    return jnp.concatenate([jnp.where(even_w, last, first), jnp.where(even_w, first, last)], 0)
+
+
+def columns_kernel(parts, info_ref, x_ref, w_ref, *out_refs):
+    chans = x_ref.shape[2] // parts
+    me = info_ref[ME]
+    ends = column_ends(x_ref[...].astype(F32), info_ref[EVEN_W] > 0)
     for k in range(parts):
         shard = lax.rem(me + k, parts)
-        out_refs[k][: 2 * cols, :chans] = jnp.concatenate([shard_of([e[i] for e in x_ends], shard) for i in range(2)], 0).astype(BF16)
-        out_refs[k][: 2 * cols, chans:] = jnp.concatenate(cot_ends, 0).astype(BF16)
-        out_refs[k][2 * cols :, :] = jnp.zeros((8, out_refs[k].shape[1]), BF16)
-        out_refs[k][2 * cols : 2 * cols + 3, : 2 * groups] = shard_of(stats, shard).astype(BF16)
-
-
-def columns_kernel(parts, info_ref, x_ref, cot_ref, w_ref, *out_refs):
-    rows, cols, cin = x_ref.shape
-    chans = cin // parts
-    me = info_ref[ME]
-    even_w = info_ref[EVEN_W] > 0
-
-    def ends(t):
-        first, last = t[:, 0, :], t[:, cols - 1, :]
-        return jnp.concatenate([jnp.where(even_w, last, first), jnp.where(even_w, first, last)], 0).astype(BF16)
-
-    cot_ends = ends(cot_ref[...].astype(F32))
-    x_ends = ends(x_ref[...].astype(F32)).astype(F32)
-    x_ends = [x_ends[:, s * chans : (s + 1) * chans] for s in range(parts)]
-    for k in range(parts):
-        out_refs[k][:, :chans] = shard_of(x_ends, lax.rem(me + k, parts)).astype(BF16)
-        out_refs[k][:, chans:] = cot_ends
-
-
-def tiles_kernel(parts, info_ref, x_ref, after_ref, *out_refs):
-    chans = x_ref.shape[2] // parts
-    me = info_ref[ME]
-    shards = [x_ref[:, :, s * chans : (s + 1) * chans].astype(F32) for s in range(parts)]
-    for k in range(parts):
-        out_refs[k][...] = shard_of(shards, lax.rem(me + k, parts)).astype(BF16)
+        out_refs[k][...] = shard_of([ends[:, s * chans : (s + 1) * chans] for s in range(parts)], shard).astype(BF16)
+        out_refs[parts + k][...] = shard_of([x_ref[:, :, s * chans : (s + 1) * chans].astype(F32) for s in range(parts)], shard).astype(BF16)
+
+
+def rows_kernel(parts, info_ref, *refs):
+    packs, cots, (near_ref, across_ref, stats_ref) = refs[:parts], refs[parts : 2 * parts], refs[2 * parts :]
+    rows, cols, outs = cots[0].shape
+    chans = packs[0].shape[1]
+    groups = stats_ref.shape[1] // (2 * parts)
+    even_h = info_ref[EVEN_H] > 0
+    packs = [ref[...].astype(F32) for ref in packs]
+    cot_ends = [row_ends(ref[...].astype(F32), even_h) for ref in cots]
+    local = [v[2 * cols : 2 * cols + 3, : 2 * groups] for v in packs]
+    terms = jnp.concatenate([v[:, :groups] for v in local] + [v[:, groups:] for v in local], 1)
+    stats_ref[...] = terms[0:1] + terms[1:2] + terms[2:3]
+    tail = jnp.concatenate([terms, jnp.zeros((3, chans + outs - terms.shape[1]), F32)], 1)
+    for half, ref in enumerate((near_ref, across_ref)):
+        strips = [jnp.concatenate([v[half * cols : (half + 1) * cols], c[half]], 1) for v, c in zip(packs, cot_ends)]
+        ref[...] = jnp.concatenate(strips + ([tail, jnp.zeros((5, chans + outs), F32)] if half == 0 else []), 0).astype(BF16)
+
+
+def cot_columns_kernel(parts, info_ref, *refs):
+    for cot_ref, ref in zip(refs[:parts], refs[parts + 1 :]):
+        ref[...] = column_ends(cot_ref[...].astype(F32), info_ref[EVEN_W] > 0).astype(BF16)
 
 
 def pack_kernel(parts, rows, cols, info_ref, near_h, across_h, stats_ref, *refs):
-    ends, (near_ref, across_ref) = refs[:parts], refs[parts:]
+    ends, cot_ends, (near_ref, across_ref) = refs[:parts], refs[parts : 2 * parts], refs[2 * parts :]
     even_w = info_ref[EVEN_W] > 0
     both = near_ref.shape[1]
     near_rows = near_h[...].astype(F32)
     across_rows = jnp.where((info_ref[UP] > 0) & (info_ref[DOWN] > 0), across_h[...].astype(F32), 0.0)
-    columns = [ref[...].astype(F32) for ref in ends]
+    columns = [jnp.concatenate([x[...].astype(F32), c[...].astype(F32)], 1) for x, c in zip(ends, cot_ends)]
     stats = jnp.concatenate([p.astype(F32) for p in three_parts(stats_ref[...])], 0)
     stats = jnp.concatenate([stats, jnp.zeros((3, both - stats.shape[1]), F32)], 1)
     for half, ref, pick_last in ((0, near_ref, even_w), (1, across_ref, jnp.logical_not(even_w))):
@@ -348,30 +354,33 @@
         [me, where[0] % 2 == 0, where[1] % 2 == 0, where[0] > 0, where[0] < last[0], where[1] > 0, where[1] < last[1]]
     ).astype(jnp.int32)
 
-    *first, x, cot = call(
+    peers = [[(i, (i + k) % parts) for i in range(parts)] for k in range(1, parts)]
+    from_peers = lambda values: [lax.ppermute(v, "dp", pairs) for v, pairs in zip(values, peers)]
+    cot_tiles = [cot, *from_peers([cot] * (parts - 1))]
+    first = call(
         functools.partial(first_kernel, parts, groups),
         "first",
-        [sds((2 * cols + 8, both), BF16)] * parts + [sds(x.shape, BF16), sds(cot.shape, BF16)],
-        [info, x, cot],
-        [pltpu.SemaphoreType.DMA((2,))],
-        in_hbm=(1, 2),
-        limit=40,
+        [sds((2 * cols + 8, chans), BF16)] * parts,
+        [info, x],
         cost=pl.CostEstimate(flops=10**10, bytes_accessed=1, transcendentals=0),
     )
-    peers = [[(i, (i + k) % parts) for i in range(parts)] for k in range(1, parts)]
-    from_peers = lambda values: [lax.ppermute(v, "dp", pairs) for v, pairs in zip(values, peers)]
     got = from_peers(first[1:])
-    ends_h = [first[0], *got]
-    local = [unpacked(v, 2 * cols, 2 * groups) for v in ends_h]
-    stats = jnp.concatenate([v[:, :groups] for v in local] + [v[:, groups:] for v in local], 1)
-    size = stats.shape[1]
-    ends_w = call(
+    columns = call(
         functools.partial(columns_kernel, parts),
         "columns",
-        [sds((2 * rows, both), BF16)] * parts,
-        [info, x, cot, conv_weight],
-    )
-    ends_w = [ends_w[0], *from_peers([v + (0.0 * got[0][:1]).astype(BF16) for v in ends_w[1:]])]
+        [sds((2 * rows, chans), BF16)] * parts + [sds((rows, cols, chans), BF16)] * parts,
+        [info, x, conv_weight],
+    )
+    zero = (0.0 * got[0][:1]).astype(BF16)
+    ends_w = [columns[0], *from_peers([v + zero for v in columns[1:parts]])]
+    x_tiles = [columns[parts], *from_peers([v + zero[None] for v in columns[parts + 1 :]])]
+    size = 2 * parts * groups
+    pack_near, pack_across, stats = call(
+        functools.partial(rows_kernel, parts),
+        "rows",
+        [sds((parts * cols + 8, both), BF16), sds((parts * cols, both), BF16), sds((1, size), F32)],
+        [info, first[0], *got, *cot_tiles],
+    )
 
     def reduced(stats, n, axis, pairings):
         for partner in pairings:
@@ -379,30 +388,26 @@
         return stats, n
 
     rounds_h, rounds_w = stats_rounds("ha"), stats_rounds("wa")
-    near_h = exchange(packed([v[:cols] for v in ends_h], stats), "ha", near)
+    near_h = exchange(pack_near, "ha", near)
+    cot_ends_w = call(
+        functools.partial(cot_columns_kernel, parts),
+        "cot_columns",
+        [sds((2 * rows, outs), BF16)] * parts,
+        [info, *cot_tiles, stats],
+    )
     stats, n = merged(stats, unpacked(near_h, parts * cols, size), n), 2 * n
-    x_tiles = call(
-        functools.partial(tiles_kernel, parts),
-        "tiles",
-        [sds((rows, cols, chans), BF16)] * parts,
-        [info, x, near_h],
-    )
-    cot_tiles = [cot, *from_peers([cotangent[0]] * (parts - 1))]
-    x_tiles = [x_tiles[0], *from_peers(x_tiles[1:])]
-
-    strips = [v[cols : 2 * cols] for v in ends_h]
     if lax.axis_size("ha") == 4:
-        across_h = exchange(packed(strips, stats), "ha", across)
+        across_h = exchange(packed([pack_across], stats), "ha", across)
         stats, n = merged(stats, unpacked(across_h, parts * cols, size), n), 2 * n
     else:
-        across_h = exchange(jnp.concatenate(strips, 0), "ha", across)
+        across_h = exchange(pack_across, "ha", across)
         stats, n = reduced(stats, n, "ha", rounds_h[1:])
     used = parts * (rows + 2)
     near_w, across_w = call(
         functools.partial(pack_kernel, parts, rows, cols),
         "pack",
         [sds((-(-(used + 3) // 8) * 8, both), BF16), sds((used, both), BF16)],
-        [info, near_h, across_h, stats, *ends_w],
+        [info, near_h, across_h, stats, *ends_w, *cot_ends_w],
     )
     near_w = exchange(near_w, "wa", near)
     across_w = exchange(across_w, "wa", across, ends=False)

time: 52.6 us -> 51.3 us (0.975)
  starting transfers between devices: 21.5 us -> 16.8 us
  waiting for transfers between devices: 13.6 us -> 16.5 us
    ppermute x9, waiting for transfers between devices: 8.17 us -> 12.1 us  [exchange(): return lax.ppermute(value, axis, pairs)]
    ppermute x9, starting transfers between devices: 12.4 us -> 9.96 us  [exchange(): return lax.ppermute(value, axis, pairs)]
    ppermute x4, starting transfers between devices: 6.64 us -> 4.29 us  [body(): lax.ppermute(v, 'dp', pairs)]
    ppermute x4, waiting for transfers between devices: 5.19 us -> 4.16 us  [body(): lax.ppermute(v, 'dp', pairs)]
    unnamed x14, local copies, waits for them, and re-layouts: 1.92 us -> 2.45 us
    pallas_call x8 -> x9, Pallas kernels: 13.4 us -> 13.7 us  [call(): pl.pallas_call(kernel, out_shape=outs, in_specs=[spec(i) for i in range(l...]
  transfers between devices with their start and end apart: 16 -> 16, of which waited for: 11 -> 11; matrix products, arithmetic and copies ran while one was open for 1% -> 1% of each run, Pallas kernels for 15% -> 18%
where the time goes in v4:
time: 51.3 us; the launch traced here: 51.1 us
  starting transfers between devices  16.8 us (33%)
  waiting for transfers between devices  16.5 us (32%)
  Pallas kernels  13.7 us (27%)
  local copies, waits for them, and re-layouts  2.53 us (5%)
  between operations  0.8 us (2%)
  other arithmetic  0.78 us (2%)
    pallas_call x9, Pallas kernels, call(): pl.pallas_call(kernel, out_shape=outs, in_specs=[spec(i) for i in range(l...  13.7 us
    ppermute x9, waiting for transfers between devices, exchange(): return lax.ppermute(value, axis, pairs)  12.1 us
    ppermute x9, starting transfers between devices, exchange(): return lax.ppermute(value, axis, pairs)  9.96 us
    ppermute x4, starting transfers between devices, body(): lax.ppermute(v, 'dp', pairs)  4.29 us
    ppermute x4, waiting for transfers between devices, body(): lax.ppermute(v, 'dp', pairs)  4.16 us
    ppermute x3, starting transfers between devices, body(): lax.ppermute(v, 'dp', [(j, i) for i, j in pairs])  2.54 us
    unnamed x14, local copies, waits for them, and re-layouts  2.45 us
  transfers between devices with their start and end apart: 16, of which 11 were waited for; matrix products, arithmetic and copies ran while one was open for 1% of the time, Pallas kernels for 18%

profile of v4, /device:TPU:0, one launch (start us, length us, event | category | flops | bytes accessed | tf_op | source)
XLA Modules:
  0.0 51.1 jit_solution(13739188048925549648)
XLA Ops:
  0.6 3.0 %collective-permute-start.2 = (bf16[16,8,640]{2,1,0:T(8,128)(2,1)}, bf16[16,8,640]{2,1,0:T(8,128)(2,1)S(1)}, u32[]{:S(2)}, u32[]{:S(2)}) collective-permute-start(bf16[16,8,640]{2,1,0:T(8,128)(2,1)} %bitcast.17), channel_id=1, source_target_pairs={{0,16},{16,0},{1,17},{17,1},{2,18},{18,2},{3,19},{19,3},{4,20},{20... | collective-permute-start | bytes 491528 | tf_op jit(solution)/shard_map/ppermute | solution.py:358
  3.7 1.0 %copy-done.2 = bf16[1,16,8,1280]{3,2,1,0:T(8,128)(2,1)S(1)} copy-done((bf16[1,16,8,1280]{3,2,1,0:T(8,128)(2,1)S(1)}, bf16[1,16,8,1280]{3,2,1,0:T(8,128)(2,1)}, u32[]{:S(2)}) %copy-start.2) | copy-done | bytes 327704
  4.7 1.5 %first.1 = (bf16[24,640]{1,0:T(8,128)(2,1)S(1)}, bf16[24,640]{1,0:T(8,128)(2,1)S(1)}) custom-call(s32[7]{0:T(128)S(1)} %stack.64.info_ref, bf16[16,8,1280]{2,1,0:T(8,128)(2,1)S(1)} %bitcast.21), custom_call_target="tpu_custom_call" | custom-call | flops 10000000000 | bytes 1 | tf_op jit(solution)/shard_map/first/pallas_call | solution.py:314
  6.4 1.4 %copy-done = bf16[3,3,640,640]{3,2,1,0:T(8,128)(2,1)S(1)} copy-done((bf16[3,3,640,640]{3,2,1,0:T(8,128)(2,1)S(1)}, bf16[3,3,640,640]{3,2,1,0:T(8,128)(2,1)}, u32[]{:S(2)}) %copy-start) | copy-done | bytes 7372824
  7.8 0.8 %columns.1 = (bf16[32,640]{1,0:T(8,128)(2,1)S(1)}, bf16[32,640]{1,0:T(8,128)(2,1)S(1)}, bf16[16,8,640]{2,1,0:T(8,128)(2,1)S(1)}, bf16[16,8,640]{2,1,0:T(8,128)(2,1)S(1)}) custom-call(s32[7]{0:T(128)S(1)} %stack.64.info_ref, bf16[16,8,1280]{2,1,0:T(8,128)(2,1)S(1)} %bitcast.22, bf16[3,3,640,640]{3,2,1,0:T(8,128)(2,1)S(1)} %copy-done), custom_call_target="tpu_custom_call" | custom-call | tf_op jit(solution)/shard_map/columns/pallas_call | solution.py:314
  8.6 1.6 %collective-permute-done.refs_1_ = bf16[24,640]{1,0:T(8,128)(2,1)S(1)} collective-permute-done((bf16[24,640]{1,0:T(8,128)(2,1)S(1)}, bf16[24,640]{1,0:T(8,128)(2,1)S(1)}, u32[]{:S(2)}, u32[]{:S(2)}) %collective-permute-start) | collective-permute-done | bytes 30752 | tf_op jit(solution)/shard_map/ppermute | solution.py:358
  10.2 0.6 %rows.1 = (bf16[24,1280]{1,0:T(8,128)(2,1)S(1)}, bf16[16,1280]{1,0:T(8,128)(2,1)S(1)}, f32[1,64]{1,0:T(1,128)S(1)}) custom-call(s32[7]{0:T(128)S(1)} %stack.64.info_ref, bf16[24,640]{1,0:T(8,128)(2,1)S(1)} %get-tuple-element.27.refs_0_, bf16[24,640]{1,0:T(8,128)(2,1)S(1)} %collective-permute-done.refs_1_, bf16[16,8,640]{2,1,0:T(8,128)(2,1)S(1)} %bitcast.18, ...), custom_call_target="tpu_custom_call" | custom-call | tf_op jit(solution)/shard_map/rows/pallas_call | solution.py:314
  10.9 1.2 %collective-permute-done.3.near_h.refs_2_ = bf16[24,1280]{1,0:T(8,128)(2,1)S(1)} collective-permute-done((bf16[24,1280]{1,0:T(8,128)(2,1)S(1)}, bf16[24,1280]{1,0:T(8,128)(2,1)S(1)}, u32[]{:S(2)}, u32[]{:S(2)}) %collective-permute-start.3) | collective-permute-done | bytes 61472 | tf_op jit(solution)/shard_map/ppermute | solution.py:23
  12.3 1.3 %collective-permute-start.4 = (bf16[19,1280]{1,0:T(8,128)(2,1)S(1)}, bf16[19,1280]{1,0:T(8,128)(2,1)S(1)}, u32[]{:S(2)}, u32[]{:S(2)}) collective-permute-start(bf16[19,1280]{1,0:T(8,128)(2,1)S(1)} %pad_maximum_fusion), channel_id=1, source_target_pairs={{0,12},{4,8},{8,4},{12,0},{1,13},{5,9},{9,5},{13,1},{2,14},{6,10},... | collective-permute-start | bytes 145928 | tf_op jit(solution)/shard_map/ppermute | solution.py:23
  13.6 0.6 %collective-permute-start.5 = (bf16[32,640]{1,0:T(8,128)(2,1)S(1)}, bf16[32,640]{1,0:T(8,128)(2,1)S(1)}, u32[]{:S(2)}, u32[]{:S(2)}) collective-permute-start(bf16[32,640]{1,0:T(8,128)(2,1)S(1)} %broadcast_add_fusion.1), channel_id=1, source_target_pairs={{0,16},{16,0},{1,17},{17,1},{2,18},{18,2},{3,19},{19,3},{4,20},{20... | collective-permute-start | bytes 122888 | tf_op jit(solution)/shard_map/ppermute | solution.py:358
  14.2 0.7 %cot_columns.1 = (bf16[32,640]{1,0:T(8,128)(2,1)S(1)}, bf16[32,640]{1,0:T(8,128)(2,1)S(1)}) custom-call(s32[7]{0:T(128)S(1)} %stack.64.info_ref, bf16[16,8,640]{2,1,0:T(8,128)(2,1)S(1)} %bitcast.19, bf16[16,8,640]{2,1,0:T(8,128)(2,1)S(1)} %collective-permute-done.2.refs_3_.refs_1_, f32[1,64]{1,0:T(1,128)S(1)} %get-tuple-element.30.refs_2_), custom_call_target="tpu_custom_call" | custom-call | tf_op jit(solution)/shard_map/cot_columns/pallas_call | solution.py:314
  14.9 1.4 %collective-permute-done.4.across_h.refs_3_ = bf16[19,1280]{1,0:T(8,128)(2,1)S(1)} collective-permute-done((bf16[19,1280]{1,0:T(8,128)(2,1)S(1)}, bf16[19,1280]{1,0:T(8,128)(2,1)S(1)}, u32[]{:S(2)}, u32[]{:S(2)}) %collective-permute-start.4) | collective-permute-done | bytes 48672 | tf_op jit(solution)/shard_map/ppermute | solution.py:23
  16.5 1.2 %collective-permute-done.5.refs_1_ = bf16[32,640]{1,0:T(8,128)(2,1)S(1)} collective-permute-done((bf16[32,640]{1,0:T(8,128)(2,1)S(1)}, bf16[32,640]{1,0:T(8,128)(2,1)S(1)}, u32[]{:S(2)}, u32[]{:S(2)}) %collective-permute-start.5) | collective-permute-done | bytes 40992 | tf_op jit(solution)/shard_map/ppermute | solution.py:358
  17.7 0.6 %pack.1 = (bf16[40,1280]{1,0:T(8,128)(2,1)S(1)}, bf16[36,1280]{1,0:T(8,128)(2,1)S(1)}) custom-call(s32[7]{0:T(128)S(1)} %stack.64.info_ref, bf16[24,1280]{1,0:T(8,128)(2,1)S(1)} %collective-permute-done.3.near_h.refs_2_, bf16[19,1280]{1,0:T(8,128)(2,1)S(1)} %collective-permute-done.4.across_h.refs_3_, f32[1,64]{1,0:T(1,128)S(1)} %pad_maximum_fusion.3.stats_ref, ...), custom_call_target="tpu_custom_call" | custom-call | tf_op jit(solution)/shard_map/pack/pallas_call | solution.py:314
  18.3 1.6 %collective-permute-start.6 = (bf16[40,1280]{1,0:T(8,128)(2,1)S(1)}, bf16[40,1280]{1,0:T(8,128)(2,1)S(1)}, u32[]{:S(2)}, u32[]{:S(2)}) collective-permute-start(bf16[40,1280]{1,0:T(8,128)(2,1)S(1)} %get-tuple-element.35), channel_id=1, source_target_pairs={{0,1},{1,0},{2,3},{3,2},{4,5},{5,4},{6,7},{7,6},{8,9},{9,8},{10,11... | collective-permute-start | bytes 307208 | tf_op jit(solution)/shard_map/ppermute | solution.py:23
  20.0 0.7 %collective-permute-start.7 = (bf16[36,1280]{1,0:T(8,128)(2,1)S(1)}, bf16[36,1280]{1,0:T(8,128)(2,1)S(1)}, u32[]{:S(2)}, u32[]{:S(2)}) collective-permute-start(bf16[36,1280]{1,0:T(8,128)(2,1)S(1)} %get-tuple-element.36), channel_id=1, source_target_pairs={{1,2},{2,1},{5,6},{6,5},{9,10},{10,9},{13,14},{14,13},{17,18},{18,... | collective-permute-start | bytes 276488 | tf_op jit(solution)/shard_map/ppermute | solution.py:23
  20.6 2.4 %collective-permute-done.6.refs_4_ = bf16[40,1280]{1,0:T(8,128)(2,1)S(1)} collective-permute-done((bf16[40,1280]{1,0:T(8,128)(2,1)S(1)}, bf16[40,1280]{1,0:T(8,128)(2,1)S(1)}, u32[]{:S(2)}, u32[]{:S(2)}) %collective-permute-start.6) | collective-permute-done | bytes 102432 | tf_op jit(solution)/shard_map/ppermute | solution.py:23
  23.2 2.6 %collective-permute-start.8 = (f32[1,64]{1,0:T(1,128)S(1)}, f32[1,64]{1,0:T(1,128)S(1)}, u32[]{:S(2)}, u32[]{:S(2)}) collective-permute-start(f32[1,64]{1,0:T(1,128)S(1)} %pad_maximum_fusion.4), channel_id=1, source_target_pairs={{0,2},{1,3},{2,0},{3,1},{4,6},{5,7},{6,4},{7,5},{8,10},{9,11},{10,... | collective-permute-start | bytes 776 | tf_op jit(solution)/shard_map/ppermute | solution.py:23
  26.4 3.2 %conv_backward.1.refs_9_ = f32[16,2,8,640]{3,2,1,0:T(8,128)S(1)} custom-call(s32[7]{0:T(128)S(1)} %stack.64.info_ref, bf16[16,8,640]{2,1,0:T(8,128)(2,1)S(1)} %bitcast.20, bf16[16,8,640]{2,1,0:T(8,128)(2,1)S(1)} %collective-permute-done.2.refs_3_.refs_1_, bf16[24,1280]{1,0:T(8,128)(2,1)S(1)} %collective-permute-done.3.near_h.refs_2_, ...), custom_call_target="tpu_custom_call" | custom-call | tf_op jit(solution)/shard_map/conv_backward/pallas_call | solution.py:314
  29.8 1.4 %collective-permute-done.1.refs_1_ = bf16[16,8,640]{2,1,0:T(8,128)(2,1)S(1)} collective-permute-done((bf16[16,8,640]{2,1,0:T(8,128)(2,1)S(1)}, bf16[16,8,640]{2,1,0:T(8,128)(2,1)S(1)}, u32[]{:S(2)}, u32[]{:S(2)}) %collective-permute-start.1) | collective-permute-done | bytes 163872 | tf_op jit(solution)/shard_map/ppermute | solution.py:358
  31.2 1.6 %terms.1 = (f32[4,16]{1,0:T(4,128)S(1)}, f32[4,16]{1,0:T(4,128)S(1)}, f32[16,8,640]{2,1,0:T(8,128)S(1)}, bf16[1,16,8,640]{3,2,1,0:T(8,128)(2,1)S(1)}, f32[18,2,16,640]{3,2,1,0:T(8,128)S(1)}) custom-call(s32[7]{0:T(128)S(1)} %stack.64.info_ref, bf16[16,8,640]{2,1,0:T(8,128)(2,1)S(1)} %get-tuple-element.24.refs_0_, ...), custom_call_target="tpu_custom_call" | custom-call | tf_op jit(solution)/shard_map/terms/pallas_call | solution.py:314
  33.4 2.8 %conv_forward.1 = (f32[16,8,640]{2,1,0:T(8,128)S(1)}, bf16[1,16,8,640]{3,2,1,0:T(8,128)(2,1)S(1)}) custom-call(f32[18,2,16,640]{3,2,1,0:T(8,128)S(1)} %get-tuple-element.39.padded_ref, bf16[3,3,640,640]{3,2,1,0:T(8,128)(2,1)S(1)} %copy-done), custom_call_target="tpu_custom_call" | custom-call | tf_op jit(solution)/shard_map/conv_forward/pallas_call | solution.py:314
  36.5 1.1 %collective-permute-done.10 = f32[2,2,16]{2,1,0:T(2,128)S(1)} collective-permute-done((f32[2,2,16]{2,1,0:T(2,128)S(1)}, f32[2,2,16]{2,1,0:T(2,128)S(1)}, u32[]{:S(2)}, u32[]{:S(2)}) %collective-permute-start.10) | collective-permute-done | bytes 288 | tf_op jit(solution)/shard_map/ppermute | solution.py:23
  37.6 0.9 %collective-permute-start.11 = (f32[2,2,16]{2,1,0:T(2,128)S(1)}, f32[2,2,16]{2,1,0:T(2,128)S(1)}, u32[]{:S(2)}, u32[]{:S(2)}) collective-permute-start(f32[2,2,16]{2,1,0:T(2,128)S(1)} %fusion.14), channel_id=1, source_target_pairs={{0,8},{4,12},{8,0},{12,4},{1,9},{5,13},{9,1},{13,5},{2,10},{6,14},... | collective-permute-start | bytes 776 | tf_op jit(solution)/shard_map/ppermute | solution.py:23
  38.5 1.3 %collective-permute-start.14 = (bf16[16,8,640]{2,1,0:T(8,128)(2,1)S(1)}, bf16[16,8,640]{2,1,0:T(8,128)(2,1)S(1)}, u32[]{:S(2)}, u32[]{:S(2)}) collective-permute-start(bf16[16,8,640]{2,1,0:T(8,128)(2,1)S(1)} %bitcast.28), channel_id=1, source_target_pairs={{16,0},{0,16},{17,1},{1,17},{18,2},{2,18},{19,3},{3,19},{20,4},{4,... | collective-permute-start | bytes 491528 | tf_op jit(solution)/shard_map/ppermute | solution.py:439
  39.8 0.7 %collective-permute-start.15 = (bf16[16,8,640]{2,1,0:T(8,128)(2,1)S(1)}, bf16[16,8,640]{2,1,0:T(8,128)(2,1)S(1)}, u32[]{:S(2)}, u32[]{:S(2)}) collective-permute-start(bf16[16,8,640]{2,1,0:T(8,128)(2,1)S(1)} %bitcast.29), channel_id=1, source_target_pairs={{16,0},{0,16},{17,1},{1,17},{18,2},{2,18},{19,3},{3,19},{20,4},{4,... | collective-permute-start | bytes 491528 | tf_op jit(solution)/shard_map/ppermute | solution.py:439
  40.5 0.7 %collective-permute-done.11 = f32[2,2,16]{2,1,0:T(2,128)S(1)} collective-permute-done((f32[2,2,16]{2,1,0:T(2,128)S(1)}, f32[2,2,16]{2,1,0:T(2,128)S(1)}, u32[]{:S(2)}, u32[]{:S(2)}) %collective-permute-start.11) | collective-permute-done | bytes 288 | tf_op jit(solution)/shard_map/ppermute | solution.py:23
  41.2 1.6 %collective-permute-start.12 = (f32[2,2,16]{2,1,0:T(2,128)S(1)}, f32[2,2,16]{2,1,0:T(2,128)S(1)}, u32[]{:S(2)}, u32[]{:S(2)}) collective-permute-start(f32[2,2,16]{2,1,0:T(2,128)S(1)} %fusion.15), channel_id=1, source_target_pairs={{0,1},{1,0},{2,3},{3,2},{4,5},{5,4},{6,7},{7,6},{8,9},{9,8},{10,11... | collective-permute-start | bytes 776 | tf_op jit(solution)/shard_map/ppermute | solution.py:23
  42.8 2.0 %collective-permute-done.12 = f32[2,2,16]{2,1,0:T(2,128)S(1)} collective-permute-done((f32[2,2,16]{2,1,0:T(2,128)S(1)}, f32[2,2,16]{2,1,0:T(2,128)S(1)}, u32[]{:S(2)}, u32[]{:S(2)}) %collective-permute-start.12) | collective-permute-done | bytes 288 | tf_op jit(solution)/shard_map/ppermute | solution.py:23
  44.8 1.3 %collective-permute-start.13 = (f32[2,2,16]{2,1,0:T(2,128)S(1)}, f32[2,2,16]{2,1,0:T(2,128)S(1)}, u32[]{:S(2)}, u32[]{:S(2)}) collective-permute-start(f32[2,2,16]{2,1,0:T(2,128)S(1)} %add.133), channel_id=1, source_target_pairs={{0,2},{1,3},{2,0},{3,1},{4,6},{5,7},{6,4},{7,5},{8,10},{9,11},{10,... | collective-permute-start | bytes 776 | tf_op jit(solution)/shard_map/ppermute | solution.py:23
  46.1 3.2 %collective-permute-done.13 = f32[2,2,16]{2,1,0:T(2,128)S(1)} collective-permute-done((f32[2,2,16]{2,1,0:T(2,128)S(1)}, f32[2,2,16]{2,1,0:T(2,128)S(1)}, u32[]{:S(2)}, u32[]{:S(2)}) %collective-permute-start.13) | collective-permute-done | bytes 288 | tf_op jit(solution)/shard_map/ppermute | solution.py:23
  49.3 1.8 %finish.1 = (bf16[16,8,640]{2,1,0:T(8,128)(2,1)}, bf16[16,8,1280]{2,1,0:T(8,128)(2,1)}) custom-call(s32[7]{0:T(128)S(1)} %stack.64.info_ref, bf16[16,8,1280]{2,1,0:T(8,128)(2,1)S(1)} %bitcast.23, f32[2,4,16]{2,1,0:T(4,128)S(1)} %pad_maximum_fusion.1.small_ref, f32[2,2,16]{2,1,0:T(2,128)S(1)} %add.134.sums_ref, f32[640]{0:T(1024)S(1)} %copy-done.6, ...), custom_call_target="tpu_custom_call" | custom-call | tf_op jit(solution)/shard_map/finish/pallas_call | solution.py:314
  (51 shorter events, 2.4 us)
Async XLA Ops:
  0.6 9.6 %collective-permute-start.2 = (bf16[16,8,640]{2,1,0:T(8,128)(2,1)}, bf16[16,8,640]{2,1,0:T(8,128)(2,1)S(1)}, u32[]{:S(2)}, u32[]{:S(2)}) collective-permute-start(bf16[16,8,640]{2,1,0:T(8,128)(2,1)} %bitcast.17), channel_id=1, source_target_pairs={{0,16},{16,0},{1,17},{17,1},{2,18},{18,2},{3,19},{19,3},{4,20},{20... | collective-permute-start | bytes 491528 | tf_op jit(solution)/shard_map/ppermute | solution.py:358
  3.7 1.0 %copy-start.2 = (bf16[1,16,8,1280]{3,2,1,0:T(8,128)(2,1)S(1)}, bf16[1,16,8,1280]{3,2,1,0:T(8,128)(2,1)}, u32[]{:S(2)}) copy-start(bf16[1,16,8,1280]{3,2,1,0:T(8,128)(2,1)} %param.6) | copy-start | bytes 983044
  4.7 3.1 %copy-start = (bf16[3,3,640,640]{3,2,1,0:T(8,128)(2,1)S(1)}, bf16[3,3,640,640]{3,2,1,0:T(8,128)(2,1)}, u32[]{:S(2)}) copy-start(bf16[3,3,640,640]{3,2,1,0:T(8,128)(2,1)} %w_ref.3) | copy-start | bytes 22118404
  6.2 4.0 %copy-start.1 = (bf16[1,16,8,640]{3,2,1,0:T(8,128)(2,1)S(1)}, bf16[1,16,8,640]{3,2,1,0:T(8,128)(2,1)}, u32[]{:S(2)}) copy-start(bf16[1,16,8,640]{3,2,1,0:T(8,128)(2,1)} %param.11) | copy-start | bytes 491524
  6.2 25.0 %copy-start.4 = (f32[1280]{0:T(1024)S(1)}, f32[1280]{0:T(1024)}, u32[]{:S(2)}) copy-start(f32[1280]{0:T(1024)} %refs_7_.1) | copy-start | bytes 15364
  6.2 25.0 %copy-start.5 = (f32[1280]{0:T(1024)S(1)}, f32[1280]{0:T(1024)}, u32[]{:S(2)}) copy-start(f32[1280]{0:T(1024)} %refs_8_.1) | copy-start | bytes 15364
  6.3 4.0 %collective-permute-start = (bf16[24,640]{1,0:T(8,128)(2,1)S(1)}, bf16[24,640]{1,0:T(8,128)(2,1)S(1)}, u32[]{:S(2)}, u32[]{:S(2)}) collective-permute-start(bf16[24,640]{1,0:T(8,128)(2,1)S(1)} %get-tuple-element.26), channel_id=1, source_target_pairs={{0,16},{16,0},{1,17},{17,1},{2,18},{18,2},{3,19},{19,3},{4,20},{20... | collective-permute-start | bytes 92168 | tf_op jit(solution)/shard_map/ppermute | solution.py:358
  10.8 1.3 %collective-permute-start.3 = (bf16[24,1280]{1,0:T(8,128)(2,1)S(1)}, bf16[24,1280]{1,0:T(8,128)(2,1)S(1)}, u32[]{:S(2)}, u32[]{:S(2)}) collective-permute-start(bf16[24,1280]{1,0:T(8,128)(2,1)S(1)} %get-tuple-element.28), channel_id=1, source_target_pairs={{0,4},{4,0},{8,12},{12,8},{1,5},{5,1},{9,13},{13,9},{2,6},{6,2},{1... | collective-permute-start | bytes 184328 | tf_op jit(solution)/shard_map/ppermute | solution.py:23
  12.3 4.0 %collective-permute-start.4 = (bf16[19,1280]{1,0:T(8,128)(2,1)S(1)}, bf16[19,1280]{1,0:T(8,128)(2,1)S(1)}, u32[]{:S(2)}, u32[]{:S(2)}) collective-permute-start(bf16[19,1280]{1,0:T(8,128)(2,1)S(1)} %pad_maximum_fusion), channel_id=1, source_target_pairs={{0,12},{4,8},{8,4},{12,0},{1,13},{5,9},{9,5},{13,1},{2,14},{6,10},... | collective-permute-start | bytes 145928 | tf_op jit(solution)/shard_map/ppermute | solution.py:23
  13.6 4.1 %collective-permute-start.5 = (bf16[32,640]{1,0:T(8,128)(2,1)S(1)}, bf16[32,640]{1,0:T(8,128)(2,1)S(1)}, u32[]{:S(2)}, u32[]{:S(2)}) collective-permute-start(bf16[32,640]{1,0:T(8,128)(2,1)S(1)} %broadcast_add_fusion.1), channel_id=1, source_target_pairs={{0,16},{16,0},{1,17},{17,1},{2,18},{18,2},{3,19},{19,3},{4,20},{20... | collective-permute-start | bytes 122888 | tf_op jit(solution)/shard_map/ppermute | solution.py:358
  18.3 4.7 %collective-permute-start.6 = (bf16[40,1280]{1,0:T(8,128)(2,1)S(1)}, bf16[40,1280]{1,0:T(8,128)(2,1)S(1)}, u32[]{:S(2)}, u32[]{:S(2)}) collective-permute-start(bf16[40,1280]{1,0:T(8,128)(2,1)S(1)} %get-tuple-element.35), channel_id=1, source_target_pairs={{0,1},{1,0},{2,3},{3,2},{4,5},{5,4},{6,7},{7,6},{8,9},{9,8},{10,11... | collective-permute-start | bytes 307208 | tf_op jit(solution)/shard_map/ppermute | solution.py:23
  20.0 6.5 %collective-permute-start.7 = (bf16[36,1280]{1,0:T(8,128)(2,1)S(1)}, bf16[36,1280]{1,0:T(8,128)(2,1)S(1)}, u32[]{:S(2)}, u32[]{:S(2)}) collective-permute-start(bf16[36,1280]{1,0:T(8,128)(2,1)S(1)} %get-tuple-element.36), channel_id=1, source_target_pairs={{1,2},{2,1},{5,6},{6,5},{9,10},{10,9},{13,14},{14,13},{17,18},{18,... | collective-permute-start | bytes 276488 | tf_op jit(solution)/shard_map/ppermute | solution.py:23
  23.2 6.5 %collective-permute-start.8 = (f32[1,64]{1,0:T(1,128)S(1)}, f32[1,64]{1,0:T(1,128)S(1)}, u32[]{:S(2)}, u32[]{:S(2)}) collective-permute-start(f32[1,64]{1,0:T(1,128)S(1)} %pad_maximum_fusion.4), channel_id=1, source_target_pairs={{0,2},{1,3},{2,0},{3,1},{4,6},{5,7},{6,4},{7,5},{8,10},{9,11},{10,... | collective-permute-start | bytes 776 | tf_op jit(solution)/shard_map/ppermute | solution.py:23
  25.8 23.5 %copy-start.3 = (bf16[1,16,8,1280]{3,2,1,0:T(8,128)(2,1)S(1)}, bf16[1,16,8,1280]{3,2,1,0:T(8,128)(2,1)}, u32[]{:S(2)}) copy-start(bf16[1,16,8,1280]{3,2,1,0:T(8,128)(2,1)} %param.6) | copy-start | bytes 983044
  25.8 23.5 %copy-start.6 = (f32[640]{0:T(1024)S(1)}, f32[640]{0:T(1024)}, u32[]{:S(2)}) copy-start(f32[640]{0:T(1024)} %bias_ref.1) | copy-start | bytes 7684
  25.9 5.4 %collective-permute-start.1 = (bf16[16,8,640]{2,1,0:T(8,128)(2,1)S(1)}, bf16[16,8,640]{2,1,0:T(8,128)(2,1)S(1)}, u32[]{:S(2)}, u32[]{:S(2)}) collective-permute-start(bf16[16,8,640]{2,1,0:T(8,128)(2,1)S(1)} %broadcast_add_fusion), channel_id=1, source_target_pairs={{0,16},{16,0},{1,17},{17,1},{2,18},{18,2},{3,19},{19,3},{4,20},{20... | collective-permute-start | bytes 491528 | tf_op jit(solution)/shard_map/ppermute | solution.py:358
  32.9 3.6 %collective-permute-start.9 = (f32[4,16]{1,0:T(4,128)S(1)}, f32[4,16]{1,0:T(4,128)S(1)}, u32[]{:S(2)}, u32[]{:S(2)}) collective-permute-start(f32[4,16]{1,0:T(4,128)S(1)} %get-tuple-element.38), channel_id=1, source_target_pairs={{16,0},{0,16},{17,1},{1,17},{18,2},{2,18},{19,3},{3,19},{20,4},{4,... | collective-permute-start | bytes 776 | tf_op jit(solution)/shard_map/ppermute | solution.py:439
  36.5 1.2 %collective-permute-start.10 = (f32[2,2,16]{2,1,0:T(2,128)S(1)}, f32[2,2,16]{2,1,0:T(2,128)S(1)}, u32[]{:S(2)}, u32[]{:S(2)}) collective-permute-start(f32[2,2,16]{2,1,0:T(2,128)S(1)} %fusion.7), channel_id=1, source_target_pairs={{0,4},{4,0},{8,12},{12,8},{1,5},{5,1},{9,13},{13,9},{2,6},{6,2},{1... | collective-permute-start | bytes 776 | tf_op jit(solution)/shard_map/ppermute | solution.py:23
  37.6 3.6 %collective-permute-start.11 = (f32[2,2,16]{2,1,0:T(2,128)S(1)}, f32[2,2,16]{2,1,0:T(2,128)S(1)}, u32[]{:S(2)}, u32[]{:S(2)}) collective-permute-start(f32[2,2,16]{2,1,0:T(2,128)S(1)} %fusion.14), channel_id=1, source_target_pairs={{0,8},{4,12},{8,0},{12,4},{1,9},{5,13},{9,1},{13,5},{2,10},{6,14},... | collective-permute-start | bytes 776 | tf_op jit(solution)/shard_map/ppermute | solution.py:23
  38.5 10.8 %collective-permute-start.14 = (bf16[16,8,640]{2,1,0:T(8,128)(2,1)S(1)}, bf16[16,8,640]{2,1,0:T(8,128)(2,1)S(1)}, u32[]{:S(2)}, u32[]{:S(2)}) collective-permute-start(bf16[16,8,640]{2,1,0:T(8,128)(2,1)S(1)} %bitcast.28), channel_id=1, source_target_pairs={{16,0},{0,16},{17,1},{1,17},{18,2},{2,18},{19,3},{3,19},{20,4},{4,... | collective-permute-start | bytes 491528 | tf_op jit(solution)/shard_map/ppermute | solution.py:439
  39.8 9.5 %collective-permute-start.15 = (bf16[16,8,640]{2,1,0:T(8,128)(2,1)S(1)}, bf16[16,8,640]{2,1,0:T(8,128)(2,1)S(1)}, u32[]{:S(2)}, u32[]{:S(2)}) collective-permute-start(bf16[16,8,640]{2,1,0:T(8,128)(2,1)S(1)} %bitcast.29), channel_id=1, source_target_pairs={{16,0},{0,16},{17,1},{1,17},{18,2},{2,18},{19,3},{3,19},{20,4},{4,... | collective-permute-start | bytes 491528 | tf_op jit(solution)/shard_map/ppermute | solution.py:439
  41.2 3.6 %collective-permute-start.12 = (f32[2,2,16]{2,1,0:T(2,128)S(1)}, f32[2,2,16]{2,1,0:T(2,128)S(1)}, u32[]{:S(2)}, u32[]{:S(2)}) collective-permute-start(f32[2,2,16]{2,1,0:T(2,128)S(1)} %fusion.15), channel_id=1, source_target_pairs={{0,1},{1,0},{2,3},{3,2},{4,5},{5,4},{6,7},{7,6},{8,9},{9,8},{10,11... | collective-permute-start | bytes 776 | tf_op jit(solution)/shard_map/ppermute | solution.py:23
  44.8 4.5 %collective-permute-start.13 = (f32[2,2,16]{2,1,0:T(2,128)S(1)}, f32[2,2,16]{2,1,0:T(2,128)S(1)}, u32[]{:S(2)}, u32[]{:S(2)}) collective-permute-start(f32[2,2,16]{2,1,0:T(2,128)S(1)} %add.133), channel_id=1, source_target_pairs={{0,2},{1,3},{2,0},{3,1},{4,6},{5,7},{6,4},{7,5},{8,10},{9,11},{10,... | collective-permute-start | bytes 776 | tf_op jit(solution)/shard_map/ppermute | solution.py:23

commit v5 on v4

--- a/solution.py
+++ b/solution.py
@@ -103,11 +103,13 @@
         squares = gathered(jnp.sum(centered * centered, axis=0, keepdims=True), groups)
         stats.append(jnp.concatenate([p.astype(F32) for p in three_parts(jnp.concatenate([mean, squares], 1))], 0))
     ends = [jnp.concatenate(row_ends(x, even_h), 0) for x in shards]
+    columns = [column_ends(x, info_ref[EVEN_W] > 0) for x in shards]
     for k, ref in enumerate(out_refs):
         shard = lax.rem(me + k, parts)
         ref[: 2 * cols, :] = shard_of(ends, shard).astype(BF16)
-        ref[2 * cols :, :] = jnp.zeros((8, chans), BF16)
+        ref[2 * cols : 2 * cols + 8, :] = jnp.zeros((8, chans), BF16)
         ref[2 * cols : 2 * cols + 3, : 2 * groups] = shard_of(stats, shard).astype(BF16)
+        ref[2 * cols + 8 :, :] = shard_of(columns, shard).astype(BF16)
 
 
 def row_ends(t, even_h):
@@ -120,14 +122,11 @@
     return jnp.concatenate([jnp.where(even_w, last, first), jnp.where(even_w, first, last)], 0)
 
 
-def columns_kernel(parts, info_ref, x_ref, w_ref, *out_refs):
+def tiles_kernel(parts, info_ref, x_ref, w_ref, *out_refs):
     chans = x_ref.shape[2] // parts
-    me = info_ref[ME]
-    ends = column_ends(x_ref[...].astype(F32), info_ref[EVEN_W] > 0)
     for k in range(parts):
-        shard = lax.rem(me + k, parts)
-        out_refs[k][...] = shard_of([ends[:, s * chans : (s + 1) * chans] for s in range(parts)], shard).astype(BF16)
-        out_refs[parts + k][...] = shard_of([x_ref[:, :, s * chans : (s + 1) * chans].astype(F32) for s in range(parts)], shard).astype(BF16)
+        shard = lax.rem(info_ref[ME] + k, parts)
+        out_refs[k][...] = shard_of([x_ref[:, :, s * chans : (s + 1) * chans].astype(F32) for s in range(parts)], shard).astype(BF16)
 
 
 def rows_kernel(parts, info_ref, *refs):
@@ -147,18 +146,22 @@
         ref[...] = jnp.concatenate(strips + ([tail, jnp.zeros((5, chans + outs), F32)] if half == 0 else []), 0).astype(BF16)
 
 
-def cot_columns_kernel(parts, info_ref, *refs):
-    for cot_ref, ref in zip(refs[:parts], refs[parts + 1 :]):
-        ref[...] = column_ends(cot_ref[...].astype(F32), info_ref[EVEN_W] > 0).astype(BF16)
+def columns_kernel(parts, info_ref, *refs):
+    even_w = info_ref[EVEN_W] > 0
+    for pack_ref, cot_ref, ref in zip(refs[:parts], refs[parts : 2 * parts], refs[2 * parts + 1 :]):
+        rows, cols, _ = cot_ref.shape
+        chans = pack_ref.shape[1]
+        ref[:, :chans] = pack_ref[...].astype(F32)[2 * cols + 8 :].astype(BF16)
+        ref[:, chans:] = column_ends(cot_ref[...].astype(F32), even_w).astype(BF16)
 
 
 def pack_kernel(parts, rows, cols, info_ref, near_h, across_h, stats_ref, *refs):
-    ends, cot_ends, (near_ref, across_ref) = refs[:parts], refs[parts : 2 * parts], refs[2 * parts :]
+    ends, (near_ref, across_ref) = refs[:parts], refs[parts:]
     even_w = info_ref[EVEN_W] > 0
     both = near_ref.shape[1]
     near_rows = near_h[...].astype(F32)
     across_rows = jnp.where((info_ref[UP] > 0) & (info_ref[DOWN] > 0), across_h[...].astype(F32), 0.0)
-    columns = [jnp.concatenate([x[...].astype(F32), c[...].astype(F32)], 1) for x, c in zip(ends, cot_ends)]
+    columns = [ref[...].astype(F32) for ref in ends]
     stats = jnp.concatenate([p.astype(F32) for p in three_parts(stats_ref[...])], 0)
     stats = jnp.concatenate([stats, jnp.zeros((3, both - stats.shape[1]), F32)], 1)
     for half, ref, pick_last in ((0, near_ref, even_w), (1, across_ref, jnp.logical_not(even_w))):
@@ -202,7 +205,7 @@
 
 
 def backward_kernel(parts, info_ref, *refs):
-    tiles, (near_h, across_h, near_w, across_w, w_ref, grad_ref, padded_ref, windows_ref) = refs[:parts], refs[parts:]
+    tiles, (near_h, across_h, near_w, across_w, w_ref, *_, grad_ref, padded_ref, windows_ref) = refs[:parts], refs[parts:]
     rows, cols, outs = tiles[0].shape
     chans = w_ref.shape[2]
     strips = halos(parts, rows, cols, info_ref, near_h, across_h, near_w, across_w, slice(chans, chans + outs))
@@ -216,48 +219,33 @@
             padded_ref[1 : rows + 1, k, at, :] = mid
             padded_ref[rows + 1, k, at : at + 1, :] = bottom
     windows(padded_ref, windows_ref, parts, cols)
-    total = None
-    for ky in range(3):
-        for kx in range(3):
-            window = windows_ref[kx, ky : ky + rows].reshape(rows * parts * cols, outs)
-            term = lax.dot_general(w_ref[2 - ky, 2 - kx], window, (((1,), (1,)), ((), ())), preferred_element_type=F32)
-            total = term if total is None else total + term
+    taps = [(ky, kx) for ky in range(3) for kx in range(3)]
+    shifted = jnp.concatenate([windows_ref[kx, ky : ky + rows].reshape(rows * parts * cols, outs) for ky, kx in taps], 1)
+    weight = jnp.concatenate([w_ref[2 - ky, 2 - kx] for ky, kx in taps], 1)
+    total = lax.dot_general(weight, shifted, (((1,), (1,)), ((), ())), preferred_element_type=F32)
     grad_ref[...] = total.T.reshape(rows, parts, cols, chans)
 
 
 def terms_kernel(parts, count, info_ref, *refs):
     tiles = refs[:parts]
-    near_h, across_h, near_w, across_w, stats_ref, gain_ref, shift_ref, grad_ref = refs[parts : parts + 8]
-    moments_refs, (gx_own_ref, gx_other_ref, padded_ref) = refs[parts + 8 : -3], refs[-3:]
+    stats_ref, gain_ref, shift_ref, grad_ref = refs[parts : parts + 4]
+    moments_refs, (gx_own_ref, gx_other_ref, padded_ref, scales_ref) = refs[parts + 4 : -4], refs[-4:]
     rows, cols, _ = tiles[0].shape
     chans = grad_ref.shape[3]
     groups = stats_ref.shape[1] // (2 * parts)
     stats = jnp.concatenate([stats_ref[:, i * groups : (i + 1) * groups] for i in range(2 * parts)], 0)
-    strips = halos(parts, rows, cols, info_ref, near_h, across_h, near_w, across_w, slice(0, chans))
     wide = expanded(jnp.concatenate([stats[:parts], lax.rsqrt(stats[parts:] / count + EPS)], 0), chans)
     means, invs = wide[:parts], wide[parts:]
     mine = lambda ref: shard_of([ref[s * chans : (s + 1) * chans].reshape(1, chans) for s in range(parts)], info_ref[ME])
     gain, shift = mine(gain_ref), mine(shift_ref)
-    up, down, left, right = (info_ref[i] > 0 for i in (UP, DOWN, LEFT, RIGHT))
+    scales_ref[...] = jnp.concatenate([wide, gain, shift], 0)
     firsts, seconds = [], []
     for k in range(parts):
         mean, inv = means[k : k + 1], invs[k : k + 1]
-
-        def act_of(t, inside):
-            z = (t - mean) * inv * gain + shift
-            return jnp.where(inside, z * jax.nn.sigmoid(z), 0.0)
-
-        above, below, before, after = strips(k)
         xhat = (tiles[k][...].astype(F32) - mean[None]) * inv[None]
         z = xhat * gain[None] + shift[None]
         sig = jax.nn.sigmoid(z)
-        padded_ref[1 : rows + 1, k, 1 : cols + 1, :] = z * sig
-        padded_ref[0, k, 1 : cols + 1, :] = act_of(above, up)
-        padded_ref[rows + 1, k, 1 : cols + 1, :] = act_of(below, down)
-        for at, (top, mid, bottom), side in ((0, before, left), (cols + 1, after, right)):
-            padded_ref[0, k, at : at + 1, :] = act_of(top, side & up)
-            padded_ref[1 : rows + 1, k, at, :] = act_of(mid, side)
-            padded_ref[rows + 1, k, at : at + 1, :] = act_of(bottom, side & down)
+        padded_ref[:, k, 1 : cols + 1, :] = z * sig
         gx = grad_ref[:, k] * sig * (1.0 + z * (1.0 - sig)) * gain[None]
         if k == 0:
             gx_own_ref[...] = gx
@@ -270,16 +258,33 @@
         ref[...] = jnp.concatenate([v[k : k + 1] for v in (sums[:parts], sums[parts:], stats[:parts], stats[parts:])], 0)
 
 
-def forward_kernel(parts, padded_ref, w_ref, conv_own_ref, conv_other_ref, windows_ref):
+def forward_kernel(parts, info_ref, given_ref, scales_ref, near_h, across_h, near_w, across_w, w_ref, conv_own_ref, conv_other_ref, padded_ref, windows_ref):
     rows, cols, outs = conv_own_ref.shape
     chans = windows_ref.shape[3]
+    strips = halos(parts, rows, cols, info_ref, near_h, across_h, near_w, across_w, slice(0, chans))
+    up, down, left, right = (info_ref[i] > 0 for i in (UP, DOWN, LEFT, RIGHT))
+    scales = scales_ref[...]
+    gain, shift = scales[2 * parts : 2 * parts + 1], scales[2 * parts + 1 : 2 * parts + 2]
+    padded_ref[1 : rows + 1] = given_ref[...]
+    for k in range(parts):
+        mean, inv = scales[k : k + 1], scales[parts + k : parts + k + 1]
+
+        def act_of(t, inside):
+            z = (t - mean) * inv * gain + shift
+            return jnp.where(inside, z * jax.nn.sigmoid(z), 0.0)
+
+        above, below, before, after = strips(k)
+        padded_ref[0, k, 1 : cols + 1, :] = act_of(above, up)
+        padded_ref[rows + 1, k, 1 : cols + 1, :] = act_of(below, down)
+        for at, (top, mid, bottom), side in ((0, before, left), (cols + 1, after, right)):
+            padded_ref[0, k, at : at + 1, :] = act_of(top, side & up)
+            padded_ref[1 : rows + 1, k, at, :] = act_of(mid, side)
+            padded_ref[rows + 1, k, at : at + 1, :] = act_of(bottom, side & down)
     windows(padded_ref, windows_ref, parts, cols)
-    total = None
-    for ky in range(3):
-        for kx in range(3):
-            window = windows_ref[kx, ky : ky + rows].reshape(rows * parts * cols, chans)
-            term = jnp.dot(window, w_ref[ky, kx], preferred_element_type=F32)
-            total = term if total is None else total + term
+    taps = [(ky, kx) for ky in range(3) for kx in range(3)]
+    shifted = jnp.concatenate([windows_ref[kx, ky : ky + rows].reshape(rows * parts * cols, chans) for ky, kx in taps], 1)
+    weight = w_ref[...].reshape(9 * chans, outs)
+    total = lax.dot_general(weight, shifted, (((0,), (1,)), ((), ())), preferred_element_type=F32).T
     total = total.reshape(rows, parts, cols, outs)
     conv_own_ref[...] = total[:, 0]
     for k in range(1, parts):
@@ -288,34 +293,48 @@
 
 def finish_kernel(parts, count, info_ref, x_ref, small_ref, sums_ref, bias_ref, gx_own_ref, conv_own_ref, *refs):
     gx_refs, conv_refs = refs[: parts - 1], refs[parts - 1 : 2 * parts - 2]
-    conv_ref, grad_ref = refs[2 * parts - 2 :]
+    conv_out, grad_out, conv_ref, grad_ref, sems = refs[2 * parts - 2 :]
+    rows = x_ref.shape[0]
+    copies = [pltpu.make_async_copy(conv_ref, conv_out, sems.at[0])]
     cin = x_ref.shape[2]
     chans = cin // parts
     conv = conv_own_ref[...] + bias_ref[...].reshape(1, 1, -1)
     for r in conv_refs:
         conv = conv + r[...].astype(F32)
     conv_ref[...] = conv.astype(BF16)
+    copies[0].start()
     wide = []
     for k in range(parts):
         stats = small_ref[k]
         wide.append(jnp.concatenate([stats[2:3], lax.rsqrt(stats[3:4] / count + EPS), sums_ref[k] / count], 0))
     wide = expanded(jnp.concatenate(wide, 0), chans)
-    gx_all = [gx_own_ref[...]] + [r[...].astype(F32) for r in gx_refs]
+    picked = []
     for s in range(parts):
-        at = slice(s * chans, (s + 1) * chans)
         k = lax.rem(s - info_ref[ME] + parts, parts)
-        mean, inv, first, second = (shard_of([wide[4 * j + i : 4 * j + i + 1] for j in range(parts)], k)[None] for i in range(4))
-        xhat = (x_ref[:, :, at].astype(F32) - mean) * inv
-        grad_ref[:, :, at] = (inv * (shard_of(gx_all, k) - first - xhat * second)).astype(BF16)
-
-
-def call(kernel, name, outs, operands, scratch=(), in_hbm=(), limit=28, scalars=True, cost=None):
+        picked.append([shard_of([wide[4 * j + i : 4 * j + i + 1] for j in range(parts)], k)[None] for i in range(4)])
+    half = rows // 2
+    for r in range(2):
+        at_rows = slice(r * half, (r + 1) * half)
+        gx_all = [ref[at_rows].astype(F32) for ref in (gx_own_ref, *gx_refs)]
+        for s in range(parts):
+            at = slice(s * chans, (s + 1) * chans)
+            k = lax.rem(s - info_ref[ME] + parts, parts)
+            mean, inv, first, second = picked[s]
+            xhat = (x_ref[at_rows, :, at].astype(F32) - mean) * inv
+            grad_ref[at_rows, :, at] = (inv * (shard_of(gx_all, k) - first - xhat * second)).astype(BF16)
+        copies.append(pltpu.make_async_copy(grad_ref.at[at_rows], grad_out.at[at_rows], sems.at[1 + r]))
+        copies[-1].start()
+    for copy in copies:
+        copy.wait()
+
+
+def call(kernel, name, outs, operands, scratch=(), in_hbm=(), limit=28, scalars=True, cost=None, outs_in_hbm=False):
     spec = lambda i: pl.BlockSpec(memory_space=pltpu.HBM if i in in_hbm else pltpu.SMEM if scalars and i == 0 else pltpu.VMEM)
     return pl.pallas_call(
         kernel,
         out_shape=outs,
         in_specs=[spec(i) for i in range(len(operands))],
-        out_specs=[pl.BlockSpec(memory_space=pltpu.VMEM)] * len(outs),
+        out_specs=[pl.BlockSpec(memory_space=pl.ANY if outs_in_hbm else pltpu.VMEM)] * len(outs),
         scratch_shapes=scratch,
         compiler_params=pltpu.CompilerParams(vmem_limit_bytes=limit * 2**20),
         cost_estimate=cost,
@@ -360,20 +379,19 @@
     first = call(
         functools.partial(first_kernel, parts, groups),
         "first",
-        [sds((2 * cols + 8, chans), BF16)] * parts,
+        [sds((2 * (rows + cols) + 8, chans), BF16)] * parts,
         [info, x],
         cost=pl.CostEstimate(flops=10**10, bytes_accessed=1, transcendentals=0),
     )
     got = from_peers(first[1:])
-    columns = call(
-        functools.partial(columns_kernel, parts),
-        "columns",
-        [sds((2 * rows, chans), BF16)] * parts + [sds((rows, cols, chans), BF16)] * parts,
+    tiles = call(
+        functools.partial(tiles_kernel, parts),
+        "tiles",
+        [sds((rows, cols, chans), BF16)] * parts,
         [info, x, conv_weight],
     )
     zero = (0.0 * got[0][:1]).astype(BF16)
-    ends_w = [columns[0], *from_peers([v + zero for v in columns[1:parts]])]
-    x_tiles = [columns[parts], *from_peers([v + zero[None] for v in columns[parts + 1 :]])]
+    x_tiles = [tiles[0], *from_peers([v + zero[None] for v in tiles[1:]])]
     size = 2 * parts * groups
     pack_near, pack_across, stats = call(
         functools.partial(rows_kernel, parts),
@@ -389,11 +407,11 @@
 
     rounds_h, rounds_w = stats_rounds("ha"), stats_rounds("wa")
     near_h = exchange(pack_near, "ha", near)
-    cot_ends_w = call(
-        functools.partial(cot_columns_kernel, parts),
-        "cot_columns",
-        [sds((2 * rows, outs), BF16)] * parts,
-        [info, *cot_tiles, stats],
+    ends_w = call(
+        functools.partial(columns_kernel, parts),
+        "columns",
+        [sds((2 * rows, both), BF16)] * parts,
+        [info, first[0], *got, *cot_tiles, stats],
     )
     stats, n = merged(stats, unpacked(near_h, parts * cols, size), n), 2 * n
     if lax.axis_size("ha") == 4:
@@ -407,7 +425,7 @@
         functools.partial(pack_kernel, parts, rows, cols),
         "pack",
         [sds((-(-(used + 3) // 8) * 8, both), BF16), sds((used, both), BF16)],
-        [info, near_h, across_h, stats, *ends_w, *cot_ends_w],
+        [info, near_h, across_h, stats, *ends_w],
     )
     near_w = exchange(near_w, "wa", near)
     across_w = exchange(across_w, "wa", across, ends=False)
@@ -421,19 +439,20 @@
         functools.partial(backward_kernel, parts),
         "conv_backward",
         [sds((rows, parts, cols, chans), F32)],
-        [info, *cot_tiles, *strips, conv_weight],
+        [info, *cot_tiles, *strips, conv_weight, *x_tiles[1:]],
         [padded(outs), pltpu.VMEM((*shifted, outs), BF16)],
     )
-    *small, gx_own, gx_other, act = call(
+    *small, gx_own, gx_other, act, scales = call(
         functools.partial(terms_kernel, parts, count),
         "terms",
         [
             *[sds((4, groups), F32)] * parts,
             sds((rows, cols, chans), F32),
             sds((parts - 1, rows, cols, chans), BF16),
-            sds((rows + 2, parts, cols + 8, chans), F32),
+            sds((rows, parts, cols + 8, chans), F32),
+            sds((2 * parts + 2, chans), F32),
         ],
-        [info, *x_tiles, *strips, stats, norm_gain, norm_shift, grad_act],
+        [info, *x_tiles, stats, norm_gain, norm_shift, grad_act],
     )
 
     to_owners = lambda values: [lax.ppermute(v, "dp", [(j, i) for i, j in pairs]) for v, pairs in zip(values, peers)]
@@ -443,9 +462,8 @@
         functools.partial(forward_kernel, parts),
         "conv_forward",
         [sds((rows, cols, outs), F32), sds((parts - 1, rows, cols, outs), BF16)],
-        [act, conv_weight],
-        [pltpu.VMEM((*shifted, chans), BF16)],
-        scalars=False,
+        [info, act, scales, *strips, conv_weight],
+        [padded(chans), pltpu.VMEM((*shifted, chans), BF16)],
     )
     conv = to_owners([conv_other[k] for k in range(parts - 1)])
     sums = tied(small[:, :2], conv_own)
@@ -457,6 +475,8 @@
         "finish",
         [sds((rows, cols, outs), BF16), sds((rows, cols, cin), BF16)],
         [info, x, small, sums, conv_bias, gx_own, conv_own, *gx, *conv],
+        [pltpu.VMEM((rows, cols, outs), BF16), pltpu.VMEM((rows, cols, cin), BF16), pltpu.SemaphoreType.DMA((3,))],
+        outs_in_hbm=True,
     )
     return conv_out[None], grad[None]
 

time: 51.3 us -> 50.1 us (0.977)
  starting transfers between devices: 16.8 us -> 20.9 us
  waiting for transfers between devices: 16.5 us -> 13.1 us
  local copies, waits for them, and re-layouts: 2.53 us -> 1.08 us
    ppermute x9, starting transfers between devices: 9.96 us -> 14.3 us  [exchange(): return lax.ppermute(value, axis, pairs)]
    ppermute x9, waiting for transfers between devices: 12.1 us -> 8.82 us  [exchange(): return lax.ppermute(value, axis, pairs)]
    unnamed x14, local copies, waits for them, and re-layouts: 2.45 us -> 1 us
    ppermute x4 -> x3, starting transfers between devices: 4.29 us -> 3.83 us  [body(): lax.ppermute(v, 'dp', pairs)]
    ppermute x4 -> x3, waiting for transfers between devices: 4.16 us -> 4.29 us  [body(): lax.ppermute(v, 'dp', pairs)]
  transfers between devices with their start and end apart: 16 -> 15, of which waited for: 11 -> 8; matrix products, arithmetic and copies ran while one was open for 1% -> 1% of each run, Pallas kernels for 18% -> 18%
where the time goes in v5:
time: 50.1 us; the launch traced here: 49.9 us
  starting transfers between devices  20.9 us (42%)
  Pallas kernels  13.3 us (27%)
  waiting for transfers between devices  13.1 us (26%)
  local copies, waits for them, and re-layouts  1.08 us (2%)
  between operations  0.79 us (2%)
  other arithmetic  0.77 us (2%)
    ppermute x9, starting transfers between devices, exchange(): return lax.ppermute(value, axis, pairs)  14.3 us
    pallas_call x9, Pallas kernels, call(): pl.pallas_call(kernel, out_shape=outs, in_specs=[spec(i) for i in range(l...  13.3 us
    ppermute x9, waiting for transfers between devices, exchange(): return lax.ppermute(value, axis, pairs)  8.82 us
    ppermute x3, waiting for transfers between devices, body(): lax.ppermute(v, 'dp', pairs)  4.29 us
    ppermute x3, starting transfers between devices, body(): lax.ppermute(v, 'dp', pairs)  3.83 us
    ppermute x3, starting transfers between devices, body(): lax.ppermute(v, 'dp', [(j, i) for i, j in pairs])  2.71 us
  transfers between devices with their start and end apart: 15, of which 8 were waited for; matrix products, arithmetic and copies ran while one was open for 1% of the time, Pallas kernels for 18%

profile of v5, /device:TPU:0, one launch (start us, length us, event | category | flops | bytes accessed | tf_op | source)
XLA Modules:
  0.0 49.9 jit_solution(13139772518125181885)
XLA Ops:
  0.6 3.0 %collective-permute-start.2 = (bf16[16,8,640]{2,1,0:T(8,128)(2,1)}, bf16[16,8,640]{2,1,0:T(8,128)(2,1)S(1)}, u32[]{:S(2)}, u32[]{:S(2)}) collective-permute-start(bf16[16,8,640]{2,1,0:T(8,128)(2,1)} %bitcast.17), channel_id=1, source_target_pairs={{0,16},{16,0},{1,17},{17,1},{2,18},{18,2},{3,19},{19,3},{4,20},{20... | collective-permute-start | bytes 491528 | tf_op jit(solution)/shard_map/ppermute | solution.py:377
  3.7 0.1 stack.64.info_ref
  3.7 1.0 %copy-done.2 = bf16[1,16,8,1280]{3,2,1,0:T(8,128)(2,1)S(1)} copy-done((bf16[1,16,8,1280]{3,2,1,0:T(8,128)(2,1)S(1)}, bf16[1,16,8,1280]{3,2,1,0:T(8,128)(2,1)}, u32[]{:S(2)}) %copy-start.2) | copy-done | bytes 327704
  4.7 1.6 %first.1 = (bf16[56,640]{1,0:T(8,128)(2,1)S(1)}, bf16[56,640]{1,0:T(8,128)(2,1)S(1)}) custom-call(s32[7]{0:T(128)S(1)} %stack.64.info_ref, bf16[16,8,1280]{2,1,0:T(8,128)(2,1)S(1)} %bitcast.21), custom_call_target="tpu_custom_call" | custom-call | flops 10000000000 | bytes 1 | tf_op jit(solution)/shard_map/first/pallas_call | solution.py:333
  6.4 4.3 %collective-permute-done.refs_1_ = bf16[56,640]{1,0:T(8,128)(2,1)S(1)} collective-permute-done((bf16[56,640]{1,0:T(8,128)(2,1)S(1)}, bf16[56,640]{1,0:T(8,128)(2,1)S(1)}, u32[]{:S(2)}, u32[]{:S(2)}) %collective-permute-start) | collective-permute-done | bytes 71712 | tf_op jit(solution)/shard_map/ppermute | solution.py:377
  10.7 0.6 %rows.1 = (bf16[24,1280]{1,0:T(8,128)(2,1)S(1)}, bf16[16,1280]{1,0:T(8,128)(2,1)S(1)}, f32[1,64]{1,0:T(1,128)S(1)}) custom-call(s32[7]{0:T(128)S(1)} %stack.64.info_ref, bf16[56,640]{1,0:T(8,128)(2,1)S(1)} %get-tuple-element.26.refs_0_, bf16[56,640]{1,0:T(8,128)(2,1)S(1)} %collective-permute-done.refs_1_, bf16[16,8,640]{2,1,0:T(8,128)(2,1)S(1)} %bitcast.18, ...), custom_call_target="tpu_custom_call" | custom-call | tf_op jit(solution)/shard_map/rows/pallas_call | solution.py:333
  11.4 0.6 %tiles.1 = (bf16[16,8,640]{2,1,0:T(8,128)(2,1)S(1)}, bf16[16,8,640]{2,1,0:T(8,128)(2,1)S(1)}) custom-call(s32[7]{0:T(128)S(1)} %stack.64.info_ref, bf16[16,8,1280]{2,1,0:T(8,128)(2,1)S(1)} %bitcast.22, bf16[3,3,640,640]{3,2,1,0:T(8,128)(2,1)S(1)} %copy-done), custom_call_target="tpu_custom_call" | custom-call | tf_op jit(solution)/shard_map/tiles/pallas_call | solution.py:333
  12.1 0.6 %collective-permute-done.3.near_h.refs_2_ = bf16[24,1280]{1,0:T(8,128)(2,1)S(1)} collective-permute-done((bf16[24,1280]{1,0:T(8,128)(2,1)S(1)}, bf16[24,1280]{1,0:T(8,128)(2,1)S(1)}, u32[]{:S(2)}, u32[]{:S(2)}) %collective-permute-start.3) | collective-permute-done | bytes 61472 | tf_op jit(solution)/shard_map/ppermute | solution.py:23
  12.7 0.1 reduce-precision_convert_fusion.1
  12.8 1.3 %collective-permute-start.4 = (bf16[19,1280]{1,0:T(8,128)(2,1)S(1)}, bf16[19,1280]{1,0:T(8,128)(2,1)S(1)}, u32[]{:S(2)}, u32[]{:S(2)}) collective-permute-start(bf16[19,1280]{1,0:T(8,128)(2,1)S(1)} %pad_maximum_fusion), channel_id=1, source_target_pairs={{0,12},{4,8},{8,4},{12,0},{1,13},{5,9},{9,5},{13,1},{2,14},{6,10},... | collective-permute-start | bytes 145928 | tf_op jit(solution)/shard_map/ppermute | solution.py:23
  14.2 0.7 %columns.1 = (bf16[32,1280]{1,0:T(8,128)(2,1)S(1)}, bf16[32,1280]{1,0:T(8,128)(2,1)S(1)}) custom-call(s32[7]{0:T(128)S(1)} %stack.64.info_ref, bf16[56,640]{1,0:T(8,128)(2,1)S(1)} %get-tuple-element.26.refs_0_, bf16[56,640]{1,0:T(8,128)(2,1)S(1)} %collective-permute-done.refs_1_, bf16[16,8,640]{2,1,0:T(8,128)(2,1)S(1)} %bitcast.19, ...), custom_call_target="tpu_custom_call" | custom-call | tf_op jit(solution)/shard_map/columns/pallas_call | solution.py:333
  14.9 1.9 %collective-permute-done.4.across_h.refs_3_ = bf16[19,1280]{1,0:T(8,128)(2,1)S(1)} collective-permute-done((bf16[19,1280]{1,0:T(8,128)(2,1)S(1)}, bf16[19,1280]{1,0:T(8,128)(2,1)S(1)}, u32[]{:S(2)}, u32[]{:S(2)}) %collective-permute-start.4) | collective-permute-done | bytes 48672 | tf_op jit(solution)/shard_map/ppermute | solution.py:23
  17.0 0.6 %pack.1 = (bf16[40,1280]{1,0:T(8,128)(2,1)S(1)}, bf16[36,1280]{1,0:T(8,128)(2,1)S(1)}) custom-call(s32[7]{0:T(128)S(1)} %stack.64.info_ref, bf16[24,1280]{1,0:T(8,128)(2,1)S(1)} %collective-permute-done.3.near_h.refs_2_, bf16[19,1280]{1,0:T(8,128)(2,1)S(1)} %collective-permute-done.4.across_h.refs_3_, f32[1,64]{1,0:T(1,128)S(1)} %pad_maximum_fusion.3.stats_ref, ...), custom_call_target="tpu_custom_call" | custom-call | tf_op jit(solution)/shard_map/pack/pallas_call | solution.py:333
  17.7 1.6 %collective-permute-start.5 = (bf16[40,1280]{1,0:T(8,128)(2,1)S(1)}, bf16[40,1280]{1,0:T(8,128)(2,1)S(1)}, u32[]{:S(2)}, u32[]{:S(2)}) collective-permute-start(bf16[40,1280]{1,0:T(8,128)(2,1)S(1)} %get-tuple-element.32), channel_id=1, source_target_pairs={{0,1},{1,0},{2,3},{3,2},{4,5},{5,4},{6,7},{7,6},{8,9},{9,8},{10,11... | collective-permute-start | bytes 307208 | tf_op jit(solution)/shard_map/ppermute | solution.py:23
  19.3 0.7 %collective-permute-start.1 = (bf16[16,8,640]{2,1,0:T(8,128)(2,1)S(1)}, bf16[16,8,640]{2,1,0:T(8,128)(2,1)S(1)}, u32[]{:S(2)}, u32[]{:S(2)}) collective-permute-start(bf16[16,8,640]{2,1,0:T(8,128)(2,1)S(1)} %broadcast_add_fusion), channel_id=1, source_target_pairs={{0,16},{16,0},{1,17},{17,1},{2,18},{18,2},{3,19},{19,3},{4,20},{20... | collective-permute-start | bytes 491528 | tf_op jit(solution)/shard_map/ppermute | solution.py:377
  20.0 0.7 %collective-permute-start.7 = (bf16[36,1280]{1,0:T(8,128)(2,1)S(1)}, bf16[36,1280]{1,0:T(8,128)(2,1)S(1)}, u32[]{:S(2)}, u32[]{:S(2)}) collective-permute-start(bf16[36,1280]{1,0:T(8,128)(2,1)S(1)} %get-tuple-element.33), channel_id=1, source_target_pairs={{1,2},{2,1},{5,6},{6,5},{9,10},{10,9},{13,14},{14,13},{17,18},{18,... | collective-permute-start | bytes 276488 | tf_op jit(solution)/shard_map/ppermute | solution.py:23
  20.7 2.0 %collective-permute-done.5.refs_4_.near_w = bf16[40,1280]{1,0:T(8,128)(2,1)S(1)} collective-permute-done((bf16[40,1280]{1,0:T(8,128)(2,1)S(1)}, bf16[40,1280]{1,0:T(8,128)(2,1)S(1)}, u32[]{:S(2)}, u32[]{:S(2)}) %collective-permute-start.5) | collective-permute-done | bytes 102432 | tf_op jit(solution)/shard_map/ppermute | solution.py:23
  22.8 2.6 %collective-permute-start.6 = (f32[1,64]{1,0:T(1,128)S(1)}, f32[1,64]{1,0:T(1,128)S(1)}, u32[]{:S(2)}, u32[]{:S(2)}) collective-permute-start(f32[1,64]{1,0:T(1,128)S(1)} %pad_maximum_fusion.4), channel_id=1, source_target_pairs={{0,2},{1,3},{2,0},{3,1},{4,6},{5,7},{6,4},{7,5},{8,10},{9,11},{10,... | collective-permute-start | bytes 776 | tf_op jit(solution)/shard_map/ppermute | solution.py:23
  25.4 3.0 %conv_backward.1.refs_5_ = f32[16,2,8,640]{3,2,1,0:T(8,128)S(1)} custom-call(s32[7]{0:T(128)S(1)} %stack.64.info_ref, bf16[16,8,640]{2,1,0:T(8,128)(2,1)S(1)} %bitcast.20, bf16[16,8,640]{2,1,0:T(8,128)(2,1)S(1)} %collective-permute-done.2.refs_3_.refs_1_, bf16[24,1280]{1,0:T(8,128)(2,1)S(1)} %collective-permute-done.3.near_h.refs_2_, ...), custom_call_target="tpu_custom_call" | custom-call | tf_op jit(solution)/shard_map/conv_backward/pallas_call | solution.py:333
  28.5 0.1 pad_maximum_fusion.5.refs_2_
  28.6 1.4 %terms.1 = (f32[4,16]{1,0:T(4,128)S(1)}, f32[4,16]{1,0:T(4,128)S(1)}, f32[16,8,640]{2,1,0:T(8,128)S(1)}, bf16[1,16,8,640]{3,2,1,0:T(8,128)(2,1)S(1)}, f32[16,2,1...) custom-call(s32[7]{0:T(128)S(1)} %stack.64.info_ref, bf16[16,8,640]{2,1,0:T(8,128)(2,1)S(1)} %get-tuple-element.23.refs_0_, ...), custom_call_target="tpu_custom_call" | custom-call | tf_op jit(solution)/shard_map/terms/pallas_call | solution.py:333
  30.0 0.7 %collective-permute-start.8 = (f32[4,16]{1,0:T(4,128)S(1)}, f32[4,16]{1,0:T(4,128)S(1)}, u32[]{:S(2)}, u32[]{:S(2)}) collective-permute-start(f32[4,16]{1,0:T(4,128)S(1)} %get-tuple-element.35), channel_id=1, source_target_pairs={{16,0},{0,16},{17,1},{1,17},{18,2},{2,18},{19,3},{3,19},{20,4},{4,... | collective-permute-start | bytes 776 | tf_op jit(solution)/shard_map/ppermute | solution.py:458
  30.7 3.1 %conv_forward.1 = (f32[16,8,640]{2,1,0:T(8,128)S(1)}, bf16[1,16,8,640]{3,2,1,0:T(8,128)(2,1)S(1)}) custom-call(s32[7]{0:T(128)S(1)} %stack.64.info_ref, f32[16,2,16,640]{3,2,1,0:T(8,128)S(1)} %get-tuple-element.36.given_ref, f32[6,640]{1,0:T(8,128)S(1)} %get-tuple-element.37.scales_ref, bf16[24,1280]{1,0:T(8,128)(2,1)S(1)} %collective-permute-done.3.near_h.refs_2_, ...), custom_call_target="tpu_custom_call" | custom-call | tf_op jit(solution)/shard_map/conv_forward/pallas_call | solution.py:333
  33.9 1.1 %collective-permute-done.9 = f32[2,2,16]{2,1,0:T(2,128)S(1)} collective-permute-done((f32[2,2,16]{2,1,0:T(2,128)S(1)}, f32[2,2,16]{2,1,0:T(2,128)S(1)}, u32[]{:S(2)}, u32[]{:S(2)}) %collective-permute-start.9) | collective-permute-done | bytes 288 | tf_op jit(solution)/shard_map/ppermute | solution.py:23
  35.0 1.5 %collective-permute-start.10 = (f32[2,2,16]{2,1,0:T(2,128)S(1)}, f32[2,2,16]{2,1,0:T(2,128)S(1)}, u32[]{:S(2)}, u32[]{:S(2)}) collective-permute-start(f32[2,2,16]{2,1,0:T(2,128)S(1)} %fusion.14), channel_id=1, source_target_pairs={{0,8},{4,12},{8,0},{12,4},{1,9},{5,13},{9,1},{13,5},{2,10},{6,14},... | collective-permute-start | bytes 776 | tf_op jit(solution)/shard_map/ppermute | solution.py:23
  36.5 1.3 %collective-permute-start.14 = (bf16[16,8,640]{2,1,0:T(8,128)(2,1)S(1)}, bf16[16,8,640]{2,1,0:T(8,128)(2,1)S(1)}, u32[]{:S(2)}, u32[]{:S(2)}) collective-permute-start(bf16[16,8,640]{2,1,0:T(8,128)(2,1)S(1)} %bitcast.29), channel_id=1, source_target_pairs={{16,0},{0,16},{17,1},{1,17},{18,2},{2,18},{19,3},{3,19},{20,4},{4,... | collective-permute-start | bytes 491528 | tf_op jit(solution)/shard_map/ppermute | solution.py:458
  37.9 0.7 %collective-permute-start.13 = (bf16[16,8,640]{2,1,0:T(8,128)(2,1)S(1)}, bf16[16,8,640]{2,1,0:T(8,128)(2,1)S(1)}, u32[]{:S(2)}, u32[]{:S(2)}) collective-permute-start(bf16[16,8,640]{2,1,0:T(8,128)(2,1)S(1)} %bitcast.28), channel_id=1, source_target_pairs={{16,0},{0,16},{17,1},{1,17},{18,2},{2,18},{19,3},{3,19},{20,4},{4,... | collective-permute-start | bytes 491528 | tf_op jit(solution)/shard_map/ppermute | solution.py:458
  38.6 3.0 %collective-permute-start.11 = (f32[2,2,16]{2,1,0:T(2,128)S(1)}, f32[2,2,16]{2,1,0:T(2,128)S(1)}, u32[]{:S(2)}, u32[]{:S(2)}) collective-permute-start(f32[2,2,16]{2,1,0:T(2,128)S(1)} %fusion.15), channel_id=1, source_target_pairs={{0,1},{1,0},{2,3},{3,2},{4,5},{5,4},{6,7},{7,6},{8,9},{9,8},{10,11... | collective-permute-start | bytes 776 | tf_op jit(solution)/shard_map/ppermute | solution.py:23
  41.7 1.6 %collective-permute-done.11 = f32[2,2,16]{2,1,0:T(2,128)S(1)} collective-permute-done((f32[2,2,16]{2,1,0:T(2,128)S(1)}, f32[2,2,16]{2,1,0:T(2,128)S(1)}, u32[]{:S(2)}, u32[]{:S(2)}) %collective-permute-start.11) | collective-permute-done | bytes 288 | tf_op jit(solution)/shard_map/ppermute | solution.py:23
  43.2 3.5 %collective-permute-start.12 = (f32[2,2,16]{2,1,0:T(2,128)S(1)}, f32[2,2,16]{2,1,0:T(2,128)S(1)}, u32[]{:S(2)}, u32[]{:S(2)}) collective-permute-start(f32[2,2,16]{2,1,0:T(2,128)S(1)} %add.123), channel_id=1, source_target_pairs={{0,2},{1,3},{2,0},{3,1},{4,6},{5,7},{6,4},{7,5},{8,10},{9,11},{10,... | collective-permute-start | bytes 776 | tf_op jit(solution)/shard_map/ppermute | solution.py:23
  46.7 1.6 %collective-permute-done.12 = f32[2,2,16]{2,1,0:T(2,128)S(1)} collective-permute-done((f32[2,2,16]{2,1,0:T(2,128)S(1)}, f32[2,2,16]{2,1,0:T(2,128)S(1)}, u32[]{:S(2)}, u32[]{:S(2)}) %collective-permute-start.12) | collective-permute-done | bytes 288 | tf_op jit(solution)/shard_map/ppermute | solution.py:23
  48.3 1.6 %finish.1 = (bf16[16,8,640]{2,1,0:T(8,128)(2,1)}, bf16[16,8,1280]{2,1,0:T(8,128)(2,1)}) custom-call(s32[7]{0:T(128)S(1)} %stack.64.info_ref, bf16[16,8,1280]{2,1,0:T(8,128)(2,1)S(1)} %bitcast.23, f32[2,4,16]{2,1,0:T(4,128)S(1)} %pad_maximum_fusion.1.small_ref, f32[2,2,16]{2,1,0:T(2,128)S(1)} %add.124.sums_ref, f32[640]{0:T(1024)S(1)} %copy-done.6, ...), custom_call_target="tpu_custom_call" | custom-call | tf_op jit(solution)/shard_map/finish/pallas_call | solution.py:333
  (48 shorter events, 0.9 us)
Async XLA Ops:
  0.6 10.1 %collective-permute-start.2 = (bf16[16,8,640]{2,1,0:T(8,128)(2,1)}, bf16[16,8,640]{2,1,0:T(8,128)(2,1)S(1)}, u32[]{:S(2)}, u32[]{:S(2)}) collective-permute-start(bf16[16,8,640]{2,1,0:T(8,128)(2,1)} %bitcast.17), channel_id=1, source_target_pairs={{0,16},{16,0},{1,17},{17,1},{2,18},{18,2},{3,19},{19,3},{4,20},{20... | collective-permute-start | bytes 491528 | tf_op jit(solution)/shard_map/ppermute | solution.py:377
  3.7 1.0 %copy-start.2 = (bf16[1,16,8,1280]{3,2,1,0:T(8,128)(2,1)S(1)}, bf16[1,16,8,1280]{3,2,1,0:T(8,128)(2,1)}, u32[]{:S(2)}) copy-start(bf16[1,16,8,1280]{3,2,1,0:T(8,128)(2,1)} %param.6) | copy-start | bytes 983044
  4.7 6.0 %copy-start.1 = (bf16[1,16,8,640]{3,2,1,0:T(8,128)(2,1)S(1)}, bf16[1,16,8,640]{3,2,1,0:T(8,128)(2,1)}, u32[]{:S(2)}) copy-start(bf16[1,16,8,640]{3,2,1,0:T(8,128)(2,1)} %param.11) | copy-start | bytes 491524
  4.7 6.7 %copy-start = (bf16[3,3,640,640]{3,2,1,0:T(8,128)(2,1)S(1)}, bf16[3,3,640,640]{3,2,1,0:T(8,128)(2,1)}, u32[]{:S(2)}) copy-start(bf16[3,3,640,640]{3,2,1,0:T(8,128)(2,1)} %w_ref.3) | copy-start | bytes 22118404
  4.7 6.7 %copy-start.3 = (bf16[1,16,8,1280]{3,2,1,0:T(8,128)(2,1)S(1)}, bf16[1,16,8,1280]{3,2,1,0:T(8,128)(2,1)}, u32[]{:S(2)}) copy-start(bf16[1,16,8,1280]{3,2,1,0:T(8,128)(2,1)} %param.6) | copy-start | bytes 983044
  6.3 4.4 %collective-permute-start = (bf16[56,640]{1,0:T(8,128)(2,1)S(1)}, bf16[56,640]{1,0:T(8,128)(2,1)S(1)}, u32[]{:S(2)}, u32[]{:S(2)}) collective-permute-start(bf16[56,640]{1,0:T(8,128)(2,1)S(1)} %get-tuple-element.25), channel_id=1, source_target_pairs={{0,16},{16,0},{1,17},{17,1},{2,18},{18,2},{3,19},{19,3},{4,20},{20... | collective-permute-start | bytes 215048 | tf_op jit(solution)/shard_map/ppermute | solution.py:377
  11.3 17.3 %copy-start.4 = (f32[1280]{0:T(1024)S(1)}, f32[1280]{0:T(1024)}, u32[]{:S(2)}) copy-start(f32[1280]{0:T(1024)} %refs_3_.1) | copy-start | bytes 15364
  11.3 17.3 %copy-start.5 = (f32[1280]{0:T(1024)S(1)}, f32[1280]{0:T(1024)}, u32[]{:S(2)}) copy-start(f32[1280]{0:T(1024)} %refs_4_.1) | copy-start | bytes 15364
  11.3 1.3 %collective-permute-start.3 = (bf16[24,1280]{1,0:T(8,128)(2,1)S(1)}, bf16[24,1280]{1,0:T(8,128)(2,1)S(1)}, u32[]{:S(2)}, u32[]{:S(2)}) collective-permute-start(bf16[24,1280]{1,0:T(8,128)(2,1)S(1)} %get-tuple-element.28), channel_id=1, source_target_pairs={{0,4},{4,0},{8,12},{12,8},{1,5},{5,1},{9,13},{13,9},{2,6},{6,2},{1... | collective-permute-start | bytes 184328 | tf_op jit(solution)/shard_map/ppermute | solution.py:23
  12.8 4.0 %collective-permute-start.4 = (bf16[19,1280]{1,0:T(8,128)(2,1)S(1)}, bf16[19,1280]{1,0:T(8,128)(2,1)S(1)}, u32[]{:S(2)}, u32[]{:S(2)}) collective-permute-start(bf16[19,1280]{1,0:T(8,128)(2,1)S(1)} %pad_maximum_fusion), channel_id=1, source_target_pairs={{0,12},{4,8},{8,4},{12,0},{1,13},{5,9},{9,5},{13,1},{2,14},{6,10},... | collective-permute-start | bytes 145928 | tf_op jit(solution)/shard_map/ppermute | solution.py:23
  17.7 5.0 %collective-permute-start.5 = (bf16[40,1280]{1,0:T(8,128)(2,1)S(1)}, bf16[40,1280]{1,0:T(8,128)(2,1)S(1)}, u32[]{:S(2)}, u32[]{:S(2)}) collective-permute-start(bf16[40,1280]{1,0:T(8,128)(2,1)S(1)} %get-tuple-element.32), channel_id=1, source_target_pairs={{0,1},{1,0},{2,3},{3,2},{4,5},{5,4},{6,7},{7,6},{8,9},{9,8},{10,11... | collective-permute-start | bytes 307208 | tf_op jit(solution)/shard_map/ppermute | solution.py:23
  19.3 6.1 %collective-permute-start.1 = (bf16[16,8,640]{2,1,0:T(8,128)(2,1)S(1)}, bf16[16,8,640]{2,1,0:T(8,128)(2,1)S(1)}, u32[]{:S(2)}, u32[]{:S(2)}) collective-permute-start(bf16[16,8,640]{2,1,0:T(8,128)(2,1)S(1)} %broadcast_add_fusion), channel_id=1, source_target_pairs={{0,16},{16,0},{1,17},{17,1},{2,18},{18,2},{3,19},{19,3},{4,20},{20... | collective-permute-start | bytes 491528 | tf_op jit(solution)/shard_map/ppermute | solution.py:377
  20.0 5.4 %collective-permute-start.7 = (bf16[36,1280]{1,0:T(8,128)(2,1)S(1)}, bf16[36,1280]{1,0:T(8,128)(2,1)S(1)}, u32[]{:S(2)}, u32[]{:S(2)}) collective-permute-start(bf16[36,1280]{1,0:T(8,128)(2,1)S(1)} %get-tuple-element.33), channel_id=1, source_target_pairs={{1,2},{2,1},{5,6},{6,5},{9,10},{10,9},{13,14},{14,13},{17,18},{18,... | collective-permute-start | bytes 276488 | tf_op jit(solution)/shard_map/ppermute | solution.py:23
  22.8 25.4 %copy-start.6 = (f32[640]{0:T(1024)S(1)}, f32[640]{0:T(1024)}, u32[]{:S(2)}) copy-start(f32[640]{0:T(1024)} %bias_ref.1) | copy-start | bytes 7684
  22.8 5.6 %collective-permute-start.6 = (f32[1,64]{1,0:T(1,128)S(1)}, f32[1,64]{1,0:T(1,128)S(1)}, u32[]{:S(2)}, u32[]{:S(2)}) collective-permute-start(f32[1,64]{1,0:T(1,128)S(1)} %pad_maximum_fusion.4), channel_id=1, source_target_pairs={{0,2},{1,3},{2,0},{3,1},{4,6},{5,7},{6,4},{7,5},{8,10},{9,11},{10,... | collective-permute-start | bytes 776 | tf_op jit(solution)/shard_map/ppermute | solution.py:23
  30.0 3.8 %collective-permute-start.8 = (f32[4,16]{1,0:T(4,128)S(1)}, f32[4,16]{1,0:T(4,128)S(1)}, u32[]{:S(2)}, u32[]{:S(2)}) collective-permute-start(f32[4,16]{1,0:T(4,128)S(1)} %get-tuple-element.35), channel_id=1, source_target_pairs={{16,0},{0,16},{17,1},{1,17},{18,2},{2,18},{19,3},{3,19},{20,4},{4,... | collective-permute-start | bytes 776 | tf_op jit(solution)/shard_map/ppermute | solution.py:458
  33.8 1.2 %collective-permute-start.9 = (f32[2,2,16]{2,1,0:T(2,128)S(1)}, f32[2,2,16]{2,1,0:T(2,128)S(1)}, u32[]{:S(2)}, u32[]{:S(2)}) collective-permute-start(f32[2,2,16]{2,1,0:T(2,128)S(1)} %fusion.7), channel_id=1, source_target_pairs={{0,4},{4,0},{8,12},{12,8},{1,5},{5,1},{9,13},{13,9},{2,6},{6,2},{1... | collective-permute-start | bytes 776 | tf_op jit(solution)/shard_map/ppermute | solution.py:23
  35.0 3.6 %collective-permute-start.10 = (f32[2,2,16]{2,1,0:T(2,128)S(1)}, f32[2,2,16]{2,1,0:T(2,128)S(1)}, u32[]{:S(2)}, u32[]{:S(2)}) collective-permute-start(f32[2,2,16]{2,1,0:T(2,128)S(1)} %fusion.14), channel_id=1, source_target_pairs={{0,8},{4,12},{8,0},{12,4},{1,9},{5,13},{9,1},{13,5},{2,10},{6,14},... | collective-permute-start | bytes 776 | tf_op jit(solution)/shard_map/ppermute | solution.py:23
  36.5 11.7 %collective-permute-start.14 = (bf16[16,8,640]{2,1,0:T(8,128)(2,1)S(1)}, bf16[16,8,640]{2,1,0:T(8,128)(2,1)S(1)}, u32[]{:S(2)}, u32[]{:S(2)}) collective-permute-start(bf16[16,8,640]{2,1,0:T(8,128)(2,1)S(1)} %bitcast.29), channel_id=1, source_target_pairs={{16,0},{0,16},{17,1},{1,17},{18,2},{2,18},{19,3},{3,19},{20,4},{4,... | collective-permute-start | bytes 491528 | tf_op jit(solution)/shard_map/ppermute | solution.py:458
  37.9 10.4 %collective-permute-start.13 = (bf16[16,8,640]{2,1,0:T(8,128)(2,1)S(1)}, bf16[16,8,640]{2,1,0:T(8,128)(2,1)S(1)}, u32[]{:S(2)}, u32[]{:S(2)}) collective-permute-start(bf16[16,8,640]{2,1,0:T(8,128)(2,1)S(1)} %bitcast.28), channel_id=1, source_target_pairs={{16,0},{0,16},{17,1},{1,17},{18,2},{2,18},{19,3},{3,19},{20,4},{4,... | collective-permute-start | bytes 491528 | tf_op jit(solution)/shard_map/ppermute | solution.py:458
  38.6 4.6 %collective-permute-start.11 = (f32[2,2,16]{2,1,0:T(2,128)S(1)}, f32[2,2,16]{2,1,0:T(2,128)S(1)}, u32[]{:S(2)}, u32[]{:S(2)}) collective-permute-start(f32[2,2,16]{2,1,0:T(2,128)S(1)} %fusion.15), channel_id=1, source_target_pairs={{0,1},{1,0},{2,3},{3,2},{4,5},{5,4},{6,7},{7,6},{8,9},{9,8},{10,11... | collective-permute-start | bytes 776 | tf_op jit(solution)/shard_map/ppermute | solution.py:23
  43.2 5.0 %collective-permute-start.12 = (f32[2,2,16]{2,1,0:T(2,128)S(1)}, f32[2,2,16]{2,1,0:T(2,128)S(1)}, u32[]{:S(2)}, u32[]{:S(2)}) collective-permute-start(f32[2,2,16]{2,1,0:T(2,128)S(1)} %add.123), channel_id=1, source_target_pairs={{0,2},{1,3},{2,0},{3,1},{4,6},{5,7},{6,4},{7,5},{8,10},{9,11},{10,... | collective-permute-start | bytes 776 | tf_op jit(solution)/shard_map/ppermute | solution.py:23

commit v6 on v5

--- a/solution.py
+++ b/solution.py
@@ -258,7 +258,7 @@
         ref[...] = jnp.concatenate([v[k : k + 1] for v in (sums[:parts], sums[parts:], stats[:parts], stats[parts:])], 0)
 
 
-def forward_kernel(parts, info_ref, given_ref, scales_ref, near_h, across_h, near_w, across_w, w_ref, conv_own_ref, conv_other_ref, padded_ref, windows_ref):
+def forward_kernel(parts, info_ref, given_ref, scales_ref, near_h, across_h, near_w, across_w, w_ref, conv_own_ref, conv_other_ref, windows_ref, padded_ref):
     rows, cols, outs = conv_own_ref.shape
     chans = windows_ref.shape[3]
     strips = halos(parts, rows, cols, info_ref, near_h, across_h, near_w, across_w, slice(0, chans))
@@ -281,9 +281,19 @@
             padded_ref[1 : rows + 1, k, at, :] = act_of(mid, side)
             padded_ref[rows + 1, k, at : at + 1, :] = act_of(bottom, side & down)
     windows(padded_ref, windows_ref, parts, cols)
+    convolved(parts, windows_ref, w_ref, slice(0, outs), conv_own_ref, conv_other_ref)
+
+
+def second_forward_kernel(parts, start, windows_ref, w_ref, after_ref, conv_own_ref, conv_other_ref):
+    convolved(parts, windows_ref, w_ref, slice(start, w_ref.shape[3]), conv_own_ref, conv_other_ref)
+
+
+def convolved(parts, windows_ref, w_ref, lanes, conv_own_ref, conv_other_ref):
+    rows, cols, outs = conv_own_ref.shape
+    chans = windows_ref.shape[3]
     taps = [(ky, kx) for ky in range(3) for kx in range(3)]
     shifted = jnp.concatenate([windows_ref[kx, ky : ky + rows].reshape(rows * parts * cols, chans) for ky, kx in taps], 1)
-    weight = w_ref[...].reshape(9 * chans, outs)
+    weight = w_ref[:, :, :, lanes].reshape(9 * chans, outs)
     total = lax.dot_general(weight, shifted, (((0,), (1,)), ((), ())), preferred_element_type=F32).T
     total = total.reshape(rows, parts, cols, outs)
     conv_own_ref[...] = total[:, 0]
@@ -291,17 +301,19 @@
         conv_other_ref[k - 1] = total[:, k].astype(BF16)
 
 
-def finish_kernel(parts, count, info_ref, x_ref, small_ref, sums_ref, bias_ref, gx_own_ref, conv_own_ref, *refs):
-    gx_refs, conv_refs = refs[: parts - 1], refs[parts - 1 : 2 * parts - 2]
-    conv_out, grad_out, conv_ref, grad_ref, sems = refs[2 * parts - 2 :]
+def finish_kernel(parts, count, info_ref, x_ref, small_ref, sums_ref, bias_ref, gx_own_ref, *refs):
+    gx_refs, conv_refs = refs[: parts - 1], refs[parts - 1 : 3 * parts - 1]
+    conv_out, grad_out, conv_ref, grad_ref, sems = refs[3 * parts - 1 :]
     rows = x_ref.shape[0]
     copies = [pltpu.make_async_copy(conv_ref, conv_out, sems.at[0])]
     cin = x_ref.shape[2]
     chans = cin // parts
-    conv = conv_own_ref[...] + bias_ref[...].reshape(1, 1, -1)
-    for r in conv_refs:
-        conv = conv + r[...].astype(F32)
-    conv_ref[...] = conv.astype(BF16)
+    start = 0
+    for i in range(2):
+        conv = sum(r[...].astype(F32) for r in conv_refs[i::2])
+        stop = start + conv.shape[2]
+        conv_ref[:, :, start:stop] = (conv + bias_ref[start:stop].reshape(1, 1, -1)).astype(BF16)
+        start = stop
     copies[0].start()
     wide = []
     for k in range(parts):
@@ -458,23 +470,38 @@
     to_owners = lambda values: [lax.ppermute(v, "dp", [(j, i) for i, j in pairs]) for v, pairs in zip(values, peers)]
     small = jnp.stack([small[0], *to_owners(small[1:])], 0)
     gx = to_owners([gx_other[k] for k in range(parts - 1)])
-    conv_own, conv_other = call(
+    start = outs * 3 // 5 // 128 * 128
+    parts_of = lambda size: [sds((rows, cols, size), F32), sds((parts - 1, rows, cols, size), BF16)]
+    conv_own, conv_other, act_windows = call(
         functools.partial(forward_kernel, parts),
         "conv_forward",
-        [sds((rows, cols, outs), F32), sds((parts - 1, rows, cols, outs), BF16)],
+        [*parts_of(start), sds((*shifted, chans), BF16)],
         [info, act, scales, *strips, conv_weight],
-        [padded(chans), pltpu.VMEM((*shifted, chans), BF16)],
-    )
-    conv = to_owners([conv_other[k] for k in range(parts - 1)])
+        [padded(chans)],
+    )
     sums = tied(small[:, :2], conv_own)
-    for axis, pairings in (("ha", rounds_h), ("wa", rounds_w)):
-        for partner in pairings:
-            sums = sums + exchange(sums, axis, partner)
+    sums = sums + exchange(sums, "ha", rounds_h[0])
+    conv_own2, conv_other2 = call(
+        functools.partial(second_forward_kernel, parts, start),
+        "conv_forward2",
+        parts_of(outs - start),
+        [act_windows, conv_weight, sums],
+        scalars=False,
+    )
+    conv = [conv_own, conv_own2]
+    for k in range(parts - 1):
+        back = [(j, i) for i, j in peers[k]]
+        conv += [lax.ppermute(v[k], "dp", back) for v in (conv_other, conv_other2)]
+    for partner in rounds_h[1:]:
+        sums = sums + exchange(sums, "ha", partner)
+    sums = tied(sums, conv_own2)
+    for partner in rounds_w:
+        sums = sums + exchange(sums, "wa", partner)
     conv_out, grad = call(
         functools.partial(finish_kernel, parts, count),
         "finish",
         [sds((rows, cols, outs), BF16), sds((rows, cols, cin), BF16)],
-        [info, x, small, sums, conv_bias, gx_own, conv_own, *gx, *conv],
+        [info, x, small, sums, conv_bias, gx_own, *gx, *conv],
         [pltpu.VMEM((rows, cols, outs), BF16), pltpu.VMEM((rows, cols, cin), BF16), pltpu.SemaphoreType.DMA((3,))],
         outs_in_hbm=True,
     )

time: 50.1 us -> 49.5 us (0.988)
  waiting for transfers between devices: 13.1 us -> 12.3 us
    ppermute x0 -> x2, starting transfers between devices: none -> 2.03 us  [body(): conv += [lax.ppermute(v[k], 'dp', back) for v in (conv_other, conv_other2)]]
    ppermute x9, waiting for transfers between devices: 8.82 us -> 7.4 us  [exchange(): return lax.ppermute(value, axis, pairs)]
    ppermute x3 -> x2, starting transfers between devices: 2.71 us -> 1.57 us  [body(): lax.ppermute(v, 'dp', [(j, i) for i, j in pairs])]
    ppermute x9, starting transfers between devices: 14.3 us -> 13.4 us  [exchange(): return lax.ppermute(value, axis, pairs)]
    ppermute x3 -> x2, waiting for transfers between devices: 0.01 us -> 0.61 us  [body(): lax.ppermute(v, 'dp', [(j, i) for i, j in pairs])]
    pallas_call x9 -> x10, Pallas kernels: 13.3 us -> 13.6 us  [call(): pl.pallas_call(kernel, out_shape=outs, in_specs=[spec(i) for i in range(l...]
    unnamed x14 -> x16, local copies, waits for them, and re-layouts: 1 us -> 1.15 us
  transfers between devices with their start and end apart: 15 -> 16, of which waited for: 8 -> 8; matrix products, arithmetic and copies ran while one was open for 1% -> 1% of each run, Pallas kernels for 18% -> 19%
where the time goes in v6:
time: 49.5 us; the launch traced here: 49.3 us
  starting transfers between devices  20.6 us (42%)
  Pallas kernels  13.6 us (27%)
  waiting for transfers between devices  12.3 us (25%)
  local copies, waits for them, and re-layouts  1.23 us (2%)
  between operations  0.81 us (2%)
  other arithmetic  0.77 us (2%)
    pallas_call x10, Pallas kernels, call(): pl.pallas_call(kernel, out_shape=outs, in_specs=[spec(i) for i in range(l...  13.6 us
    ppermute x9, starting transfers between devices, exchange(): return lax.ppermute(value, axis, pairs)  13.4 us
    ppermute x9, waiting for transfers between devices, exchange(): return lax.ppermute(value, axis, pairs)  7.4 us
    ppermute x3, waiting for transfers between devices, body(): lax.ppermute(v, 'dp', pairs)  4.29 us
    ppermute x3, starting transfers between devices, body(): lax.ppermute(v, 'dp', pairs)  3.67 us
    ppermute x2, starting transfers between devices, body(): conv += [lax.ppermute(v[k], 'dp', back) for v in (conv_other, conv_other2)]  2.03 us
    ppermute x2, starting transfers between devices, body(): lax.ppermute(v, 'dp', [(j, i) for i, j in pairs])  1.57 us
    unnamed x16, local copies, waits for them, and re-layouts  1.15 us
  transfers between devices with their start and end apart: 16, of which 8 were waited for; matrix products, arithmetic and copies ran while one was open for 1% of the time, Pallas kernels for 19%

profile of v6, /device:TPU:0, one launch (start us, length us, event | category | flops | bytes accessed | tf_op | source)
XLA Modules:
  0.0 49.3 jit_solution(18052800135329556656)
XLA Ops:
  0.6 3.0 %collective-permute-start.2 = (bf16[16,8,640]{2,1,0:T(8,128)(2,1)}, bf16[16,8,640]{2,1,0:T(8,128)(2,1)S(1)}, u32[]{:S(2)}, u32[]{:S(2)}) collective-permute-start(bf16[16,8,640]{2,1,0:T(8,128)(2,1)} %bitcast.22), channel_id=1, source_target_pairs={{0,16},{16,0},{1,17},{17,1},{2,18},{18,2},{3,19},{19,3},{4,20},{20... | collective-permute-start | bytes 491528 | tf_op jit(solution)/shard_map/ppermute | solution.py:389
  3.8 1.1 %copy-done.1 = bf16[1,16,8,1280]{3,2,1,0:T(8,128)(2,1)S(1)} copy-done((bf16[1,16,8,1280]{3,2,1,0:T(8,128)(2,1)S(1)}, bf16[1,16,8,1280]{3,2,1,0:T(8,128)(2,1)}, u32[]{:S(2)}) %copy-start.1) | copy-done | bytes 327704
  4.9 1.6 %first.1 = (bf16[56,640]{1,0:T(8,128)(2,1)S(1)}, bf16[56,640]{1,0:T(8,128)(2,1)S(1)}) custom-call(s32[7]{0:T(128)S(1)} %stack.64.info_ref, bf16[16,8,1280]{2,1,0:T(8,128)(2,1)S(1)} %bitcast.26), custom_call_target="tpu_custom_call" | custom-call | flops 10000000000 | bytes 1 | tf_op jit(solution)/shard_map/first/pallas_call | solution.py:345
  6.6 4.3 %collective-permute-done.refs_1_ = bf16[56,640]{1,0:T(8,128)(2,1)S(1)} collective-permute-done((bf16[56,640]{1,0:T(8,128)(2,1)S(1)}, bf16[56,640]{1,0:T(8,128)(2,1)S(1)}, u32[]{:S(2)}, u32[]{:S(2)}) %collective-permute-start) | collective-permute-done | bytes 71712 | tf_op jit(solution)/shard_map/ppermute | solution.py:389
  10.8 0.6 %rows.1 = (bf16[24,1280]{1,0:T(8,128)(2,1)S(1)}, bf16[16,1280]{1,0:T(8,128)(2,1)S(1)}, f32[1,64]{1,0:T(1,128)S(1)}) custom-call(s32[7]{0:T(128)S(1)} %stack.64.info_ref, bf16[56,640]{1,0:T(8,128)(2,1)S(1)} %get-tuple-element.29.refs_0_, bf16[56,640]{1,0:T(8,128)(2,1)S(1)} %collective-permute-done.refs_1_, bf16[16,8,640]{2,1,0:T(8,128)(2,1)S(1)} %bitcast.23, ...), custom_call_target="tpu_custom_call" | custom-call | tf_op jit(solution)/shard_map/rows/pallas_call | solution.py:345
  11.5 0.6 %tiles.1 = (bf16[16,8,640]{2,1,0:T(8,128)(2,1)S(1)}, bf16[16,8,640]{2,1,0:T(8,128)(2,1)S(1)}) custom-call(s32[7]{0:T(128)S(1)} %stack.64.info_ref, bf16[16,8,1280]{2,1,0:T(8,128)(2,1)S(1)} %bitcast.27, bf16[3,3,640,640]{3,2,1,0:T(8,128)(2,1)S(1)} %bitcast.21), custom_call_target="tpu_custom_call" | custom-call | tf_op jit(solution)/shard_map/tiles/pallas_call | solution.py:345
  12.2 0.6 %collective-permute-done.3.near_h.refs_2_ = bf16[24,1280]{1,0:T(8,128)(2,1)S(1)} collective-permute-done((bf16[24,1280]{1,0:T(8,128)(2,1)S(1)}, bf16[24,1280]{1,0:T(8,128)(2,1)S(1)}, u32[]{:S(2)}, u32[]{:S(2)}) %collective-permute-start.3) | collective-permute-done | bytes 61472 | tf_op jit(solution)/shard_map/ppermute | solution.py:23
  12.9 1.3 %collective-permute-start.4 = (bf16[19,1280]{1,0:T(8,128)(2,1)S(1)}, bf16[19,1280]{1,0:T(8,128)(2,1)S(1)}, u32[]{:S(2)}, u32[]{:S(2)}) collective-permute-start(bf16[19,1280]{1,0:T(8,128)(2,1)S(1)} %pad_maximum_fusion), channel_id=1, source_target_pairs={{0,12},{4,8},{8,4},{12,0},{1,13},{5,9},{9,5},{13,1},{2,14},{6,10},... | collective-permute-start | bytes 145928 | tf_op jit(solution)/shard_map/ppermute | solution.py:23
  14.3 0.7 %columns.1 = (bf16[32,1280]{1,0:T(8,128)(2,1)S(1)}, bf16[32,1280]{1,0:T(8,128)(2,1)S(1)}) custom-call(s32[7]{0:T(128)S(1)} %stack.64.info_ref, bf16[56,640]{1,0:T(8,128)(2,1)S(1)} %get-tuple-element.29.refs_0_, bf16[56,640]{1,0:T(8,128)(2,1)S(1)} %collective-permute-done.refs_1_, bf16[16,8,640]{2,1,0:T(8,128)(2,1)S(1)} %bitcast.24, ...), custom_call_target="tpu_custom_call" | custom-call | tf_op jit(solution)/shard_map/columns/pallas_call | solution.py:345
  15.0 1.9 %collective-permute-done.4.across_h.refs_3_ = bf16[19,1280]{1,0:T(8,128)(2,1)S(1)} collective-permute-done((bf16[19,1280]{1,0:T(8,128)(2,1)S(1)}, bf16[19,1280]{1,0:T(8,128)(2,1)S(1)}, u32[]{:S(2)}, u32[]{:S(2)}) %collective-permute-start.4) | collective-permute-done | bytes 48672 | tf_op jit(solution)/shard_map/ppermute | solution.py:23
  17.1 0.6 %pack.1 = (bf16[40,1280]{1,0:T(8,128)(2,1)S(1)}, bf16[36,1280]{1,0:T(8,128)(2,1)S(1)}) custom-call(s32[7]{0:T(128)S(1)} %stack.64.info_ref, bf16[24,1280]{1,0:T(8,128)(2,1)S(1)} %collective-permute-done.3.near_h.refs_2_, bf16[19,1280]{1,0:T(8,128)(2,1)S(1)} %collective-permute-done.4.across_h.refs_3_, f32[1,64]{1,0:T(1,128)S(1)} %pad_maximum_fusion.3.stats_ref, ...), custom_call_target="tpu_custom_call" | custom-call | tf_op jit(solution)/shard_map/pack/pallas_call | solution.py:345
  17.7 1.6 %collective-permute-start.5 = (bf16[40,1280]{1,0:T(8,128)(2,1)S(1)}, bf16[40,1280]{1,0:T(8,128)(2,1)S(1)}, u32[]{:S(2)}, u32[]{:S(2)}) collective-permute-start(bf16[40,1280]{1,0:T(8,128)(2,1)S(1)} %get-tuple-element.35), channel_id=1, source_target_pairs={{0,1},{1,0},{2,3},{3,2},{4,5},{5,4},{6,7},{7,6},{8,9},{9,8},{10,11... | collective-permute-start | bytes 307208 | tf_op jit(solution)/shard_map/ppermute | solution.py:23
  19.4 0.6 %collective-permute-start.1 = (bf16[16,8,640]{2,1,0:T(8,128)(2,1)S(1)}, bf16[16,8,640]{2,1,0:T(8,128)(2,1)S(1)}, u32[]{:S(2)}, u32[]{:S(2)}) collective-permute-start(bf16[16,8,640]{2,1,0:T(8,128)(2,1)S(1)} %broadcast_add_fusion), channel_id=1, source_target_pairs={{0,16},{16,0},{1,17},{17,1},{2,18},{18,2},{3,19},{19,3},{4,20},{20... | collective-permute-start | bytes 491528 | tf_op jit(solution)/shard_map/ppermute | solution.py:389
  20.0 0.7 %collective-permute-start.7 = (bf16[36,1280]{1,0:T(8,128)(2,1)S(1)}, bf16[36,1280]{1,0:T(8,128)(2,1)S(1)}, u32[]{:S(2)}, u32[]{:S(2)}) collective-permute-start(bf16[36,1280]{1,0:T(8,128)(2,1)S(1)} %get-tuple-element.36), channel_id=1, source_target_pairs={{1,2},{2,1},{5,6},{6,5},{9,10},{10,9},{13,14},{14,13},{17,18},{18,... | collective-permute-start | bytes 276488 | tf_op jit(solution)/shard_map/ppermute | solution.py:23
  20.6 2.1 %collective-permute-done.5.refs_4_.near_w = bf16[40,1280]{1,0:T(8,128)(2,1)S(1)} collective-permute-done((bf16[40,1280]{1,0:T(8,128)(2,1)S(1)}, bf16[40,1280]{1,0:T(8,128)(2,1)S(1)}, u32[]{:S(2)}, u32[]{:S(2)}) %collective-permute-start.5) | collective-permute-done | bytes 102432 | tf_op jit(solution)/shard_map/ppermute | solution.py:23
  22.9 2.6 %collective-permute-start.6 = (f32[1,64]{1,0:T(1,128)S(1)}, f32[1,64]{1,0:T(1,128)S(1)}, u32[]{:S(2)}, u32[]{:S(2)}) collective-permute-start(f32[1,64]{1,0:T(1,128)S(1)} %pad_maximum_fusion.4), channel_id=1, source_target_pairs={{0,2},{1,3},{2,0},{3,1},{4,6},{5,7},{6,4},{7,5},{8,10},{9,11},{10,... | collective-permute-start | bytes 776 | tf_op jit(solution)/shard_map/ppermute | solution.py:23
  25.5 3.0 %conv_backward.1.refs_5_ = f32[16,2,8,640]{3,2,1,0:T(8,128)S(1)} custom-call(s32[7]{0:T(128)S(1)} %stack.64.info_ref, bf16[16,8,640]{2,1,0:T(8,128)(2,1)S(1)} %bitcast.25, bf16[16,8,640]{2,1,0:T(8,128)(2,1)S(1)} %collective-permute-done.2.refs_3_.refs_1_, bf16[24,1280]{1,0:T(8,128)(2,1)S(1)} %collective-permute-done.3.near_h.refs_2_, ...), custom_call_target="tpu_custom_call" | custom-call | tf_op jit(solution)/shard_map/conv_backward/pallas_call | solution.py:345
  28.7 1.4 %terms.1 = (f32[4,16]{1,0:T(4,128)S(1)}, f32[4,16]{1,0:T(4,128)S(1)}, f32[16,8,640]{2,1,0:T(8,128)S(1)}, bf16[1,16,8,640]{3,2,1,0:T(8,128)(2,1)S(1)}, f32[16,2,1...) custom-call(s32[7]{0:T(128)S(1)} %stack.64.info_ref, bf16[16,8,640]{2,1,0:T(8,128)(2,1)S(1)} %get-tuple-element.26.refs_0_, ...), custom_call_target="tpu_custom_call" | custom-call | tf_op jit(solution)/shard_map/terms/pallas_call | solution.py:345
  30.1 0.7 %collective-permute-start.8 = (f32[4,16]{1,0:T(4,128)S(1)}, f32[4,16]{1,0:T(4,128)S(1)}, u32[]{:S(2)}, u32[]{:S(2)}) collective-permute-start(f32[4,16]{1,0:T(4,128)S(1)} %get-tuple-element.38), channel_id=1, source_target_pairs={{16,0},{0,16},{17,1},{1,17},{18,2},{2,18},{19,3},{3,19},{20,4},{4,... | collective-permute-start | bytes 776 | tf_op jit(solution)/shard_map/ppermute | solution.py:470
  30.8 2.3 %conv_forward.1 = (f32[16,8,384]{2,1,0:T(8,128)S(1)}, bf16[1,16,8,384]{3,2,1,0:T(8,128)(2,1)S(1)}, bf16[3,18,16,640]{3,2,1,0:T(8,128)(2,1)S(1)}) custom-call(s32[7]{0:T(128)S(1)} %stack.64.info_ref, f32[16,2,16,640]{3,2,1,0:T(8,128)S(1)} %get-tuple-element.39.given_ref, f32[6,640]{1,0:T(8,128)S(1)} %get-tuple-element.40.scales_ref, ...), custom_call_target="tpu_custom_call" | custom-call | tf_op jit(solution)/shard_map/conv_forward/pallas_call | solution.py:345
  33.1 0.6 %collective-permute-done.8 = f32[4,16]{1,0:T(4,128)S(1)} collective-permute-done((f32[4,16]{1,0:T(4,128)S(1)}, f32[4,16]{1,0:T(4,128)S(1)}, u32[]{:S(2)}, u32[]{:S(2)}) %collective-permute-start.8) | collective-permute-done | bytes 288 | tf_op jit(solution)/shard_map/ppermute | solution.py:470
  33.7 0.9 %collective-permute-start.13 = (bf16[16,8,640]{2,1,0:T(8,128)(2,1)S(1)}, bf16[16,8,640]{2,1,0:T(8,128)(2,1)S(1)}, u32[]{:S(2)}, u32[]{:S(2)}) collective-permute-start(bf16[16,8,640]{2,1,0:T(8,128)(2,1)S(1)} %bitcast.32), channel_id=1, source_target_pairs={{16,0},{0,16},{17,1},{1,17},{18,2},{2,18},{19,3},{3,19},{20,4},{4,... | collective-permute-start | bytes 491528 | tf_op jit(solution)/shard_map/ppermute | solution.py:470
  34.6 0.3 collective-permute-done.9
  34.8 1.5 %collective-permute-start.10 = (f32[2,2,16]{2,1,0:T(2,128)S(1)}, f32[2,2,16]{2,1,0:T(2,128)S(1)}, u32[]{:S(2)}, u32[]{:S(2)}) collective-permute-start(f32[2,2,16]{2,1,0:T(2,128)S(1)} %fusion.14.after_ref), channel_id=1, source_target_pairs={{0,8},{4,12},{8,0},{12,4},{1,9},{5,13},{9,1},{13,5},{2,10},{6,14},... | collective-permute-start | bytes 776 | tf_op jit(solution)/shard_map/ppermute | solution.py:23
  36.3 1.1 %conv_forward2.1 = (f32[16,8,256]{2,1,0:T(8,128)S(1)}, bf16[1,16,8,256]{3,2,1,0:T(8,128)(2,1)S(1)}) custom-call(bf16[3,18,16,640]{3,2,1,0:T(8,128)(2,1)S(1)} %get-tuple-element.42.windows_ref, bf16[3,3,640,640]{3,2,1,0:T(8,128)(2,1)S(1)} %bitcast.21, f32[2,2,16]{2,1,0:T(2,128)S(1)} %fusion.14.after_ref), custom_call_target="tpu_custom_call" | custom-call | tf_op jit(solution)/shard_map/conv_forward2/pallas_call | solution.py:345
  37.5 1.0 %collective-permute-done.10 = f32[2,2,16]{2,1,0:T(2,128)S(1)} collective-permute-done((f32[2,2,16]{2,1,0:T(2,128)S(1)}, f32[2,2,16]{2,1,0:T(2,128)S(1)}, u32[]{:S(2)}, u32[]{:S(2)}) %collective-permute-start.10) | collective-permute-done | bytes 288 | tf_op jit(solution)/shard_map/ppermute | solution.py:23
  38.4 2.6 %collective-permute-start.11 = (f32[2,2,16]{2,1,0:T(2,128)S(1)}, f32[2,2,16]{2,1,0:T(2,128)S(1)}, u32[]{:S(2)}, u32[]{:S(2)}) collective-permute-start(f32[2,2,16]{2,1,0:T(2,128)S(1)} %add_add_fusion), channel_id=1, source_target_pairs={{0,1},{1,0},{2,3},{3,2},{4,5},{5,4},{6,7},{7,6},{8,9},{9,8},{10,11... | collective-permute-start | bytes 776 | tf_op jit(solution)/shard_map/ppermute | solution.py:23
  41.1 1.0 %collective-permute-start.14 = (bf16[16,8,384]{2,1,0:T(8,128)(2,1)S(1)}, bf16[16,8,384]{2,1,0:T(8,128)(2,1)S(1)}, u32[]{:S(2)}, u32[]{:S(2)}) collective-permute-start(bf16[16,8,384]{2,1,0:T(8,128)(2,1)S(1)} %bitcast.33), channel_id=1, source_target_pairs={{16,0},{0,16},{17,1},{1,17},{18,2},{2,18},{19,3},{3,19},{20,4},{4,... | collective-permute-start | bytes 294920 | tf_op jit(solution)/shard_map/ppermute | solution.py:494
  42.1 1.0 %collective-permute-start.15 = (bf16[16,8,256]{2,1,0:T(8,128)(2,1)S(1)}, bf16[16,8,256]{2,1,0:T(8,128)(2,1)S(1)}, u32[]{:S(2)}, u32[]{:S(2)}) collective-permute-start(bf16[16,8,256]{2,1,0:T(8,128)(2,1)S(1)} %bitcast.34), channel_id=1, source_target_pairs={{16,0},{0,16},{17,1},{1,17},{18,2},{2,18},{19,3},{3,19},{20,4},{4,... | collective-permute-start | bytes 196616 | tf_op jit(solution)/shard_map/ppermute | solution.py:494
  43.1 3.0 %collective-permute-start.12 = (f32[2,2,16]{2,1,0:T(2,128)S(1)}, f32[2,2,16]{2,1,0:T(2,128)S(1)}, u32[]{:S(2)}, u32[]{:S(2)}) collective-permute-start(f32[2,2,16]{2,1,0:T(2,128)S(1)} %add.136), channel_id=1, source_target_pairs={{0,2},{1,3},{2,0},{3,1},{4,6},{5,7},{6,4},{7,5},{8,10},{9,11},{10,... | collective-permute-start | bytes 776 | tf_op jit(solution)/shard_map/ppermute | solution.py:23
  46.1 1.6 %collective-permute-done.12 = f32[2,2,16]{2,1,0:T(2,128)S(1)} collective-permute-done((f32[2,2,16]{2,1,0:T(2,128)S(1)}, f32[2,2,16]{2,1,0:T(2,128)S(1)}, u32[]{:S(2)}, u32[]{:S(2)}) %collective-permute-start.12) | collective-permute-done | bytes 288 | tf_op jit(solution)/shard_map/ppermute | solution.py:23
  47.7 1.6 %finish.1 = (bf16[16,8,640]{2,1,0:T(8,128)(2,1)}, bf16[16,8,1280]{2,1,0:T(8,128)(2,1)}) custom-call(s32[7]{0:T(128)S(1)} %stack.64.info_ref, bf16[16,8,1280]{2,1,0:T(8,128)(2,1)S(1)} %bitcast.28, f32[2,4,16]{2,1,0:T(4,128)S(1)} %pad_maximum_fusion.1.small_ref, f32[2,2,16]{2,1,0:T(2,128)S(1)} %add.137.sums_ref, f32[640]{0:T(1024)S(1)} %copy-done.5, ...), custom_call_target="tpu_custom_call" | custom-call | tf_op jit(solution)/shard_map/finish/pallas_call | solution.py:345
  (55 shorter events, 1.0 us)
Async XLA Ops:
  0.6 10.2 %collective-permute-start.2 = (bf16[16,8,640]{2,1,0:T(8,128)(2,1)}, bf16[16,8,640]{2,1,0:T(8,128)(2,1)S(1)}, u32[]{:S(2)}, u32[]{:S(2)}) collective-permute-start(bf16[16,8,640]{2,1,0:T(8,128)(2,1)} %bitcast.22), channel_id=1, source_target_pairs={{0,16},{16,0},{1,17},{17,1},{2,18},{18,2},{3,19},{19,3},{4,20},{20... | collective-permute-start | bytes 491528 | tf_op jit(solution)/shard_map/ppermute | solution.py:389
  3.7 7.7 %slice-start = ((s8[7372800]{0:T(1024)(128)(4,1)}), s8[4194304]{0:T(1024)(128)(4,1)S(1)}, s32[]{:S(2)}) async-start(s8[7372800]{0:T(1024)(128)(4,1)} %bitcast.20), calls=%async_computation | async-start | bytes 8388608
  3.7 1.1 %copy-start.1 = (bf16[1,16,8,1280]{3,2,1,0:T(8,128)(2,1)S(1)}, bf16[1,16,8,1280]{3,2,1,0:T(8,128)(2,1)}, u32[]{:S(2)}) copy-start(bf16[1,16,8,1280]{3,2,1,0:T(8,128)(2,1)} %param.6) | copy-start | bytes 983044
  4.9 6.0 %copy-start = (bf16[1,16,8,640]{3,2,1,0:T(8,128)(2,1)S(1)}, bf16[1,16,8,640]{3,2,1,0:T(8,128)(2,1)}, u32[]{:S(2)}) copy-start(bf16[1,16,8,640]{3,2,1,0:T(8,128)(2,1)} %param.11) | copy-start | bytes 491524
  4.9 6.6 %slice-start.1 = ((s8[7372800]{0:T(1024)(128)(4,1)}), s8[3178496]{0:T(1024)(128)(4,1)S(1)}, s32[]{:S(2)}) async-start(s8[7372800]{0:T(1024)(128)(4,1)} %bitcast.20), calls=%async_computation.1 | async-start | bytes 6356992
  4.9 6.6 %copy-start.2 = (bf16[1,16,8,1280]{3,2,1,0:T(8,128)(2,1)S(1)}, bf16[1,16,8,1280]{3,2,1,0:T(8,128)(2,1)}, u32[]{:S(2)}) copy-start(bf16[1,16,8,1280]{3,2,1,0:T(8,128)(2,1)} %param.6) | copy-start | bytes 983044
  6.5 4.4 %collective-permute-start = (bf16[56,640]{1,0:T(8,128)(2,1)S(1)}, bf16[56,640]{1,0:T(8,128)(2,1)S(1)}, u32[]{:S(2)}, u32[]{:S(2)}) collective-permute-start(bf16[56,640]{1,0:T(8,128)(2,1)S(1)} %get-tuple-element.28), channel_id=1, source_target_pairs={{0,16},{16,0},{1,17},{17,1},{2,18},{18,2},{3,19},{19,3},{4,20},{20... | collective-permute-start | bytes 215048 | tf_op jit(solution)/shard_map/ppermute | solution.py:389
  11.5 1.3 %collective-permute-start.3 = (bf16[24,1280]{1,0:T(8,128)(2,1)S(1)}, bf16[24,1280]{1,0:T(8,128)(2,1)S(1)}, u32[]{:S(2)}, u32[]{:S(2)}) collective-permute-start(bf16[24,1280]{1,0:T(8,128)(2,1)S(1)} %get-tuple-element.31), channel_id=1, source_target_pairs={{0,4},{4,0},{8,12},{12,8},{1,5},{5,1},{9,13},{13,9},{2,6},{6,2},{1... | collective-permute-start | bytes 184328 | tf_op jit(solution)/shard_map/ppermute | solution.py:23
  12.9 4.0 %collective-permute-start.4 = (bf16[19,1280]{1,0:T(8,128)(2,1)S(1)}, bf16[19,1280]{1,0:T(8,128)(2,1)S(1)}, u32[]{:S(2)}, u32[]{:S(2)}) collective-permute-start(bf16[19,1280]{1,0:T(8,128)(2,1)S(1)} %pad_maximum_fusion), channel_id=1, source_target_pairs={{0,12},{4,8},{8,4},{12,0},{1,13},{5,9},{9,5},{13,1},{2,14},{6,10},... | collective-permute-start | bytes 145928 | tf_op jit(solution)/shard_map/ppermute | solution.py:23
  17.7 5.0 %collective-permute-start.5 = (bf16[40,1280]{1,0:T(8,128)(2,1)S(1)}, bf16[40,1280]{1,0:T(8,128)(2,1)S(1)}, u32[]{:S(2)}, u32[]{:S(2)}) collective-permute-start(bf16[40,1280]{1,0:T(8,128)(2,1)S(1)} %get-tuple-element.35), channel_id=1, source_target_pairs={{0,1},{1,0},{2,3},{3,2},{4,5},{5,4},{6,7},{7,6},{8,9},{9,8},{10,11... | collective-permute-start | bytes 307208 | tf_op jit(solution)/shard_map/ppermute | solution.py:23
  19.4 6.1 %collective-permute-start.1 = (bf16[16,8,640]{2,1,0:T(8,128)(2,1)S(1)}, bf16[16,8,640]{2,1,0:T(8,128)(2,1)S(1)}, u32[]{:S(2)}, u32[]{:S(2)}) collective-permute-start(bf16[16,8,640]{2,1,0:T(8,128)(2,1)S(1)} %broadcast_add_fusion), channel_id=1, source_target_pairs={{0,16},{16,0},{1,17},{17,1},{2,18},{18,2},{3,19},{19,3},{4,20},{20... | collective-permute-start | bytes 491528 | tf_op jit(solution)/shard_map/ppermute | solution.py:389
  20.0 5.6 %collective-permute-start.7 = (bf16[36,1280]{1,0:T(8,128)(2,1)S(1)}, bf16[36,1280]{1,0:T(8,128)(2,1)S(1)}, u32[]{:S(2)}, u32[]{:S(2)}) collective-permute-start(bf16[36,1280]{1,0:T(8,128)(2,1)S(1)} %get-tuple-element.36), channel_id=1, source_target_pairs={{1,2},{2,1},{5,6},{6,5},{9,10},{10,9},{13,14},{14,13},{17,18},{18,... | collective-permute-start | bytes 276488 | tf_op jit(solution)/shard_map/ppermute | solution.py:23
  22.9 5.8 %copy-start.3 = (f32[1280]{0:T(1024)S(1)}, f32[1280]{0:T(1024)}, u32[]{:S(2)}) copy-start(f32[1280]{0:T(1024)} %refs_3_.1) | copy-start | bytes 15364
  22.9 5.8 %copy-start.4 = (f32[1280]{0:T(1024)S(1)}, f32[1280]{0:T(1024)}, u32[]{:S(2)}) copy-start(f32[1280]{0:T(1024)} %refs_4_.1) | copy-start | bytes 15364
  22.9 5.6 %collective-permute-start.6 = (f32[1,64]{1,0:T(1,128)S(1)}, f32[1,64]{1,0:T(1,128)S(1)}, u32[]{:S(2)}, u32[]{:S(2)}) collective-permute-start(f32[1,64]{1,0:T(1,128)S(1)} %pad_maximum_fusion.4), channel_id=1, source_target_pairs={{0,2},{1,3},{2,0},{3,1},{4,6},{5,7},{6,4},{7,5},{8,10},{9,11},{10,... | collective-permute-start | bytes 776 | tf_op jit(solution)/shard_map/ppermute | solution.py:23
  30.1 3.6 %collective-permute-start.8 = (f32[4,16]{1,0:T(4,128)S(1)}, f32[4,16]{1,0:T(4,128)S(1)}, u32[]{:S(2)}, u32[]{:S(2)}) collective-permute-start(f32[4,16]{1,0:T(4,128)S(1)} %get-tuple-element.38), channel_id=1, source_target_pairs={{16,0},{0,16},{17,1},{1,17},{18,2},{2,18},{19,3},{3,19},{20,4},{4,... | collective-permute-start | bytes 776 | tf_op jit(solution)/shard_map/ppermute | solution.py:470
  33.7 1.2 %collective-permute-start.9 = (f32[2,2,16]{2,1,0:T(2,128)S(1)}, f32[2,2,16]{2,1,0:T(2,128)S(1)}, u32[]{:S(2)}, u32[]{:S(2)}) collective-permute-start(f32[2,2,16]{2,1,0:T(2,128)S(1)} %fusion.7), channel_id=1, source_target_pairs={{0,4},{4,0},{8,12},{12,8},{1,5},{5,1},{9,13},{13,9},{2,6},{6,2},{1... | collective-permute-start | bytes 776 | tf_op jit(solution)/shard_map/ppermute | solution.py:23
  33.7 14.0 %collective-permute-start.13 = (bf16[16,8,640]{2,1,0:T(8,128)(2,1)S(1)}, bf16[16,8,640]{2,1,0:T(8,128)(2,1)S(1)}, u32[]{:S(2)}, u32[]{:S(2)}) collective-permute-start(bf16[16,8,640]{2,1,0:T(8,128)(2,1)S(1)} %bitcast.32), channel_id=1, source_target_pairs={{16,0},{0,16},{17,1},{1,17},{18,2},{2,18},{19,3},{3,19},{20,4},{4,... | collective-permute-start | bytes 491528 | tf_op jit(solution)/shard_map/ppermute | solution.py:470
  34.8 3.6 %collective-permute-start.10 = (f32[2,2,16]{2,1,0:T(2,128)S(1)}, f32[2,2,16]{2,1,0:T(2,128)S(1)}, u32[]{:S(2)}, u32[]{:S(2)}) collective-permute-start(f32[2,2,16]{2,1,0:T(2,128)S(1)} %fusion.14.after_ref), channel_id=1, source_target_pairs={{0,8},{4,12},{8,0},{12,4},{1,9},{5,13},{9,1},{13,5},{2,10},{6,14},... | collective-permute-start | bytes 776 | tf_op jit(solution)/shard_map/ppermute | solution.py:23
  36.3 11.4 %copy-start.5 = (f32[640]{0:T(1024)S(1)}, f32[640]{0:T(1024)}, u32[]{:S(2)}) copy-start(f32[640]{0:T(1024)} %bias_ref.1) | copy-start | bytes 7684
  38.4 4.7 %collective-permute-start.11 = (f32[2,2,16]{2,1,0:T(2,128)S(1)}, f32[2,2,16]{2,1,0:T(2,128)S(1)}, u32[]{:S(2)}, u32[]{:S(2)}) collective-permute-start(f32[2,2,16]{2,1,0:T(2,128)S(1)} %add_add_fusion), channel_id=1, source_target_pairs={{0,1},{1,0},{2,3},{3,2},{4,5},{5,4},{6,7},{7,6},{8,9},{9,8},{10,11... | collective-permute-start | bytes 776 | tf_op jit(solution)/shard_map/ppermute | solution.py:23
  41.1 6.6 %collective-permute-start.14 = (bf16[16,8,384]{2,1,0:T(8,128)(2,1)S(1)}, bf16[16,8,384]{2,1,0:T(8,128)(2,1)S(1)}, u32[]{:S(2)}, u32[]{:S(2)}) collective-permute-start(bf16[16,8,384]{2,1,0:T(8,128)(2,1)S(1)} %bitcast.33), channel_id=1, source_target_pairs={{16,0},{0,16},{17,1},{1,17},{18,2},{2,18},{19,3},{3,19},{20,4},{4,... | collective-permute-start | bytes 294920 | tf_op jit(solution)/shard_map/ppermute | solution.py:494
  42.1 5.6 %collective-permute-start.15 = (bf16[16,8,256]{2,1,0:T(8,128)(2,1)S(1)}, bf16[16,8,256]{2,1,0:T(8,128)(2,1)S(1)}, u32[]{:S(2)}, u32[]{:S(2)}) collective-permute-start(bf16[16,8,256]{2,1,0:T(8,128)(2,1)S(1)} %bitcast.34), channel_id=1, source_target_pairs={{16,0},{0,16},{17,1},{1,17},{18,2},{2,18},{19,3},{3,19},{20,4},{4,... | collective-permute-start | bytes 196616 | tf_op jit(solution)/shard_map/ppermute | solution.py:494
  43.1 4.6 %collective-permute-start.12 = (f32[2,2,16]{2,1,0:T(2,128)S(1)}, f32[2,2,16]{2,1,0:T(2,128)S(1)}, u32[]{:S(2)}, u32[]{:S(2)}) collective-permute-start(f32[2,2,16]{2,1,0:T(2,128)S(1)} %add.136), channel_id=1, source_target_pairs={{0,2},{1,3},{2,0},{3,1},{4,6},{5,7},{6,4},{7,5},{8,10},{9,11},{10,... | collective-permute-start | bytes 776 | tf_op jit(solution)/shard_map/ppermute | solution.py:23

commit v7 on v6

--- a/solution.py
+++ b/solution.py
@@ -102,14 +102,12 @@
         centered = flat - expanded(mean, chans)
         squares = gathered(jnp.sum(centered * centered, axis=0, keepdims=True), groups)
         stats.append(jnp.concatenate([p.astype(F32) for p in three_parts(jnp.concatenate([mean, squares], 1))], 0))
-    ends = [jnp.concatenate(row_ends(x, even_h), 0) for x in shards]
-    columns = [column_ends(x, info_ref[EVEN_W] > 0) for x in shards]
+    pieces = []
+    for x, terms in zip(shards, stats):
+        terms = jnp.concatenate([terms, jnp.zeros((3, chans - 2 * groups), F32)], 1)
+        pieces.append(jnp.concatenate([*row_ends(x, even_h), terms, jnp.zeros((5, chans), F32), column_ends(x, info_ref[EVEN_W] > 0)], 0))
     for k, ref in enumerate(out_refs):
-        shard = lax.rem(me + k, parts)
-        ref[: 2 * cols, :] = shard_of(ends, shard).astype(BF16)
-        ref[2 * cols : 2 * cols + 8, :] = jnp.zeros((8, chans), BF16)
-        ref[2 * cols : 2 * cols + 3, : 2 * groups] = shard_of(stats, shard).astype(BF16)
-        ref[2 * cols + 8 :, :] = shard_of(columns, shard).astype(BF16)
+        ref[...] = shard_of(pieces, lax.rem(me + k, parts)).astype(BF16)
 
 
 def row_ends(t, even_h):
@@ -303,9 +301,7 @@
 
 def finish_kernel(parts, count, info_ref, x_ref, small_ref, sums_ref, bias_ref, gx_own_ref, *refs):
     gx_refs, conv_refs = refs[: parts - 1], refs[parts - 1 : 3 * parts - 1]
-    conv_out, grad_out, conv_ref, grad_ref, sems = refs[3 * parts - 1 :]
-    rows = x_ref.shape[0]
-    copies = [pltpu.make_async_copy(conv_ref, conv_out, sems.at[0])]
+    conv_ref, grad_ref = refs[3 * parts - 1 :]
     cin = x_ref.shape[2]
     chans = cin // parts
     start = 0
@@ -314,41 +310,29 @@
         stop = start + conv.shape[2]
         conv_ref[:, :, start:stop] = (conv + bias_ref[start:stop].reshape(1, 1, -1)).astype(BF16)
         start = stop
-    copies[0].start()
     wide = []
     for k in range(parts):
         stats = small_ref[k]
         wide.append(jnp.concatenate([stats[2:3], lax.rsqrt(stats[3:4] / count + EPS), sums_ref[k] / count], 0))
     wide = expanded(jnp.concatenate(wide, 0), chans)
-    picked = []
+    gx_all = [ref[...].astype(F32) for ref in (gx_own_ref, *gx_refs)]
     for s in range(parts):
+        at = slice(s * chans, (s + 1) * chans)
         k = lax.rem(s - info_ref[ME] + parts, parts)
-        picked.append([shard_of([wide[4 * j + i : 4 * j + i + 1] for j in range(parts)], k)[None] for i in range(4)])
-    half = rows // 2
-    for r in range(2):
-        at_rows = slice(r * half, (r + 1) * half)
-        gx_all = [ref[at_rows].astype(F32) for ref in (gx_own_ref, *gx_refs)]
-        for s in range(parts):
-            at = slice(s * chans, (s + 1) * chans)
-            k = lax.rem(s - info_ref[ME] + parts, parts)
-            mean, inv, first, second = picked[s]
-            xhat = (x_ref[at_rows, :, at].astype(F32) - mean) * inv
-            grad_ref[at_rows, :, at] = (inv * (shard_of(gx_all, k) - first - xhat * second)).astype(BF16)
-        copies.append(pltpu.make_async_copy(grad_ref.at[at_rows], grad_out.at[at_rows], sems.at[1 + r]))
-        copies[-1].start()
-    for copy in copies:
-        copy.wait()
-
-
-def call(kernel, name, outs, operands, scratch=(), in_hbm=(), limit=28, scalars=True, cost=None, outs_in_hbm=False):
-    spec = lambda i: pl.BlockSpec(memory_space=pltpu.HBM if i in in_hbm else pltpu.SMEM if scalars and i == 0 else pltpu.VMEM)
+        mean, inv, first, second = (shard_of([wide[4 * j + i : 4 * j + i + 1] for j in range(parts)], k)[None] for i in range(4))
+        xhat = (x_ref[:, :, at].astype(F32) - mean) * inv
+        grad_ref[:, :, at] = (inv * (shard_of(gx_all, k) - first - xhat * second)).astype(BF16)
+
+
+def call(kernel, name, outs, operands, scratch=(), scalars=True, cost=None):
+    spec = lambda i: pl.BlockSpec(memory_space=pltpu.SMEM if scalars and i == 0 else pltpu.VMEM)
     return pl.pallas_call(
         kernel,
         out_shape=outs,
         in_specs=[spec(i) for i in range(len(operands))],
-        out_specs=[pl.BlockSpec(memory_space=pl.ANY if outs_in_hbm else pltpu.VMEM)] * len(outs),
+        out_specs=[pl.BlockSpec(memory_space=pltpu.VMEM)] * len(outs),
         scratch_shapes=scratch,
-        compiler_params=pltpu.CompilerParams(vmem_limit_bytes=limit * 2**20),
+        compiler_params=pltpu.CompilerParams(vmem_limit_bytes=28 * 2**20),
         cost_estimate=cost,
         name=name,
     )(*operands)
@@ -502,8 +486,6 @@
         "finish",
         [sds((rows, cols, outs), BF16), sds((rows, cols, cin), BF16)],
         [info, x, small, sums, conv_bias, gx_own, *gx, *conv],
-        [pltpu.VMEM((rows, cols, outs), BF16), pltpu.VMEM((rows, cols, cin), BF16), pltpu.SemaphoreType.DMA((3,))],
-        outs_in_hbm=True,
     )
     return conv_out[None], grad[None]
 

time: 49.5 us -> 49.6 us (level)
  no operation moved by 1% of the time
where the time goes in v7:
time: 49.6 us; the launch traced here: 49.5 us
  starting transfers between devices  20.7 us (42%)
  Pallas kernels  13.7 us (28%)
  waiting for transfers between devices  12.3 us (25%)
  local copies, waits for them, and re-layouts  1.23 us (2%)
  between operations  0.81 us (2%)
  other arithmetic  0.77 us (2%)
    pallas_call x10, Pallas kernels, call(): pl.pallas_call(kernel, out_shape=outs, in_specs=[spec(i) for i in range(l...  13.7 us
    ppermute x9, starting transfers between devices, exchange(): return lax.ppermute(value, axis, pairs)  13.4 us
    ppermute x9, waiting for transfers between devices, exchange(): return lax.ppermute(value, axis, pairs)  7.4 us
    ppermute x3, waiting for transfers between devices, body(): lax.ppermute(v, 'dp', pairs)  4.29 us
    ppermute x3, starting transfers between devices, body(): lax.ppermute(v, 'dp', pairs)  3.72 us
    ppermute x2, starting transfers between devices, body(): conv += [lax.ppermute(v[k], 'dp', back) for v in (conv_other, conv_other2)]  2.03 us
    ppermute x2, starting transfers between devices, body(): lax.ppermute(v, 'dp', [(j, i) for i, j in pairs])  1.57 us
    unnamed x16, local copies, waits for them, and re-layouts  1.15 us
  transfers between devices with their start and end apart: 16, of which 8 were waited for; matrix products, arithmetic and copies ran while one was open for 1% of the time, Pallas kernels for 19%

profile of v7, /device:TPU:0, one launch (start us, length us, event | category | flops | bytes accessed | tf_op | source)
XLA Modules:
  0.0 49.5 jit_solution(13164248197889871011)
XLA Ops:
  0.6 3.0 %collective-permute-start.2 = (bf16[16,8,640]{2,1,0:T(8,128)(2,1)}, bf16[16,8,640]{2,1,0:T(8,128)(2,1)S(1)}, u32[]{:S(2)}, u32[]{:S(2)}) collective-permute-start(bf16[16,8,640]{2,1,0:T(8,128)(2,1)} %bitcast.22), channel_id=1, source_target_pairs={{0,16},{16,0},{1,17},{17,1},{2,18},{18,2},{3,19},{19,3},{4,20},{20... | collective-permute-start | bytes 491528 | tf_op jit(solution)/shard_map/ppermute | solution.py:373
  3.8 1.1 %copy-done.1 = bf16[1,16,8,1280]{3,2,1,0:T(8,128)(2,1)S(1)} copy-done((bf16[1,16,8,1280]{3,2,1,0:T(8,128)(2,1)S(1)}, bf16[1,16,8,1280]{3,2,1,0:T(8,128)(2,1)}, u32[]{:S(2)}) %copy-start.1) | copy-done | bytes 327704
  4.9 1.6 %first.1 = (bf16[56,640]{1,0:T(8,128)(2,1)S(1)}, bf16[56,640]{1,0:T(8,128)(2,1)S(1)}) custom-call(s32[7]{0:T(128)S(1)} %stack.64.info_ref, bf16[16,8,1280]{2,1,0:T(8,128)(2,1)S(1)} %bitcast.26), custom_call_target="tpu_custom_call" | custom-call | flops 10000000000 | bytes 1 | tf_op jit(solution)/shard_map/first/pallas_call | solution.py:329
  6.6 4.3 %collective-permute-done.refs_1_ = bf16[56,640]{1,0:T(8,128)(2,1)S(1)} collective-permute-done((bf16[56,640]{1,0:T(8,128)(2,1)S(1)}, bf16[56,640]{1,0:T(8,128)(2,1)S(1)}, u32[]{:S(2)}, u32[]{:S(2)}) %collective-permute-start) | collective-permute-done | bytes 71712 | tf_op jit(solution)/shard_map/ppermute | solution.py:373
  10.9 0.6 %rows.1 = (bf16[24,1280]{1,0:T(8,128)(2,1)S(1)}, bf16[16,1280]{1,0:T(8,128)(2,1)S(1)}, f32[1,64]{1,0:T(1,128)S(1)}) custom-call(s32[7]{0:T(128)S(1)} %stack.64.info_ref, bf16[56,640]{1,0:T(8,128)(2,1)S(1)} %get-tuple-element.29.refs_0_, bf16[56,640]{1,0:T(8,128)(2,1)S(1)} %collective-permute-done.refs_1_, bf16[16,8,640]{2,1,0:T(8,128)(2,1)S(1)} %bitcast.23, ...), custom_call_target="tpu_custom_call" | custom-call | tf_op jit(solution)/shard_map/rows/pallas_call | solution.py:329
  11.6 0.6 %tiles.1 = (bf16[16,8,640]{2,1,0:T(8,128)(2,1)S(1)}, bf16[16,8,640]{2,1,0:T(8,128)(2,1)S(1)}) custom-call(s32[7]{0:T(128)S(1)} %stack.64.info_ref, bf16[16,8,1280]{2,1,0:T(8,128)(2,1)S(1)} %bitcast.27, bf16[3,3,640,640]{3,2,1,0:T(8,128)(2,1)S(1)} %bitcast.21), custom_call_target="tpu_custom_call" | custom-call | tf_op jit(solution)/shard_map/tiles/pallas_call | solution.py:329
  12.2 0.6 %collective-permute-done.3.near_h.refs_2_ = bf16[24,1280]{1,0:T(8,128)(2,1)S(1)} collective-permute-done((bf16[24,1280]{1,0:T(8,128)(2,1)S(1)}, bf16[24,1280]{1,0:T(8,128)(2,1)S(1)}, u32[]{:S(2)}, u32[]{:S(2)}) %collective-permute-start.3) | collective-permute-done | bytes 61472 | tf_op jit(solution)/shard_map/ppermute | solution.py:23
  13.0 1.3 %collective-permute-start.4 = (bf16[19,1280]{1,0:T(8,128)(2,1)S(1)}, bf16[19,1280]{1,0:T(8,128)(2,1)S(1)}, u32[]{:S(2)}, u32[]{:S(2)}) collective-permute-start(bf16[19,1280]{1,0:T(8,128)(2,1)S(1)} %pad_maximum_fusion), channel_id=1, source_target_pairs={{0,12},{4,8},{8,4},{12,0},{1,13},{5,9},{9,5},{13,1},{2,14},{6,10},... | collective-permute-start | bytes 145928 | tf_op jit(solution)/shard_map/ppermute | solution.py:23
  14.3 0.7 %columns.1 = (bf16[32,1280]{1,0:T(8,128)(2,1)S(1)}, bf16[32,1280]{1,0:T(8,128)(2,1)S(1)}) custom-call(s32[7]{0:T(128)S(1)} %stack.64.info_ref, bf16[56,640]{1,0:T(8,128)(2,1)S(1)} %get-tuple-element.29.refs_0_, bf16[56,640]{1,0:T(8,128)(2,1)S(1)} %collective-permute-done.refs_1_, bf16[16,8,640]{2,1,0:T(8,128)(2,1)S(1)} %bitcast.24, ...), custom_call_target="tpu_custom_call" | custom-call | tf_op jit(solution)/shard_map/columns/pallas_call | solution.py:329
  15.1 1.9 %collective-permute-done.4.across_h.refs_3_ = bf16[19,1280]{1,0:T(8,128)(2,1)S(1)} collective-permute-done((bf16[19,1280]{1,0:T(8,128)(2,1)S(1)}, bf16[19,1280]{1,0:T(8,128)(2,1)S(1)}, u32[]{:S(2)}, u32[]{:S(2)}) %collective-permute-start.4) | collective-permute-done | bytes 48672 | tf_op jit(solution)/shard_map/ppermute | solution.py:23
  17.2 0.6 %pack.1 = (bf16[40,1280]{1,0:T(8,128)(2,1)S(1)}, bf16[36,1280]{1,0:T(8,128)(2,1)S(1)}) custom-call(s32[7]{0:T(128)S(1)} %stack.64.info_ref, bf16[24,1280]{1,0:T(8,128)(2,1)S(1)} %collective-permute-done.3.near_h.refs_2_, bf16[19,1280]{1,0:T(8,128)(2,1)S(1)} %collective-permute-done.4.across_h.refs_3_, f32[1,64]{1,0:T(1,128)S(1)} %pad_maximum_fusion.3.stats_ref, ...), custom_call_target="tpu_custom_call" | custom-call | tf_op jit(solution)/shard_map/pack/pallas_call | solution.py:329
  17.8 1.6 %collective-permute-start.5 = (bf16[40,1280]{1,0:T(8,128)(2,1)S(1)}, bf16[40,1280]{1,0:T(8,128)(2,1)S(1)}, u32[]{:S(2)}, u32[]{:S(2)}) collective-permute-start(bf16[40,1280]{1,0:T(8,128)(2,1)S(1)} %get-tuple-element.35), channel_id=1, source_target_pairs={{0,1},{1,0},{2,3},{3,2},{4,5},{5,4},{6,7},{7,6},{8,9},{9,8},{10,11... | collective-permute-start | bytes 307208 | tf_op jit(solution)/shard_map/ppermute | solution.py:23
  19.5 0.6 %collective-permute-start.1 = (bf16[16,8,640]{2,1,0:T(8,128)(2,1)S(1)}, bf16[16,8,640]{2,1,0:T(8,128)(2,1)S(1)}, u32[]{:S(2)}, u32[]{:S(2)}) collective-permute-start(bf16[16,8,640]{2,1,0:T(8,128)(2,1)S(1)} %broadcast_add_fusion), channel_id=1, source_target_pairs={{0,16},{16,0},{1,17},{17,1},{2,18},{18,2},{3,19},{19,3},{4,20},{20... | collective-permute-start | bytes 491528 | tf_op jit(solution)/shard_map/ppermute | solution.py:373
  20.0 0.7 %collective-permute-start.7 = (bf16[36,1280]{1,0:T(8,128)(2,1)S(1)}, bf16[36,1280]{1,0:T(8,128)(2,1)S(1)}, u32[]{:S(2)}, u32[]{:S(2)}) collective-permute-start(bf16[36,1280]{1,0:T(8,128)(2,1)S(1)} %get-tuple-element.36), channel_id=1, source_target_pairs={{1,2},{2,1},{5,6},{6,5},{9,10},{10,9},{13,14},{14,13},{17,18},{18,... | collective-permute-start | bytes 276488 | tf_op jit(solution)/shard_map/ppermute | solution.py:23
  20.7 2.1 %collective-permute-done.5.refs_4_.near_w = bf16[40,1280]{1,0:T(8,128)(2,1)S(1)} collective-permute-done((bf16[40,1280]{1,0:T(8,128)(2,1)S(1)}, bf16[40,1280]{1,0:T(8,128)(2,1)S(1)}, u32[]{:S(2)}, u32[]{:S(2)}) %collective-permute-start.5) | collective-permute-done | bytes 102432 | tf_op jit(solution)/shard_map/ppermute | solution.py:23
  23.0 2.6 %collective-permute-start.6 = (f32[1,64]{1,0:T(1,128)S(1)}, f32[1,64]{1,0:T(1,128)S(1)}, u32[]{:S(2)}, u32[]{:S(2)}) collective-permute-start(f32[1,64]{1,0:T(1,128)S(1)} %pad_maximum_fusion.4), channel_id=1, source_target_pairs={{0,2},{1,3},{2,0},{3,1},{4,6},{5,7},{6,4},{7,5},{8,10},{9,11},{10,... | collective-permute-start | bytes 776 | tf_op jit(solution)/shard_map/ppermute | solution.py:23
  25.6 3.0 %conv_backward.1.refs_5_ = f32[16,2,8,640]{3,2,1,0:T(8,128)S(1)} custom-call(s32[7]{0:T(128)S(1)} %stack.64.info_ref, bf16[16,8,640]{2,1,0:T(8,128)(2,1)S(1)} %bitcast.25, bf16[16,8,640]{2,1,0:T(8,128)(2,1)S(1)} %collective-permute-done.2.refs_3_.refs_1_, bf16[24,1280]{1,0:T(8,128)(2,1)S(1)} %collective-permute-done.3.near_h.refs_2_, ...), custom_call_target="tpu_custom_call" | custom-call | tf_op jit(solution)/shard_map/conv_backward/pallas_call | solution.py:329
  28.7 1.4 %terms.1 = (f32[4,16]{1,0:T(4,128)S(1)}, f32[4,16]{1,0:T(4,128)S(1)}, f32[16,8,640]{2,1,0:T(8,128)S(1)}, bf16[1,16,8,640]{3,2,1,0:T(8,128)(2,1)S(1)}, f32[16,2,1...) custom-call(s32[7]{0:T(128)S(1)} %stack.64.info_ref, bf16[16,8,640]{2,1,0:T(8,128)(2,1)S(1)} %get-tuple-element.26.refs_0_, ...), custom_call_target="tpu_custom_call" | custom-call | tf_op jit(solution)/shard_map/terms/pallas_call | solution.py:329
  30.1 0.7 %collective-permute-start.8 = (f32[4,16]{1,0:T(4,128)S(1)}, f32[4,16]{1,0:T(4,128)S(1)}, u32[]{:S(2)}, u32[]{:S(2)}) collective-permute-start(f32[4,16]{1,0:T(4,128)S(1)} %get-tuple-element.38), channel_id=1, source_target_pairs={{16,0},{0,16},{17,1},{1,17},{18,2},{2,18},{19,3},{3,19},{20,4},{4,... | collective-permute-start | bytes 776 | tf_op jit(solution)/shard_map/ppermute | solution.py:454
  30.8 2.3 %conv_forward.1 = (f32[16,8,384]{2,1,0:T(8,128)S(1)}, bf16[1,16,8,384]{3,2,1,0:T(8,128)(2,1)S(1)}, bf16[3,18,16,640]{3,2,1,0:T(8,128)(2,1)S(1)}) custom-call(s32[7]{0:T(128)S(1)} %stack.64.info_ref, f32[16,2,16,640]{3,2,1,0:T(8,128)S(1)} %get-tuple-element.39.given_ref, f32[6,640]{1,0:T(8,128)S(1)} %get-tuple-element.40.scales_ref, ...), custom_call_target="tpu_custom_call" | custom-call | tf_op jit(solution)/shard_map/conv_forward/pallas_call | solution.py:329
  33.1 0.6 %collective-permute-done.8 = f32[4,16]{1,0:T(4,128)S(1)} collective-permute-done((f32[4,16]{1,0:T(4,128)S(1)}, f32[4,16]{1,0:T(4,128)S(1)}, u32[]{:S(2)}, u32[]{:S(2)}) %collective-permute-start.8) | collective-permute-done | bytes 288 | tf_op jit(solution)/shard_map/ppermute | solution.py:454
  33.7 0.9 %collective-permute-start.13 = (bf16[16,8,640]{2,1,0:T(8,128)(2,1)S(1)}, bf16[16,8,640]{2,1,0:T(8,128)(2,1)S(1)}, u32[]{:S(2)}, u32[]{:S(2)}) collective-permute-start(bf16[16,8,640]{2,1,0:T(8,128)(2,1)S(1)} %bitcast.32), channel_id=1, source_target_pairs={{16,0},{0,16},{17,1},{1,17},{18,2},{2,18},{19,3},{3,19},{20,4},{4,... | collective-permute-start | bytes 491528 | tf_op jit(solution)/shard_map/ppermute | solution.py:454
  34.6 0.3 collective-permute-done.9
  34.9 1.5 %collective-permute-start.10 = (f32[2,2,16]{2,1,0:T(2,128)S(1)}, f32[2,2,16]{2,1,0:T(2,128)S(1)}, u32[]{:S(2)}, u32[]{:S(2)}) collective-permute-start(f32[2,2,16]{2,1,0:T(2,128)S(1)} %fusion.14.after_ref), channel_id=1, source_target_pairs={{0,8},{4,12},{8,0},{12,4},{1,9},{5,13},{9,1},{13,5},{2,10},{6,14},... | collective-permute-start | bytes 776 | tf_op jit(solution)/shard_map/ppermute | solution.py:23
  36.4 1.1 %conv_forward2.1 = (f32[16,8,256]{2,1,0:T(8,128)S(1)}, bf16[1,16,8,256]{3,2,1,0:T(8,128)(2,1)S(1)}) custom-call(bf16[3,18,16,640]{3,2,1,0:T(8,128)(2,1)S(1)} %get-tuple-element.42.windows_ref, bf16[3,3,640,640]{3,2,1,0:T(8,128)(2,1)S(1)} %bitcast.21, f32[2,2,16]{2,1,0:T(2,128)S(1)} %fusion.14.after_ref), custom_call_target="tpu_custom_call" | custom-call | tf_op jit(solution)/shard_map/conv_forward2/pallas_call | solution.py:329
  37.5 1.0 %collective-permute-done.10 = f32[2,2,16]{2,1,0:T(2,128)S(1)} collective-permute-done((f32[2,2,16]{2,1,0:T(2,128)S(1)}, f32[2,2,16]{2,1,0:T(2,128)S(1)}, u32[]{:S(2)}, u32[]{:S(2)}) %collective-permute-start.10) | collective-permute-done | bytes 288 | tf_op jit(solution)/shard_map/ppermute | solution.py:23
  38.5 2.6 %collective-permute-start.11 = (f32[2,2,16]{2,1,0:T(2,128)S(1)}, f32[2,2,16]{2,1,0:T(2,128)S(1)}, u32[]{:S(2)}, u32[]{:S(2)}) collective-permute-start(f32[2,2,16]{2,1,0:T(2,128)S(1)} %add_add_fusion), channel_id=1, source_target_pairs={{0,1},{1,0},{2,3},{3,2},{4,5},{5,4},{6,7},{7,6},{8,9},{9,8},{10,11... | collective-permute-start | bytes 776 | tf_op jit(solution)/shard_map/ppermute | solution.py:23
  41.1 1.0 %collective-permute-start.14 = (bf16[16,8,384]{2,1,0:T(8,128)(2,1)S(1)}, bf16[16,8,384]{2,1,0:T(8,128)(2,1)S(1)}, u32[]{:S(2)}, u32[]{:S(2)}) collective-permute-start(bf16[16,8,384]{2,1,0:T(8,128)(2,1)S(1)} %bitcast.33), channel_id=1, source_target_pairs={{16,0},{0,16},{17,1},{1,17},{18,2},{2,18},{19,3},{3,19},{20,4},{4,... | collective-permute-start | bytes 294920 | tf_op jit(solution)/shard_map/ppermute | solution.py:478
  42.1 1.0 %collective-permute-start.15 = (bf16[16,8,256]{2,1,0:T(8,128)(2,1)S(1)}, bf16[16,8,256]{2,1,0:T(8,128)(2,1)S(1)}, u32[]{:S(2)}, u32[]{:S(2)}) collective-permute-start(bf16[16,8,256]{2,1,0:T(8,128)(2,1)S(1)} %bitcast.34), channel_id=1, source_target_pairs={{16,0},{0,16},{17,1},{1,17},{18,2},{2,18},{19,3},{3,19},{20,4},{4,... | collective-permute-start | bytes 196616 | tf_op jit(solution)/shard_map/ppermute | solution.py:478
  43.2 3.0 %collective-permute-start.12 = (f32[2,2,16]{2,1,0:T(2,128)S(1)}, f32[2,2,16]{2,1,0:T(2,128)S(1)}, u32[]{:S(2)}, u32[]{:S(2)}) collective-permute-start(f32[2,2,16]{2,1,0:T(2,128)S(1)} %add.136), channel_id=1, source_target_pairs={{0,2},{1,3},{2,0},{3,1},{4,6},{5,7},{6,4},{7,5},{8,10},{9,11},{10,... | collective-permute-start | bytes 776 | tf_op jit(solution)/shard_map/ppermute | solution.py:23
  46.2 1.6 %collective-permute-done.12 = f32[2,2,16]{2,1,0:T(2,128)S(1)} collective-permute-done((f32[2,2,16]{2,1,0:T(2,128)S(1)}, f32[2,2,16]{2,1,0:T(2,128)S(1)}, u32[]{:S(2)}, u32[]{:S(2)}) %collective-permute-start.12) | collective-permute-done | bytes 288 | tf_op jit(solution)/shard_map/ppermute | solution.py:23
  47.7 1.7 %finish.1 = (bf16[16,8,640]{2,1,0:T(8,128)(2,1)}, bf16[16,8,1280]{2,1,0:T(8,128)(2,1)}) custom-call(s32[7]{0:T(128)S(1)} %stack.64.info_ref, bf16[16,8,1280]{2,1,0:T(8,128)(2,1)S(1)} %bitcast.28, f32[2,4,16]{2,1,0:T(4,128)S(1)} %pad_maximum_fusion.1.small_ref, f32[2,2,16]{2,1,0:T(2,128)S(1)} %add.137.sums_ref, f32[640]{0:T(1024)S(1)} %copy-done.5, ...), custom_call_target="tpu_custom_call" | custom-call | tf_op jit(solution)/shard_map/finish/pallas_call | solution.py:329
  (55 shorter events, 1.0 us)
Async XLA Ops:
  0.6 10.3 %collective-permute-start.2 = (bf16[16,8,640]{2,1,0:T(8,128)(2,1)}, bf16[16,8,640]{2,1,0:T(8,128)(2,1)S(1)}, u32[]{:S(2)}, u32[]{:S(2)}) collective-permute-start(bf16[16,8,640]{2,1,0:T(8,128)(2,1)} %bitcast.22), channel_id=1, source_target_pairs={{0,16},{16,0},{1,17},{17,1},{2,18},{18,2},{3,19},{19,3},{4,20},{20... | collective-permute-start | bytes 491528 | tf_op jit(solution)/shard_map/ppermute | solution.py:373
  3.7 7.8 %slice-start = ((s8[7372800]{0:T(1024)(128)(4,1)}), s8[4194304]{0:T(1024)(128)(4,1)S(1)}, s32[]{:S(2)}) async-start(s8[7372800]{0:T(1024)(128)(4,1)} %bitcast.20), calls=%async_computation | async-start | bytes 8388608
  3.7 1.1 %copy-start.1 = (bf16[1,16,8,1280]{3,2,1,0:T(8,128)(2,1)S(1)}, bf16[1,16,8,1280]{3,2,1,0:T(8,128)(2,1)}, u32[]{:S(2)}) copy-start(bf16[1,16,8,1280]{3,2,1,0:T(8,128)(2,1)} %param.6) | copy-start | bytes 983044
  4.9 6.0 %copy-start = (bf16[1,16,8,640]{3,2,1,0:T(8,128)(2,1)S(1)}, bf16[1,16,8,640]{3,2,1,0:T(8,128)(2,1)}, u32[]{:S(2)}) copy-start(bf16[1,16,8,640]{3,2,1,0:T(8,128)(2,1)} %param.11) | copy-start | bytes 491524
  4.9 6.7 %slice-start.1 = ((s8[7372800]{0:T(1024)(128)(4,1)}), s8[3178496]{0:T(1024)(128)(4,1)S(1)}, s32[]{:S(2)}) async-start(s8[7372800]{0:T(1024)(128)(4,1)} %bitcast.20), calls=%async_computation.1 | async-start | bytes 6356992
  4.9 6.7 %copy-start.2 = (bf16[1,16,8,1280]{3,2,1,0:T(8,128)(2,1)S(1)}, bf16[1,16,8,1280]{3,2,1,0:T(8,128)(2,1)}, u32[]{:S(2)}) copy-start(bf16[1,16,8,1280]{3,2,1,0:T(8,128)(2,1)} %param.6) | copy-start | bytes 983044
  6.5 4.4 %collective-permute-start = (bf16[56,640]{1,0:T(8,128)(2,1)S(1)}, bf16[56,640]{1,0:T(8,128)(2,1)S(1)}, u32[]{:S(2)}, u32[]{:S(2)}) collective-permute-start(bf16[56,640]{1,0:T(8,128)(2,1)S(1)} %get-tuple-element.28), channel_id=1, source_target_pairs={{0,16},{16,0},{1,17},{17,1},{2,18},{18,2},{3,19},{19,3},{4,20},{20... | collective-permute-start | bytes 215048 | tf_op jit(solution)/shard_map/ppermute | solution.py:373
  11.5 1.3 %collective-permute-start.3 = (bf16[24,1280]{1,0:T(8,128)(2,1)S(1)}, bf16[24,1280]{1,0:T(8,128)(2,1)S(1)}, u32[]{:S(2)}, u32[]{:S(2)}) collective-permute-start(bf16[24,1280]{1,0:T(8,128)(2,1)S(1)} %get-tuple-element.31), channel_id=1, source_target_pairs={{0,4},{4,0},{8,12},{12,8},{1,5},{5,1},{9,13},{13,9},{2,6},{6,2},{1... | collective-permute-start | bytes 184328 | tf_op jit(solution)/shard_map/ppermute | solution.py:23
  13.0 4.0 %collective-permute-start.4 = (bf16[19,1280]{1,0:T(8,128)(2,1)S(1)}, bf16[19,1280]{1,0:T(8,128)(2,1)S(1)}, u32[]{:S(2)}, u32[]{:S(2)}) collective-permute-start(bf16[19,1280]{1,0:T(8,128)(2,1)S(1)} %pad_maximum_fusion), channel_id=1, source_target_pairs={{0,12},{4,8},{8,4},{12,0},{1,13},{5,9},{9,5},{13,1},{2,14},{6,10},... | collective-permute-start | bytes 145928 | tf_op jit(solution)/shard_map/ppermute | solution.py:23
  17.8 5.0 %collective-permute-start.5 = (bf16[40,1280]{1,0:T(8,128)(2,1)S(1)}, bf16[40,1280]{1,0:T(8,128)(2,1)S(1)}, u32[]{:S(2)}, u32[]{:S(2)}) collective-permute-start(bf16[40,1280]{1,0:T(8,128)(2,1)S(1)} %get-tuple-element.35), channel_id=1, source_target_pairs={{0,1},{1,0},{2,3},{3,2},{4,5},{5,4},{6,7},{7,6},{8,9},{9,8},{10,11... | collective-permute-start | bytes 307208 | tf_op jit(solution)/shard_map/ppermute | solution.py:23
  19.5 6.1 %collective-permute-start.1 = (bf16[16,8,640]{2,1,0:T(8,128)(2,1)S(1)}, bf16[16,8,640]{2,1,0:T(8,128)(2,1)S(1)}, u32[]{:S(2)}, u32[]{:S(2)}) collective-permute-start(bf16[16,8,640]{2,1,0:T(8,128)(2,1)S(1)} %broadcast_add_fusion), channel_id=1, source_target_pairs={{0,16},{16,0},{1,17},{17,1},{2,18},{18,2},{3,19},{19,3},{4,20},{20... | collective-permute-start | bytes 491528 | tf_op jit(solution)/shard_map/ppermute | solution.py:373
  20.0 5.6 %collective-permute-start.7 = (bf16[36,1280]{1,0:T(8,128)(2,1)S(1)}, bf16[36,1280]{1,0:T(8,128)(2,1)S(1)}, u32[]{:S(2)}, u32[]{:S(2)}) collective-permute-start(bf16[36,1280]{1,0:T(8,128)(2,1)S(1)} %get-tuple-element.36), channel_id=1, source_target_pairs={{1,2},{2,1},{5,6},{6,5},{9,10},{10,9},{13,14},{14,13},{17,18},{18,... | collective-permute-start | bytes 276488 | tf_op jit(solution)/shard_map/ppermute | solution.py:23
  23.0 5.8 %copy-start.3 = (f32[1280]{0:T(1024)S(1)}, f32[1280]{0:T(1024)}, u32[]{:S(2)}) copy-start(f32[1280]{0:T(1024)} %refs_3_.1) | copy-start | bytes 15364
  23.0 5.8 %copy-start.4 = (f32[1280]{0:T(1024)S(1)}, f32[1280]{0:T(1024)}, u32[]{:S(2)}) copy-start(f32[1280]{0:T(1024)} %refs_4_.1) | copy-start | bytes 15364
  23.0 5.6 %collective-permute-start.6 = (f32[1,64]{1,0:T(1,128)S(1)}, f32[1,64]{1,0:T(1,128)S(1)}, u32[]{:S(2)}, u32[]{:S(2)}) collective-permute-start(f32[1,64]{1,0:T(1,128)S(1)} %pad_maximum_fusion.4), channel_id=1, source_target_pairs={{0,2},{1,3},{2,0},{3,1},{4,6},{5,7},{6,4},{7,5},{8,10},{9,11},{10,... | collective-permute-start | bytes 776 | tf_op jit(solution)/shard_map/ppermute | solution.py:23
  30.1 3.6 %collective-permute-start.8 = (f32[4,16]{1,0:T(4,128)S(1)}, f32[4,16]{1,0:T(4,128)S(1)}, u32[]{:S(2)}, u32[]{:S(2)}) collective-permute-start(f32[4,16]{1,0:T(4,128)S(1)} %get-tuple-element.38), channel_id=1, source_target_pairs={{16,0},{0,16},{17,1},{1,17},{18,2},{2,18},{19,3},{3,19},{20,4},{4,... | collective-permute-start | bytes 776 | tf_op jit(solution)/shard_map/ppermute | solution.py:454
  33.7 1.2 %collective-permute-start.9 = (f32[2,2,16]{2,1,0:T(2,128)S(1)}, f32[2,2,16]{2,1,0:T(2,128)S(1)}, u32[]{:S(2)}, u32[]{:S(2)}) collective-permute-start(f32[2,2,16]{2,1,0:T(2,128)S(1)} %fusion.7), channel_id=1, source_target_pairs={{0,4},{4,0},{8,12},{12,8},{1,5},{5,1},{9,13},{13,9},{2,6},{6,2},{1... | collective-permute-start | bytes 776 | tf_op jit(solution)/shard_map/ppermute | solution.py:23
  33.7 14.0 %collective-permute-start.13 = (bf16[16,8,640]{2,1,0:T(8,128)(2,1)S(1)}, bf16[16,8,640]{2,1,0:T(8,128)(2,1)S(1)}, u32[]{:S(2)}, u32[]{:S(2)}) collective-permute-start(bf16[16,8,640]{2,1,0:T(8,128)(2,1)S(1)} %bitcast.32), channel_id=1, source_target_pairs={{16,0},{0,16},{17,1},{1,17},{18,2},{2,18},{19,3},{3,19},{20,4},{4,... | collective-permute-start | bytes 491528 | tf_op jit(solution)/shard_map/ppermute | solution.py:454
  34.9 3.6 %collective-permute-start.10 = (f32[2,2,16]{2,1,0:T(2,128)S(1)}, f32[2,2,16]{2,1,0:T(2,128)S(1)}, u32[]{:S(2)}, u32[]{:S(2)}) collective-permute-start(f32[2,2,16]{2,1,0:T(2,128)S(1)} %fusion.14.after_ref), channel_id=1, source_target_pairs={{0,8},{4,12},{8,0},{12,4},{1,9},{5,13},{9,1},{13,5},{2,10},{6,14},... | collective-permute-start | bytes 776 | tf_op jit(solution)/shard_map/ppermute | solution.py:23
  36.4 11.4 %copy-start.5 = (f32[640]{0:T(1024)S(1)}, f32[640]{0:T(1024)}, u32[]{:S(2)}) copy-start(f32[640]{0:T(1024)} %bias_ref.1) | copy-start | bytes 7684
  38.5 4.7 %collective-permute-start.11 = (f32[2,2,16]{2,1,0:T(2,128)S(1)}, f32[2,2,16]{2,1,0:T(2,128)S(1)}, u32[]{:S(2)}, u32[]{:S(2)}) collective-permute-start(f32[2,2,16]{2,1,0:T(2,128)S(1)} %add_add_fusion), channel_id=1, source_target_pairs={{0,1},{1,0},{2,3},{3,2},{4,5},{5,4},{6,7},{7,6},{8,9},{9,8},{10,11... | collective-permute-start | bytes 776 | tf_op jit(solution)/shard_map/ppermute | solution.py:23
  41.1 6.6 %collective-permute-start.14 = (bf16[16,8,384]{2,1,0:T(8,128)(2,1)S(1)}, bf16[16,8,384]{2,1,0:T(8,128)(2,1)S(1)}, u32[]{:S(2)}, u32[]{:S(2)}) collective-permute-start(bf16[16,8,384]{2,1,0:T(8,128)(2,1)S(1)} %bitcast.33), channel_id=1, source_target_pairs={{16,0},{0,16},{17,1},{1,17},{18,2},{2,18},{19,3},{3,19},{20,4},{4,... | collective-permute-start | bytes 294920 | tf_op jit(solution)/shard_map/ppermute | solution.py:478
  42.1 5.6 %collective-permute-start.15 = (bf16[16,8,256]{2,1,0:T(8,128)(2,1)S(1)}, bf16[16,8,256]{2,1,0:T(8,128)(2,1)S(1)}, u32[]{:S(2)}, u32[]{:S(2)}) collective-permute-start(bf16[16,8,256]{2,1,0:T(8,128)(2,1)S(1)} %bitcast.34), channel_id=1, source_target_pairs={{16,0},{0,16},{17,1},{1,17},{18,2},{2,18},{19,3},{3,19},{20,4},{4,... | collective-permute-start | bytes 196616 | tf_op jit(solution)/shard_map/ppermute | solution.py:478
  43.2 4.6 %collective-permute-start.12 = (f32[2,2,16]{2,1,0:T(2,128)S(1)}, f32[2,2,16]{2,1,0:T(2,128)S(1)}, u32[]{:S(2)}, u32[]{:S(2)}) collective-permute-start(f32[2,2,16]{2,1,0:T(2,128)S(1)} %add.136), channel_id=1, source_target_pairs={{0,2},{1,3},{2,0},{3,1},{4,6},{5,7},{6,4},{7,5},{8,10},{9,11},{10,... | collective-permute-start | bytes 776 | tf_op jit(solution)/shard_map/ppermute | solution.py:23

commit v8 on v7

--- a/solution.py
+++ b/solution.py
@@ -159,7 +159,6 @@
     both = near_ref.shape[1]
     near_rows = near_h[...].astype(F32)
     across_rows = jnp.where((info_ref[UP] > 0) & (info_ref[DOWN] > 0), across_h[...].astype(F32), 0.0)
-    columns = [ref[...].astype(F32) for ref in ends]
     stats = jnp.concatenate([p.astype(F32) for p in three_parts(stats_ref[...])], 0)
     stats = jnp.concatenate([stats, jnp.zeros((3, both - stats.shape[1]), F32)], 1)
     for half, ref, pick_last in ((0, near_ref, even_w), (1, across_ref, jnp.logical_not(even_w))):
@@ -168,11 +167,13 @@
             for k in range(parts):
                 first, last = t[k * cols : k * cols + 1], t[(k + 1) * cols - 1 : (k + 1) * cols]
                 corners.append(jnp.where(pick_last, last, first))
-        pieces = [v[half * rows : (half + 1) * rows] for v in columns] + corners + ([stats] if half == 0 else [])
+        for k in range(parts):
+            ref[k * rows : (k + 1) * rows, :] = ends[k][half * rows : (half + 1) * rows, :]
+        pieces = corners + ([stats] if half == 0 else [])
         used = parts * (rows + 2) + (3 if half == 0 else 0)
         if ref.shape[0] > used:
             pieces.append(jnp.zeros((ref.shape[0] - used, both), F32))
-        ref[...] = jnp.concatenate(pieces, 0).astype(BF16)
+        ref[parts * rows :, :] = jnp.concatenate(pieces, 0).astype(BF16)
 
 
 def halos(parts, rows, cols, info_ref, near_h, across_h, near_w, across_w, lanes):
@@ -454,7 +455,7 @@
     to_owners = lambda values: [lax.ppermute(v, "dp", [(j, i) for i, j in pairs]) for v, pairs in zip(values, peers)]
     small = jnp.stack([small[0], *to_owners(small[1:])], 0)
     gx = to_owners([gx_other[k] for k in range(parts - 1)])
-    start = outs * 3 // 5 // 128 * 128
+    start = outs * 2 // 5 // 128 * 128
     parts_of = lambda size: [sds((rows, cols, size), F32), sds((parts - 1, rows, cols, size), BF16)]
     conv_own, conv_other, act_windows = call(
         functools.partial(forward_kernel, parts),

time: 49.6 us -> 49.6 us (level)
  no operation moved by 1% of the time
where the time goes in v8:
time: 49.6 us; the launch traced here: 49.5 us
  starting transfers between devices  20.5 us (41%)
  Pallas kernels  13.7 us (28%)
  waiting for transfers between devices  12.4 us (25%)
  local copies, waits for them, and re-layouts  1.23 us (2%)
  between operations  0.81 us (2%)
  other arithmetic  0.77 us (2%)
    pallas_call x10, Pallas kernels, call(): pl.pallas_call(kernel, out_shape=outs, in_specs=[spec(i) for i in range(l...  13.7 us
    ppermute x9, starting transfers between devices, exchange(): return lax.ppermute(value, axis, pairs)  13.4 us
    ppermute x9, waiting for transfers between devices, exchange(): return lax.ppermute(value, axis, pairs)  7.16 us
    ppermute x3, waiting for transfers between devices, body(): lax.ppermute(v, 'dp', pairs)  4.29 us
    ppermute x3, starting transfers between devices, body(): lax.ppermute(v, 'dp', pairs)  3.72 us
    ppermute x2, starting transfers between devices, body(): conv += [lax.ppermute(v[k], 'dp', back) for v in (conv_other, conv_other2)]  2.03 us
    ppermute x2, starting transfers between devices, body(): lax.ppermute(v, 'dp', [(j, i) for i, j in pairs])  1.43 us
    unnamed x16, local copies, waits for them, and re-layouts  1.15 us
  transfers between devices with their start and end apart: 16, of which 8 were waited for; matrix products, arithmetic and copies ran while one was open for 1% of the time, Pallas kernels for 19%

profile of v8, /device:TPU:0, one launch (start us, length us, event | category | flops | bytes accessed | tf_op | source)
XLA Modules:
  0.0 49.5 jit_solution(1892157107980192578)
XLA Ops:
  0.6 3.0 %collective-permute-start.2 = (bf16[16,8,640]{2,1,0:T(8,128)(2,1)}, bf16[16,8,640]{2,1,0:T(8,128)(2,1)S(1)}, u32[]{:S(2)}, u32[]{:S(2)}) collective-permute-start(bf16[16,8,640]{2,1,0:T(8,128)(2,1)} %bitcast.22), channel_id=1, source_target_pairs={{0,16},{16,0},{1,17},{17,1},{2,18},{18,2},{3,19},{19,3},{4,20},{20... | collective-permute-start | bytes 491528 | tf_op jit(solution)/shard_map/ppermute | solution.py:374
  3.8 1.1 %copy-done.1 = bf16[1,16,8,1280]{3,2,1,0:T(8,128)(2,1)S(1)} copy-done((bf16[1,16,8,1280]{3,2,1,0:T(8,128)(2,1)S(1)}, bf16[1,16,8,1280]{3,2,1,0:T(8,128)(2,1)}, u32[]{:S(2)}) %copy-start.1) | copy-done | bytes 327704
  4.9 1.6 %first.1 = (bf16[56,640]{1,0:T(8,128)(2,1)S(1)}, bf16[56,640]{1,0:T(8,128)(2,1)S(1)}) custom-call(s32[7]{0:T(128)S(1)} %stack.64.info_ref, bf16[16,8,1280]{2,1,0:T(8,128)(2,1)S(1)} %bitcast.26), custom_call_target="tpu_custom_call" | custom-call | flops 10000000000 | bytes 1 | tf_op jit(solution)/shard_map/first/pallas_call | solution.py:330
  6.6 4.3 %collective-permute-done.refs_1_ = bf16[56,640]{1,0:T(8,128)(2,1)S(1)} collective-permute-done((bf16[56,640]{1,0:T(8,128)(2,1)S(1)}, bf16[56,640]{1,0:T(8,128)(2,1)S(1)}, u32[]{:S(2)}, u32[]{:S(2)}) %collective-permute-start) | collective-permute-done | bytes 71712 | tf_op jit(solution)/shard_map/ppermute | solution.py:374
  10.9 0.6 %rows.1 = (bf16[24,1280]{1,0:T(8,128)(2,1)S(1)}, bf16[16,1280]{1,0:T(8,128)(2,1)S(1)}, f32[1,64]{1,0:T(1,128)S(1)}) custom-call(s32[7]{0:T(128)S(1)} %stack.64.info_ref, bf16[56,640]{1,0:T(8,128)(2,1)S(1)} %get-tuple-element.29.refs_0_, bf16[56,640]{1,0:T(8,128)(2,1)S(1)} %collective-permute-done.refs_1_, bf16[16,8,640]{2,1,0:T(8,128)(2,1)S(1)} %bitcast.23, ...), custom_call_target="tpu_custom_call" | custom-call | tf_op jit(solution)/shard_map/rows/pallas_call | solution.py:330
  11.6 0.6 %tiles.1 = (bf16[16,8,640]{2,1,0:T(8,128)(2,1)S(1)}, bf16[16,8,640]{2,1,0:T(8,128)(2,1)S(1)}) custom-call(s32[7]{0:T(128)S(1)} %stack.64.info_ref, bf16[16,8,1280]{2,1,0:T(8,128)(2,1)S(1)} %bitcast.27, bf16[3,3,640,640]{3,2,1,0:T(8,128)(2,1)S(1)} %bitcast.21), custom_call_target="tpu_custom_call" | custom-call | tf_op jit(solution)/shard_map/tiles/pallas_call | solution.py:330
  12.2 0.6 %collective-permute-done.3.near_h.refs_2_ = bf16[24,1280]{1,0:T(8,128)(2,1)S(1)} collective-permute-done((bf16[24,1280]{1,0:T(8,128)(2,1)S(1)}, bf16[24,1280]{1,0:T(8,128)(2,1)S(1)}, u32[]{:S(2)}, u32[]{:S(2)}) %collective-permute-start.3) | collective-permute-done | bytes 61472 | tf_op jit(solution)/shard_map/ppermute | solution.py:23
  13.0 1.3 %collective-permute-start.4 = (bf16[19,1280]{1,0:T(8,128)(2,1)S(1)}, bf16[19,1280]{1,0:T(8,128)(2,1)S(1)}, u32[]{:S(2)}, u32[]{:S(2)}) collective-permute-start(bf16[19,1280]{1,0:T(8,128)(2,1)S(1)} %pad_maximum_fusion), channel_id=1, source_target_pairs={{0,12},{4,8},{8,4},{12,0},{1,13},{5,9},{9,5},{13,1},{2,14},{6,10},... | collective-permute-start | bytes 145928 | tf_op jit(solution)/shard_map/ppermute | solution.py:23
  14.3 0.7 %columns.1 = (bf16[32,1280]{1,0:T(8,128)(2,1)S(1)}, bf16[32,1280]{1,0:T(8,128)(2,1)S(1)}) custom-call(s32[7]{0:T(128)S(1)} %stack.64.info_ref, bf16[56,640]{1,0:T(8,128)(2,1)S(1)} %get-tuple-element.29.refs_0_, bf16[56,640]{1,0:T(8,128)(2,1)S(1)} %collective-permute-done.refs_1_, bf16[16,8,640]{2,1,0:T(8,128)(2,1)S(1)} %bitcast.24, ...), custom_call_target="tpu_custom_call" | custom-call | tf_op jit(solution)/shard_map/columns/pallas_call | solution.py:330
  15.1 1.9 %collective-permute-done.4.across_h.refs_3_ = bf16[19,1280]{1,0:T(8,128)(2,1)S(1)} collective-permute-done((bf16[19,1280]{1,0:T(8,128)(2,1)S(1)}, bf16[19,1280]{1,0:T(8,128)(2,1)S(1)}, u32[]{:S(2)}, u32[]{:S(2)}) %collective-permute-start.4) | collective-permute-done | bytes 48672 | tf_op jit(solution)/shard_map/ppermute | solution.py:23
  17.2 0.6 %pack.1 = (bf16[40,1280]{1,0:T(8,128)(2,1)S(1)}, bf16[36,1280]{1,0:T(8,128)(2,1)S(1)}) custom-call(s32[7]{0:T(128)S(1)} %stack.64.info_ref, bf16[24,1280]{1,0:T(8,128)(2,1)S(1)} %collective-permute-done.3.near_h.refs_2_, bf16[19,1280]{1,0:T(8,128)(2,1)S(1)} %collective-permute-done.4.across_h.refs_3_, f32[1,64]{1,0:T(1,128)S(1)} %pad_maximum_fusion.3.stats_ref, ...), custom_call_target="tpu_custom_call" | custom-call | tf_op jit(solution)/shard_map/pack/pallas_call | solution.py:330
  17.8 1.6 %collective-permute-start.5 = (bf16[40,1280]{1,0:T(8,128)(2,1)S(1)}, bf16[40,1280]{1,0:T(8,128)(2,1)S(1)}, u32[]{:S(2)}, u32[]{:S(2)}) collective-permute-start(bf16[40,1280]{1,0:T(8,128)(2,1)S(1)} %get-tuple-element.35), channel_id=1, source_target_pairs={{0,1},{1,0},{2,3},{3,2},{4,5},{5,4},{6,7},{7,6},{8,9},{9,8},{10,11... | collective-permute-start | bytes 307208 | tf_op jit(solution)/shard_map/ppermute | solution.py:23
  19.5 0.6 %collective-permute-start.1 = (bf16[16,8,640]{2,1,0:T(8,128)(2,1)S(1)}, bf16[16,8,640]{2,1,0:T(8,128)(2,1)S(1)}, u32[]{:S(2)}, u32[]{:S(2)}) collective-permute-start(bf16[16,8,640]{2,1,0:T(8,128)(2,1)S(1)} %broadcast_add_fusion), channel_id=1, source_target_pairs={{0,16},{16,0},{1,17},{17,1},{2,18},{18,2},{3,19},{19,3},{4,20},{20... | collective-permute-start | bytes 491528 | tf_op jit(solution)/shard_map/ppermute | solution.py:374
  20.0 0.7 %collective-permute-start.7 = (bf16[36,1280]{1,0:T(8,128)(2,1)S(1)}, bf16[36,1280]{1,0:T(8,128)(2,1)S(1)}, u32[]{:S(2)}, u32[]{:S(2)}) collective-permute-start(bf16[36,1280]{1,0:T(8,128)(2,1)S(1)} %get-tuple-element.36), channel_id=1, source_target_pairs={{1,2},{2,1},{5,6},{6,5},{9,10},{10,9},{13,14},{14,13},{17,18},{18,... | collective-permute-start | bytes 276488 | tf_op jit(solution)/shard_map/ppermute | solution.py:23
  20.7 2.1 %collective-permute-done.5.refs_4_.near_w = bf16[40,1280]{1,0:T(8,128)(2,1)S(1)} collective-permute-done((bf16[40,1280]{1,0:T(8,128)(2,1)S(1)}, bf16[40,1280]{1,0:T(8,128)(2,1)S(1)}, u32[]{:S(2)}, u32[]{:S(2)}) %collective-permute-start.5) | collective-permute-done | bytes 102432 | tf_op jit(solution)/shard_map/ppermute | solution.py:23
  23.0 2.6 %collective-permute-start.6 = (f32[1,64]{1,0:T(1,128)S(1)}, f32[1,64]{1,0:T(1,128)S(1)}, u32[]{:S(2)}, u32[]{:S(2)}) collective-permute-start(f32[1,64]{1,0:T(1,128)S(1)} %pad_maximum_fusion.4), channel_id=1, source_target_pairs={{0,2},{1,3},{2,0},{3,1},{4,6},{5,7},{6,4},{7,5},{8,10},{9,11},{10,... | collective-permute-start | bytes 776 | tf_op jit(solution)/shard_map/ppermute | solution.py:23
  25.6 3.0 %conv_backward.1.refs_5_ = f32[16,2,8,640]{3,2,1,0:T(8,128)S(1)} custom-call(s32[7]{0:T(128)S(1)} %stack.64.info_ref, bf16[16,8,640]{2,1,0:T(8,128)(2,1)S(1)} %bitcast.25, bf16[16,8,640]{2,1,0:T(8,128)(2,1)S(1)} %collective-permute-done.2.refs_3_.refs_1_, bf16[24,1280]{1,0:T(8,128)(2,1)S(1)} %collective-permute-done.3.near_h.refs_2_, ...), custom_call_target="tpu_custom_call" | custom-call | tf_op jit(solution)/shard_map/conv_backward/pallas_call | solution.py:330
  28.7 1.4 %terms.1 = (f32[4,16]{1,0:T(4,128)S(1)}, f32[4,16]{1,0:T(4,128)S(1)}, f32[16,8,640]{2,1,0:T(8,128)S(1)}, bf16[1,16,8,640]{3,2,1,0:T(8,128)(2,1)S(1)}, f32[16,2,1...) custom-call(s32[7]{0:T(128)S(1)} %stack.64.info_ref, bf16[16,8,640]{2,1,0:T(8,128)(2,1)S(1)} %get-tuple-element.26.refs_0_, ...), custom_call_target="tpu_custom_call" | custom-call | tf_op jit(solution)/shard_map/terms/pallas_call | solution.py:330
  30.1 0.7 %collective-permute-start.8 = (f32[4,16]{1,0:T(4,128)S(1)}, f32[4,16]{1,0:T(4,128)S(1)}, u32[]{:S(2)}, u32[]{:S(2)}) collective-permute-start(f32[4,16]{1,0:T(4,128)S(1)} %get-tuple-element.38), channel_id=1, source_target_pairs={{16,0},{0,16},{17,1},{1,17},{18,2},{2,18},{19,3},{3,19},{20,4},{4,... | collective-permute-start | bytes 776 | tf_op jit(solution)/shard_map/ppermute | solution.py:455
  30.8 1.9 %conv_forward.1 = (f32[16,8,256]{2,1,0:T(8,128)S(1)}, bf16[1,16,8,256]{3,2,1,0:T(8,128)(2,1)S(1)}, bf16[3,18,16,640]{3,2,1,0:T(8,128)(2,1)S(1)}) custom-call(s32[7]{0:T(128)S(1)} %stack.64.info_ref, f32[16,2,16,640]{3,2,1,0:T(8,128)S(1)} %get-tuple-element.39.given_ref, f32[6,640]{1,0:T(8,128)S(1)} %get-tuple-element.40.scales_ref, ...), custom_call_target="tpu_custom_call" | custom-call | tf_op jit(solution)/shard_map/conv_forward/pallas_call | solution.py:330
  32.8 1.0 %collective-permute-done.8 = f32[4,16]{1,0:T(4,128)S(1)} collective-permute-done((f32[4,16]{1,0:T(4,128)S(1)}, f32[4,16]{1,0:T(4,128)S(1)}, u32[]{:S(2)}, u32[]{:S(2)}) %collective-permute-start.8) | collective-permute-done | bytes 288 | tf_op jit(solution)/shard_map/ppermute | solution.py:455
  33.7 0.7 %collective-permute-start.13 = (bf16[16,8,640]{2,1,0:T(8,128)(2,1)S(1)}, bf16[16,8,640]{2,1,0:T(8,128)(2,1)S(1)}, u32[]{:S(2)}, u32[]{:S(2)}) collective-permute-start(bf16[16,8,640]{2,1,0:T(8,128)(2,1)S(1)} %bitcast.32), channel_id=1, source_target_pairs={{16,0},{0,16},{17,1},{1,17},{18,2},{2,18},{19,3},{3,19},{20,4},{4,... | collective-permute-start | bytes 491528 | tf_op jit(solution)/shard_map/ppermute | solution.py:455
  34.5 0.4 collective-permute-done.9
  34.9 1.5 %collective-permute-start.10 = (f32[2,2,16]{2,1,0:T(2,128)S(1)}, f32[2,2,16]{2,1,0:T(2,128)S(1)}, u32[]{:S(2)}, u32[]{:S(2)}) collective-permute-start(f32[2,2,16]{2,1,0:T(2,128)S(1)} %fusion.14.after_ref), channel_id=1, source_target_pairs={{0,8},{4,12},{8,0},{12,4},{1,9},{5,13},{9,1},{13,5},{2,10},{6,14},... | collective-permute-start | bytes 776 | tf_op jit(solution)/shard_map/ppermute | solution.py:23
  36.4 1.5 %conv_forward2.1 = (f32[16,8,384]{2,1,0:T(8,128)S(1)}, bf16[1,16,8,384]{3,2,1,0:T(8,128)(2,1)S(1)}) custom-call(bf16[3,18,16,640]{3,2,1,0:T(8,128)(2,1)S(1)} %get-tuple-element.42.windows_ref, bf16[3,3,640,640]{3,2,1,0:T(8,128)(2,1)S(1)} %bitcast.21, f32[2,2,16]{2,1,0:T(2,128)S(1)} %fusion.14.after_ref), custom_call_target="tpu_custom_call" | custom-call | tf_op jit(solution)/shard_map/conv_forward2/pallas_call | solution.py:330
  37.9 0.6 %collective-permute-done.10 = f32[2,2,16]{2,1,0:T(2,128)S(1)} collective-permute-done((f32[2,2,16]{2,1,0:T(2,128)S(1)}, f32[2,2,16]{2,1,0:T(2,128)S(1)}, u32[]{:S(2)}, u32[]{:S(2)}) %collective-permute-start.10) | collective-permute-done | bytes 288 | tf_op jit(solution)/shard_map/ppermute | solution.py:23
  38.5 2.6 %collective-permute-start.11 = (f32[2,2,16]{2,1,0:T(2,128)S(1)}, f32[2,2,16]{2,1,0:T(2,128)S(1)}, u32[]{:S(2)}, u32[]{:S(2)}) collective-permute-start(f32[2,2,16]{2,1,0:T(2,128)S(1)} %add_add_fusion), channel_id=1, source_target_pairs={{0,1},{1,0},{2,3},{3,2},{4,5},{5,4},{6,7},{7,6},{8,9},{9,8},{10,11... | collective-permute-start | bytes 776 | tf_op jit(solution)/shard_map/ppermute | solution.py:23
  41.1 1.0 %collective-permute-start.14 = (bf16[16,8,256]{2,1,0:T(8,128)(2,1)S(1)}, bf16[16,8,256]{2,1,0:T(8,128)(2,1)S(1)}, u32[]{:S(2)}, u32[]{:S(2)}) collective-permute-start(bf16[16,8,256]{2,1,0:T(8,128)(2,1)S(1)} %bitcast.34), channel_id=1, source_target_pairs={{16,0},{0,16},{17,1},{1,17},{18,2},{2,18},{19,3},{3,19},{20,4},{4,... | collective-permute-start | bytes 196616 | tf_op jit(solution)/shard_map/ppermute | solution.py:479
  42.1 1.0 %collective-permute-start.15 = (bf16[16,8,384]{2,1,0:T(8,128)(2,1)S(1)}, bf16[16,8,384]{2,1,0:T(8,128)(2,1)S(1)}, u32[]{:S(2)}, u32[]{:S(2)}) collective-permute-start(bf16[16,8,384]{2,1,0:T(8,128)(2,1)S(1)} %bitcast.33), channel_id=1, source_target_pairs={{16,0},{0,16},{17,1},{1,17},{18,2},{2,18},{19,3},{3,19},{20,4},{4,... | collective-permute-start | bytes 294920 | tf_op jit(solution)/shard_map/ppermute | solution.py:479
  43.2 3.0 %collective-permute-start.12 = (f32[2,2,16]{2,1,0:T(2,128)S(1)}, f32[2,2,16]{2,1,0:T(2,128)S(1)}, u32[]{:S(2)}, u32[]{:S(2)}) collective-permute-start(f32[2,2,16]{2,1,0:T(2,128)S(1)} %add.136), channel_id=1, source_target_pairs={{0,2},{1,3},{2,0},{3,1},{4,6},{5,7},{6,4},{7,5},{8,10},{9,11},{10,... | collective-permute-start | bytes 776 | tf_op jit(solution)/shard_map/ppermute | solution.py:23
  46.2 1.6 %collective-permute-done.12 = f32[2,2,16]{2,1,0:T(2,128)S(1)} collective-permute-done((f32[2,2,16]{2,1,0:T(2,128)S(1)}, f32[2,2,16]{2,1,0:T(2,128)S(1)}, u32[]{:S(2)}, u32[]{:S(2)}) %collective-permute-start.12) | collective-permute-done | bytes 288 | tf_op jit(solution)/shard_map/ppermute | solution.py:23
  47.7 1.7 %finish.1 = (bf16[16,8,640]{2,1,0:T(8,128)(2,1)}, bf16[16,8,1280]{2,1,0:T(8,128)(2,1)}) custom-call(s32[7]{0:T(128)S(1)} %stack.64.info_ref, bf16[16,8,1280]{2,1,0:T(8,128)(2,1)S(1)} %bitcast.28, f32[2,4,16]{2,1,0:T(4,128)S(1)} %pad_maximum_fusion.1.small_ref, f32[2,2,16]{2,1,0:T(2,128)S(1)} %add.137.sums_ref, f32[640]{0:T(1024)S(1)} %copy-done.5, ...), custom_call_target="tpu_custom_call" | custom-call | tf_op jit(solution)/shard_map/finish/pallas_call | solution.py:330
  (55 shorter events, 1.0 us)
Async XLA Ops:
  0.6 10.3 %collective-permute-start.2 = (bf16[16,8,640]{2,1,0:T(8,128)(2,1)}, bf16[16,8,640]{2,1,0:T(8,128)(2,1)S(1)}, u32[]{:S(2)}, u32[]{:S(2)}) collective-permute-start(bf16[16,8,640]{2,1,0:T(8,128)(2,1)} %bitcast.22), channel_id=1, source_target_pairs={{0,16},{16,0},{1,17},{17,1},{2,18},{18,2},{3,19},{19,3},{4,20},{20... | collective-permute-start | bytes 491528 | tf_op jit(solution)/shard_map/ppermute | solution.py:374
  3.7 7.8 %slice-start = ((s8[7372800]{0:T(1024)(128)(4,1)}), s8[4194304]{0:T(1024)(128)(4,1)S(1)}, s32[]{:S(2)}) async-start(s8[7372800]{0:T(1024)(128)(4,1)} %bitcast.20), calls=%async_computation | async-start | bytes 8388608
  3.7 1.1 %copy-start.1 = (bf16[1,16,8,1280]{3,2,1,0:T(8,128)(2,1)S(1)}, bf16[1,16,8,1280]{3,2,1,0:T(8,128)(2,1)}, u32[]{:S(2)}) copy-start(bf16[1,16,8,1280]{3,2,1,0:T(8,128)(2,1)} %param.6) | copy-start | bytes 983044
  4.9 6.0 %copy-start = (bf16[1,16,8,640]{3,2,1,0:T(8,128)(2,1)S(1)}, bf16[1,16,8,640]{3,2,1,0:T(8,128)(2,1)}, u32[]{:S(2)}) copy-start(bf16[1,16,8,640]{3,2,1,0:T(8,128)(2,1)} %param.11) | copy-start | bytes 491524
  4.9 6.7 %slice-start.1 = ((s8[7372800]{0:T(1024)(128)(4,1)}), s8[3178496]{0:T(1024)(128)(4,1)S(1)}, s32[]{:S(2)}) async-start(s8[7372800]{0:T(1024)(128)(4,1)} %bitcast.20), calls=%async_computation.1 | async-start | bytes 6356992
  4.9 6.7 %copy-start.2 = (bf16[1,16,8,1280]{3,2,1,0:T(8,128)(2,1)S(1)}, bf16[1,16,8,1280]{3,2,1,0:T(8,128)(2,1)}, u32[]{:S(2)}) copy-start(bf16[1,16,8,1280]{3,2,1,0:T(8,128)(2,1)} %param.6) | copy-start | bytes 983044
  6.5 4.4 %collective-permute-start = (bf16[56,640]{1,0:T(8,128)(2,1)S(1)}, bf16[56,640]{1,0:T(8,128)(2,1)S(1)}, u32[]{:S(2)}, u32[]{:S(2)}) collective-permute-start(bf16[56,640]{1,0:T(8,128)(2,1)S(1)} %get-tuple-element.28), channel_id=1, source_target_pairs={{0,16},{16,0},{1,17},{17,1},{2,18},{18,2},{3,19},{19,3},{4,20},{20... | collective-permute-start | bytes 215048 | tf_op jit(solution)/shard_map/ppermute | solution.py:374
  11.5 1.3 %collective-permute-start.3 = (bf16[24,1280]{1,0:T(8,128)(2,1)S(1)}, bf16[24,1280]{1,0:T(8,128)(2,1)S(1)}, u32[]{:S(2)}, u32[]{:S(2)}) collective-permute-start(bf16[24,1280]{1,0:T(8,128)(2,1)S(1)} %get-tuple-element.31), channel_id=1, source_target_pairs={{0,4},{4,0},{8,12},{12,8},{1,5},{5,1},{9,13},{13,9},{2,6},{6,2},{1... | collective-permute-start | bytes 184328 | tf_op jit(solution)/shard_map/ppermute | solution.py:23
  13.0 4.0 %collective-permute-start.4 = (bf16[19,1280]{1,0:T(8,128)(2,1)S(1)}, bf16[19,1280]{1,0:T(8,128)(2,1)S(1)}, u32[]{:S(2)}, u32[]{:S(2)}) collective-permute-start(bf16[19,1280]{1,0:T(8,128)(2,1)S(1)} %pad_maximum_fusion), channel_id=1, source_target_pairs={{0,12},{4,8},{8,4},{12,0},{1,13},{5,9},{9,5},{13,1},{2,14},{6,10},... | collective-permute-start | bytes 145928 | tf_op jit(solution)/shard_map/ppermute | solution.py:23
  17.8 5.0 %collective-permute-start.5 = (bf16[40,1280]{1,0:T(8,128)(2,1)S(1)}, bf16[40,1280]{1,0:T(8,128)(2,1)S(1)}, u32[]{:S(2)}, u32[]{:S(2)}) collective-permute-start(bf16[40,1280]{1,0:T(8,128)(2,1)S(1)} %get-tuple-element.35), channel_id=1, source_target_pairs={{0,1},{1,0},{2,3},{3,2},{4,5},{5,4},{6,7},{7,6},{8,9},{9,8},{10,11... | collective-permute-start | bytes 307208 | tf_op jit(solution)/shard_map/ppermute | solution.py:23
  19.5 6.1 %collective-permute-start.1 = (bf16[16,8,640]{2,1,0:T(8,128)(2,1)S(1)}, bf16[16,8,640]{2,1,0:T(8,128)(2,1)S(1)}, u32[]{:S(2)}, u32[]{:S(2)}) collective-permute-start(bf16[16,8,640]{2,1,0:T(8,128)(2,1)S(1)} %broadcast_add_fusion), channel_id=1, source_target_pairs={{0,16},{16,0},{1,17},{17,1},{2,18},{18,2},{3,19},{19,3},{4,20},{20... | collective-permute-start | bytes 491528 | tf_op jit(solution)/shard_map/ppermute | solution.py:374
  20.0 5.6 %collective-permute-start.7 = (bf16[36,1280]{1,0:T(8,128)(2,1)S(1)}, bf16[36,1280]{1,0:T(8,128)(2,1)S(1)}, u32[]{:S(2)}, u32[]{:S(2)}) collective-permute-start(bf16[36,1280]{1,0:T(8,128)(2,1)S(1)} %get-tuple-element.36), channel_id=1, source_target_pairs={{1,2},{2,1},{5,6},{6,5},{9,10},{10,9},{13,14},{14,13},{17,18},{18,... | collective-permute-start | bytes 276488 | tf_op jit(solution)/shard_map/ppermute | solution.py:23
  23.0 5.8 %copy-start.3 = (f32[1280]{0:T(1024)S(1)}, f32[1280]{0:T(1024)}, u32[]{:S(2)}) copy-start(f32[1280]{0:T(1024)} %refs_3_.1) | copy-start | bytes 15364
  23.0 5.8 %copy-start.4 = (f32[1280]{0:T(1024)S(1)}, f32[1280]{0:T(1024)}, u32[]{:S(2)}) copy-start(f32[1280]{0:T(1024)} %refs_4_.1) | copy-start | bytes 15364
  23.0 5.6 %collective-permute-start.6 = (f32[1,64]{1,0:T(1,128)S(1)}, f32[1,64]{1,0:T(1,128)S(1)}, u32[]{:S(2)}, u32[]{:S(2)}) collective-permute-start(f32[1,64]{1,0:T(1,128)S(1)} %pad_maximum_fusion.4), channel_id=1, source_target_pairs={{0,2},{1,3},{2,0},{3,1},{4,6},{5,7},{6,4},{7,5},{8,10},{9,11},{10,... | collective-permute-start | bytes 776 | tf_op jit(solution)/shard_map/ppermute | solution.py:23
  30.1 3.6 %collective-permute-start.8 = (f32[4,16]{1,0:T(4,128)S(1)}, f32[4,16]{1,0:T(4,128)S(1)}, u32[]{:S(2)}, u32[]{:S(2)}) collective-permute-start(f32[4,16]{1,0:T(4,128)S(1)} %get-tuple-element.38), channel_id=1, source_target_pairs={{16,0},{0,16},{17,1},{1,17},{18,2},{2,18},{19,3},{3,19},{20,4},{4,... | collective-permute-start | bytes 776 | tf_op jit(solution)/shard_map/ppermute | solution.py:455
  33.7 1.2 %collective-permute-start.9 = (f32[2,2,16]{2,1,0:T(2,128)S(1)}, f32[2,2,16]{2,1,0:T(2,128)S(1)}, u32[]{:S(2)}, u32[]{:S(2)}) collective-permute-start(f32[2,2,16]{2,1,0:T(2,128)S(1)} %fusion.7), channel_id=1, source_target_pairs={{0,4},{4,0},{8,12},{12,8},{1,5},{5,1},{9,13},{13,9},{2,6},{6,2},{1... | collective-permute-start | bytes 776 | tf_op jit(solution)/shard_map/ppermute | solution.py:23
  33.7 14.0 %collective-permute-start.13 = (bf16[16,8,640]{2,1,0:T(8,128)(2,1)S(1)}, bf16[16,8,640]{2,1,0:T(8,128)(2,1)S(1)}, u32[]{:S(2)}, u32[]{:S(2)}) collective-permute-start(bf16[16,8,640]{2,1,0:T(8,128)(2,1)S(1)} %bitcast.32), channel_id=1, source_target_pairs={{16,0},{0,16},{17,1},{1,17},{18,2},{2,18},{19,3},{3,19},{20,4},{4,... | collective-permute-start | bytes 491528 | tf_op jit(solution)/shard_map/ppermute | solution.py:455
  34.9 3.6 %collective-permute-start.10 = (f32[2,2,16]{2,1,0:T(2,128)S(1)}, f32[2,2,16]{2,1,0:T(2,128)S(1)}, u32[]{:S(2)}, u32[]{:S(2)}) collective-permute-start(f32[2,2,16]{2,1,0:T(2,128)S(1)} %fusion.14.after_ref), channel_id=1, source_target_pairs={{0,8},{4,12},{8,0},{12,4},{1,9},{5,13},{9,1},{13,5},{2,10},{6,14},... | collective-permute-start | bytes 776 | tf_op jit(solution)/shard_map/ppermute | solution.py:23
  36.4 11.4 %copy-start.5 = (f32[640]{0:T(1024)S(1)}, f32[640]{0:T(1024)}, u32[]{:S(2)}) copy-start(f32[640]{0:T(1024)} %bias_ref.1) | copy-start | bytes 7684
  38.5 4.7 %collective-permute-start.11 = (f32[2,2,16]{2,1,0:T(2,128)S(1)}, f32[2,2,16]{2,1,0:T(2,128)S(1)}, u32[]{:S(2)}, u32[]{:S(2)}) collective-permute-start(f32[2,2,16]{2,1,0:T(2,128)S(1)} %add_add_fusion), channel_id=1, source_target_pairs={{0,1},{1,0},{2,3},{3,2},{4,5},{5,4},{6,7},{7,6},{8,9},{9,8},{10,11... | collective-permute-start | bytes 776 | tf_op jit(solution)/shard_map/ppermute | solution.py:23
  41.1 6.6 %collective-permute-start.14 = (bf16[16,8,256]{2,1,0:T(8,128)(2,1)S(1)}, bf16[16,8,256]{2,1,0:T(8,128)(2,1)S(1)}, u32[]{:S(2)}, u32[]{:S(2)}) collective-permute-start(bf16[16,8,256]{2,1,0:T(8,128)(2,1)S(1)} %bitcast.34), channel_id=1, source_target_pairs={{16,0},{0,16},{17,1},{1,17},{18,2},{2,18},{19,3},{3,19},{20,4},{4,... | collective-permute-start | bytes 196616 | tf_op jit(solution)/shard_map/ppermute | solution.py:479
  42.1 5.6 %collective-permute-start.15 = (bf16[16,8,384]{2,1,0:T(8,128)(2,1)S(1)}, bf16[16,8,384]{2,1,0:T(8,128)(2,1)S(1)}, u32[]{:S(2)}, u32[]{:S(2)}) collective-permute-start(bf16[16,8,384]{2,1,0:T(8,128)(2,1)S(1)} %bitcast.33), channel_id=1, source_target_pairs={{16,0},{0,16},{17,1},{1,17},{18,2},{2,18},{19,3},{3,19},{20,4},{4,... | collective-permute-start | bytes 294920 | tf_op jit(solution)/shard_map/ppermute | solution.py:479
  43.2 4.6 %collective-permute-start.12 = (f32[2,2,16]{2,1,0:T(2,128)S(1)}, f32[2,2,16]{2,1,0:T(2,128)S(1)}, u32[]{:S(2)}, u32[]{:S(2)}) collective-permute-start(f32[2,2,16]{2,1,0:T(2,128)S(1)} %add.136), channel_id=1, source_target_pairs={{0,2},{1,3},{2,0},{3,1},{4,6},{5,7},{6,4},{7,5},{8,10},{9,11},{10,... | collective-permute-start | bytes 776 | tf_op jit(solution)/shard_map/ppermute | solution.py:23

commit v9 on v7

--- a/solution.py
+++ b/solution.py
@@ -386,8 +386,7 @@
         [sds((rows, cols, chans), BF16)] * parts,
         [info, x, conv_weight],
     )
-    zero = (0.0 * got[0][:1]).astype(BF16)
-    x_tiles = [tiles[0], *from_peers([v + zero[None] for v in tiles[1:]])]
+    x_tiles = [tiles[0], *from_peers(tiles[1:])]
     size = 2 * parts * groups
     pack_near, pack_across, stats = call(
         functools.partial(rows_kernel, parts),

time: 49.6 us -> 50.3 us (1.014)
  waiting for transfers between devices: 12.3 us -> 12.9 us
    ppermute x3, waiting for transfers between devices: 4.29 us -> 4.84 us  [body(): lax.ppermute(v, 'dp', pairs)]
  transfers between devices with their start and end apart: 16 -> 16, of which waited for: 8 -> 9; matrix products, arithmetic and copies ran while one was open for 1% -> 1% of each run, Pallas kernels for 19% -> 19%
where the time goes in v9:
time: 50.3 us; the launch traced here: 50.1 us
  starting transfers between devices  20.8 us (41%)
  Pallas kernels  13.7 us (27%)
  waiting for transfers between devices  12.9 us (26%)
  local copies, waits for them, and re-layouts  1.24 us (2%)
  between operations  0.79 us (2%)
  other arithmetic  0.72 us (1%)
    pallas_call x10, Pallas kernels, call(): pl.pallas_call(kernel, out_shape=outs, in_specs=[spec(i) for i in range(l...  13.7 us
    ppermute x9, starting transfers between devices, exchange(): return lax.ppermute(value, axis, pairs)  13.4 us
    ppermute x9, waiting for transfers between devices, exchange(): return lax.ppermute(value, axis, pairs)  7.47 us
    ppermute x3, waiting for transfers between devices, body(): lax.ppermute(v, 'dp', pairs)  4.84 us
    ppermute x3, starting transfers between devices, body(): lax.ppermute(v, 'dp', pairs)  3.72 us
    ppermute x2, starting transfers between devices, body(): conv += [lax.ppermute(v[k], 'dp', back) for v in (conv_other, conv_other2)]  2.03 us
    ppermute x2, starting transfers between devices, body(): lax.ppermute(v, 'dp', [(j, i) for i, j in pairs])  1.65 us
    unnamed x16, local copies, waits for them, and re-layouts  1.15 us
  transfers between devices with their start and end apart: 16, of which 9 were waited for; matrix products, arithmetic and copies ran while one was open for 1% of the time, Pallas kernels for 19%

profile of v9, /device:TPU:0, one launch (start us, length us, event | category | flops | bytes accessed | tf_op | source)
XLA Modules:
  0.0 50.1 jit_solution(5069269828497524588)
XLA Ops:
  0.6 3.0 %collective-permute-start.2 = (bf16[16,8,640]{2,1,0:T(8,128)(2,1)}, bf16[16,8,640]{2,1,0:T(8,128)(2,1)S(1)}, u32[]{:S(2)}, u32[]{:S(2)}) collective-permute-start(bf16[16,8,640]{2,1,0:T(8,128)(2,1)} %bitcast.22), channel_id=1, source_target_pairs={{0,16},{16,0},{1,17},{17,1},{2,18},{18,2},{3,19},{19,3},{4,20},{20... | collective-permute-start | bytes 491528 | tf_op jit(solution)/shard_map/ppermute | solution.py:373
  3.8 1.1 %copy-done.1 = bf16[1,16,8,1280]{3,2,1,0:T(8,128)(2,1)S(1)} copy-done((bf16[1,16,8,1280]{3,2,1,0:T(8,128)(2,1)S(1)}, bf16[1,16,8,1280]{3,2,1,0:T(8,128)(2,1)}, u32[]{:S(2)}) %copy-start.1) | copy-done | bytes 327704
  4.9 1.6 %first.1 = (bf16[56,640]{1,0:T(8,128)(2,1)S(1)}, bf16[56,640]{1,0:T(8,128)(2,1)S(1)}) custom-call(s32[7]{0:T(128)S(1)} %stack.64.info_ref, bf16[16,8,1280]{2,1,0:T(8,128)(2,1)S(1)} %bitcast.26), custom_call_target="tpu_custom_call" | custom-call | flops 10000000000 | bytes 1 | tf_op jit(solution)/shard_map/first/pallas_call | solution.py:329
  6.6 4.3 %collective-permute-done.1.refs_1_ = bf16[56,640]{1,0:T(8,128)(2,1)S(1)} collective-permute-done((bf16[56,640]{1,0:T(8,128)(2,1)S(1)}, bf16[56,640]{1,0:T(8,128)(2,1)S(1)}, u32[]{:S(2)}, u32[]{:S(2)}) %collective-permute-start.1) | collective-permute-done | bytes 71712 | tf_op jit(solution)/shard_map/ppermute | solution.py:373
  10.9 0.6 %rows.1 = (bf16[24,1280]{1,0:T(8,128)(2,1)S(1)}, bf16[16,1280]{1,0:T(8,128)(2,1)S(1)}, f32[1,64]{1,0:T(1,128)S(1)}) custom-call(s32[7]{0:T(128)S(1)} %stack.64.info_ref, bf16[56,640]{1,0:T(8,128)(2,1)S(1)} %get-tuple-element.28.refs_0_, bf16[56,640]{1,0:T(8,128)(2,1)S(1)} %collective-permute-done.1.refs_1_, bf16[16,8,640]{2,1,0:T(8,128)(2,1)S(1)} %bitcast.23, ...), custom_call_target="tpu_custom_call" | custom-call | tf_op jit(solution)/shard_map/rows/pallas_call | solution.py:329
  11.5 1.2 %collective-permute-done.3.near_h.refs_2_ = bf16[24,1280]{1,0:T(8,128)(2,1)S(1)} collective-permute-done((bf16[24,1280]{1,0:T(8,128)(2,1)S(1)}, bf16[24,1280]{1,0:T(8,128)(2,1)S(1)}, u32[]{:S(2)}, u32[]{:S(2)}) %collective-permute-start.3) | collective-permute-done | bytes 61472 | tf_op jit(solution)/shard_map/ppermute | solution.py:23
  13.0 1.3 %collective-permute-start.4 = (bf16[19,1280]{1,0:T(8,128)(2,1)S(1)}, bf16[19,1280]{1,0:T(8,128)(2,1)S(1)}, u32[]{:S(2)}, u32[]{:S(2)}) collective-permute-start(bf16[19,1280]{1,0:T(8,128)(2,1)S(1)} %pad_maximum_fusion), channel_id=1, source_target_pairs={{0,12},{4,8},{8,4},{12,0},{1,13},{5,9},{9,5},{13,1},{2,14},{6,10},... | collective-permute-start | bytes 145928 | tf_op jit(solution)/shard_map/ppermute | solution.py:23
  14.3 0.7 %columns.1 = (bf16[32,1280]{1,0:T(8,128)(2,1)S(1)}, bf16[32,1280]{1,0:T(8,128)(2,1)S(1)}) custom-call(s32[7]{0:T(128)S(1)} %stack.64.info_ref, bf16[56,640]{1,0:T(8,128)(2,1)S(1)} %get-tuple-element.28.refs_0_, bf16[56,640]{1,0:T(8,128)(2,1)S(1)} %collective-permute-done.1.refs_1_, bf16[16,8,640]{2,1,0:T(8,128)(2,1)S(1)} %bitcast.24, ...), custom_call_target="tpu_custom_call" | custom-call | tf_op jit(solution)/shard_map/columns/pallas_call | solution.py:329
  15.1 2.0 %collective-permute-done.4.across_h.refs_3_ = bf16[19,1280]{1,0:T(8,128)(2,1)S(1)} collective-permute-done((bf16[19,1280]{1,0:T(8,128)(2,1)S(1)}, bf16[19,1280]{1,0:T(8,128)(2,1)S(1)}, u32[]{:S(2)}, u32[]{:S(2)}) %collective-permute-start.4) | collective-permute-done | bytes 48672 | tf_op jit(solution)/shard_map/ppermute | solution.py:23
  17.2 0.6 %pack.1 = (bf16[40,1280]{1,0:T(8,128)(2,1)S(1)}, bf16[36,1280]{1,0:T(8,128)(2,1)S(1)}) custom-call(s32[7]{0:T(128)S(1)} %stack.64.info_ref, bf16[24,1280]{1,0:T(8,128)(2,1)S(1)} %collective-permute-done.3.near_h.refs_2_, bf16[19,1280]{1,0:T(8,128)(2,1)S(1)} %collective-permute-done.4.across_h.refs_3_, f32[1,64]{1,0:T(1,128)S(1)} %pad_maximum_fusion.3.stats_ref, ...), custom_call_target="tpu_custom_call" | custom-call | tf_op jit(solution)/shard_map/pack/pallas_call | solution.py:329
  17.8 1.6 %collective-permute-start.5 = (bf16[40,1280]{1,0:T(8,128)(2,1)S(1)}, bf16[40,1280]{1,0:T(8,128)(2,1)S(1)}, u32[]{:S(2)}, u32[]{:S(2)}) collective-permute-start(bf16[40,1280]{1,0:T(8,128)(2,1)S(1)} %get-tuple-element.35), channel_id=1, source_target_pairs={{0,1},{1,0},{2,3},{3,2},{4,5},{5,4},{6,7},{7,6},{8,9},{9,8},{10,11... | collective-permute-start | bytes 307208 | tf_op jit(solution)/shard_map/ppermute | solution.py:23
  19.5 0.6 %tiles.1 = (bf16[16,8,640]{2,1,0:T(8,128)(2,1)S(1)}, bf16[16,8,640]{2,1,0:T(8,128)(2,1)S(1)}) custom-call(s32[7]{0:T(128)S(1)} %stack.64.info_ref, bf16[16,8,1280]{2,1,0:T(8,128)(2,1)S(1)} %bitcast.27, bf16[3,3,640,640]{3,2,1,0:T(8,128)(2,1)S(1)} %bitcast.21), custom_call_target="tpu_custom_call" | custom-call | tf_op jit(solution)/shard_map/tiles/pallas_call | solution.py:329
  20.1 0.6 %collective-permute-start = (bf16[16,8,640]{2,1,0:T(8,128)(2,1)S(1)}, bf16[16,8,640]{2,1,0:T(8,128)(2,1)S(1)}, u32[]{:S(2)}, u32[]{:S(2)}) collective-permute-start(bf16[16,8,640]{2,1,0:T(8,128)(2,1)S(1)} %get-tuple-element.27), channel_id=1, source_target_pairs={{0,16},{16,0},{1,17},{17,1},{2,18},{18,2},{3,19},{19,3},{4,20},{20... | collective-permute-start | bytes 491528 | tf_op jit(solution)/shard_map/ppermute | solution.py:373
  20.7 0.7 %collective-permute-start.7 = (bf16[36,1280]{1,0:T(8,128)(2,1)S(1)}, bf16[36,1280]{1,0:T(8,128)(2,1)S(1)}, u32[]{:S(2)}, u32[]{:S(2)}) collective-permute-start(bf16[36,1280]{1,0:T(8,128)(2,1)S(1)} %get-tuple-element.36), channel_id=1, source_target_pairs={{1,2},{2,1},{5,6},{6,5},{9,10},{10,9},{13,14},{14,13},{17,18},{18,... | collective-permute-start | bytes 276488 | tf_op jit(solution)/shard_map/ppermute | solution.py:23
  21.3 1.5 %collective-permute-done.5.refs_4_.near_w = bf16[40,1280]{1,0:T(8,128)(2,1)S(1)} collective-permute-done((bf16[40,1280]{1,0:T(8,128)(2,1)S(1)}, bf16[40,1280]{1,0:T(8,128)(2,1)S(1)}, u32[]{:S(2)}, u32[]{:S(2)}) %collective-permute-start.5) | collective-permute-done | bytes 102432 | tf_op jit(solution)/shard_map/ppermute | solution.py:23
  23.0 2.6 %collective-permute-start.6 = (f32[1,64]{1,0:T(1,128)S(1)}, f32[1,64]{1,0:T(1,128)S(1)}, u32[]{:S(2)}, u32[]{:S(2)}) collective-permute-start(f32[1,64]{1,0:T(1,128)S(1)} %pad_maximum_fusion.4), channel_id=1, source_target_pairs={{0,2},{1,3},{2,0},{3,1},{4,6},{5,7},{6,4},{7,5},{8,10},{9,11},{10,... | collective-permute-start | bytes 776 | tf_op jit(solution)/shard_map/ppermute | solution.py:23
  25.6 0.6 %collective-permute-done.refs_7_.refs_1_ = bf16[16,8,640]{2,1,0:T(8,128)(2,1)S(1)} collective-permute-done((bf16[16,8,640]{2,1,0:T(8,128)(2,1)S(1)}, bf16[16,8,640]{2,1,0:T(8,128)(2,1)S(1)}, u32[]{:S(2)}, u32[]{:S(2)}) %collective-permute-start) | collective-permute-done | bytes 163872 | tf_op jit(solution)/shard_map/ppermute | solution.py:373
  26.2 3.0 %conv_backward.1.refs_5_ = f32[16,2,8,640]{3,2,1,0:T(8,128)S(1)} custom-call(s32[7]{0:T(128)S(1)} %stack.64.info_ref, bf16[16,8,640]{2,1,0:T(8,128)(2,1)S(1)} %bitcast.25, bf16[16,8,640]{2,1,0:T(8,128)(2,1)S(1)} %collective-permute-done.2.refs_3_.refs_1_, bf16[24,1280]{1,0:T(8,128)(2,1)S(1)} %collective-permute-done.3.near_h.refs_2_, ...), custom_call_target="tpu_custom_call" | custom-call | tf_op jit(solution)/shard_map/conv_backward/pallas_call | solution.py:329
  29.3 1.4 %terms.1 = (f32[4,16]{1,0:T(4,128)S(1)}, f32[4,16]{1,0:T(4,128)S(1)}, f32[16,8,640]{2,1,0:T(8,128)S(1)}, bf16[1,16,8,640]{3,2,1,0:T(8,128)(2,1)S(1)}, f32[16,2,1...) custom-call(s32[7]{0:T(128)S(1)} %stack.64.info_ref, bf16[16,8,640]{2,1,0:T(8,128)(2,1)S(1)} %get-tuple-element.26.refs_0_, ...), custom_call_target="tpu_custom_call" | custom-call | tf_op jit(solution)/shard_map/terms/pallas_call | solution.py:329
  30.7 0.8 %collective-permute-start.8 = (f32[4,16]{1,0:T(4,128)S(1)}, f32[4,16]{1,0:T(4,128)S(1)}, u32[]{:S(2)}, u32[]{:S(2)}) collective-permute-start(f32[4,16]{1,0:T(4,128)S(1)} %get-tuple-element.38), channel_id=1, source_target_pairs={{16,0},{0,16},{17,1},{1,17},{18,2},{2,18},{19,3},{3,19},{20,4},{4,... | collective-permute-start | bytes 776 | tf_op jit(solution)/shard_map/ppermute | solution.py:453
  31.4 2.3 %conv_forward.1 = (f32[16,8,384]{2,1,0:T(8,128)S(1)}, bf16[1,16,8,384]{3,2,1,0:T(8,128)(2,1)S(1)}, bf16[3,18,16,640]{3,2,1,0:T(8,128)(2,1)S(1)}) custom-call(s32[7]{0:T(128)S(1)} %stack.64.info_ref, f32[16,2,16,640]{3,2,1,0:T(8,128)S(1)} %get-tuple-element.39.given_ref, f32[6,640]{1,0:T(8,128)S(1)} %get-tuple-element.40.scales_ref, ...), custom_call_target="tpu_custom_call" | custom-call | tf_op jit(solution)/shard_map/conv_forward/pallas_call | solution.py:329
  33.7 0.5 %collective-permute-done.8 = f32[4,16]{1,0:T(4,128)S(1)} collective-permute-done((f32[4,16]{1,0:T(4,128)S(1)}, f32[4,16]{1,0:T(4,128)S(1)}, u32[]{:S(2)}, u32[]{:S(2)}) %collective-permute-start.8) | collective-permute-done | bytes 288 | tf_op jit(solution)/shard_map/ppermute | solution.py:453
  34.3 0.9 %collective-permute-start.13 = (bf16[16,8,640]{2,1,0:T(8,128)(2,1)S(1)}, bf16[16,8,640]{2,1,0:T(8,128)(2,1)S(1)}, u32[]{:S(2)}, u32[]{:S(2)}) collective-permute-start(bf16[16,8,640]{2,1,0:T(8,128)(2,1)S(1)} %bitcast.32), channel_id=1, source_target_pairs={{16,0},{0,16},{17,1},{1,17},{18,2},{2,18},{19,3},{3,19},{20,4},{4,... | collective-permute-start | bytes 491528 | tf_op jit(solution)/shard_map/ppermute | solution.py:453
  35.5 1.5 %collective-permute-start.10 = (f32[2,2,16]{2,1,0:T(2,128)S(1)}, f32[2,2,16]{2,1,0:T(2,128)S(1)}, u32[]{:S(2)}, u32[]{:S(2)}) collective-permute-start(f32[2,2,16]{2,1,0:T(2,128)S(1)} %fusion.13.after_ref), channel_id=1, source_target_pairs={{0,8},{4,12},{8,0},{12,4},{1,9},{5,13},{9,1},{13,5},{2,10},{6,14},... | collective-permute-start | bytes 776 | tf_op jit(solution)/shard_map/ppermute | solution.py:23
  36.9 1.1 %conv_forward2.1 = (f32[16,8,256]{2,1,0:T(8,128)S(1)}, bf16[1,16,8,256]{3,2,1,0:T(8,128)(2,1)S(1)}) custom-call(bf16[3,18,16,640]{3,2,1,0:T(8,128)(2,1)S(1)} %get-tuple-element.42.windows_ref, bf16[3,3,640,640]{3,2,1,0:T(8,128)(2,1)S(1)} %bitcast.21, f32[2,2,16]{2,1,0:T(2,128)S(1)} %fusion.13.after_ref), custom_call_target="tpu_custom_call" | custom-call | tf_op jit(solution)/shard_map/conv_forward2/pallas_call | solution.py:329
  38.1 1.0 %collective-permute-done.10 = f32[2,2,16]{2,1,0:T(2,128)S(1)} collective-permute-done((f32[2,2,16]{2,1,0:T(2,128)S(1)}, f32[2,2,16]{2,1,0:T(2,128)S(1)}, u32[]{:S(2)}, u32[]{:S(2)}) %collective-permute-start.10) | collective-permute-done | bytes 288 | tf_op jit(solution)/shard_map/ppermute | solution.py:23
  39.0 2.7 %collective-permute-start.11 = (f32[2,2,16]{2,1,0:T(2,128)S(1)}, f32[2,2,16]{2,1,0:T(2,128)S(1)}, u32[]{:S(2)}, u32[]{:S(2)}) collective-permute-start(f32[2,2,16]{2,1,0:T(2,128)S(1)} %add_add_fusion), channel_id=1, source_target_pairs={{0,1},{1,0},{2,3},{3,2},{4,5},{5,4},{6,7},{7,6},{8,9},{9,8},{10,11... | collective-permute-start | bytes 776 | tf_op jit(solution)/shard_map/ppermute | solution.py:23
  41.8 1.0 %collective-permute-start.14 = (bf16[16,8,384]{2,1,0:T(8,128)(2,1)S(1)}, bf16[16,8,384]{2,1,0:T(8,128)(2,1)S(1)}, u32[]{:S(2)}, u32[]{:S(2)}) collective-permute-start(bf16[16,8,384]{2,1,0:T(8,128)(2,1)S(1)} %bitcast.33), channel_id=1, source_target_pairs={{16,0},{0,16},{17,1},{1,17},{18,2},{2,18},{19,3},{3,19},{20,4},{4,... | collective-permute-start | bytes 294920 | tf_op jit(solution)/shard_map/ppermute | solution.py:477
  42.8 1.0 %collective-permute-start.15 = (bf16[16,8,256]{2,1,0:T(8,128)(2,1)S(1)}, bf16[16,8,256]{2,1,0:T(8,128)(2,1)S(1)}, u32[]{:S(2)}, u32[]{:S(2)}) collective-permute-start(bf16[16,8,256]{2,1,0:T(8,128)(2,1)S(1)} %bitcast.34), channel_id=1, source_target_pairs={{16,0},{0,16},{17,1},{1,17},{18,2},{2,18},{19,3},{3,19},{20,4},{4,... | collective-permute-start | bytes 196616 | tf_op jit(solution)/shard_map/ppermute | solution.py:477
  43.8 3.0 %collective-permute-start.12 = (f32[2,2,16]{2,1,0:T(2,128)S(1)}, f32[2,2,16]{2,1,0:T(2,128)S(1)}, u32[]{:S(2)}, u32[]{:S(2)}) collective-permute-start(f32[2,2,16]{2,1,0:T(2,128)S(1)} %add.123), channel_id=1, source_target_pairs={{0,2},{1,3},{2,0},{3,1},{4,6},{5,7},{6,4},{7,5},{8,10},{9,11},{10,... | collective-permute-start | bytes 776 | tf_op jit(solution)/shard_map/ppermute | solution.py:23
  46.8 1.6 %collective-permute-done.12 = f32[2,2,16]{2,1,0:T(2,128)S(1)} collective-permute-done((f32[2,2,16]{2,1,0:T(2,128)S(1)}, f32[2,2,16]{2,1,0:T(2,128)S(1)}, u32[]{:S(2)}, u32[]{:S(2)}) %collective-permute-start.12) | collective-permute-done | bytes 288 | tf_op jit(solution)/shard_map/ppermute | solution.py:23
  48.4 1.7 %finish.1 = (bf16[16,8,640]{2,1,0:T(8,128)(2,1)}, bf16[16,8,1280]{2,1,0:T(8,128)(2,1)}) custom-call(s32[7]{0:T(128)S(1)} %stack.64.info_ref, bf16[16,8,1280]{2,1,0:T(8,128)(2,1)S(1)} %bitcast.28, f32[2,4,16]{2,1,0:T(4,128)S(1)} %pad_maximum_fusion.1.small_ref, f32[2,2,16]{2,1,0:T(2,128)S(1)} %add.124.sums_ref, f32[640]{0:T(1024)S(1)} %copy-done.5, ...), custom_call_target="tpu_custom_call" | custom-call | tf_op jit(solution)/shard_map/finish/pallas_call | solution.py:329
  (53 shorter events, 1.2 us)
Async XLA Ops:
  0.6 10.3 %collective-permute-start.2 = (bf16[16,8,640]{2,1,0:T(8,128)(2,1)}, bf16[16,8,640]{2,1,0:T(8,128)(2,1)S(1)}, u32[]{:S(2)}, u32[]{:S(2)}) collective-permute-start(bf16[16,8,640]{2,1,0:T(8,128)(2,1)} %bitcast.22), channel_id=1, source_target_pairs={{0,16},{16,0},{1,17},{17,1},{2,18},{18,2},{3,19},{19,3},{4,20},{20... | collective-permute-start | bytes 491528 | tf_op jit(solution)/shard_map/ppermute | solution.py:373
  3.7 15.7 %slice-start = ((s8[7372800]{0:T(1024)(128)(4,1)}), s8[4194304]{0:T(1024)(128)(4,1)S(1)}, s32[]{:S(2)}) async-start(s8[7372800]{0:T(1024)(128)(4,1)} %bitcast.20), calls=%async_computation | async-start | bytes 8388608
  3.7 1.1 %copy-start.1 = (bf16[1,16,8,1280]{3,2,1,0:T(8,128)(2,1)S(1)}, bf16[1,16,8,1280]{3,2,1,0:T(8,128)(2,1)}, u32[]{:S(2)}) copy-start(bf16[1,16,8,1280]{3,2,1,0:T(8,128)(2,1)} %param.6) | copy-start | bytes 983044
  4.9 6.0 %copy-start = (bf16[1,16,8,640]{3,2,1,0:T(8,128)(2,1)S(1)}, bf16[1,16,8,640]{3,2,1,0:T(8,128)(2,1)}, u32[]{:S(2)}) copy-start(bf16[1,16,8,640]{3,2,1,0:T(8,128)(2,1)} %param.11) | copy-start | bytes 491524
  4.9 14.6 %slice-start.1 = ((s8[7372800]{0:T(1024)(128)(4,1)}), s8[3178496]{0:T(1024)(128)(4,1)S(1)}, s32[]{:S(2)}) async-start(s8[7372800]{0:T(1024)(128)(4,1)} %bitcast.20), calls=%async_computation.1 | async-start | bytes 6356992
  6.5 13.0 %copy-start.2 = (bf16[1,16,8,1280]{3,2,1,0:T(8,128)(2,1)S(1)}, bf16[1,16,8,1280]{3,2,1,0:T(8,128)(2,1)}, u32[]{:S(2)}) copy-start(bf16[1,16,8,1280]{3,2,1,0:T(8,128)(2,1)} %param.6) | copy-start | bytes 983044
  6.5 4.4 %collective-permute-start.1 = (bf16[56,640]{1,0:T(8,128)(2,1)S(1)}, bf16[56,640]{1,0:T(8,128)(2,1)S(1)}, u32[]{:S(2)}, u32[]{:S(2)}) collective-permute-start(bf16[56,640]{1,0:T(8,128)(2,1)S(1)} %get-tuple-element.29), channel_id=1, source_target_pairs={{0,16},{16,0},{1,17},{17,1},{2,18},{18,2},{3,19},{19,3},{4,20},{20... | collective-permute-start | bytes 215048 | tf_op jit(solution)/shard_map/ppermute | solution.py:373
  11.5 1.3 %collective-permute-start.3 = (bf16[24,1280]{1,0:T(8,128)(2,1)S(1)}, bf16[24,1280]{1,0:T(8,128)(2,1)S(1)}, u32[]{:S(2)}, u32[]{:S(2)}) collective-permute-start(bf16[24,1280]{1,0:T(8,128)(2,1)S(1)} %get-tuple-element.31), channel_id=1, source_target_pairs={{0,4},{4,0},{8,12},{12,8},{1,5},{5,1},{9,13},{13,9},{2,6},{6,2},{1... | collective-permute-start | bytes 184328 | tf_op jit(solution)/shard_map/ppermute | solution.py:23
  13.0 4.0 %collective-permute-start.4 = (bf16[19,1280]{1,0:T(8,128)(2,1)S(1)}, bf16[19,1280]{1,0:T(8,128)(2,1)S(1)}, u32[]{:S(2)}, u32[]{:S(2)}) collective-permute-start(bf16[19,1280]{1,0:T(8,128)(2,1)S(1)} %pad_maximum_fusion), channel_id=1, source_target_pairs={{0,12},{4,8},{8,4},{12,0},{1,13},{5,9},{9,5},{13,1},{2,14},{6,10},... | collective-permute-start | bytes 145928 | tf_op jit(solution)/shard_map/ppermute | solution.py:23
  17.8 5.0 %collective-permute-start.5 = (bf16[40,1280]{1,0:T(8,128)(2,1)S(1)}, bf16[40,1280]{1,0:T(8,128)(2,1)S(1)}, u32[]{:S(2)}, u32[]{:S(2)}) collective-permute-start(bf16[40,1280]{1,0:T(8,128)(2,1)S(1)} %get-tuple-element.35), channel_id=1, source_target_pairs={{0,1},{1,0},{2,3},{3,2},{4,5},{5,4},{6,7},{7,6},{8,9},{9,8},{10,11... | collective-permute-start | bytes 307208 | tf_op jit(solution)/shard_map/ppermute | solution.py:23
  20.1 6.1 %collective-permute-start = (bf16[16,8,640]{2,1,0:T(8,128)(2,1)S(1)}, bf16[16,8,640]{2,1,0:T(8,128)(2,1)S(1)}, u32[]{:S(2)}, u32[]{:S(2)}) collective-permute-start(bf16[16,8,640]{2,1,0:T(8,128)(2,1)S(1)} %get-tuple-element.27), channel_id=1, source_target_pairs={{0,16},{16,0},{1,17},{17,1},{2,18},{18,2},{3,19},{19,3},{4,20},{20... | collective-permute-start | bytes 491528 | tf_op jit(solution)/shard_map/ppermute | solution.py:373
  20.7 5.5 %collective-permute-start.7 = (bf16[36,1280]{1,0:T(8,128)(2,1)S(1)}, bf16[36,1280]{1,0:T(8,128)(2,1)S(1)}, u32[]{:S(2)}, u32[]{:S(2)}) collective-permute-start(bf16[36,1280]{1,0:T(8,128)(2,1)S(1)} %get-tuple-element.36), channel_id=1, source_target_pairs={{1,2},{2,1},{5,6},{6,5},{9,10},{10,9},{13,14},{14,13},{17,18},{18,... | collective-permute-start | bytes 276488 | tf_op jit(solution)/shard_map/ppermute | solution.py:23
  23.0 6.3 %copy-start.3 = (f32[1280]{0:T(1024)S(1)}, f32[1280]{0:T(1024)}, u32[]{:S(2)}) copy-start(f32[1280]{0:T(1024)} %refs_3_.1) | copy-start | bytes 15364
  23.0 6.3 %copy-start.4 = (f32[1280]{0:T(1024)S(1)}, f32[1280]{0:T(1024)}, u32[]{:S(2)}) copy-start(f32[1280]{0:T(1024)} %refs_4_.1) | copy-start | bytes 15364
  23.0 6.1 %collective-permute-start.6 = (f32[1,64]{1,0:T(1,128)S(1)}, f32[1,64]{1,0:T(1,128)S(1)}, u32[]{:S(2)}, u32[]{:S(2)}) collective-permute-start(f32[1,64]{1,0:T(1,128)S(1)} %pad_maximum_fusion.4), channel_id=1, source_target_pairs={{0,2},{1,3},{2,0},{3,1},{4,6},{5,7},{6,4},{7,5},{8,10},{9,11},{10,... | collective-permute-start | bytes 776 | tf_op jit(solution)/shard_map/ppermute | solution.py:23
  30.7 3.6 %collective-permute-start.8 = (f32[4,16]{1,0:T(4,128)S(1)}, f32[4,16]{1,0:T(4,128)S(1)}, u32[]{:S(2)}, u32[]{:S(2)}) collective-permute-start(f32[4,16]{1,0:T(4,128)S(1)} %get-tuple-element.38), channel_id=1, source_target_pairs={{16,0},{0,16},{17,1},{1,17},{18,2},{2,18},{19,3},{3,19},{20,4},{4,... | collective-permute-start | bytes 776 | tf_op jit(solution)/shard_map/ppermute | solution.py:453
  34.3 1.2 %collective-permute-start.9 = (f32[2,2,16]{2,1,0:T(2,128)S(1)}, f32[2,2,16]{2,1,0:T(2,128)S(1)}, u32[]{:S(2)}, u32[]{:S(2)}) collective-permute-start(f32[2,2,16]{2,1,0:T(2,128)S(1)} %fusion.6), channel_id=1, source_target_pairs={{0,4},{4,0},{8,12},{12,8},{1,5},{5,1},{9,13},{13,9},{2,6},{6,2},{1... | collective-permute-start | bytes 776 | tf_op jit(solution)/shard_map/ppermute | solution.py:23
  34.3 14.1 %collective-permute-start.13 = (bf16[16,8,640]{2,1,0:T(8,128)(2,1)S(1)}, bf16[16,8,640]{2,1,0:T(8,128)(2,1)S(1)}, u32[]{:S(2)}, u32[]{:S(2)}) collective-permute-start(bf16[16,8,640]{2,1,0:T(8,128)(2,1)S(1)} %bitcast.32), channel_id=1, source_target_pairs={{16,0},{0,16},{17,1},{1,17},{18,2},{2,18},{19,3},{3,19},{20,4},{4,... | collective-permute-start | bytes 491528 | tf_op jit(solution)/shard_map/ppermute | solution.py:453
  35.5 3.6 %collective-permute-start.10 = (f32[2,2,16]{2,1,0:T(2,128)S(1)}, f32[2,2,16]{2,1,0:T(2,128)S(1)}, u32[]{:S(2)}, u32[]{:S(2)}) collective-permute-start(f32[2,2,16]{2,1,0:T(2,128)S(1)} %fusion.13.after_ref), channel_id=1, source_target_pairs={{0,8},{4,12},{8,0},{12,4},{1,9},{5,13},{9,1},{13,5},{2,10},{6,14},... | collective-permute-start | bytes 776 | tf_op jit(solution)/shard_map/ppermute | solution.py:23
  36.9 11.4 %copy-start.5 = (f32[640]{0:T(1024)S(1)}, f32[640]{0:T(1024)}, u32[]{:S(2)}) copy-start(f32[640]{0:T(1024)} %bias_ref.1) | copy-start | bytes 7684
  39.0 4.7 %collective-permute-start.11 = (f32[2,2,16]{2,1,0:T(2,128)S(1)}, f32[2,2,16]{2,1,0:T(2,128)S(1)}, u32[]{:S(2)}, u32[]{:S(2)}) collective-permute-start(f32[2,2,16]{2,1,0:T(2,128)S(1)} %add_add_fusion), channel_id=1, source_target_pairs={{0,1},{1,0},{2,3},{3,2},{4,5},{5,4},{6,7},{7,6},{8,9},{9,8},{10,11... | collective-permute-start | bytes 776 | tf_op jit(solution)/shard_map/ppermute | solution.py:23
  41.8 6.6 %collective-permute-start.14 = (bf16[16,8,384]{2,1,0:T(8,128)(2,1)S(1)}, bf16[16,8,384]{2,1,0:T(8,128)(2,1)S(1)}, u32[]{:S(2)}, u32[]{:S(2)}) collective-permute-start(bf16[16,8,384]{2,1,0:T(8,128)(2,1)S(1)} %bitcast.33), channel_id=1, source_target_pairs={{16,0},{0,16},{17,1},{1,17},{18,2},{2,18},{19,3},{3,19},{20,4},{4,... | collective-permute-start | bytes 294920 | tf_op jit(solution)/shard_map/ppermute | solution.py:477
  42.8 5.6 %collective-permute-start.15 = (bf16[16,8,256]{2,1,0:T(8,128)(2,1)S(1)}, bf16[16,8,256]{2,1,0:T(8,128)(2,1)S(1)}, u32[]{:S(2)}, u32[]{:S(2)}) collective-permute-start(bf16[16,8,256]{2,1,0:T(8,128)(2,1)S(1)} %bitcast.34), channel_id=1, source_target_pairs={{16,0},{0,16},{17,1},{1,17},{18,2},{2,18},{19,3},{3,19},{20,4},{4,... | collective-permute-start | bytes 196616 | tf_op jit(solution)/shard_map/ppermute | solution.py:477
  43.8 4.6 %collective-permute-start.12 = (f32[2,2,16]{2,1,0:T(2,128)S(1)}, f32[2,2,16]{2,1,0:T(2,128)S(1)}, u32[]{:S(2)}, u32[]{:S(2)}) collective-permute-start(f32[2,2,16]{2,1,0:T(2,128)S(1)} %add.123), channel_id=1, source_target_pairs={{0,2},{1,3},{2,0},{3,1},{4,6},{5,7},{6,4},{7,5},{8,10},{9,11},{10,... | collective-permute-start | bytes 776 | tf_op jit(solution)/shard_map/ppermute | solution.py:23
